TPU v7x, 32 devices: a whole 2x2x4 slice. The times are simulated.
32 devices in a mesh: ctx: 8 (over y, x, core), fsdp: 4 (over z).
Axes of the slice: x: 2, y: 2, z: 4, core: 2. Of those that a mesh axis runs over, the one named last changes fastest.
Arguments:
- tokens: bfloat16 [8, 2048, 1536], P('fsdp', 'ctx'), may hold values from -16 to 16
- block_pairs: int32 [8, 2], replicated, may hold values from 0 to 15, as said below
- cotangent: bfloat16 [8, 2048, 1536], P('fsdp', 'ctx'), may hold values from -6 to 6
- attention_gain: bfloat16 [1536], P('fsdp'), may hold values from 0.099609375 to 1.8984375
- query_weight: bfloat16 [1536, 1536], P('fsdp'), may hold values from -0.15625 to 0.15625
- key_matrix: bfloat16 [1536, 768], P('fsdp'), may hold values from -0.15625 to 0.15625
- value_matrix: bfloat16 [1536, 768], P('fsdp'), may hold values from -0.15625 to 0.15625
- output_weight: bfloat16 [1536, 1536], P('fsdp'), may hold values from -4 to 4
- feedforward_gain: bfloat16 [1536], P('fsdp'), may hold values from 0.099609375 to 1.8984375
- gate_weight: bfloat16 [1536, 4096], P('fsdp'), may hold values from -0.15625 to 0.15625
- up_weight: bfloat16 [1536, 4096], P('fsdp'), may hold values from -0.15625 to 0.15625
- down_weight: bfloat16 [4096, 1536], P('fsdp'), may hold values from -0.09375 to 0.09375
Outputs:
- layer_out: bfloat16 [8, 2048, 1536], P('fsdp', 'ctx')
- tokens_grad: bfloat16 [8, 2048, 1536], P('fsdp', 'ctx')
- attention_gain_grad: float32 [1536], P('fsdp')
- query_grad: float32 [1536, 1536], P('fsdp')
- key_grad: float32 [1536, 768], P('fsdp')
- value_grad: float32 [1536, 768], P('fsdp')
- output_grad: float32 [1536, 1536], P('fsdp')
- feedforward_gain_grad: float32 [1536], P('fsdp')
- gate_grad: float32 [1536, 4096], P('fsdp')
- up_grad: float32 [1536, 4096], P('fsdp')
- down_grad: float32 [4096, 1536], P('fsdp')
Inputs may be any that keep to these rules, and one draw needn't show every extreme that they name: `block_pairs`: row c names block b and block 15 - b for some b below 8, in either order; every block is named once.
All inputs are finite; a program needn't handle non-finite values.
Results may differ from a plain program's by a relative error of at most 0.023.
Values may be sent and summed in bfloat16 or wider, within the bound.
A program may use at most 448 MiB of HBM per device.

v0:
```python
import math

import jax
import jax.numpy as jnp
from jax import lax
from jax.sharding import PartitionSpec as P

QUERY_HEADS = 16
KEY_HEADS = 8
HEAD_WIDTH = 96


EPS = 1e-05
THETA = 100000.0


def rope_tables(positions, head_size):
    half_size = head_size // 2
    frequency = THETA ** (-jnp.arange(half_size, dtype=jnp.float32) * 2.0 / head_size)
    angles = positions.astype(jnp.float32)[:, None] * frequency[None, :]
    cosine_lookup = jnp.cos(angles)
    sine_lookup = jnp.sin(angles)
    return (
        jnp.concatenate([cosine_lookup, cosine_lookup], -1),
        jnp.concatenate([sine_lookup, sine_lookup], -1),
    )


def rotary_apply(value_rows, cosine_lookup, sine_lookup):
    half_size = value_rows.shape[-1] // 2
    turned = jnp.concatenate([-value_rows[..., half_size:], value_rows[..., :half_size]], -1)
    return value_rows * cosine_lookup + turned * sine_lookup


def rotary_inverse(incoming, cosine_lookup, sine_lookup):
    half_size = incoming.shape[-1] // 2
    scaled = incoming * sine_lookup
    turned = jnp.concatenate([scaled[..., half_size:], -scaled[..., :half_size]], -1)
    return incoming * cosine_lookup + turned


def linear_projector(left, right):
    return jnp.dot(left, right, preferred_element_type=jnp.float32)


def project_back(left, weight):
    return lax.dot_general(
        left, weight, (((2,), (1,)), ((), ())), preferred_element_type=jnp.float32
    )


def token_outer(left, right):
    return lax.dot_general(
        left, right, (((0, 1), (0, 1)), ((), ())), preferred_element_type=jnp.float32
    )


def norm_back(incoming, unit, inverse, gain):
    scaled = incoming * gain
    return inverse * (scaled - unit * jnp.mean(scaled * unit, -1, keepdims=True))


def body(
    tokens,
    block_pairs,
    cotangent,
    attention_gain,
    query_weight,
    key_matrix,
    value_matrix,
    output_weight,
    feedforward_gain,
    gate_weight,
    up_weight,
    down_weight,
):
    sequence_count, local_length = (tokens.shape[0], tokens.shape[1])
    ctx_size = lax.axis_size("ctx")
    block_len = local_length // 2
    total_length = local_length * ctx_size
    query_group_width = QUERY_HEADS // KEY_HEADS
    score_scale = HEAD_WIDTH ** (-0.5)
    key_tile_block = math.gcd(total_length, 512)
    block_count = total_length // key_tile_block
    offsets = jnp.arange(block_len, dtype=jnp.int32)
    all_positions = (block_pairs[:, :, None] * block_len + offsets[None, None, :]).reshape(
        total_length
    )
    query_positions = lax.dynamic_slice_in_dim(
        all_positions, lax.axis_index("ctx") * local_length, local_length
    )
    cosine_lookup, sine_lookup = rope_tables(query_positions, HEAD_WIDTH)
    cosine_lookup = cosine_lookup[None, :, None, :]
    sine_lookup = sine_lookup[None, :, None, :]
    attention_set = (
        lax.all_gather(attention_gain, "fsdp", axis=0, tiled=True),
        lax.all_gather(query_weight, "fsdp", axis=0, tiled=True),
        lax.all_gather(key_matrix, "fsdp", axis=0, tiled=True),
        lax.all_gather(value_matrix, "fsdp", axis=0, tiled=True),
        lax.all_gather(output_weight, "fsdp", axis=0, tiled=True),
    )
    gain_first, query_full, key_complete, value_full, output_full = attention_set
    residual_in = tokens.astype(jnp.float32)
    inverse_first = lax.rsqrt(jnp.mean(residual_in * residual_in, -1, keepdims=True) + EPS)
    unit_first = residual_in * inverse_first
    first_normalized = (unit_first * gain_first.astype(jnp.float32)).astype(jnp.bfloat16)
    query_rows = rotary_apply(
        linear_projector(first_normalized, query_full).reshape(
            sequence_count, local_length, QUERY_HEADS, HEAD_WIDTH
        ),
        cosine_lookup,
        sine_lookup,
    ).astype(jnp.bfloat16)
    keys_local = (
        rotary_apply(
            linear_projector(first_normalized, key_complete).reshape(
                sequence_count, local_length, KEY_HEADS, HEAD_WIDTH
            ),
            cosine_lookup,
            sine_lookup,
        )
        .astype(jnp.bfloat16)
        .reshape(sequence_count, local_length, KEY_HEADS * HEAD_WIDTH)
    )
    values_local = linear_projector(first_normalized, value_full).astype(jnp.bfloat16)
    keys_all, values_all = (
        lax.all_gather(keys_local, "ctx", axis=1, tiled=True),
        lax.all_gather(values_local, "ctx", axis=1, tiled=True),
    )
    query_lattice = query_rows.reshape(
        sequence_count, local_length, KEY_HEADS, query_group_width, HEAD_WIDTH
    )

    def block_scores(block_index):
        key_offset = block_index * key_tile_block
        key_part = lax.dynamic_slice_in_dim(keys_all, key_offset, key_tile_block, 1).reshape(
            sequence_count, key_tile_block, KEY_HEADS, HEAD_WIDTH
        )
        value_part = lax.dynamic_slice_in_dim(values_all, key_offset, key_tile_block, 1).reshape(
            sequence_count, key_tile_block, KEY_HEADS, HEAD_WIDTH
        )
        key_positions = lax.dynamic_slice_in_dim(all_positions, key_offset, key_tile_block)
        scores = (
            jnp.einsum(
                "sigrd,sjgd->sgrij", query_lattice, key_part, preferred_element_type=jnp.float32
            )
            * score_scale
        )
        allowed = query_positions[:, None] >= key_positions[None, :]
        return (jnp.where(allowed, scores, -jnp.inf), key_part, value_part)

    def forward_block(running, block_index):
        row_peak, row_total, weighted = running
        scores, key_part, value_part = block_scores(block_index)
        new_peak = jnp.maximum(row_peak, jnp.max(scores, -1))
        weights = jnp.exp(scores - new_peak[..., None])
        shrink = jnp.exp(row_peak - new_peak)
        row_total = row_total * shrink + jnp.sum(weights, -1)
        weighted = weighted * shrink[..., None] + jnp.einsum(
            "sgrij,sjgd->sgrid",
            weights.astype(jnp.bfloat16),
            value_part,
            preferred_element_type=jnp.float32,
        )
        return ((new_peak, row_total, weighted), None)

    statistic_layout = (sequence_count, KEY_HEADS, query_group_width, local_length)
    start_running = (
        jnp.full(statistic_layout, -1e30, jnp.float32),
        jnp.zeros(statistic_layout, jnp.float32),
        jnp.zeros(statistic_layout + (HEAD_WIDTH,), jnp.float32),
    )
    (row_peak, row_total, weighted), unused = lax.scan(
        forward_block, start_running, jnp.arange(block_count)
    )
    attention_grid = weighted / row_total[..., None]
    log_total = row_peak + jnp.log(row_total)
    attention_rows = jnp.transpose(attention_grid, (0, 3, 1, 2, 4)).reshape(
        sequence_count, local_length, QUERY_HEADS * HEAD_WIDTH
    )
    attention_low = attention_rows.astype(jnp.bfloat16)
    residual_mid = residual_in + linear_projector(attention_low, output_full)
    inverse_second = lax.rsqrt(jnp.mean(residual_mid * residual_mid, -1, keepdims=True) + EPS)
    unit_second = residual_mid * inverse_second
    feedforward_set = (
        lax.all_gather(feedforward_gain, "fsdp", axis=0, tiled=True),
        lax.all_gather(gate_weight, "fsdp", axis=0, tiled=True),
        lax.all_gather(up_weight, "fsdp", axis=0, tiled=True),
        lax.all_gather(down_weight, "fsdp", axis=0, tiled=True),
    )
    gain_second, gate_full, up_full, down_full = feedforward_set
    normed_second = (unit_second * gain_second.astype(jnp.float32)).astype(jnp.bfloat16)
    gate_pre = linear_projector(normed_second, gate_full)
    up_pre = linear_projector(normed_second, up_full)
    sigmoid_gate = jax.nn.sigmoid(gate_pre)
    silu_gate = gate_pre * sigmoid_gate
    hidden = (silu_gate * up_pre).astype(jnp.bfloat16)
    layer_out = (residual_mid + linear_projector(hidden, down_full)).astype(jnp.bfloat16)
    gain_second, gate_full, up_full, down_full = (
        lax.all_gather(feedforward_gain, "fsdp", axis=0, tiled=True),
        lax.all_gather(gate_weight, "fsdp", axis=0, tiled=True),
        lax.all_gather(up_weight, "fsdp", axis=0, tiled=True),
        lax.all_gather(down_weight, "fsdp", axis=0, tiled=True),
    )
    down_grad = token_outer(hidden, cotangent)
    hidden_grad = project_back(cotangent, down_full)
    gate_low = (
        hidden_grad * up_pre * sigmoid_gate * (1.0 + gate_pre * (1.0 - sigmoid_gate))
    ).astype(jnp.bfloat16)
    up_low = (hidden_grad * silu_gate).astype(jnp.bfloat16)
    gate_grad = token_outer(normed_second, gate_low)
    up_grad = token_outer(normed_second, up_low)
    normed_second_grad = project_back(gate_low, gate_full) + project_back(up_low, up_full)
    feedforward_gain_grad = jnp.sum(normed_second_grad * unit_second, axis=(0, 1))
    middle_grad = cotangent.astype(jnp.float32) + norm_back(
        normed_second_grad, unit_second, inverse_second, gain_second.astype(jnp.float32)
    )
    gain_share, gate_share, up_share, down_share = (
        lax.psum_scatter(
            feedforward_gain_grad.astype(jnp.bfloat16), "fsdp", scatter_dimension=0, tiled=True
        ).astype(jnp.float32),
        lax.psum_scatter(
            gate_grad.astype(jnp.bfloat16), "fsdp", scatter_dimension=0, tiled=True
        ).astype(jnp.float32),
        lax.psum_scatter(
            up_grad.astype(jnp.bfloat16), "fsdp", scatter_dimension=0, tiled=True
        ).astype(jnp.float32),
        lax.psum_scatter(
            down_grad.astype(jnp.bfloat16), "fsdp", scatter_dimension=0, tiled=True
        ).astype(jnp.float32),
    )
    feedforward_results = (
        lax.psum(gain_share.astype(jnp.bfloat16), "ctx").astype(jnp.float32),
        lax.psum(gate_share.astype(jnp.bfloat16), "ctx").astype(jnp.float32),
        lax.psum(up_share.astype(jnp.bfloat16), "ctx").astype(jnp.float32),
        lax.psum(down_share.astype(jnp.bfloat16), "ctx").astype(jnp.float32),
    )
    gain_first, query_full, key_complete, value_full, output_full = (
        lax.all_gather(attention_gain, "fsdp", axis=0, tiled=True),
        lax.all_gather(query_weight, "fsdp", axis=0, tiled=True),
        lax.all_gather(key_matrix, "fsdp", axis=0, tiled=True),
        lax.all_gather(value_matrix, "fsdp", axis=0, tiled=True),
        lax.all_gather(output_weight, "fsdp", axis=0, tiled=True),
    )
    middle_low = middle_grad.astype(jnp.bfloat16)
    output_grad = token_outer(attention_low, middle_low)
    attention_backward = project_back(middle_low, output_full).astype(jnp.bfloat16)
    backward_lattice = attention_backward.reshape(
        sequence_count, local_length, KEY_HEADS, query_group_width, HEAD_WIDTH
    )
    row_delta = jnp.sum(
        attention_grid * jnp.transpose(backward_lattice.astype(jnp.float32), (0, 2, 3, 1, 4)), -1
    )

    def backward_block(running, block_index):
        query_total, key_gradient_sum, value_gradient_sum = running
        scores, key_part, value_part = block_scores(block_index)
        probability = jnp.exp(scores - log_total[..., None])
        value_gradient_term = jnp.einsum(
            "sgrij,sigrd->sjgd",
            probability.astype(jnp.bfloat16),
            backward_lattice,
            preferred_element_type=jnp.float32,
        )
        prob_grad = jnp.einsum(
            "sigrd,sjgd->sgrij", backward_lattice, value_part, preferred_element_type=jnp.float32
        )
        score_low = (probability * (prob_grad - row_delta[..., None])).astype(jnp.bfloat16)
        query_total = (
            query_total
            + jnp.einsum(
                "sgrij,sjgd->sigrd", score_low, key_part, preferred_element_type=jnp.float32
            )
            * score_scale
        )
        key_gradient_term = (
            jnp.einsum(
                "sgrij,sigrd->sjgd", score_low, query_lattice, preferred_element_type=jnp.float32
            )
            * score_scale
        )
        key_offset = block_index * key_tile_block
        key_gradient_sum = lax.dynamic_update_slice_in_dim(
            key_gradient_sum,
            key_gradient_term.reshape(sequence_count, key_tile_block, KEY_HEADS * HEAD_WIDTH),
            key_offset,
            1,
        )
        value_gradient_sum = lax.dynamic_update_slice_in_dim(
            value_gradient_sum,
            value_gradient_term.reshape(sequence_count, key_tile_block, KEY_HEADS * HEAD_WIDTH),
            key_offset,
            1,
        )
        return ((query_total, key_gradient_sum, value_gradient_sum), None)

    pairwise_layout = (sequence_count, total_length, KEY_HEADS * HEAD_WIDTH)
    start_back = (
        jnp.zeros(
            (sequence_count, local_length, KEY_HEADS, query_group_width, HEAD_WIDTH), jnp.float32
        ),
        jnp.zeros(pairwise_layout, jnp.float32),
        jnp.zeros(pairwise_layout, jnp.float32),
    )
    (query_total, key_gradient_sum, value_gradient_sum), unused = lax.scan(
        backward_block, start_back, jnp.arange(block_count)
    )
    key_portion, value_share = (
        lax.psum_scatter(
            key_gradient_sum.astype(jnp.bfloat16), "ctx", scatter_dimension=1, tiled=True
        ).astype(jnp.float32),
        lax.psum_scatter(
            value_gradient_sum.astype(jnp.bfloat16), "ctx", scatter_dimension=1, tiled=True
        ).astype(jnp.float32),
    )
    query_low = (
        rotary_inverse(
            query_total.reshape(sequence_count, local_length, QUERY_HEADS, HEAD_WIDTH),
            cosine_lookup,
            sine_lookup,
        )
        .astype(jnp.bfloat16)
        .reshape(sequence_count, local_length, QUERY_HEADS * HEAD_WIDTH)
    )
    key_low = (
        rotary_inverse(
            key_portion.reshape(sequence_count, local_length, KEY_HEADS, HEAD_WIDTH),
            cosine_lookup,
            sine_lookup,
        )
        .astype(jnp.bfloat16)
        .reshape(sequence_count, local_length, KEY_HEADS * HEAD_WIDTH)
    )
    value_low = value_share.astype(jnp.bfloat16)
    query_grad = token_outer(first_normalized, query_low)
    key_grad = token_outer(first_normalized, key_low)
    value_grad = token_outer(first_normalized, value_low)
    normed_first_grad = (
        project_back(query_low, query_full)
        + project_back(key_low, key_complete)
        + project_back(value_low, value_full)
    )
    attention_gain_grad = jnp.sum(normed_first_grad * unit_first, axis=(0, 1))
    tokens_grad = (
        middle_grad
        + norm_back(normed_first_grad, unit_first, inverse_first, gain_first.astype(jnp.float32))
    ).astype(jnp.bfloat16)
    again_gain, again_query, again_key, again_value, again_output = (
        lax.psum_scatter(
            attention_gain_grad.astype(jnp.bfloat16), "fsdp", scatter_dimension=0, tiled=True
        ).astype(jnp.float32),
        lax.psum_scatter(
            query_grad.astype(jnp.bfloat16), "fsdp", scatter_dimension=0, tiled=True
        ).astype(jnp.float32),
        lax.psum_scatter(
            key_grad.astype(jnp.bfloat16), "fsdp", scatter_dimension=0, tiled=True
        ).astype(jnp.float32),
        lax.psum_scatter(
            value_grad.astype(jnp.bfloat16), "fsdp", scatter_dimension=0, tiled=True
        ).astype(jnp.float32),
        lax.psum_scatter(
            output_grad.astype(jnp.bfloat16), "fsdp", scatter_dimension=0, tiled=True
        ).astype(jnp.float32),
    )
    attention_results = (
        lax.psum(again_gain.astype(jnp.bfloat16), "ctx").astype(jnp.float32),
        lax.psum(again_query.astype(jnp.bfloat16), "ctx").astype(jnp.float32),
        lax.psum(again_key.astype(jnp.bfloat16), "ctx").astype(jnp.float32),
        lax.psum(again_value.astype(jnp.bfloat16), "ctx").astype(jnp.float32),
        lax.psum(again_output.astype(jnp.bfloat16), "ctx").astype(jnp.float32),
    )
    return (
        layer_out,
        tokens_grad,
        attention_results[0],
        attention_results[1],
        attention_results[2],
        attention_results[3],
        attention_results[4],
        feedforward_results[0],
        feedforward_results[1],
        feedforward_results[2],
        feedforward_results[3],
    )


def solution(mesh):
    in_specs = (
        P("fsdp", "ctx", None),
        P(),
        P("fsdp", "ctx", None),
        P("fsdp"),
        P("fsdp", None),
        P("fsdp", None),
        P("fsdp", None),
        P("fsdp", None),
        P("fsdp"),
        P("fsdp", None),
        P("fsdp", None),
        P("fsdp", None),
    )
    out_specs = (
        P("fsdp", "ctx", None),
        P("fsdp", "ctx", None),
        P("fsdp"),
        P("fsdp", None),
        P("fsdp", None),
        P("fsdp", None),
        P("fsdp", None),
        P("fsdp"),
        P("fsdp", None),
        P("fsdp", None),
        P("fsdp", None),
    )
    return jax.shard_map(body, mesh=mesh, in_specs=in_specs, out_specs=out_specs, check_vma=False)
```

profile of v0, /device:TPU:0, one launch (start us, length us, event | category | flops | bytes accessed | tf_op | source)
XLA Modules:
  0.0 2567.5 jit_solution(8835168845323018607)
XLA Ops:
  10.1 13.5 all-gather
  26.9 35.9 %all-gather.12.cloned.1.call-done = bf16[1536,768]{1,0:T(8,128)(2,1)} async-done(((bf16[384,768]{1,0:T(8,128)(2,1)}), bf16[1536,768]{1,0:T(8,128)(2,1)}) %all-gather.12.cloned.1.call-update) | async-done | bytes 2359312 | tf_op jit(solution)/shard_map/all_gather | solution.py:98
  79.1 34.6 %all-gather.18.cloned.1.call-done = bf16[1536,768]{1,0:T(8,128)(2,1)} async-done(((bf16[384,768]{1,0:T(8,128)(2,1)}), bf16[1536,768]{1,0:T(8,128)(2,1)}) %all-gather.18.cloned.1.call-update) | async-done | bytes 2359312 | tf_op jit(solution)/shard_map/all_gather | solution.py:99
  120.6 12.0 all-gather.1
  132.7 70.9 %all-gather.16.cloned.1.call-done = bf16[1536,1536]{1,0:T(8,128)(2,1)} async-done(((bf16[384,1536]{1,0:T(8,128)(2,1)}), bf16[1536,1536]{1,0:T(8,128)(2,1)}) %all-gather.16.cloned.1.call-update) | async-done | bytes 4718608 | tf_op jit(solution)/shard_map/all_gather | solution.py:97
  209.4 40.6 %all-gather.14.cloned.1.call-done = bf16[2,2048,768]{2,1,0:T(8,128)(2,1)} async-done(((bf16[2,256,768]{2,1,0:T(8,128)(2,1)}), bf16[2,2048,768]{2,1,0:T(8,128)(2,1)}) %all-gather.14.cloned.1.call-update) | async-done | bytes 6291472 | tf_op jit(solution)/shard_map/all_gather | solution.py:127
  258.5 39.3 %all-gather.20.cloned.1.call-done = bf16[2,2048,768]{2,1,0:T(8,128)(2,1)} async-done(((bf16[2,256,768]{2,1,0:T(8,128)(2,1)}), bf16[2,2048,768]{2,1,0:T(8,128)(2,1)}) %all-gather.20.cloned.1.call-update) | async-done | bytes 6291472 | tf_op jit(solution)/shard_map/all_gather | solution.py:128
  306.4 137.9 %while.30 = (s32[]{:T(128)}, f32[2,8,2,256]{3,2,1,0:T(2,128)S(1)}, f32[2,8,2,256]{3,2,1,0:T(2,128)S(1)}, f32[2,8,2,256,96]{3,4,2,1,0:T(8,128)}, s32[256]{0:T(256...) while((s32[]{:T(128)}, f32[2,8,2,256]{3,2,1,0:T(2,128)S(1)}, ...), condition=%wide.region_4.5_spmd.clone, body=%wide.region_1.4_spmd.clone.sunk | while | flops 1659281408 | bytes 74980584 | solution.py:173
  318.9 9.4 fusion.156
  328.5 11.7 fusion.158
  352.1 9.4 fusion.156
  361.6 12.6 fusion.158
  386.1 9.3 fusion.156
  395.5 14.8 fusion.158
  422.3 9.4 fusion.156
  431.8 12.5 fusion.158
  455.4 151.6 %all-gather.26.cloned.1.call-done = bf16[1536,4096]{1,0:T(8,128)(2,1)} async-done(((bf16[384,4096]{1,0:T(8,128)(2,1)}), bf16[1536,4096]{1,0:T(8,128)(2,1)}) %all-gather.26.cloned.1.call-update) | async-done | bytes 12582928 | tf_op jit(solution)/shard_map/all_gather | solution.py:188
  606.9 24.3 fusion.29
  631.2 193.7 %all-gather.28.cloned.1.call-done = bf16[4096,1536]{1,0:T(8,128)(2,1)} async-done(((bf16[1024,1536]{1,0:T(8,128)(2,1)}), bf16[4096,1536]{1,0:T(8,128)(2,1)}) %all-gather.28.cloned.1.call-update) | async-done | bytes 12582928 | tf_op jit(solution)/shard_map/all_gather | solution.py:189
  824.9 12.1 fusion.23
  837.1 205.9 %all-gather.24.cloned.1.call-done = bf16[1536,4096]{1,0:T(8,128)(2,1)} async-done(((bf16[384,4096]{1,0:T(8,128)(2,1)}), bf16[1536,4096]{1,0:T(8,128)(2,1)}) %all-gather.24.cloned.1.call-update) | async-done | bytes 12582928 | tf_op jit(solution)/shard_map/all_gather | solution.py:187
  1042.9 19.9 multiply_convert_fusion.1
  1062.8 10.7 fusion.27
  1073.6 11.9 multiply_reduce_fusion
  1103.2 206.1 %while.31 = (s32[]{:T(128)}, f32[2,256,8,2,96]{1,4,3,2,0:T(8,128)}, bf16[2,2048,768]{2,1,0:T(8,128)(2,1)}, bf16[2,2048,768]{1,2,0:T(8,128)(2,1)}, s32[4]{0:T(128...) while((s32[]{:T(128)}, f32[2,256,8,2,96]{1,4,3,2,0:T(8,128)}, ...), condition=%wide.region_9.10_spmd.clone, body=%wide.region_8.9_spmd.clone.sunk | while | flops 4072538112 | bytes 145726736 | solution.py:305
  1114.8 11.5 fusion.170
  1129.7 9.1 fusion.171
  1165.5 11.5 fusion.170
  1180.5 9.1 fusion.171
  1217.2 11.5 fusion.170
  1232.1 9.1 fusion.171
  1268.8 11.5 fusion.170
  1327.7 41.7 %reduce-scatter.10.cloned.1.call-done = bf16[2,256,768]{2,1,0:T(8,128)(2,1)} async-done(((bf16[2,2048,768]{2,1,0:T(8,128)(2,1)}), bf16[2,256,768]{2,1,0:T(8,128)(2,1)}) %reduce-scatter.10.cloned.1.call-update) | async-done | bytes 786448 | tf_op jit(solution)/shard_map/reduce_scatter | solution.py:309
  1380.3 54.7 %reduce-scatter.12.cloned.1.call-done = bf16[2,256,768]{1,2,0:T(8,128)(2,1)} async-done(((bf16[2,2048,768]{1,2,0:T(8,128)(2,1)}), bf16[2,256,768]{1,2,0:T(8,128)(2,1)}) %reduce-scatter.12.cloned.1.call-update) | async-done | bytes 786448 | tf_op jit(solution)/shard_map/reduce_scatter | solution.py:312
  1439.4 11.7 bitcast_convert_fusion.2
  1451.2 11.6 bitcast_convert_fusion.1
  1462.9 11.7 bitcast_convert_fusion
  1474.9 48.1 %reduce-scatter.14.cloned.1.call-done = bf16[384,1536]{1,0:T(8,128)(2,1)} async-done(((bf16[1536,1536]{1,0:T(8,128)(2,1)}), bf16[384,1536]{1,0:T(8,128)(2,1)}) %reduce-scatter.14.cloned.1.call-update) | async-done | bytes 1179664 | tf_op jit(solution)/shard_map/reduce_scatter | solution.py:352
  1523.0 88.7 %reduce-scatter.20.cloned.1.call-done = bf16[384,1536]{1,0:T(8,128)(2,1)} async-done(((bf16[1536,1536]{1,0:T(8,128)(2,1)}), bf16[384,1536]{1,0:T(8,128)(2,1)}) %reduce-scatter.20.cloned.1.call-update) | async-done | bytes 1179664 | tf_op jit(solution)/shard_map/reduce_scatter | solution.py:361
  1611.7 51.3 %reduce-scatter.16.cloned.1.call-done = bf16[384,768]{1,0:T(8,128)(2,1)} async-done(((bf16[1536,768]{1,0:T(8,128)(2,1)}), bf16[384,768]{1,0:T(8,128)(2,1)}) %reduce-scatter.16.cloned.1.call-update) | async-done | bytes 589840 | tf_op jit(solution)/shard_map/reduce_scatter | solution.py:355
  1663.0 50.3 %reduce-scatter.18.cloned.1.call-done = bf16[384,768]{1,0:T(8,128)(2,1)} async-done(((bf16[1536,768]{1,0:T(8,128)(2,1)}), bf16[384,768]{1,0:T(8,128)(2,1)}) %reduce-scatter.18.cloned.1.call-update) | async-done | bytes 589840 | tf_op jit(solution)/shard_map/reduce_scatter | solution.py:358
  1713.3 213.6 %reduce-scatter.22.cloned.1.call-done = bf16[384,4096]{1,0:T(8,128)(2,1)} async-done(((bf16[1536,4096]{1,0:T(8,128)(2,1)}), bf16[384,4096]{1,0:T(8,128)(2,1)}) %reduce-scatter.22.cloned.1.call-update) | async-done | bytes 3145744 | tf_op jit(solution)/shard_map/reduce_scatter | solution.py:222
  1926.9 215.1 %reduce-scatter.24.cloned.1.call-done = bf16[384,4096]{1,0:T(8,128)(2,1)} async-done(((bf16[1536,4096]{1,0:T(8,128)(2,1)}), bf16[384,4096]{1,0:T(8,128)(2,1)}) %reduce-scatter.24.cloned.1.call-update) | async-done | bytes 3145744 | tf_op jit(solution)/shard_map/reduce_scatter | solution.py:225
  2142.0 215.1 %reduce-scatter.26.cloned.1.call-done = bf16[1024,1536]{1,0:T(8,128)(2,1)} async-done(((bf16[4096,1536]{1,0:T(8,128)(2,1)}), bf16[1024,1536]{1,0:T(8,128)(2,1)}) %reduce-scatter.26.cloned.1.call-update) | async-done | bytes 3145744 | tf_op jit(solution)/shard_map/reduce_scatter | solution.py:228
  2364.3 10.7 fusion.71
  2380.6 11.6 all-reduce.4
  2392.4 12.4 all-reduce.2
  2410.9 131.4 %all-reduce.7.cloned.1.call-done = (bf16[384,1536]{1,0:T(8,128)(2,1)}, bf16[384,768]{1,0:T(8,128)(2,1)}, bf16[384,768]{1,0:T(8,128)(2,1)}, bf16[384,1536]{1,0:T(...) async-done(((bf16[384,1536]{1,0:T(8,128)(2,1)}, bf16[384,768]{1,0:T(8,128)(2,1)}, bf16[384,768]{1,0:T(8,128)(2,1)}, ...) | async-done | bytes 12976144 | tf_op jit(solution)/shard_map/psum | solution.py:367
  (286 shorter events, 326.5 us)
Async XLA Ops:
  7.2 55.6 %all-gather.12.cloned.1.call-start = ((), (), s32[]{:S(2)}) async-start(), calls=%async_computation.9 | async-start | bytes 2949120 | tf_op jit(solution)/shard_map/all_gather | solution.py:98
  7.9 105.8 %all-gather.18.cloned.1.call-start = ((), (), s32[]{:S(2)}) async-start(), calls=%async_computation.12 | async-start | bytes 2949120 | tf_op jit(solution)/shard_map/all_gather | solution.py:99
  8.7 17.9 copy-start.6
  8.7 194.9 %all-gather.16.cloned.1.call-start = ((), (), s32[]{:S(2)}) async-start(), calls=%async_computation.11 | async-start | bytes 5898240 | tf_op jit(solution)/shard_map/all_gather | solution.py:97
  9.4 240.5 %all-gather.14.cloned.1.call-start = ((), (), s32[]{:S(2)}) async-start(), calls=%async_computation.10 | async-start | bytes 7077888 | tf_op jit(solution)/shard_map/all_gather | solution.py:127
  23.7 179.8 %copy-start.28 = (f32[1536]{0:T(1024)}, f32[1536]{0:T(1024)S(1)}, u32[]{:S(2)}) copy-start(f32[1536]{0:T(1024)S(1)} %reshape.141) | copy-start | bytes 18436
  24.9 183.6 %copy-start.17 = (f32[256,96]{0,1:T(8,128)}, f32[256,96]{0,1:T(8,128)S(1)}, u32[]{:S(2)}) copy-start(f32[256,96]{0,1:T(8,128)S(1)} %get-tuple-element.373) | copy-start | bytes 294916
  25.0 183.6 %copy-start.20 = (f32[256,96]{0,1:T(8,128)}, f32[256,96]{0,1:T(8,128)S(1)}, u32[]{:S(2)}) copy-start(f32[256,96]{0,1:T(8,128)S(1)} %get-tuple-element.372) | copy-start | bytes 294916
  25.3 50.6 %copy-start.12 = (f32[256,768]{1,0:T(8,128)}, f32[256,768]{1,0:T(8,128)S(1)}, u32[]{:S(2)}) copy-start(f32[256,768]{1,0:T(8,128)S(1)} %copy.88) | copy-start | bytes 2359300
  26.9 176.6 %copy-start.30 = (f32[2,256]{1,0:T(2,128)}, f32[2,256]{1,0:T(2,128)S(1)}, u32[]{:S(2)}) copy-start(f32[2,256]{1,0:T(2,128)S(1)} %add_rsqrt_fusion.1) | copy-start | bytes 6148
  71.7 4.3 copy-start.16
  79.0 218.8 %all-gather.20.cloned.1.call-start = ((), (), s32[]{:S(2)}) async-start(), calls=%async_computation.13 | async-start | bytes 7077888 | tf_op jit(solution)/shard_map/all_gather | solution.py:128
  117.7 330.2 %all-gather.22.cloned.1.call-start = ((), (), s32[]{:S(2)}) async-start(), calls=%async_computation.14 | async-start | bytes 5898240 | tf_op jit(solution)/shard_map/all_gather | solution.py:100
  118.3 488.7 %all-gather.26.cloned.1.call-start = ((), (), s32[]{:S(2)}) async-start(), calls=%async_computation.16 | async-start | bytes 15728640 | tf_op jit(solution)/shard_map/all_gather | solution.py:188
  119.0 705.9 %all-gather.28.cloned.1.call-start = ((), (), s32[]{:S(2)}) async-start(), calls=%async_computation.17 | async-start | bytes 15728640 | tf_op jit(solution)/shard_map/all_gather | solution.py:189
  119.8 923.1 %all-gather.24.cloned.1.call-start = ((), (), s32[]{:S(2)}) async-start(), calls=%async_computation.15 | async-start | bytes 15728640 | tf_op jit(solution)/shard_map/all_gather | solution.py:187
  120.5 1248.9 %reduce-scatter.10.cloned.1.call-start = ((), (), s32[]{:S(2)}) async-start(), calls=%async_computation.18 | async-start | bytes 7077888 | tf_op jit(solution)/shard_map/reduce_scatter | solution.py:309
  318.9 9.5 copy-start.2
  352.1 9.5 copy-start.2
  386.1 9.4 copy-start.2
  422.3 9.5 copy-start.2
  444.4 3.5 copy-start.7
  455.3 587.6 %copy-start.23 = (bf16[2,256,1536]{2,1,0:T(8,128)(2,1)}, bf16[2,256,1536]{2,1,0:T(8,128)(2,1)S(1)}, u32[]{:S(2)}) copy-start(bf16[2,256,1536]{2,1,0:T(8,128)(2,1)S(1)} %multiply_convert_fusion.3) | copy-start | bytes 4718596
  1062.8 10.8 copy-start.4
  1062.8 26.6 %slice-start = ((s8[4718592]{0:T(1024)(128)(4,1)}), s8[4194304]{0:T(1024)(128)(4,1)S(1)}, s32[]{:S(2)}) async-start(s8[4718592]{0:T(1024)(128)(4,1)} %bitcast.273), calls=%async_computation.28 | async-start | bytes 8388608
  1073.6 15.9 slice-start.1
  1138.8 3.9 copy-start
  1189.6 3.9 copy-start
  1241.2 3.9 copy-start
  1292.9 3.9 copy-start
  1309.4 125.7 %reduce-scatter.12.cloned.1.call-start = ((), (), s32[]{:S(2)}) async-start(), calls=%async_computation.19 | async-start | bytes 7077888 | tf_op jit(solution)/shard_map/reduce_scatter | solution.py:312
  1310.1 212.9 %reduce-scatter.14.cloned.1.call-start = ((), (), s32[]{:S(2)}) async-start(), calls=%async_computation.20 | async-start | bytes 5898240 | tf_op jit(solution)/shard_map/reduce_scatter | solution.py:352
  1319.6 292.1 %reduce-scatter.20.cloned.1.call-start = ((), (), s32[]{:S(2)}) async-start(), calls=%async_computation.23 | async-start | bytes 5898240 | tf_op jit(solution)/shard_map/reduce_scatter | solution.py:361
  1327.7 335.4 %reduce-scatter.16.cloned.1.call-start = ((), (), s32[]{:S(2)}) async-start(), calls=%async_computation.21 | async-start | bytes 2949120 | tf_op jit(solution)/shard_map/reduce_scatter | solution.py:355
  1371.1 4.4 copy-start.13
  1372.3 5.0 copy-start.9
  1380.3 333.0 %reduce-scatter.18.cloned.1.call-start = ((), (), s32[]{:S(2)}) async-start(), calls=%async_computation.22 | async-start | bytes 2949120 | tf_op jit(solution)/shard_map/reduce_scatter | solution.py:358
  1439.2 487.7 %reduce-scatter.22.cloned.1.call-start = ((), (), s32[]{:S(2)}) async-start(), calls=%async_computation.24 | async-start | bytes 15728640 | tf_op jit(solution)/shard_map/reduce_scatter | solution.py:222
  1451.1 690.9 %reduce-scatter.24.cloned.1.call-start = ((), (), s32[]{:S(2)}) async-start(), calls=%async_computation.25 | async-start | bytes 15728640 | tf_op jit(solution)/shard_map/reduce_scatter | solution.py:225
  1462.8 894.3 %reduce-scatter.26.cloned.1.call-start = ((), (), s32[]{:S(2)}) async-start(), calls=%async_computation.26 | async-start | bytes 15728640 | tf_op jit(solution)/shard_map/reduce_scatter | solution.py:228
  1474.6 1067.7 %all-reduce.7.cloned.1.call-start = ((), (), s32[]{:S(2)}) async-start(), calls=%async_computation.27 | async-start | bytes 25952256 | tf_op jit(solution)/shard_map/psum | solution.py:367
  2359.0 5.2 copy-start.5
  2359.1 5.2 copy-start.37
  2364.3 10.8 copy-start.19
  2376.9 3.7 copy-start.32
  2542.3 5.5 copy-start.15
  2547.8 3.5 copy-start.14
  2551.3 3.6 copy-start.25
  (17 other events, 30.8 us)
Sparse Core Ops, SparseCore 0:
  9.6 53.1 all-gather.11
  64.4 49.2 all-gather.17
  115.3 88.2 all-gather.15
  205.9 44.0 all-gather.13
  252.2 45.5 all-gather.19
  299.2 89.4 all-gather.21
  390.2 216.6 all-gather.25
  608.5 216.3 all-gather.27
  826.5 216.3 all-gather.23
  1309.5 59.9 reduce-scatter.9
  1373.2 61.7 reduce-scatter.11
  1437.7 85.2 reduce-scatter.13
  1525.9 85.7 reduce-scatter.19
  1614.4 48.5 reduce-scatter.15
  1665.7 47.5 reduce-scatter.17
  1715.5 211.3 reduce-scatter.21
  1929.1 212.8 reduce-scatter.23
  2144.2 212.8 reduce-scatter.25
  2362.1 180.1 all-reduce.6
where the time goes:
time: 2580 us; the launch traced here: 2570 us
  waiting for transfers between devices  1890 us (73%)
  matrix products  413 us (16%)
  local copies, waits for them, and re-layouts  108 us (4%)
  other arithmetic  85.8 us (3%)
  blocking collectives  49.5 us (2%)
    reduce_scatter x1, waiting for transfers between devices, body(): lax.psum_scatter(down_grad.astype(jnp.bfloat16), 'fsdp', scatter_dimensio...  215 us
    reduce_scatter x1, waiting for transfers between devices, body(): lax.psum_scatter(up_grad.astype(jnp.bfloat16), 'fsdp', scatter_dimension=...  215 us
    reduce_scatter x1, waiting for transfers between devices, body(): lax.psum_scatter(gate_grad.astype(jnp.bfloat16), 'fsdp', scatter_dimensio...  214 us
    all_gather x1, waiting for transfers between devices, body(): lax.all_gather(gate_weight, 'fsdp', axis=0, tiled=True)  206 us
    all_gather x1, waiting for transfers between devices, body(): lax.all_gather(down_weight, 'fsdp', axis=0, tiled=True)  194 us
    all_gather x1, waiting for transfers between devices, body(): lax.all_gather(up_weight, 'fsdp', axis=0, tiled=True)  152 us
    psum x1, waiting for transfers between devices, body(): lax.psum(again_query.astype(jnp.bfloat16), 'ctx').astype(jnp.float32)  131 us
    reduce_scatter x1, waiting for transfers between devices, body(): lax.psum_scatter(output_grad.astype(jnp.bfloat16), 'fsdp', scatter_dimens...  88.7 us
  transfers between devices with their start and end apart: 19, of which 18 were waited for; matrix products, arithmetic and copies ran while one was open for 12% of the time, Pallas kernels for 0%

commit v1 on v0

v1 whole, which is shorter than its diff:
```python
import functools

import jax
import jax.numpy as jnp
from jax import lax
from jax.experimental import pallas as pl
from jax.experimental.pallas import tpu as pltpu
from jax.sharding import PartitionSpec as P

QUERY_HEADS = 16
KEY_HEADS = 8
HEAD_WIDTH = 96
EPS = 1e-05
THETA = 100000.0
BLK = 128
SCALE = HEAD_WIDTH ** -0.5
BF = jnp.bfloat16
F32 = jnp.float32

LOG2E = 1.4426950408889634

def attn_setup(nchip, g_refs, nat, tr):
    for r in range(nchip):
        for j in range(g_refs[r].shape[1] // 128):
            n = r * (g_refs[r].shape[1] // 128) + j
            block = g_refs[r][:, 128 * j:128 * (j + 1)]
            if nat is not None:
                nat[n] = block.T
            if tr is not None:
                tr[n] = block


def fwd_kernel(nchip, scale, ids_ref, inv_ref, q_ref, *rest):
    k_refs, v_refs = rest[:nchip], rest[nchip:2 * nchip]
    o_ref, lse_ref, knat, vtr, qs, m_s, l_s, acc = rest[2 * nchip:]
    nq = q_ref.shape[1] // 128
    nb = knat.shape[0]
    c = scale * LOG2E
    attn_setup(nchip, k_refs, knat, None)
    attn_setup(nchip, v_refs, None, vtr)
    for qi in range(nq):
        qs[qi] = jnp.concatenate([q_ref[0:96, 128 * qi:128 * (qi + 1)], q_ref[96:192, 128 * qi:128 * (qi + 1)]], axis=1)
    m_s[...] = jnp.full(m_s.shape, -1e30, jnp.float32)
    l_s[...] = jnp.zeros(l_s.shape, jnp.float32)
    acc[...] = jnp.zeros(acc.shape, jnp.float32)
    diff = lax.broadcasted_iota(jnp.int32, (128, 256), 0) - lax.rem(lax.broadcasted_iota(jnp.int32, (128, 256), 1), 128)

    def step(t, _):
        for sl in range(nq // 2):
            first = ids_ref[2 * sl]
            late = (t > first).astype(jnp.int32)
            qi = 2 * sl + late
            kpos = t - late * (first + 1)
            qid = ids_ref[qi]
            n = inv_ref[kpos]
            s = jnp.dot(knat[n], qs[qi], preferred_element_type=jnp.float32)
            s = jnp.where(diff <= (qid - kpos) * 128, s, -jnp.inf)
            m_old = m_s[qi]
            m_new = jnp.maximum(m_old, jnp.max(s, axis=0, keepdims=True))
            p = jnp.exp2((s - m_new) * c)
            alpha = jnp.exp2((m_old - m_new) * c)
            l_s[qi] = l_s[qi] * alpha + jnp.sum(p, axis=0, keepdims=True)
            m_s[qi] = m_new
            acc[qi] = acc[qi] * alpha + jnp.dot(vtr[n], p.astype(jnp.bfloat16), preferred_element_type=jnp.float32)
        return 0

    lax.fori_loop(0, nb + 1, step, 0)
    for qi in range(nq):
        l = l_s[qi]
        o = acc[qi] / l
        lse_ref[qi] = m_s[qi] * c + jnp.log2(l)
        o_ref[0:96, 128 * qi:128 * (qi + 1)] = o[:, :128].astype(jnp.bfloat16)
        o_ref[96:192, 128 * qi:128 * (qi + 1)] = o[:, 128:].astype(jnp.bfloat16)


def attn_fwd(ids, inv, qT, ks, vs, heads):
    nchip = len(ks)
    T = qT.shape[1]
    nq = T // 128
    nb = nchip * nq
    grid_spec = pltpu.PrefetchScalarGridSpec(
        num_scalar_prefetch=2,
        grid=(heads,),
        in_specs=[pl.BlockSpec((192, T), lambda g, *_: (g, 0))] + [pl.BlockSpec((96, T), lambda g, *_: (g, 0))] * (2 * nchip),
        out_specs=[pl.BlockSpec((192, T), lambda g, *_: (g, 0)), pl.BlockSpec((None, nq, 1, 256), lambda g, *_: (g, 0, 0, 0))],
        scratch_shapes=[
            pltpu.VMEM((nb, 128, 96), jnp.bfloat16),
            pltpu.VMEM((nb, 96, 128), jnp.bfloat16),
            pltpu.VMEM((nq, 96, 256), jnp.bfloat16),
            pltpu.VMEM((nq, 1, 256), jnp.float32),
            pltpu.VMEM((nq, 1, 256), jnp.float32),
            pltpu.VMEM((nq, 96, 256), jnp.float32),
        ],
    )
    return pl.pallas_call(
        functools.partial(fwd_kernel, nchip, SCALE),
        grid_spec=grid_spec,
        out_shape=[jax.ShapeDtypeStruct((heads * 192, T), jnp.bfloat16), jax.ShapeDtypeStruct((heads, nq, 1, 256), jnp.float32)],
        name="attention_forward",
    )(ids, inv, qT, *ks, *vs)


def bwd_kernel(nchip, scale, ids_ref, inv_ref, q_ref, o_ref, do_ref, lse_ref, *rest):
    k_refs, v_refs = rest[:nchip], rest[nchip:2 * nchip]
    dq_ref = rest[2 * nchip]
    dk_refs, dv_refs = rest[2 * nchip + 1:3 * nchip + 1], rest[3 * nchip + 1:4 * nchip + 1]
    knat, ktr, vnat, qs, dos, delta, dq_s, dk_s, dv_s = rest[4 * nchip + 1:]
    nq = q_ref.shape[1] // 128
    nb = knat.shape[0]
    nsl = nq // 2
    c = scale * LOG2E
    attn_setup(nchip, k_refs, knat, ktr)
    attn_setup(nchip, v_refs, vnat, None)
    for qi in range(nq):
        lanes = slice(128 * qi, 128 * (qi + 1))
        qs[qi] = jnp.concatenate([q_ref[0:96, lanes], q_ref[96:192, lanes]], axis=1)
        do = jnp.concatenate([do_ref[0:96, lanes], do_ref[96:192, lanes]], axis=1)
        dos[qi] = do
        o = jnp.concatenate([o_ref[0:96, lanes], o_ref[96:192, lanes]], axis=1)
        delta[qi] = jnp.sum(o.astype(jnp.float32) * do.astype(jnp.float32), axis=0, keepdims=True)
    dq_s[...] = jnp.zeros(dq_s.shape, jnp.float32)
    dk_s[...] = jnp.zeros(dk_s.shape, jnp.float32)
    dv_s[...] = jnp.zeros(dv_s.shape, jnp.float32)
    diff = lax.broadcasted_iota(jnp.int32, (128, 256), 0) - lax.rem(lax.broadcasted_iota(jnp.int32, (128, 256), 1), 128)
    nt = (((1,), (1,)), ((), ()))

    def step(t, _):
        for sl in range(nsl):
            first = ids_ref[2 * sl]
            late = (t > first).astype(jnp.int32)
            qi = 2 * sl + late
            kpos = t - late * (first + 1)
            qid = ids_ref[qi]
            n = inv_ref[kpos]
            q, do = qs[qi], dos[qi]
            s = jnp.dot(knat[n], q, preferred_element_type=jnp.float32)
            p = jnp.exp2(jnp.where(diff <= (qid - kpos) * 128, s * c - lse_ref[qi], -jnp.inf))
            dp = jnp.dot(vnat[n], do, preferred_element_type=jnp.float32)
            ds = (p * (dp - delta[qi])).astype(jnp.bfloat16)
            dv_s[sl, n] += lax.dot_general(do, p.astype(jnp.bfloat16), nt, preferred_element_type=jnp.float32)
            dk_s[sl, n] += lax.dot_general(q, ds, nt, preferred_element_type=jnp.float32)
            dq_s[qi] += jnp.dot(ktr[n], ds, preferred_element_type=jnp.float32)
        return 0

    lax.fori_loop(0, nb + 1, step, 0)
    for qi in range(nq):
        lanes = slice(128 * qi, 128 * (qi + 1))
        dq_ref[0:96, lanes] = dq_s[qi][:, :128] * scale
        dq_ref[96:192, lanes] = dq_s[qi][:, 128:] * scale
    for r in range(nchip):
        for j in range(nq):
            n = r * nq + j
            dk = dk_s[0, n]
            dv = dv_s[0, n]
            for sl in range(1, nsl):
                dk = dk + dk_s[sl, n]
                dv = dv + dv_s[sl, n]
            dk_refs[r][:, 128 * j:128 * (j + 1)] = (dk * scale).astype(jnp.bfloat16)
            dv_refs[r][:, 128 * j:128 * (j + 1)] = dv.astype(jnp.bfloat16)


def attn_bwd(ids, inv, qT, oT, doT, lse, ks, vs, heads):
    nchip = len(ks)
    T = qT.shape[1]
    nq = T // 128
    nb = nchip * nq
    wide = pl.BlockSpec((192, T), lambda g, *_: (g, 0))
    slim = pl.BlockSpec((96, T), lambda g, *_: (g, 0))
    grid_spec = pltpu.PrefetchScalarGridSpec(
        num_scalar_prefetch=2,
        grid=(heads,),
        in_specs=[wide, wide, wide, pl.BlockSpec((None, nq, 1, 256), lambda g, *_: (g, 0, 0, 0))] + [slim] * (2 * nchip),
        out_specs=[wide] + [slim] * (2 * nchip),
        scratch_shapes=[
            pltpu.VMEM((nb, 128, 96), jnp.bfloat16),
            pltpu.VMEM((nb, 96, 128), jnp.bfloat16),
            pltpu.VMEM((nb, 128, 96), jnp.bfloat16),
            pltpu.VMEM((nq, 96, 256), jnp.bfloat16),
            pltpu.VMEM((nq, 96, 256), jnp.bfloat16),
            pltpu.VMEM((nq, 1, 256), jnp.float32),
            pltpu.VMEM((nq, 96, 256), jnp.float32),
            pltpu.VMEM((nq // 2, nb, 96, 128), jnp.float32),
            pltpu.VMEM((nq // 2, nb, 96, 128), jnp.float32),
        ],
    )
    slab = jax.ShapeDtypeStruct((heads * 96, T), jnp.bfloat16)
    outs = pl.pallas_call(
        functools.partial(bwd_kernel, nchip, SCALE),
        grid_spec=grid_spec,
        out_shape=[jax.ShapeDtypeStruct((heads * 192, T), jnp.float32)] + [slab] * (2 * nchip),
        name="attention_backward",
    )(ids, inv, qT, oT, doT, lse, *ks, *vs)
    return outs[0], outs[1:1 + nchip], outs[1 + nchip:]


def mm(left, right, left_dim, right_dim):
    return lax.dot_general(left, right, (((left_dim,), (right_dim,)), ((), ())), preferred_element_type=F32)


def swap(a):
    return lax.ppermute(a, "ctx", [(i, i ^ 1) for i in range(lax.axis_size("ctx"))])


def hop(a, r):
    return lax.ppermute(a, "ctx", [(i, i ^ (2 * r)) for i in range(lax.axis_size("ctx"))])


def ring(a):
    n = lax.axis_size("fsdp")
    return lax.ppermute(a, "fsdp", [(i, (i + 1) % n) for i in range(n)])


def pick(a, index, axis=0):
    return lax.dynamic_index_in_dim(a, index, axis, keepdims=False)


def place(buffer, piece, index, axis=0):
    return lax.dynamic_update_slice_in_dim(buffer, jnp.expand_dims(piece, axis), index, axis)


def depth_gather(piece, depth):
    n = lax.axis_size("fsdp")
    buffer = place(jnp.zeros((n,) + piece.shape, piece.dtype), piece, depth)
    for s in range(1, n):
        piece = ring(piece)
        buffer = place(buffer, piece, lax.rem(depth + n - s, n))
    return buffer


def depth_scatter(parts, depth):
    n = lax.axis_size("fsdp")
    total = pick(parts, lax.rem(depth + n - 1, n))
    for s in range(n - 1):
        total = ring(total.astype(BF))
        total = total.astype(F32) + pick(parts, lax.rem(depth + 2 * n - 2 - s, n)).astype(F32)
    return total


def plane_gather(piece, index):
    n = lax.axis_size("ctx")
    chips = n // 2
    pieces = jnp.stack([piece] + [hop(piece, r) for r in range(1, chips)])
    others = swap(pieces)
    buffer = jnp.zeros((n,) + piece.shape, piece.dtype)
    for r in range(chips):
        buffer = place(buffer, pieces[r], index ^ (2 * r))
        buffer = place(buffer, others[r], index ^ (2 * r + 1))
    return buffer


def rotate(v, cosine, sine):
    heads = v.reshape(-1, 2, HEAD_WIDTH // 2, v.shape[-1])
    a, b = heads[:, 0], heads[:, 1]
    return jnp.stack([a * cosine - b * sine, b * cosine + a * sine], 1).reshape(v.shape)


def rotate_back(v, cosine, sine):
    heads = v.reshape(-1, 2, HEAD_WIDTH // 2, v.shape[-1])
    a, b = heads[:, 0], heads[:, 1]
    return jnp.stack([a * cosine + b * sine, b * cosine - a * sine], 1).reshape(v.shape)


def norm_back(incoming, unit, inverse, gain):
    scaled = incoming * gain
    return inverse * (scaled - unit * jnp.mean(scaled * unit, -1, keepdims=True))


def body(
    tokens,
    block_pairs,
    cotangent,
    attention_gain,
    query_weight,
    key_matrix,
    value_matrix,
    output_weight,
    feedforward_gain,
    gate_weight,
    up_weight,
    down_weight,
):
    slice_len, width = tokens.shape[1], tokens.shape[2]
    ctx = lax.axis_size("ctx")
    zsize = lax.axis_size("fsdp")
    chips = ctx // 2
    diag = chips - 1
    near = range(1, chips - 1)
    index = lax.axis_index("ctx")
    chip, core = index // 2, lax.rem(index, 2)
    depth = lax.axis_index("fsdp")
    rows = width // zsize
    strip = rows // ctx
    hidden_rows = down_weight.shape[0]
    fine = hidden_rows // ctx
    chunk = fine * zsize
    kv_rows = KEY_HEADS * HEAD_WIDTH

    gains = jnp.stack([attention_gain, feedforward_gain])
    gain_buffer = place(jnp.zeros((zsize, 2, rows), BF), gains, depth)
    for s in range(1, zsize):
        moved = lax.ppermute(gains, "fsdp", [(k, (k + s) % zsize) for k in range(zsize)])
        gain_buffer = place(gain_buffer, moved, lax.rem(depth + zsize - s, zsize))
    gains_full = jnp.transpose(gain_buffer, (1, 0, 2)).reshape(2, width).astype(F32)
    gain_first, gain_second = gains_full[0], gains_full[1]

    def gather_square(shard):
        strips = shard.reshape(ctx, strip, shard.shape[1])
        pair = jnp.stack([pick(strips, index), pick(strips, index ^ (2 * diag))])
        pair = depth_gather(pair, depth)
        own, far = pair[:, 0], pair[:, 1]
        found = {0: own, diag: far}
        for r in near:
            found[r] = hop(own, r)
        full = jnp.zeros((zsize, ctx, strip, shard.shape[1]), BF)
        for r in range(chips):
            full = place(full, found[r], index ^ (2 * r), 1)
            full = place(full, swap(found[r]), index ^ (2 * r + 1), 1)
        return full.reshape(width, shard.shape[1])

    key_value_full = gather_square(jnp.concatenate([key_matrix, value_matrix], 1))
    query_full = gather_square(query_weight)
    output_full = gather_square(output_weight)

    gate_cut = gate_weight.reshape(rows, zsize, 2, chips, fine)
    up_cut = up_weight.reshape(rows, zsize, 2, chips, fine)
    down_cut = down_weight.reshape(2, chips, fine, width)

    def own_piece(r):
        gate = pick(pick(gate_cut, core, 2), chip ^ r, 2).reshape(rows, chunk)
        up = pick(pick(up_cut, core, 2), chip ^ r, 2).reshape(rows, chunk)
        down = pick(pick(down_cut, core), chip ^ r)
        return jnp.concatenate([gate, up], 1), down

    gate_up, down = {}, {}
    for r in (0, diag):
        wide, tall = own_piece(r)
        gate_up[r] = depth_gather(wide, depth).reshape(width, 2 * chunk)
        down[r] = depth_gather(tall, depth).reshape(chunk, width)
    for r in near:
        gate_up[r] = hop(gate_up[0], r)
        down[r] = hop(down[0], r)

    x = jnp.concatenate([pick(tokens, core), swap(pick(tokens, 1 - core))]).astype(F32)
    cot_there = swap(cotangent)
    cot = jnp.concatenate(
        [pick(cotangent, core), pick(cot_there, core), pick(cot_there, 1 - core), pick(cotangent, 1 - core)]
    )
    length = x.shape[0]

    ids_all = jnp.concatenate([pick(block_pairs, index ^ r) for r in range(ctx)])
    ids = ids_all[:4]
    blocks = ids_all.shape[0]
    order = jnp.sum(
        jnp.where(ids_all[None, :] == jnp.arange(blocks, dtype=jnp.int32)[:, None], jnp.arange(blocks, dtype=jnp.int32)[None, :], 0), 1
    )
    positions = (ids[:, None] * BLK + jnp.arange(BLK, dtype=jnp.int32)[None, :]).reshape(length)
    half = HEAD_WIDTH // 2
    frequency = THETA ** (-jnp.arange(half, dtype=F32) * 2.0 / HEAD_WIDTH)
    angles = frequency[:, None] * positions.astype(F32)[None, :]
    cosine, sine = jnp.cos(angles), jnp.sin(angles)

    inverse_first = lax.rsqrt(jnp.mean(x * x, -1, keepdims=True) + EPS)
    unit_first = x * inverse_first
    first = (unit_first * gain_first).astype(BF)
    first_t = jnp.transpose(first)
    kv = mm(key_value_full, first_t, 0, 0)
    keys = {0: rotate(kv[:kv_rows], cosine, sine).astype(BF)}
    values = {0: kv[kv_rows:].astype(BF)}
    top = 1
    while top < chips:
        top *= 2
    for r in range(1, chips):
        high = 1 << (r.bit_length() - 1)
        low = r & -r
        keys[r] = hop(keys[r ^ high], high)
        values[r] = hop(values[r ^ low], low)
    query = rotate(mm(query_full, first_t, 0, 0), cosine, sine).astype(BF)
    key_list = [keys[r] for r in range(chips)]
    value_list = [values[r] for r in range(chips)]
    attended, log_total = attn_fwd(ids, order, query, key_list, value_list, KEY_HEADS)

    middle = x + mm(attended, output_full, 0, 0)
    inverse_second = lax.rsqrt(jnp.mean(middle * middle, -1, keepdims=True) + EPS)
    unit_second = middle * inverse_second
    second = (unit_second * gain_second).astype(BF)
    second = jnp.concatenate([second, swap(second)])
    out_part = 0.0
    second_grad = 0.0
    wide_grad, tall_grad = {}, {}
    for r in list(near) + [0, diag]:
        pre = mm(second, gate_up[r], 1, 0)
        gate_pre, up_pre = pre[:, :chunk], pre[:, chunk:]
        hidden_grad = mm(cot, down[r], 1, 1)
        sigmoid = jax.nn.sigmoid(gate_pre)
        silu = gate_pre * sigmoid
        hidden = (silu * up_pre).astype(BF)
        gate_low = (hidden_grad * up_pre * sigmoid * (1.0 + gate_pre * (1.0 - sigmoid))).astype(BF)
        up_low = (hidden_grad * silu).astype(BF)
        both_low = jnp.concatenate([gate_low, up_low], 1)
        tall_grad[r] = mm(hidden, cot, 0, 0).astype(BF)
        wide_grad[r] = mm(second, both_low, 0, 0).astype(BF)
        out_part = out_part + mm(hidden, down[r], 1, 0)
        second_grad = second_grad + mm(both_low, gate_up[r], 1, 1)

    q = slice_len
    out_part = jnp.concatenate([out_part[:length] + middle, out_part[length:]])
    came = swap(jnp.concatenate([out_part[2 * q:3 * q], out_part[q:2 * q]]))
    out_here = (out_part[:q] + came[:q]).astype(BF)
    out_there = (out_part[3 * q:] + came[q:]).astype(BF)

    def stored(here, there):
        return jnp.where(core == 0, jnp.stack([here, there]), jnp.stack([there, here]))

    layer_out = stored(out_here, out_there)

    second_grad = second_grad[:length] + swap(second_grad[length:])
    gain_second_part = jnp.sum(second_grad * unit_second, 0)
    middle_grad = cot[:length].astype(F32) + norm_back(second_grad, unit_second, inverse_second, gain_second)

    def scatter(parts):
        total = parts[0].astype(F32)
        for r in near:
            total = total + hop(parts[r], r).astype(F32)
        far = hop(depth_scatter(parts[diag], depth).astype(BF), diag)
        total = depth_scatter(total.astype(BF), depth) + far.astype(F32)
        return total.astype(BF)

    tall_piece = scatter({r: tall_grad[r].reshape(zsize, fine, width) for r in range(chips)})
    wide_piece = scatter({r: wide_grad[r].reshape(zsize, rows, 2 * chunk) for r in range(chips)})
    tall_all = plane_gather(tall_piece, index)
    wide_all = plane_gather(wide_piece, index)
    down_grad = jnp.transpose(tall_all.reshape(chips, 2, fine, width), (1, 0, 2, 3)).reshape(hidden_rows, width).astype(F32)
    wide_all = wide_all.reshape(chips, 2, rows, 2, zsize, fine)
    gate_grad = jnp.transpose(wide_all[:, :, :, 0], (2, 3, 1, 0, 4)).reshape(rows, -1).astype(F32)
    up_grad = jnp.transpose(wide_all[:, :, :, 1], (2, 3, 1, 0, 4)).reshape(rows, -1).astype(F32)

    middle_low = middle_grad.astype(BF)
    attended_grad = mm(output_full, middle_low, 1, 1).astype(BF)
    query_total, key_parts, value_parts = attn_bwd(
        ids, order, query, attended, attended_grad, log_total, key_list, value_list, KEY_HEADS
    )
    key_sum = [part for part in key_parts]
    value_sum = [part for part in value_parts]
    for r in range(chips - 1, 0, -1):
        high = 1 << (r.bit_length() - 1)
        low = r & -r
        key_sum[r ^ high] = key_sum[r ^ high].astype(F32) + hop(key_sum[r].astype(BF), high).astype(F32)
        value_sum[r ^ low] = value_sum[r ^ low].astype(F32) + hop(value_sum[r].astype(BF), low).astype(F32)
    query_low = rotate_back(query_total, cosine, sine).astype(BF)
    key_low = rotate_back(key_sum[0], cosine, sine).astype(BF)
    value_low = value_sum[0].astype(BF)
    kv_low = jnp.concatenate([key_low, value_low])

    def halves(a):
        cut = a.reshape(zsize, chips, 2, strip, length)
        here = pick(cut, core, 2).reshape(-1, length)
        there = swap(pick(cut, 1 - core, 2).reshape(-1, length))
        return jnp.concatenate([here, there], 1)

    def square_grad(product):
        parts = product.astype(BF).reshape(zsize, chips, strip, width)
        piece = scatter({r: pick(parts, chip ^ r, 1) for r in range(chips)})
        return plane_gather(piece, index).reshape(rows, width).astype(F32)

    first_half = halves(first_t)
    output_grad = square_grad(mm(halves(attended), jnp.concatenate([middle_low, swap(middle_low)]), 1, 0))
    query_grad = square_grad(mm(first_half, jnp.concatenate([query_low, swap(query_low)], 1), 1, 1))
    kv_grad = square_grad(mm(first_half, jnp.concatenate([kv_low, swap(kv_low)], 1), 1, 1))

    first_grad = mm(query_low, query_full, 0, 1) + mm(kv_low, key_value_full, 0, 1)
    gain_first_part = jnp.sum(first_grad * unit_first, 0)
    tokens_part = (middle_grad + norm_back(first_grad, unit_first, inverse_first, gain_first)).astype(BF)
    tokens_grad = stored(tokens_part[:q], swap(tokens_part[q:]))

    def gain_total(part):
        return lax.dynamic_slice_in_dim(lax.psum(part, ("ctx", "fsdp")), depth * rows, rows)

    return (
        layer_out,
        tokens_grad,
        gain_total(gain_first_part),
        query_grad,
        kv_grad[:, :kv_rows],
        kv_grad[:, kv_rows:],
        output_grad,
        gain_total(gain_second_part),
        gate_grad,
        up_grad,
        down_grad,
    )


def solution(mesh):
    line, square, grid = P("fsdp"), P("fsdp", None), P("fsdp", "ctx", None)
    in_specs = (grid, P(), grid, line, square, square, square, square, line, square, square, square)
    out_specs = (grid, grid, line, square, square, square, square, line, square, square, square)
    return jax.shard_map(body, mesh=mesh, in_specs=in_specs, out_specs=out_specs, check_vma=False)
```

time: 2580 us -> 1220 us (0.47)
  waiting for transfers between devices: 1890 us -> 422 us
  matrix products: 413 us -> 184 us
  Pallas kernels: 0 us -> 172 us
  local copies, waits for them, and re-layouts: 108 us -> 211 us
  starting transfers between devices: 1.4 us -> 92.4 us
    reduce_scatter x9 -> x0, waiting for transfers between devices: 979 us -> none  [the longest x1 215 us: body(): lax.psum_scatter(down_grad.astype(jnp.bfloat16), 'fsdp', scatter_dimensio...]
    all_gather x9 -> x0, waiting for transfers between devices: 772 us -> none  [the longest x1 206 us: body(): lax.all_gather(gate_weight, 'fsdp', axis=0, tiled=True)]
    ppermute x0 -> x134, waiting for transfers between devices: none -> 422 us  [the longest x51 240 us: ring(): return lax.ppermute(a, 'fsdp', [(i, (i + 1) % n) for i in range(n)])]
    dot_general x49 -> x33, matrix products: 413 us -> 184 us  [mm(): lax.dot_general(left, right, (((left_dim,), (right_dim,)), ((), ())), pre...]
    pallas_call x0 -> x2, Pallas kernels: none -> 172 us  [the longest x1 87.5 us: attn_bwd(): pl.pallas_call(functools.partial(bwd_kernel, nchip, SCALE), grid_spec=gri...]
    psum x1 -> x0, waiting for transfers between devices: 131 us -> none  [body(): lax.psum(again_query.astype(jnp.bfloat16), 'ctx').astype(jnp.float32)]
    ppermute x0 -> x134, starting transfers between devices: none -> 92.4 us  [the longest x52 58.3 us: hop(): lax.ppermute(a, 'ctx', [(i, i ^ 2 * r) for i in range(lax.axis_size('ctx'...]
    dynamic_update_slice x12 -> x85, local copies, waits for them, and re-layouts: 34.7 us -> 67.3 us  [place(): lax.dynamic_update_slice_in_dim(buffer, jnp.expand_dims(piece, axis), ind...]
  transfers between devices with their start and end apart: 19 -> 134, of which waited for: 18 -> 56; matrix products, arithmetic and copies ran while one was open for 12% -> 36% of each run, Pallas kernels for 0% -> 14%
where the time goes in v1:
time: 1220 us; the launch traced here: 1210 us
  waiting for transfers between devices  422 us (35%)
  local copies, waits for them, and re-layouts  211 us (17%)
  matrix products  184 us (15%)
  Pallas kernels  172 us (14%)
  starting transfers between devices  92.4 us (8%)
  other arithmetic  85.5 us (7%)
  blocking collectives  39.6 us (3%)
    ppermute x51, waiting for transfers between devices, ring(): return lax.ppermute(a, 'fsdp', [(i, (i + 1) % n) for i in range(n)])  240 us
    dot_general x33, matrix products, mm(): lax.dot_general(left, right, (((left_dim,), (right_dim,)), ((), ())), pre...  184 us
    ppermute x52, waiting for transfers between devices, hop(): lax.ppermute(a, 'ctx', [(i, i ^ 2 * r) for i in range(lax.axis_size('ctx'...  179 us
    pallas_call x1, Pallas kernels, attn_bwd(): pl.pallas_call(functools.partial(bwd_kernel, nchip, SCALE), grid_spec=gri...  87.5 us
    pallas_call x1, Pallas kernels, attn_fwd(): pl.pallas_call(functools.partial(fwd_kernel, nchip, SCALE), grid_spec=gri...  84.3 us
    dynamic_update_slice x85, local copies, waits for them, and re-layouts, place(): lax.dynamic_update_slice_in_dim(buffer, jnp.expand_dims(piece, axis), ind...  67.3 us
    ppermute x52, starting transfers between devices, hop(): lax.ppermute(a, 'ctx', [(i, i ^ 2 * r) for i in range(lax.axis_size('ctx'...  58.3 us
    unnamed x219, local copies, waits for them, and re-layouts  44 us
  transfers between devices with their start and end apart: 134, of which 56 were waited for; matrix products, arithmetic and copies ran while one was open for 36% of the time, Pallas kernels for 14%

profile of v1, /device:TPU:0, one launch (start us, length us, event | category | flops | bytes accessed | tf_op | source)
XLA Modules:
  0.0 1208.6 jit_solution(4612266834620401442)
XLA Ops:
  74.8 23.5 %collective-permute-done.42 = bf16[128,1536]{1,0:T(8,128)(2,1)S(1)} collective-permute-done((bf16[128,1536]{1,0:T(8,128)(2,1)}, bf16[128,1536]{1,0:T(8,128)(2,1)S(1)}, u32[]{:S(2)}, u32[]{:S(2)}) %collective-permute-start.42) | collective-permute-done | bytes 393248 | tf_op jit(solution)/shard_map/ppermute | solution.py:210
  99.1 24.6 %collective-permute-done.51 = bf16[128,1536]{1,0:T(8,128)(2,1)} collective-permute-done((bf16[128,1536]{1,0:T(8,128)(2,1)}, bf16[128,1536]{1,0:T(8,128)(2,1)}, u32[]{:S(2)}, u32[]{:S(2)}) %collective-permute-start.51) | collective-permute-done | bytes 393248 | tf_op jit(solution)/shard_map/ppermute | solution.py:210
  143.3 7.6 collective-permute-done.43
  190.0 13.3 %collective-permute-done.44 = bf16[128,1536]{1,0:T(8,128)(2,1)S(1)} collective-permute-done((bf16[128,1536]{1,0:T(8,128)(2,1)S(1)}, bf16[128,1536]{1,0:T(8,128)(2,1)S(1)}, u32[]{:S(2)}, u32[]{:S(2)}) %collective-permute-start.44) | collective-permute-done | bytes 393248 | tf_op jit(solution)/shard_map/ppermute | solution.py:210
  208.8 10.9 collective-permute-done.17
  222.3 12.4 %collective-permute-done.32 = bf16[4,48,1536]{2,1,0:T(8,128)(2,1)S(1)} collective-permute-done((bf16[4,48,1536]{2,1,0:T(8,128)(2,1)S(1)}, bf16[4,48,1536]{2,1,0:T(8,128)(2,1)S(1)}, u32[]{:S(2)}, u32[]{:S(2)}) %collective-permute-start.32) | collective-permute-done | bytes 589856 | tf_op jit(solution)/shard_map/ppermute | solution.py:205
  263.8 6.6 copy.157
  276.9 17.8 %collective-permute-done.26.rest_6_ = bf16[768,512]{1,0:T(8,128)(2,1)} collective-permute-done((bf16[768,512]{1,0:T(8,128)(2,1)}, bf16[768,512]{1,0:T(8,128)(2,1)}, u32[]{:S(2)}, u32[]{:S(2)}) %collective-permute-start.26) | collective-permute-done | bytes 786464 | tf_op jit(solution)/shard_map/ppermute | solution.py:205
  299.2 11.2 collective-permute-done.24.rest_3_
  312.5 84.3 %attention_forward.1 = (bf16[1536,512]{1,0:T(8,128)(2,1)}, f32[8,4,1,256]{3,2,1,0:T(1,128)}) custom-call(s32[4]{0:T(128)} %get-tuple-element.84.ids_ref, s32[16]{0:T(128)} %select_reduce_fusion.inv_ref, bf16[1536,512]{1,0:T(8,128)(2,1)} %bitcast.507, bf16[768,512]{1,0:T(8,128)(2,1)} %bitcast.63.rest_0_, bf16[768,512]{1,0:T(8,128)(2,1)} %collective-permute-done.22.rest_1_, ...), custom_call_target="tpu_custom_call" | custom-call | tf_op jit(solution)/shard_map/attention_forward/pallas_call | solution.py:95
  420.7 10.9 collective-permute-done.50
  434.6 6.6 fusion.108
  441.3 7.6 multiply_convert_fusion.4
  454.3 7.0 multiply_convert_fusion.2
  461.3 7.3 convolution_convert_fusion
  473.1 6.4 fusion.124
  479.6 7.8 convolution_convert_fusion.3
  512.6 6.7 fusion.110
  519.3 7.0 multiply_convert_fusion.8
  526.3 8.0 fusion.45
  534.4 6.5 fusion.109
  540.9 7.0 multiply_convert_fusion.6
  549.1 7.7 fusion.44
  556.8 7.4 add_add_fusion
  591.7 7.8 convolution_convert_fusion.1
  620.3 24.7 %collective-permute-done.123 = bf16[128,1536]{1,0:T(8,128)(2,1)S(1)} collective-permute-done((bf16[128,1536]{1,0:T(8,128)(2,1)S(1)}, bf16[128,1536]{1,0:T(8,128)(2,1)S(1)}, u32[]{:S(2)}, u32[]{:S(2)}) %collective-permute-start.123) | collective-permute-done | bytes 393248 | tf_op jit(solution)/shard_map/ppermute | solution.py:210
  645.5 7.9 collective-permute-done.128
  663.0 7.6 convolution_convert_fusion.2
  696.0 6.5 fusion.120
  702.5 6.8 convolution_convert_fusion.11.do_ref
  709.3 42.3 %collective-permute-done.108 = bf16[4,384,1024]{1,2,0:T(8,128)(2,1)S(1)} collective-permute-done((bf16[4,384,1024]{1,2,0:T(8,128)(2,1)}, bf16[4,384,1024]{1,2,0:T(8,128)(2,1)S(1)}, u32[]{:S(2)}, u32[]{:S(2)}) %collective-permute-start.108) | collective-permute-done | bytes 3145760 | tf_op jit(solution)/shard_map/ppermute | solution.py:205
  757.3 87.5 %attention_backward.1 = (f32[1536,512]{1,0:T(8,128)}, bf16[768,512]{1,0:T(8,128)(2,1)}, bf16[768,512]{1,0:T(8,128)(2,1)}, bf16[768,512]{1,0:T(8,128)(2,1)}, bf16...) custom-call(s32[4]{0:T(128)} %get-tuple-element.84.ids_ref, ...), custom_call_target="tpu_custom_call" | custom-call | tf_op jit(solution)/shard_map/attention_backward/pallas_call | solution.py:187
  864.2 24.3 %collective-permute-done.58 = bf16[768,512]{1,0:T(8,128)(2,1)S(1)} collective-permute-done((bf16[768,512]{1,0:T(8,128)(2,1)S(1)}, bf16[768,512]{1,0:T(8,128)(2,1)S(1)}, u32[]{:S(2)}, u32[]{:S(2)}) %collective-permute-start.58) | collective-permute-done | bytes 786464 | tf_op jit(solution)/shard_map/ppermute | solution.py:205
  897.9 11.1 collective-permute-done.57
  913.2 11.2 collective-permute-done.61
  959.3 39.6 %all-reduce = (f32[1536]{0:T(1024)S(1)}, f32[1536]{0:T(1024)S(1)}) all-reduce(f32[1536]{0:T(1024)S(1)} %get-tuple-element.57, f32[1536]{0:T(1024)S(1)} %get-tuple-element.55), channel_id=1, replica_groups=mesh['ctx'=8,'fsdp'=4] {'ctx','fsdp'}, use_global_device_ids=true, to_apply=%region_6.7 | all-reduce | flops 3072 | bytes 24576 | tf_op jit(solution)/shard_map/psum | solution.py:476
  1012.8 6.5 collective-permute-done.101
  1043.1 13.8 %collective-permute-done.112 = bf16[384,1024]{0,1:T(8,128)(2,1)S(1)} collective-permute-done((bf16[384,1024]{0,1:T(8,128)(2,1)S(1)}, bf16[384,1024]{0,1:T(8,128)(2,1)S(1)}, u32[]{:S(2)}, u32[]{:S(2)}) %collective-permute-start.112) | collective-permute-done | bytes 786464 | tf_op jit(solution)/shard_map/ppermute | solution.py:210
  1065.0 7.2 collective-permute-done.99
  1087.2 6.6 collective-permute-done.73
  1093.9 6.9 collective-permute-done.68
  1108.5 13.0 %collective-permute-done.118 = bf16[384,1024]{0,1:T(8,128)(2,1)S(1)} collective-permute-done((bf16[384,1024]{0,1:T(8,128)(2,1)S(1)}, bf16[384,1024]{0,1:T(8,128)(2,1)S(1)}, u32[]{:S(2)}, u32[]{:S(2)}) %collective-permute-start.118) | collective-permute-done | bytes 786464 | tf_op jit(solution)/shard_map/ppermute | solution.py:205
  1128.8 8.2 collective-permute-done.70
  1147.1 6.3 collective-permute-done.82
  1153.9 6.5 collective-permute-done.83
  1160.9 6.8 collective-permute-done.84
  1189.2 6.6 copy.202
  1201.8 6.6 copy.203
  (729 shorter events, 516.9 us)
Async XLA Ops:
  2.6 52.3 %collective-permute-start.10 = (bf16[2,384]{1,0:T(2,128)(2,1)}, bf16[2,384]{1,0:T(2,128)(2,1)}, u32[]{:S(2)}, u32[]{:S(2)}) collective-permute-start(bf16[2,384]{1,0:T(2,128)(2,1)} %get-tuple-element.86), channel_id=1, source_target_pairs={{0,1},{1,2},{2,3},{3,0},{4,5},{5,6},{6,7},{7,4},{8,9},{9,10},{10,1... | collective-permute-start | bytes 4616 | tf_op jit(solution)/shard_map/ppermute | solution.py:301
  5.6 49.9 %collective-permute-start.11 = (bf16[2,384]{1,0:T(2,128)(2,1)}, bf16[2,384]{1,0:T(2,128)(2,1)}, u32[]{:S(2)}, u32[]{:S(2)}) collective-permute-start(bf16[2,384]{1,0:T(2,128)(2,1)} %get-tuple-element.86), channel_id=1, source_target_pairs={{0,2},{1,3},{2,0},{3,1},{4,6},{5,7},{6,4},{7,5},{8,10},{9,11},{10,... | collective-permute-start | bytes 4616 | tf_op jit(solution)/shard_map/ppermute | solution.py:301
  8.2 48.9 %collective-permute-start.12 = (bf16[2,384]{1,0:T(2,128)(2,1)}, bf16[2,384]{1,0:T(2,128)(2,1)S(1)}, u32[]{:S(2)}, u32[]{:S(2)}) collective-permute-start(bf16[2,384]{1,0:T(2,128)(2,1)} %get-tuple-element.86), channel_id=1, source_target_pairs={{0,3},{1,0},{2,1},{3,2},{4,7},{5,4},{6,5},{7,6},{8,11},{9,8},{10,9... | collective-permute-start | bytes 4616 | tf_op jit(solution)/shard_map/ppermute | solution.py:301
  11.5 49.2 %collective-permute-start.1 = (bf16[2,48,1536]{2,1,0:T(8,128)(2,1)}, bf16[2,48,1536]{2,1,0:T(8,128)(2,1)}, u32[]{:S(2)}, u32[]{:S(2)}) collective-permute-start(bf16[2,48,1536]{2,1,0:T(8,128)(2,1)} %pad_maximum_fusion.31), channel_id=1, source_target_pairs={{0,1},{1,2},{2,3},{3,0},{4,5},{5,6},{6,7},{7,4},{8,9},{9,10},{10,1... | collective-permute-start | bytes 884744 | tf_op jit(solution)/shard_map/ppermute | solution.py:210
  14.7 140.1 %collective-permute-start = (bf16[256,1536]{1,0:T(8,128)(2,1)}, bf16[256,1536]{1,0:T(8,128)(2,1)}, u32[]{:S(2)}, u32[]{:S(2)}) collective-permute-start(bf16[256,1536]{1,0:T(8,128)(2,1)} %get-tuple-element.142), channel_id=1, source_target_pairs={{0,4},{4,0},{8,12},{12,8},{16,20},{20,16},{24,28},{28,24},{1,5},{5... | collective-permute-start | bytes 2359304 | tf_op jit(solution)/shard_map/ppermute | solution.py:201
  57.2 95.3 %collective-permute-start.38 = (bf16[384,1024]{0,1:T(8,128)(2,1)}, bf16[384,1024]{0,1:T(8,128)(2,1)}, u32[]{:S(2)}, u32[]{:S(2)}) collective-permute-start(bf16[384,1024]{0,1:T(8,128)(2,1)} %get-tuple-element.155), channel_id=1, source_target_pairs={{0,1},{1,2},{2,3},{3,0},{4,5},{5,6},{6,7},{7,4},{8,9},{9,10},{10,1... | collective-permute-start | bytes 2359304 | tf_op jit(solution)/shard_map/ppermute | solution.py:210
  60.7 37.6 %collective-permute-start.42 = (bf16[128,1536]{1,0:T(8,128)(2,1)}, bf16[128,1536]{1,0:T(8,128)(2,1)S(1)}, u32[]{:S(2)}, u32[]{:S(2)}) collective-permute-start(bf16[128,1536]{1,0:T(8,128)(2,1)} %get-tuple-element.112), channel_id=1, source_target_pairs={{0,1},{1,2},{2,3},{3,0},{4,5},{5,6},{6,7},{7,4},{8,9},{9,10},{10,1... | collective-permute-start | bytes 1179656 | tf_op jit(solution)/shard_map/ppermute | solution.py:210
  66.8 97.8 %collective-permute-start.48 = (bf16[384,1024]{1,0:T(8,128)(2,1)}, bf16[384,1024]{1,0:T(8,128)(2,1)}, u32[]{:S(2)}, u32[]{:S(2)}) collective-permute-start(bf16[384,1024]{1,0:T(8,128)(2,1)} %pad_maximum_fusion.26), channel_id=1, source_target_pairs={{0,1},{1,2},{2,3},{3,0},{4,5},{5,6},{6,7},{7,4},{8,9},{9,10},{10,1... | collective-permute-start | bytes 2359304 | tf_op jit(solution)/shard_map/ppermute | solution.py:210
  73.1 50.6 %collective-permute-start.51 = (bf16[128,1536]{1,0:T(8,128)(2,1)}, bf16[128,1536]{1,0:T(8,128)(2,1)}, u32[]{:S(2)}, u32[]{:S(2)}) collective-permute-start(bf16[128,1536]{1,0:T(8,128)(2,1)} %get-tuple-element.113), channel_id=1, source_target_pairs={{0,1},{1,2},{2,3},{3,0},{4,5},{5,6},{6,7},{7,4},{8,9},{9,10},{10,1... | collective-permute-start | bytes 1179656 | tf_op jit(solution)/shard_map/ppermute | solution.py:210
  163.3 135.7 %collective-permute-start.39 = (bf16[384,1024]{0,1:T(8,128)(2,1)}, bf16[384,1024]{0,1:T(8,128)(2,1)}, u32[]{:S(2)}, u32[]{:S(2)}) collective-permute-start(bf16[384,1024]{0,1:T(8,128)(2,1)} %collective-permute-done.38), channel_id=1, source_target_pairs={{0,1},{1,2},{2,3},{3,0},{4,5},{5,6},{6,7},{7,4},{8,9},{9,10},{10,1... | collective-permute-start | bytes 2359304 | tf_op jit(solution)/shard_map/ppermute | solution.py:210
  164.6 38.6 %collective-permute-start.44 = (bf16[128,1536]{1,0:T(8,128)(2,1)S(1)}, bf16[128,1536]{1,0:T(8,128)(2,1)S(1)}, u32[]{:S(2)}, u32[]{:S(2)}) collective-permute-start(bf16[128,1536]{1,0:T(8,128)(2,1)S(1)} %copy-done.65), channel_id=1, source_target_pairs={{0,1},{1,2},{2,3},{3,0},{4,5},{5,6},{6,7},{7,4},{8,9},{9,10},{10,1... | collective-permute-start | bytes 1179656 | tf_op jit(solution)/shard_map/ppermute | solution.py:210
  181.0 65.8 %collective-permute-start.7 = (bf16[4,48,1536]{2,1,0:T(8,128)(2,1)S(1)}, bf16[4,48,1536]{2,1,0:T(8,128)(2,1)S(1)}, u32[]{:S(2)}, u32[]{:S(2)}) collective-permute-start(bf16[4,48,1536]{2,1,0:T(8,128)(2,1)S(1)} %get-tuple-element.152), channel_id=1, source_target_pairs={{0,16},{4,20},{8,24},{12,28},{16,0},{20,4},{24,8},{28,12},{1,17},{... | collective-permute-start | bytes 1769480 | tf_op jit(solution)/shard_map/ppermute | solution.py:205
  257.1 42.0 %collective-permute-start.23 = (bf16[768,512]{1,0:T(8,128)(2,1)}, bf16[768,512]{1,0:T(8,128)(2,1)}, u32[]{:S(2)}, u32[]{:S(2)}) collective-permute-start(bf16[768,512]{1,0:T(8,128)(2,1)} %bitcast.63.rest_0_), channel_id=1, source_target_pairs={{0,16},{4,20},{8,24},{12,28},{16,0},{20,4},{24,8},{28,12},{1,17},{... | collective-permute-start | bytes 2359304 | tf_op jit(solution)/shard_map/ppermute | solution.py:205
  276.1 34.4 %collective-permute-start.24 = (bf16[768,512]{1,0:T(8,128)(2,1)}, bf16[768,512]{1,0:T(8,128)(2,1)}, u32[]{:S(2)}, u32[]{:S(2)}) collective-permute-start(bf16[768,512]{1,0:T(8,128)(2,1)} %collective-permute-done.22.rest_1_), channel_id=1, source_target_pairs={{0,16},{4,20},{8,24},{12,28},{16,0},{20,4},{24,8},{28,12},{1,17},{... | collective-permute-start | bytes 2359304 | tf_op jit(solution)/shard_map/ppermute | solution.py:205
  299.1 113.5 %collective-permute-start.55 = (bf16[2,256,1536]{2,1,0:T(8,128)(2,1)}, bf16[2,256,1536]{2,1,0:T(8,128)(2,1)}, u32[]{:S(2)}, u32[]{:S(2)}) collective-permute-start(bf16[2,256,1536]{2,1,0:T(8,128)(2,1)} %param.14), channel_id=1, source_target_pairs={{0,4},{4,0},{8,12},{12,8},{16,20},{20,16},{24,28},{28,24},{1,5},{5... | collective-permute-start | bytes 4718600 | tf_op jit(solution)/shard_map/ppermute | solution.py:201
  299.1 110.2 %collective-permute-start.49 = (bf16[384,1024]{1,0:T(8,128)(2,1)}, bf16[384,1024]{1,0:T(8,128)(2,1)}, u32[]{:S(2)}, u32[]{:S(2)}) collective-permute-start(bf16[384,1024]{1,0:T(8,128)(2,1)} %collective-permute-done.48), channel_id=1, source_target_pairs={{0,1},{1,2},{2,3},{3,0},{4,5},{5,6},{6,7},{7,4},{8,9},{9,10},{10,1... | collective-permute-start | bytes 2359304 | tf_op jit(solution)/shard_map/ppermute | solution.py:210
  299.1 107.1 %collective-permute-start.53 = (bf16[128,1536]{1,0:T(8,128)(2,1)}, bf16[128,1536]{1,0:T(8,128)(2,1)S(1)}, u32[]{:S(2)}, u32[]{:S(2)}) collective-permute-start(bf16[128,1536]{1,0:T(8,128)(2,1)} %collective-permute-done.52), channel_id=1, source_target_pairs={{0,1},{1,2},{2,3},{3,0},{4,5},{5,6},{6,7},{7,4},{8,9},{9,10},{10,1... | collective-permute-start | bytes 1179656 | tf_op jit(solution)/shard_map/ppermute | solution.py:210
  310.5 208.8 %collective-permute-start.45 = (bf16[512,1536]{1,0:T(8,128)(2,1)}, bf16[512,1536]{1,0:T(8,128)(2,1)}, u32[]{:S(2)}, u32[]{:S(2)}) collective-permute-start(bf16[512,1536]{1,0:T(8,128)(2,1)} %bitcast.104), channel_id=1, source_target_pairs={{0,8},{4,12},{8,0},{12,4},{16,24},{20,28},{24,16},{28,20},{1,9},{5... | collective-permute-start | bytes 4718600 | tf_op jit(solution)/shard_map/ppermute | solution.py:205
  312.4 103.4 %collective-permute-start.40 = (bf16[384,1024]{0,1:T(8,128)(2,1)}, bf16[384,1024]{0,1:T(8,128)(2,1)}, u32[]{:S(2)}, u32[]{:S(2)}) collective-permute-start(bf16[384,1024]{0,1:T(8,128)(2,1)} %collective-permute-done.39), channel_id=1, source_target_pairs={{0,1},{1,2},{2,3},{3,0},{4,5},{5,6},{6,7},{7,4},{8,9},{9,10},{10,1... | collective-permute-start | bytes 2359304 | tf_op jit(solution)/shard_map/ppermute | solution.py:210
  412.6 128.3 %collective-permute-start.47 = (bf16[512,1536]{1,0:T(8,128)(2,1)}, bf16[512,1536]{1,0:T(8,128)(2,1)}, u32[]{:S(2)}, u32[]{:S(2)}) collective-permute-start(bf16[512,1536]{1,0:T(8,128)(2,1)} %bitcast.104), channel_id=1, source_target_pairs={{0,16},{4,20},{8,24},{12,28},{16,0},{20,4},{24,8},{28,12},{1,17},{... | collective-permute-start | bytes 4718600 | tf_op jit(solution)/shard_map/ppermute | solution.py:205
  420.2 91.7 %collective-permute-start.41 = (bf16[1536,1024]{1,0:T(8,128)(2,1)}, bf16[1536,1024]{1,0:T(8,128)(2,1)}, u32[]{:S(2)}, u32[]{:S(2)}) collective-permute-start(bf16[1536,1024]{1,0:T(8,128)(2,1)} %bitcast.97), channel_id=1, source_target_pairs={{0,8},{4,12},{8,0},{12,4},{16,24},{20,28},{24,16},{28,20},{1,9},{5... | collective-permute-start | bytes 9437192 | tf_op jit(solution)/shard_map/ppermute | solution.py:205
  431.6 102.7 %collective-permute-start.46 = (bf16[1536,1024]{1,0:T(8,128)(2,1)}, bf16[1536,1024]{1,0:T(8,128)(2,1)}, u32[]{:S(2)}, u32[]{:S(2)}) collective-permute-start(bf16[1536,1024]{1,0:T(8,128)(2,1)} %bitcast.97), channel_id=1, source_target_pairs={{0,16},{4,20},{8,24},{12,28},{16,0},{20,4},{24,8},{28,12},{1,17},{... | collective-permute-start | bytes 9437192 | tf_op jit(solution)/shard_map/ppermute | solution.py:205
  472.7 133.1 %collective-permute-start.113 = (bf16[384,1024]{0,1:T(8,128)(2,1)}, bf16[384,1024]{0,1:T(8,128)(2,1)}, u32[]{:S(2)}, u32[]{:S(2)}) collective-permute-start(bf16[384,1024]{0,1:T(8,128)(2,1)} %bitcast.565), channel_id=1, source_target_pairs={{0,1},{1,2},{2,3},{3,0},{4,5},{5,6},{6,7},{7,4},{8,9},{9,10},{10,1... | collective-permute-start | bytes 2359304 | tf_op jit(solution)/shard_map/ppermute | solution.py:210
  512.0 92.2 %collective-permute-start.126 = (bf16[128,1536]{1,0:T(8,128)(2,1)S(1)}, bf16[128,1536]{1,0:T(8,128)(2,1)}, u32[]{:S(2)}, u32[]{:S(2)}) collective-permute-start(bf16[128,1536]{1,0:T(8,128)(2,1)S(1)} %dynamic-slice_bitcast_fusion.13), channel_id=1, source_target_pairs={{0,1},{1,2},{2,3},{3,0},{4,5},{5,6},{6,7},{7,4},{8,9},{9,10},{10,1... | collective-permute-start | bytes 1179656 | tf_op jit(solution)/shard_map/ppermute | solution.py:210
  568.8 123.6 %collective-permute-start.56 = (f32[512,1536]{1,0:T(8,128)}, f32[512,1536]{1,0:T(8,128)S(1)}, u32[]{:S(2)}, u32[]{:S(2)}) collective-permute-start(f32[512,1536]{1,0:T(8,128)} %slice.284), channel_id=1, source_target_pairs={{0,4},{4,0},{8,12},{12,8},{16,20},{20,16},{24,28},{28,24},{1,5},{5... | collective-permute-start | bytes 9437192 | tf_op jit(solution)/shard_map/ppermute | solution.py:201
  572.4 37.6 %collective-permute-start.122 = (bf16[4,128,1536]{2,1,0:T(8,128)(2,1)}, bf16[4,128,1536]{2,1,0:T(8,128)(2,1)}, u32[]{:S(2)}, u32[]{:S(2)}) collective-permute-start(bf16[4,128,1536]{2,1,0:T(8,128)(2,1)} %bitcast.214), channel_id=1, source_target_pairs={{0,16},{4,20},{8,24},{12,28},{16,0},{20,4},{24,8},{28,12},{1,17},{... | collective-permute-start | bytes 4718600 | tf_op jit(solution)/shard_map/ppermute | solution.py:205
  576.9 36.2 %collective-permute-start.121 = (bf16[4,128,1536]{2,1,0:T(8,128)(2,1)}, bf16[4,128,1536]{2,1,0:T(8,128)(2,1)}, u32[]{:S(2)}, u32[]{:S(2)}) collective-permute-start(bf16[4,128,1536]{2,1,0:T(8,128)(2,1)} %bitcast.213), channel_id=1, source_target_pairs={{0,8},{4,12},{8,0},{12,4},{16,24},{20,28},{24,16},{28,20},{1,9},{5... | collective-permute-start | bytes 4718600 | tf_op jit(solution)/shard_map/ppermute | solution.py:205
  604.1 105.1 %collective-permute-start.109 = (bf16[4,384,1024]{1,2,0:T(8,128)(2,1)}, bf16[4,384,1024]{1,2,0:T(8,128)(2,1)}, u32[]{:S(2)}, u32[]{:S(2)}) collective-permute-start(bf16[4,384,1024]{1,2,0:T(8,128)(2,1)} %copy.194), channel_id=1, source_target_pairs={{0,16},{4,20},{8,24},{12,28},{16,0},{20,4},{24,8},{28,12},{1,17},{... | collective-permute-start | bytes 9437192 | tf_op jit(solution)/shard_map/ppermute | solution.py:205
  610.0 46.6 %collective-permute-start.114 = (bf16[384,1024]{0,1:T(8,128)(2,1)S(1)}, bf16[384,1024]{0,1:T(8,128)(2,1)S(1)}, u32[]{:S(2)}, u32[]{:S(2)}) collective-permute-start(bf16[384,1024]{0,1:T(8,128)(2,1)S(1)} %fusion.36), channel_id=1, source_target_pairs={{0,1},{1,2},{2,3},{3,0},{4,5},{5,6},{6,7},{7,4},{8,9},{9,10},{10,1... | collective-permute-start | bytes 2359304 | tf_op jit(solution)/shard_map/ppermute | solution.py:210
  680.3 71.2 %collective-permute-start.108 = (bf16[4,384,1024]{1,2,0:T(8,128)(2,1)}, bf16[4,384,1024]{1,2,0:T(8,128)(2,1)S(1)}, u32[]{:S(2)}, u32[]{:S(2)}) collective-permute-start(bf16[4,384,1024]{1,2,0:T(8,128)(2,1)} %copy.192), channel_id=1, source_target_pairs={{0,8},{4,12},{8,0},{12,4},{16,24},{20,28},{24,16},{28,20},{1,9},{5... | collective-permute-start | bytes 9437192 | tf_op jit(solution)/shard_map/ppermute | solution.py:205
  689.4 159.4 %collective-permute-start.132 = (bf16[128,1536]{1,0:T(8,128)(2,1)}, bf16[128,1536]{1,0:T(8,128)(2,1)}, u32[]{:S(2)}, u32[]{:S(2)}) collective-permute-start(bf16[128,1536]{1,0:T(8,128)(2,1)} %get-tuple-element.72), channel_id=1, source_target_pairs={{0,24},{4,28},{8,16},{12,20},{16,8},{20,12},{24,0},{28,4},{1,25},{... | collective-permute-start | bytes 1179656 | tf_op jit(solution)/shard_map/ppermute | solution.py:205
  691.9 159.7 %collective-permute-start.131 = (bf16[128,1536]{1,0:T(8,128)(2,1)}, bf16[128,1536]{1,0:T(8,128)(2,1)}, u32[]{:S(2)}, u32[]{:S(2)}) collective-permute-start(bf16[128,1536]{1,0:T(8,128)(2,1)} %get-tuple-element.72), channel_id=1, source_target_pairs={{0,16},{4,20},{8,24},{12,28},{16,0},{20,4},{24,8},{28,12},{1,17},{... | collective-permute-start | bytes 1179656 | tf_op jit(solution)/shard_map/ppermute | solution.py:205
  692.4 159.3 %collective-permute-start.130 = (bf16[128,1536]{1,0:T(8,128)(2,1)}, bf16[128,1536]{1,0:T(8,128)(2,1)}, u32[]{:S(2)}, u32[]{:S(2)}) collective-permute-start(bf16[128,1536]{1,0:T(8,128)(2,1)} %get-tuple-element.72), channel_id=1, source_target_pairs={{0,8},{4,12},{8,0},{12,4},{16,24},{20,28},{24,16},{28,20},{1,9},{5... | collective-permute-start | bytes 1179656 | tf_op jit(solution)/shard_map/ppermute | solution.py:205
  709.3 181.6 %collective-permute-start.94 = (bf16[512,1536]{1,0:T(8,128)(2,1)}, bf16[512,1536]{1,0:T(8,128)(2,1)}, u32[]{:S(2)}, u32[]{:S(2)}) collective-permute-start(bf16[512,1536]{1,0:T(8,128)(2,1)} %get-tuple-element.81), channel_id=1, source_target_pairs={{0,4},{4,0},{8,12},{12,8},{16,20},{20,16},{24,28},{28,24},{1,5},{5... | collective-permute-start | bytes 4718600 | tf_op jit(solution)/shard_map/ppermute | solution.py:201
  757.3 97.3 %collective-permute-start.110 = (bf16[384,1024]{0,1:T(8,128)(2,1)}, bf16[384,1024]{0,1:T(8,128)(2,1)}, u32[]{:S(2)}, u32[]{:S(2)}) collective-permute-start(bf16[384,1024]{0,1:T(8,128)(2,1)} %dynamic-slice_bitcast_fusion), channel_id=1, source_target_pairs={{0,1},{1,2},{2,3},{3,0},{4,5},{5,6},{6,7},{7,4},{8,9},{9,10},{10,1... | collective-permute-start | bytes 2359304 | tf_op jit(solution)/shard_map/ppermute | solution.py:210
  851.6 38.2 %collective-permute-start.93 = (bf16[768,512]{1,0:T(8,128)(2,1)S(1)}, bf16[768,512]{1,0:T(8,128)(2,1)S(1)}, u32[]{:S(2)}, u32[]{:S(2)}) collective-permute-start(bf16[768,512]{1,0:T(8,128)(2,1)S(1)} %bitcast.570), channel_id=1, source_target_pairs={{0,4},{4,0},{8,12},{12,8},{16,20},{20,16},{24,28},{28,24},{1,5},{5... | collective-permute-start | bytes 2359304 | tf_op jit(solution)/shard_map/ppermute | solution.py:201
  851.7 36.8 %collective-permute-start.58 = (bf16[768,512]{1,0:T(8,128)(2,1)S(1)}, bf16[768,512]{1,0:T(8,128)(2,1)S(1)}, u32[]{:S(2)}, u32[]{:S(2)}) collective-permute-start(bf16[768,512]{1,0:T(8,128)(2,1)S(1)} %copy-done.81), channel_id=1, source_target_pairs={{0,16},{4,20},{8,24},{12,28},{16,0},{20,4},{24,8},{28,12},{1,17},{... | collective-permute-start | bytes 2359304 | tf_op jit(solution)/shard_map/ppermute | solution.py:205
  854.6 188.4 %collective-permute-start.116 = (bf16[384,1024]{0,1:T(8,128)(2,1)}, bf16[384,1024]{0,1:T(8,128)(2,1)}, u32[]{:S(2)}, u32[]{:S(2)}) collective-permute-start(bf16[384,1024]{0,1:T(8,128)(2,1)} %fusion.34), channel_id=1, source_target_pairs={{0,24},{4,28},{8,16},{12,20},{16,8},{20,12},{24,0},{28,4},{1,25},{... | collective-permute-start | bytes 2359304 | tf_op jit(solution)/shard_map/ppermute | solution.py:205
  863.9 48.3 %collective-permute-start.62 = (bf16[768,512]{1,0:T(8,128)(2,1)S(1)}, bf16[768,512]{1,0:T(8,128)(2,1)S(1)}, u32[]{:S(2)}, u32[]{:S(2)}) collective-permute-start(bf16[768,512]{1,0:T(8,128)(2,1)S(1)} %copy-done.79), channel_id=1, source_target_pairs={{0,8},{4,12},{8,0},{12,4},{16,24},{20,28},{24,16},{28,20},{1,9},{5... | collective-permute-start | bytes 2359304 | tf_op jit(solution)/shard_map/ppermute | solution.py:205
  889.8 34.6 %collective-permute-start.61 = (bf16[768,512]{1,0:T(8,128)(2,1)S(1)}, bf16[768,512]{1,0:T(8,128)(2,1)S(1)}, u32[]{:S(2)}, u32[]{:S(2)}) collective-permute-start(bf16[768,512]{1,0:T(8,128)(2,1)S(1)} %add_convert_fusion.2), channel_id=1, source_target_pairs={{0,16},{4,20},{8,24},{12,28},{16,0},{20,4},{24,8},{28,12},{1,17},{... | collective-permute-start | bytes 2359304 | tf_op jit(solution)/shard_map/ppermute | solution.py:205
  909.0 127.1 %collective-permute-start.65 = (bf16[1536,512]{1,0:T(8,128)(2,1)}, bf16[1536,512]{1,0:T(8,128)(2,1)}, u32[]{:S(2)}, u32[]{:S(2)}) collective-permute-start(bf16[1536,512]{1,0:T(8,128)(2,1)} %bitcast.125), channel_id=1, source_target_pairs={{0,4},{4,0},{8,12},{12,8},{16,20},{20,16},{24,28},{28,24},{1,5},{5... | collective-permute-start | bytes 4718600 | tf_op jit(solution)/shard_map/ppermute | solution.py:201
  912.2 95.5 %collective-permute-start.111 = (bf16[384,1024]{0,1:T(8,128)(2,1)}, bf16[384,1024]{0,1:T(8,128)(2,1)}, u32[]{:S(2)}, u32[]{:S(2)}) collective-permute-start(bf16[384,1024]{0,1:T(8,128)(2,1)} %fusion.40), channel_id=1, source_target_pairs={{0,1},{1,2},{2,3},{3,0},{4,5},{5,6},{6,7},{7,4},{8,9},{9,10},{10,1... | collective-permute-start | bytes 2359304 | tf_op jit(solution)/shard_map/ppermute | solution.py:210
  924.4 87.0 %collective-permute-start.100 = (bf16[48,1536]{1,0:T(8,128)(2,1)S(1)}, bf16[48,1536]{1,0:T(8,128)(2,1)S(1)}, u32[]{:S(2)}, u32[]{:S(2)}) collective-permute-start(bf16[48,1536]{1,0:T(8,128)(2,1)S(1)} %dynamic-slice_bitcast_fusion.17), channel_id=1, source_target_pairs={{0,1},{1,2},{2,3},{3,0},{4,5},{5,6},{6,7},{7,4},{8,9},{9,10},{10,1... | collective-permute-start | bytes 442376 | tf_op jit(solution)/shard_map/ppermute | solution.py:210
  937.9 82.5 %collective-permute-start.96 = (bf16[4,48,1536]{2,1,0:T(8,128)(2,1)}, bf16[4,48,1536]{2,1,0:T(8,128)(2,1)}, u32[]{:S(2)}, u32[]{:S(2)}) collective-permute-start(bf16[4,48,1536]{2,1,0:T(8,128)(2,1)} %get-tuple-element.119), channel_id=1, source_target_pairs={{0,16},{4,20},{8,24},{12,28},{16,0},{20,4},{24,8},{28,12},{1,17},{... | collective-permute-start | bytes 1769480 | tf_op jit(solution)/shard_map/ppermute | solution.py:205
  1019.4 83.3 %collective-permute-start.54 = (f32[512,1536]{1,0:T(8,128)S(1)}, f32[512,1536]{1,0:T(8,128)S(1)}, u32[]{:S(2)}, u32[]{:S(2)}) collective-permute-start(f32[512,1536]{1,0:T(8,128)S(1)} %copy-done.28), channel_id=1, source_target_pairs={{0,4},{4,0},{8,12},{12,8},{16,20},{20,16},{24,28},{28,24},{1,5},{5... | collective-permute-start | bytes 9437192 | tf_op jit(solution)/shard_map/ppermute | solution.py:201
  1036.0 36.5 %collective-permute-start.63 = (bf16[256,1536]{1,0:T(8,128)(2,1)S(1)}, bf16[256,1536]{1,0:T(8,128)(2,1)S(1)}, u32[]{:S(2)}, u32[]{:S(2)}) collective-permute-start(bf16[256,1536]{1,0:T(8,128)(2,1)S(1)} %get-tuple-element.136), channel_id=1, source_target_pairs={{0,4},{4,0},{8,12},{12,8},{16,20},{20,16},{24,28},{28,24},{1,5},{5... | collective-permute-start | bytes 2359304 | tf_op jit(solution)/shard_map/ppermute | solution.py:201
  1086.0 35.6 %collective-permute-start.118 = (bf16[384,1024]{0,1:T(8,128)(2,1)S(1)}, bf16[384,1024]{0,1:T(8,128)(2,1)S(1)}, u32[]{:S(2)}, u32[]{:S(2)}) collective-permute-start(bf16[384,1024]{0,1:T(8,128)(2,1)S(1)} %get-tuple-element.74), channel_id=1, source_target_pairs={{0,16},{4,20},{8,24},{12,28},{16,0},{20,4},{24,8},{28,12},{1,17},{... | collective-permute-start | bytes 2359304 | tf_op jit(solution)/shard_map/ppermute | solution.py:205
  1128.5 52.5 %collective-permute-start.120 = (bf16[4,384,1024]{1,2,0:T(8,128)(2,1)S(1)}, bf16[4,384,1024]{1,2,0:T(8,128)(2,1)S(1)}, u32[]{:S(2)}, u32[]{:S(2)}) collective-permute-start(bf16[4,384,1024]{1,2,0:T(8,128)(2,1)S(1)} %pad_maximum_fusion.3), channel_id=1, source_target_pairs={{0,4},{4,0},{8,12},{12,8},{16,20},{20,16},{24,28},{28,24},{1,5},{5... | collective-permute-start | bytes 9437192 | tf_op jit(solution)/shard_map/ppermute | solution.py:201
  (193 other events, 3804.6 us)

commit v2 on v1

--- a/solution.py
+++ b/solution.py
@@ -96,6 +96,7 @@
         functools.partial(fwd_kernel, nchip, SCALE),
         grid_spec=grid_spec,
         out_shape=[jax.ShapeDtypeStruct((heads * 192, T), jnp.bfloat16), jax.ShapeDtypeStruct((heads, nq, 1, 256), jnp.float32)],
+        cost_estimate=pl.CostEstimate(flops=90 * 10**9, bytes_accessed=16 * 2**20, transcendentals=0),
         name="attention_forward",
     )(ids, inv, qT, *ks, *vs)
 
@@ -188,9 +189,283 @@
         functools.partial(bwd_kernel, nchip, SCALE),
         grid_spec=grid_spec,
         out_shape=[jax.ShapeDtypeStruct((heads * 192, T), jnp.float32)] + [slab] * (2 * nchip),
+        cost_estimate=pl.CostEstimate(flops=90 * 10**9, bytes_accessed=24 * 2**20, transcendentals=0),
         name="attention_backward",
     )(ids, inv, qT, oT, doT, lse, *ks, *vs)
     return outs[0], outs[1:1 + nchip], outs[1 + nchip:]
+
+
+def front_kernel(zsize, *refs):
+    (tok, gains, key_w, value_w, query_w, out_w, gate_w, up_w, down_w, cos, sin) = refs[:11]
+    (full_kv, full_q, full_o, wide, tall, far_wide, far_tall, x_out, first, q_out, gains_out, k0, k1, k2, k3, v0, v1, v2, v3) = refs[11:30]
+    x_s, gain_s, kv_w, q_w, kv_s, ss, rs, ls, gs, gr = refs[30:]
+    ks, vs = (k0, k1, k2, k3), (v0, v1, v2, v3)
+    index, depth = lax.axis_index("ctx"), lax.axis_index("fsdp")
+    chip, core = index // 2, lax.rem(index, 2)
+    fine = tall.shape[1]
+    chunk = fine * zsize
+    width = first.shape[1]
+    length = first.shape[0]
+    kv_rows = k0.shape[0]
+    nxt, prv = lax.rem(depth + 1, zsize), lax.rem(depth + zsize - 1, zsize)
+    to_next, to_prev = (index, nxt), (index, prv)
+    chip_x, chip_y, chip_d = chip + 1 - 2 * lax.rem(chip, 2), lax.rem(chip + 2, 4), 3 - chip
+    to_x, to_y, to_core = (chip_x * 2 + core, depth), (chip_y * 2 + core, depth), (chip * 2 + 1 - core, depth)
+
+    barrier = pltpu.get_barrier_semaphore()
+    for target in (to_next, to_prev, to_x, to_y, to_core):
+        pl.semaphore_signal(barrier, inc=1, device_id=target, device_id_type=pl.DeviceIdType.MESH)
+    pl.semaphore_wait(barrier, 5)
+
+    count = [0, 0]
+    sent = []
+
+    def send(src, dst, target):
+        k = count[0]
+        count[0] += 1
+        copy = pltpu.make_async_remote_copy(
+            src_ref=src, dst_ref=dst, send_sem=ss.at[k], recv_sem=rs.at[k], device_id=target, device_id_type=pl.DeviceIdType.MESH
+        )
+        copy.start()
+        sent.append(copy)
+        return copy
+
+    def local(src, dst):
+        k = count[1]
+        count[1] += 1
+        copy = pltpu.make_async_copy(src, dst, ls.at[k])
+        copy.start()
+        return copy
+
+    def slot(s):
+        return lax.rem(depth + zsize - s, zsize)
+
+    steps = range(1, zsize)
+    last = zsize - 1
+    tokens_there = send(tok.at[1 - core], x_s.at[1], to_core)
+    own_kv = [local(key_w, full_kv.at[depth, :, :, :, pl.ds(0, kv_rows)]), local(value_w, full_kv.at[depth, :, :, :, pl.ds(kv_rows, kv_rows)])]
+    gain_s[depth] = gains[...]
+    for copy in own_kv:
+        copy.wait()
+
+    weights = {"kv": full_kv, "q": full_q, "o": full_o}
+    shards = {"q": query_w, "o": out_w}
+    moves = {}
+
+    def ring_step(name, s):
+        full = weights[name]
+        place = full.at[slot(s - 1), chip, core]
+        source = shards[name].at[chip, core] if name in shards and s == 1 else place
+        moves[name, "ring", s] = send(source, place, to_next)
+
+    def spread(name, s):
+        place = weights[name].at[slot(s), chip, core]
+        moves[name, "x", s] = send(place, place, to_x)
+        moves[name, "y", s] = send(place, place, to_y)
+
+    def forward(name, s):
+        mid = width // 2
+        moves[name, "x", s].wait_recv()
+        left = weights[name].at[slot(s), chip_x, core, :, pl.ds(0, mid)]
+        moves[name, "fy", s] = send(left, left, to_y)
+        moves[name, "y", s].wait_recv()
+        right = weights[name].at[slot(s), chip_y, core, :, pl.ds(mid, mid)]
+        moves[name, "fx", s] = send(right, right, to_x)
+
+    def cross(name, s):
+        moves[name, "fx", s].wait_recv()
+        moves[name, "fy", s].wait_recv()
+        column = weights[name].at[slot(s), :, core]
+        moves[name, "core", s] = send(column, column, to_core)
+
+    def gain_step(s):
+        place = gain_s.at[slot(s - 1)]
+        copy = pltpu.make_async_remote_copy(
+            src_ref=place, dst_ref=place, send_sem=gs.at[s], recv_sem=gr.at[s], device_id=to_next, device_id_type=pl.DeviceIdType.MESH
+        )
+        copy.start()
+        sent.append(copy)
+        moves["gain", s] = copy
+
+    ring_step("kv", 1)
+    gain_step(1)
+    own_late = [local(query_w, full_q.at[depth]), local(out_w, full_o.at[depth])]
+    own_ffn = [local(down_w.at[pl.ds(pl.multiple_of(core * (4 * fine) + chip * fine, fine), fine)], tall.at[depth])]
+    for part in range(zsize):
+        column = pl.multiple_of(part * (8 * fine) + core * (4 * fine) + chip * fine, fine)
+        own_ffn.append(local(gate_w.at[:, pl.ds(column, fine)], wide.at[depth, :, pl.ds(part * fine, fine)]))
+        own_ffn.append(local(up_w.at[:, pl.ds(column, fine)], wide.at[depth, :, pl.ds(chunk + part * fine, fine)]))
+    far_ffn = [local(down_w.at[pl.ds(pl.multiple_of(core * (4 * fine) + chip_d * fine, fine), fine)], far_tall)]
+    for part in range(zsize):
+        column = pl.multiple_of(part * (8 * fine) + core * (4 * fine) + chip_d * fine, fine)
+        far_ffn.append(local(gate_w.at[:, pl.ds(column, fine)], far_wide.at[:, pl.ds(part * fine, fine)]))
+        far_ffn.append(local(up_w.at[:, pl.ds(column, fine)], far_wide.at[:, pl.ds(chunk + part * fine, fine)]))
+
+    for s in steps:
+        moves["kv", "ring", s].wait_recv()
+        moves["gain", s].wait_recv()
+        if s < last:
+            ring_step("kv", s + 1)
+            gain_step(s + 1)
+        else:
+            ring_step("q", 1)
+        spread("kv", s)
+    for s in steps:
+        forward("kv", s)
+        moves["q", "ring", s].wait_recv()
+        ring_step("q", s + 1) if s < last else ring_step("o", 1)
+        spread("q", s)
+    for s in steps:
+        cross("kv", s)
+
+    tokens_there.wait_recv()
+    x_out[0:length // 2] = tok[core]
+    x_out[length // 2:] = x_s[1]
+    gain_rows = [gain_s[place] for place in range(zsize)]
+    gains_full = jnp.concatenate(gain_rows, axis=1)
+    gains_out[...] = gains_full
+    gain = gains_full[0:1]
+    rows = 64
+
+    def normalize(t, _):
+        part = pl.ds(pl.multiple_of(t * rows, rows), rows)
+        v = x_out[part].astype(F32)
+        inverse = lax.rsqrt(jnp.mean(v * v, -1, keepdims=True) + EPS)
+        first[part] = (v * inverse * gain).astype(BF)
+        return 0
+
+    lax.fori_loop(0, length // rows, normalize, 0)
+
+    moves["o", "ring", 1].wait_recv()
+    if last > 1:
+        ring_step("o", 2)
+    spread("o", 1)
+    for s in steps:
+        moves["kv", "core", s].wait_recv()
+    load_kv = local(full_kv, kv_w)
+    if last > 1:
+        moves["o", "ring", 2].wait_recv()
+        if last > 2:
+            ring_step("o", 3)
+        spread("o", 2)
+    load_kv.wait()
+    tile = 384
+
+    def project(weight, t, turn):
+        cols = pl.ds(pl.multiple_of(t * tile, tile), tile)
+        w = weight[:, :, :, :, cols].reshape(width, tile)
+        r = jnp.dot(first[...], w, preferred_element_type=F32).T
+        if turn:
+            r = rotate(r, cos[...], sin[...])
+        return r.astype(BF)
+
+    def project_kv(t, turn):
+        kv_s[pl.ds(pl.multiple_of(t * tile, tile), tile)] = project(kv_w, t, turn)
+        return 0
+
+    per = kv_rows // tile
+    lax.fori_loop(0, per, lambda t, _: project_kv(t, True), 0)
+    k_here, v_here = kv_s.at[pl.ds(0, kv_rows)], kv_s.at[pl.ds(kv_rows, kv_rows)]
+    k_x, k_y = send(k_here, k1, to_x), send(k_here, k2, to_y)
+    lax.fori_loop(per, 2 * per, lambda t, _: project_kv(t, False), 0)
+    v_y, v_x = send(v_here, v2, to_y), send(v_here, v1, to_x)
+    keep = [local(k_here, k0), local(v_here, v0)]
+
+    for s in range(3, zsize):
+        moves["o", "ring", s].wait_recv()
+        if s < last:
+            ring_step("o", s + 1)
+        spread("o", s)
+    for copy in own_ffn:
+        copy.wait()
+
+    def ffn_step(s):
+        a, b = wide.at[slot(s - 1)], tall.at[slot(s - 1)]
+        moves["ffn", s] = (send(a, a, to_next), send(b, b, to_next))
+
+    ffn_step(1)
+    for s in steps:
+        forward("q", s)
+    for s in steps:
+        cross("q", s)
+    for s in steps:
+        forward("o", s)
+    for s in steps:
+        cross("o", s)
+    for s in steps:
+        moves["q", "core", s].wait_recv()
+    for copy in own_late:
+        copy.wait()
+    local(full_q, q_w).wait()
+
+    def project_q(t, _):
+        q_out[pl.ds(pl.multiple_of(t * tile, tile), tile)] = project(q_w, t, True)
+        return 0
+
+    lax.fori_loop(0, width // tile, project_q, 0)
+    k_x.wait_recv()
+    k_d = send(k1, k3, to_y)
+    v_y.wait_recv()
+    v_d = send(v2, v3, to_x)
+    for s in steps:
+        for copy in moves["ffn", s]:
+            copy.wait_recv()
+        if s < last:
+            ffn_step(s + 1)
+    for s in steps:
+        moves["o", "core", s].wait_recv()
+    for copy in (k_y, v_x, k_d, v_d):
+        copy.wait_recv()
+    for copy in keep + far_ffn:
+        copy.wait()
+    for copy in sent:
+        copy.wait_send()
+
+
+def front(tokens, gains, key_w, value_w, query_w, out_w, gate_w, up_w, down_w, cosine, sine, zsize, ctx):
+    width = tokens.shape[2]
+    length = 2 * tokens.shape[1]
+    rows = width // zsize
+    strip = rows // ctx
+    fine = down_w.shape[0] // ctx
+    chunk = fine * zsize
+    kv_rows = key_w.shape[1]
+    chips = ctx // 2
+    cut = lambda w: w.reshape(chips, 2, strip, w.shape[1])
+    square = jax.ShapeDtypeStruct((zsize, chips, 2, strip, width), BF)
+    flat = jax.ShapeDtypeStruct((kv_rows, length), BF)
+    hbm, vmem = pl.BlockSpec(memory_space=pl.ANY), pl.BlockSpec(memory_space=pltpu.VMEM)
+    copies = 18 * (zsize - 1) + 2 * (zsize - 1) + 8
+    return pl.pallas_call(
+        functools.partial(front_kernel, zsize),
+        out_shape=[
+            square, square, square,
+            jax.ShapeDtypeStruct((zsize, rows, 2 * chunk), BF),
+            jax.ShapeDtypeStruct((zsize, fine, width), BF),
+            jax.ShapeDtypeStruct((rows, 2 * chunk), BF),
+            jax.ShapeDtypeStruct((fine, width), BF),
+            jax.ShapeDtypeStruct((length, width), BF),
+            jax.ShapeDtypeStruct((length, width), BF),
+            jax.ShapeDtypeStruct((width, length), BF),
+            jax.ShapeDtypeStruct((2, width), F32),
+        ] + [flat] * 8,
+        in_specs=[vmem, vmem] + [hbm] * 7 + [vmem] * 2,
+        out_specs=[hbm] * 7 + [vmem] * 4 + [hbm] * 8,
+        scratch_shapes=[
+            pltpu.VMEM((2, length // 2, width), BF),
+            pltpu.VMEM((zsize, 2, rows), F32),
+            pltpu.VMEM(square.shape, BF),
+            pltpu.VMEM(square.shape, BF),
+            pltpu.VMEM((2 * kv_rows, length), BF),
+            pltpu.SemaphoreType.DMA((copies,)),
+            pltpu.SemaphoreType.DMA((copies,)),
+            pltpu.SemaphoreType.DMA((10 + 4 * zsize,)),
+            pltpu.SemaphoreType.DMA((zsize,)),
+            pltpu.SemaphoreType.DMA((zsize,)),
+        ],
+        compiler_params=pltpu.CompilerParams(collective_id=0, has_side_effects=True, vmem_limit_bytes=40 * 2**20),
+        name="front",
+    )(tokens, gains, cut(key_w), cut(value_w), cut(query_w), cut(out_w), gate_w, up_w, down_w, cosine, sine)
 
 
 def mm(left, right, left_dim, right_dim):
@@ -224,6 +499,15 @@
     for s in range(1, n):
         piece = ring(piece)
         buffer = place(buffer, piece, lax.rem(depth + n - s, n))
+    return buffer
+
+
+def depth_gather_direct(piece, depth):
+    n = lax.axis_size("fsdp")
+    buffer = place(jnp.zeros((n,) + piece.shape, piece.dtype), piece, depth)
+    for s in range(1, n):
+        moved = lax.ppermute(piece, "fsdp", [(k, (k + s) % n) for k in range(n)])
+        buffer = place(buffer, moved, lax.rem(depth + n - s, n))
     return buffer
 
 
@@ -295,57 +579,11 @@
     chunk = fine * zsize
     kv_rows = KEY_HEADS * HEAD_WIDTH
 
-    gains = jnp.stack([attention_gain, feedforward_gain])
-    gain_buffer = place(jnp.zeros((zsize, 2, rows), BF), gains, depth)
-    for s in range(1, zsize):
-        moved = lax.ppermute(gains, "fsdp", [(k, (k + s) % zsize) for k in range(zsize)])
-        gain_buffer = place(gain_buffer, moved, lax.rem(depth + zsize - s, zsize))
-    gains_full = jnp.transpose(gain_buffer, (1, 0, 2)).reshape(2, width).astype(F32)
-    gain_first, gain_second = gains_full[0], gains_full[1]
-
-    def gather_square(shard):
-        strips = shard.reshape(ctx, strip, shard.shape[1])
-        pair = jnp.stack([pick(strips, index), pick(strips, index ^ (2 * diag))])
-        pair = depth_gather(pair, depth)
-        own, far = pair[:, 0], pair[:, 1]
-        found = {0: own, diag: far}
-        for r in near:
-            found[r] = hop(own, r)
-        full = jnp.zeros((zsize, ctx, strip, shard.shape[1]), BF)
-        for r in range(chips):
-            full = place(full, found[r], index ^ (2 * r), 1)
-            full = place(full, swap(found[r]), index ^ (2 * r + 1), 1)
-        return full.reshape(width, shard.shape[1])
-
-    key_value_full = gather_square(jnp.concatenate([key_matrix, value_matrix], 1))
-    query_full = gather_square(query_weight)
-    output_full = gather_square(output_weight)
-
-    gate_cut = gate_weight.reshape(rows, zsize, 2, chips, fine)
-    up_cut = up_weight.reshape(rows, zsize, 2, chips, fine)
-    down_cut = down_weight.reshape(2, chips, fine, width)
-
-    def own_piece(r):
-        gate = pick(pick(gate_cut, core, 2), chip ^ r, 2).reshape(rows, chunk)
-        up = pick(pick(up_cut, core, 2), chip ^ r, 2).reshape(rows, chunk)
-        down = pick(pick(down_cut, core), chip ^ r)
-        return jnp.concatenate([gate, up], 1), down
-
-    gate_up, down = {}, {}
-    for r in (0, diag):
-        wide, tall = own_piece(r)
-        gate_up[r] = depth_gather(wide, depth).reshape(width, 2 * chunk)
-        down[r] = depth_gather(tall, depth).reshape(chunk, width)
-    for r in near:
-        gate_up[r] = hop(gate_up[0], r)
-        down[r] = hop(down[0], r)
-
-    x = jnp.concatenate([pick(tokens, core), swap(pick(tokens, 1 - core))]).astype(F32)
     cot_there = swap(cotangent)
     cot = jnp.concatenate(
         [pick(cotangent, core), pick(cot_there, core), pick(cot_there, 1 - core), pick(cotangent, 1 - core)]
     )
-    length = x.shape[0]
+    length = 2 * slice_len
 
     ids_all = jnp.concatenate([pick(block_pairs, index ^ r) for r in range(ctx)])
     ids = ids_all[:4]
@@ -359,22 +597,86 @@
     angles = frequency[:, None] * positions.astype(F32)[None, :]
     cosine, sine = jnp.cos(angles), jnp.sin(angles)
 
-    inverse_first = lax.rsqrt(jnp.mean(x * x, -1, keepdims=True) + EPS)
-    unit_first = x * inverse_first
-    first = (unit_first * gain_first).astype(BF)
-    first_t = jnp.transpose(first)
-    kv = mm(key_value_full, first_t, 0, 0)
-    keys = {0: rotate(kv[:kv_rows], cosine, sine).astype(BF)}
-    values = {0: kv[kv_rows:].astype(BF)}
-    top = 1
-    while top < chips:
-        top *= 2
-    for r in range(1, chips):
-        high = 1 << (r.bit_length() - 1)
-        low = r & -r
-        keys[r] = hop(keys[r ^ high], high)
-        values[r] = hop(values[r ^ low], low)
-    query = rotate(mm(query_full, first_t, 0, 0), cosine, sine).astype(BF)
+    gate_up, down, keys, values = {}, {}, {}, {}
+    fast = chips == 4 and strip % 16 == 0 and fine % 128 == 0
+    if fast:
+        (key_value_full, query_full, output_full, wide, tall, far_wide, far_tall, x, first, query, gains_full, *kv) = front(
+            tokens, jnp.stack([attention_gain, feedforward_gain]).astype(F32), key_matrix, value_matrix, query_weight,
+            output_weight, gate_weight, up_weight, down_weight, cosine, sine, zsize, ctx,
+        )
+        key_value_full, query_full, output_full = (w.reshape(width, width) for w in (key_value_full, query_full, output_full))
+        gate_up[0], down[0] = wide.reshape(width, 2 * chunk), tall.reshape(chunk, width)
+        for r in range(chips):
+            keys[r], values[r] = kv[r], kv[chips + r]
+        x = x.astype(F32)
+        gain_first, gain_second = gains_full[0], gains_full[1]
+        inverse_first = lax.rsqrt(jnp.mean(x * x, -1, keepdims=True) + EPS)
+        unit_first = x * inverse_first
+        first_t = jnp.transpose(first)
+        gate_up[diag] = depth_gather_direct(far_wide, depth).reshape(width, 2 * chunk)
+        down[diag] = depth_gather_direct(far_tall, depth).reshape(chunk, width)
+    else:
+        gate_cut = gate_weight.reshape(rows, zsize, 2, chips, fine)
+        up_cut = up_weight.reshape(rows, zsize, 2, chips, fine)
+        down_cut = down_weight.reshape(2, chips, fine, width)
+
+        def own_piece(r):
+            gate = pick(pick(gate_cut, core, 2), chip ^ r, 2).reshape(rows, chunk)
+            up = pick(pick(up_cut, core, 2), chip ^ r, 2).reshape(rows, chunk)
+            down = pick(pick(down_cut, core), chip ^ r)
+            return jnp.concatenate([gate, up], 1), down
+
+        gains = jnp.stack([attention_gain, feedforward_gain])
+        gain_buffer = place(jnp.zeros((zsize, 2, rows), BF), gains, depth)
+        for s in range(1, zsize):
+            moved = lax.ppermute(gains, "fsdp", [(k, (k + s) % zsize) for k in range(zsize)])
+            gain_buffer = place(gain_buffer, moved, lax.rem(depth + zsize - s, zsize))
+        gains_full = jnp.transpose(gain_buffer, (1, 0, 2)).reshape(2, width).astype(F32)
+        gain_first, gain_second = gains_full[0], gains_full[1]
+
+        def gather_square(shard):
+            strips = shard.reshape(ctx, strip, shard.shape[1])
+            pair = jnp.stack([pick(strips, index), pick(strips, index ^ (2 * diag))])
+            pair = depth_gather(pair, depth)
+            own, far = pair[:, 0], pair[:, 1]
+            found = {0: own, diag: far}
+            for r in near:
+                found[r] = hop(own, r)
+            full = jnp.zeros((zsize, ctx, strip, shard.shape[1]), BF)
+            for r in range(chips):
+                full = place(full, found[r], index ^ (2 * r), 1)
+                full = place(full, swap(found[r]), index ^ (2 * r + 1), 1)
+            return full.reshape(width, shard.shape[1])
+
+        key_value_full = gather_square(jnp.concatenate([key_matrix, value_matrix], 1))
+        query_full = gather_square(query_weight)
+        output_full = gather_square(output_weight)
+
+        x = jnp.concatenate([pick(tokens, core), swap(pick(tokens, 1 - core))]).astype(F32)
+        wide, tall = own_piece(0)
+        gate_up[0] = depth_gather(wide, depth).reshape(width, 2 * chunk)
+        down[0] = depth_gather(tall, depth).reshape(chunk, width)
+        inverse_first = lax.rsqrt(jnp.mean(x * x, -1, keepdims=True) + EPS)
+        unit_first = x * inverse_first
+        first = (unit_first * gain_first).astype(BF)
+        first_t = jnp.transpose(first)
+        kv = mm(key_value_full, first_t, 0, 0)
+        keys[0] = rotate(kv[:kv_rows], cosine, sine).astype(BF)
+        values[0] = kv[kv_rows:].astype(BF)
+        for r in range(1, chips):
+            high = 1 << (r.bit_length() - 1)
+            low = r & -r
+            keys[r] = hop(keys[r ^ high], high)
+            values[r] = hop(values[r ^ low], low)
+        query = rotate(mm(query_full, first_t, 0, 0), cosine, sine).astype(BF)
+        wide, tall = own_piece(diag)
+        gate_up[diag] = depth_gather(wide, depth).reshape(width, 2 * chunk)
+        down[diag] = depth_gather(tall, depth).reshape(chunk, width)
+
+    for r in near:
+        gate_up[r] = hop(gate_up[0], r)
+        down[r] = hop(down[0], r)
+
     key_list = [keys[r] for r in range(chips)]
     value_list = [values[r] for r in range(chips)]
     attended, log_total = attn_fwd(ids, order, query, key_list, value_list, KEY_HEADS)
@@ -387,7 +689,7 @@
     out_part = 0.0
     second_grad = 0.0
     wide_grad, tall_grad = {}, {}
-    for r in list(near) + [0, diag]:
+    for r in [0] + list(near) + [diag]:
         pre = mm(second, gate_up[r], 1, 0)
         gate_pre, up_pre = pre[:, :chunk], pre[:, chunk:]
         hidden_grad = mm(cot, down[r], 1, 1)
@@ -473,7 +775,18 @@
     tokens_grad = stored(tokens_part[:q], swap(tokens_part[q:]))
 
     def gain_total(part):
-        return lax.dynamic_slice_in_dim(lax.psum(part, ("ctx", "fsdp")), depth * rows, rows)
+        cut = part.reshape(zsize, rows)
+        total = pick(cut, depth)
+        for s in range(1, zsize):
+            total = total + lax.ppermute(
+                pick(cut, lax.rem(depth + s, zsize)), "fsdp", [(k, (k + s) % zsize) for k in range(zsize)]
+            )
+        total = total + swap(total)
+        bit = 1
+        while bit < chips:
+            total = total + hop(total, bit)
+            bit *= 2
+        return total
 
     return (
         layer_out,

time: 1220 us -> 1060 us (0.87)
  Pallas kernels: 172 us -> 332 us
  waiting for transfers between devices: 422 us -> 275 us
  local copies, waits for them, and re-layouts: 211 us -> 110 us
  blocking collectives: 39.6 us -> 0 us
  matrix products: 184 us -> 169 us
    pallas_call x0 -> x1, Pallas kernels: none -> 160 us  [front(): pl.pallas_call(functools.partial(front_kernel, zsize), out_shape=[square,...]
    ppermute x51 -> x30, waiting for transfers between devices: 240 us -> 137 us  [ring(): return lax.ppermute(a, 'fsdp', [(i, (i + 1) % n) for i in range(n)])]
    ppermute x52 -> x44, waiting for transfers between devices: 179 us -> 120 us  [hop(): lax.ppermute(a, 'ctx', [(i, i ^ 2 * r) for i in range(lax.axis_size('ctx'...]
    dynamic_update_slice x85 -> x42, local copies, waits for them, and re-layouts: 67.3 us -> 15.2 us  [place(): lax.dynamic_update_slice_in_dim(buffer, jnp.expand_dims(piece, axis), ind...]
    psum x1 -> x0, blocking collectives: 39.6 us -> none  [gain_total(): lax.psum(part, ('ctx', 'fsdp'))]
    ppermute x3 -> x12, waiting for transfers between devices: 0.01 us -> 17.1 us  [the longest x6 17.1 us: depth_gather_direct(): moved = lax.ppermute(piece, 'fsdp', [(k, (k + s) % n) for k in range(n)])]
    dot_general x33 -> x31, matrix products: 184 us -> 169 us  [mm(): lax.dot_general(left, right, (((left_dim,), (right_dim,)), ((), ())), pre...]
    another operation x15 -> x5, local copies, waits for them, and re-layouts: 15.9 us -> 1.65 us  [the longest x2 1.37 us: body(): jnp.stack([attention_gain, feedforward_gain]).astype(F32)]
  transfers between devices with their start and end apart: 134 -> 103, of which waited for: 56 -> 42; matrix products, arithmetic and copies ran while one was open for 36% -> 29% of each run, Pallas kernels for 14% -> 16%
where the time goes in v2:
time: 1060 us; the launch traced here: 1050 us
  Pallas kernels  332 us (31%)
  waiting for transfers between devices  275 us (26%)
  matrix products  169 us (16%)
  local copies, waits for them, and re-layouts  110 us (10%)
  starting transfers between devices  84.5 us (8%)
  other arithmetic  78.5 us (7%)
    dot_general x31, matrix products, mm(): lax.dot_general(left, right, (((left_dim,), (right_dim,)), ((), ())), pre...  169 us
    pallas_call x1, Pallas kernels, front(): pl.pallas_call(functools.partial(front_kernel, zsize), out_shape=[square,...  160 us
    ppermute x30, waiting for transfers between devices, ring(): return lax.ppermute(a, 'fsdp', [(i, (i + 1) % n) for i in range(n)])  137 us
    ppermute x44, waiting for transfers between devices, hop(): lax.ppermute(a, 'ctx', [(i, i ^ 2 * r) for i in range(lax.axis_size('ctx'...  120 us
    pallas_call x1, Pallas kernels, attn_bwd(): pl.pallas_call(functools.partial(bwd_kernel, nchip, SCALE), grid_spec=gri...  87.4 us
    pallas_call x1, Pallas kernels, attn_fwd(): pl.pallas_call(functools.partial(fwd_kernel, nchip, SCALE), grid_spec=gri...  84.2 us
    ppermute x44, starting transfers between devices, hop(): lax.ppermute(a, 'ctx', [(i, i ^ 2 * r) for i in range(lax.axis_size('ctx'...  51.3 us
    unnamed x223, local copies, waits for them, and re-layouts  37.4 us
  transfers between devices with their start and end apart: 103, of which 42 were waited for; matrix products, arithmetic and copies ran while one was open for 29% of the time, Pallas kernels for 16%

profile of v2, /device:TPU:0, one launch (start us, length us, event | category | flops | bytes accessed | tf_op | source)
XLA Modules:
  0.0 1051.4 jit_solution(15561020793820133592)
XLA Ops:
  9.3 160.0 %front.1 = (bf16[4,4,2,48,1536]{4,3,2,1,0:T(8,128)(2,1)}, bf16[4,4,2,48,1536]{4,3,2,1,0:T(8,128)(2,1)}, bf16[4,4,2,48,1536]{4,3,2,1,0:T(8,128)(2,1)}, bf16[4,384...) custom-call(bf16[2,256,1536]{2,1,0:T(8,128)(2,1)} %refs_0_.1, ...), custom_call_target="tpu_custom_call" | custom-call | tf_op jit(solution)/shard_map/front/pallas_call | solution.py:439
  184.2 84.2 %attention_forward.1 = (bf16[1536,512]{1,0:T(8,128)(2,1)}, f32[8,4,1,256]{3,2,1,0:T(1,128)}) custom-call(s32[4]{0:T(128)} %get-tuple-element.128.ids_ref, s32[16]{0:T(128)} %select_reduce_fusion.inv_ref, bf16[1536,512]{1,0:T(8,128)(2,1)} %get-tuple-element.42.q_ref, bf16[768,512]{1,0:T(8,128)(2,1)} %copy-done.12, bf16[768,512]{1,0:T(8,128)(2,1)} %copy-done.13, ...), custom_call_target="tpu_custom_call" | custom-call | flops 89999998976 | bytes 16777216 | tf_op jit(solution)/shard_map/attention_forward/pallas_call | solution.py:95
  268.4 7.3 multiply_reduce_fusion.2
  294.7 7.4 collective-permute-done.10
  312.9 9.7 collective-permute-done.7
  327.4 6.6 fusion.109
  334.0 6.0 multiply_convert_fusion.8
  340.0 5.5 fusion.106
  345.5 5.6 multiply_convert_fusion.2
  364.5 15.9 %fusion.42 = f32[1024,1536]{1,0:T(8,128)} fusion(bf16[1536,1024]{1,0:T(8,128)(2,1)} %bitcast.6, bf16[1024,512]{0,1:T(8,128)(2,1)S(1)} %copy-done.94, bf16[1024,512]{0,1:T(8,128)(2,1)S(1)} %copy-done.93), kind=kOutput, calls=%fused_computation.118 | convolution fusion | flops 3225419776 | bytes 11534336 | tf_op jit(solution)/shard_map/dot_general | solution.py:472
  393.1 5.8 collective-permute-done.96
  411.4 5.5 copy.58
  423.6 5.5 fusion.107
  429.1 6.4 multiply_convert_fusion.4
  439.6 5.5 fusion.108
  445.1 9.1 collective-permute-done.2
  462.6 7.5 fusion.40
  470.1 7.9 fusion.41
  478.1 8.1 add_add_fusion
  526.7 12.8 %collective-permute-done.93 = bf16[128,1536]{1,0:T(8,128)(2,1)S(1)} collective-permute-done((bf16[128,1536]{1,0:T(8,128)(2,1)}, bf16[128,1536]{1,0:T(8,128)(2,1)S(1)}, u32[]{:S(2)}, u32[]{:S(2)}) %collective-permute-start.93) | collective-permute-done | bytes 393248 | tf_op jit(solution)/shard_map/ppermute | solution.py:485
  541.5 7.6 convolution_convert_fusion.2
  565.1 6.0 fusion.119
  579.3 87.4 %attention_backward.1 = (f32[1536,512]{1,0:T(8,128)}, bf16[768,512]{1,0:T(8,128)(2,1)}, bf16[768,512]{1,0:T(8,128)(2,1)}, bf16[768,512]{1,0:T(8,128)(2,1)}, bf16...) custom-call(s32[4]{0:T(128)} %get-tuple-element.128.ids_ref, ...), custom_call_target="tpu_custom_call" | custom-call | flops 89999998976 | bytes 25165824 | tf_op jit(solution)/shard_map/attention_backward/pallas_call | solution.py:188
  670.4 7.4 fusion.124
  690.9 14.0 %collective-permute-done.75 = f32[384]{0:T(512)S(1)} collective-permute-done((f32[384]{0:T(512)S(1)}, f32[384]{0:T(512)S(1)}, u32[]{:S(2)}, u32[]{:S(2)}) %collective-permute-start.75) | collective-permute-done | bytes 1568 | tf_op jit(solution)/shard_map/ppermute | solution.py:480
  706.3 7.7 collective-permute-done.15
  723.6 14.1 %collective-permute-done.76 = f32[384]{0:T(512)S(1)} collective-permute-done((f32[384]{0:T(512)S(1)}, f32[384]{0:T(512)S(1)}, u32[]{:S(2)}, u32[]{:S(2)}) %collective-permute-start.76) | collective-permute-done | bytes 1568 | tf_op jit(solution)/shard_map/ppermute | solution.py:480
  744.1 14.1 %collective-permute-done.19 = bf16[768,512]{1,0:T(8,128)(2,1)S(1)} collective-permute-done((bf16[768,512]{1,0:T(8,128)(2,1)S(1)}, bf16[768,512]{1,0:T(8,128)(2,1)S(1)}, u32[]{:S(2)}, u32[]{:S(2)}) %collective-permute-start.19) | collective-permute-done | bytes 786464 | tf_op jit(solution)/shard_map/ppermute | solution.py:480
  781.5 6.3 collective-permute-done.80
  813.9 6.5 collective-permute-done.63
  821.4 6.0 collective-permute-done.35
  827.4 8.1 collective-permute-done.64
  836.5 6.8 collective-permute-done.36
  843.3 6.9 collective-permute-done.65
  853.5 13.5 %collective-permute-done.59 = bf16[4,48,1536]{2,1,0:T(8,128)(2,1)S(1)} collective-permute-done((bf16[4,48,1536]{2,1,0:T(8,128)(2,1)S(1)}, bf16[4,48,1536]{2,1,0:T(8,128)(2,1)S(1)}, u32[]{:S(2)}, u32[]{:S(2)}) %collective-permute-start.59) | collective-permute-done | bytes 589856 | tf_op jit(solution)/shard_map/ppermute | solution.py:480
  868.9 22.2 %collective-permute-done.31 = bf16[48,1536]{1,0:T(8,128)(2,1)S(1)} collective-permute-done((bf16[48,1536]{1,0:T(8,128)(2,1)S(1)}, bf16[48,1536]{1,0:T(8,128)(2,1)S(1)}, u32[]{:S(2)}, u32[]{:S(2)}) %collective-permute-start.31) | collective-permute-done | bytes 147488 | tf_op jit(solution)/shard_map/ppermute | solution.py:485
  891.1 6.9 collective-permute-done.60
  904.6 6.1 collective-permute-done.32
  910.8 6.9 collective-permute-done.61
  917.8 6.9 collective-permute-done.33
  941.1 14.2 %collective-permute-done.68 = bf16[48,1536]{1,0:T(8,128)(2,1)S(1)} collective-permute-done((bf16[48,1536]{1,0:T(8,128)(2,1)S(1)}, bf16[48,1536]{1,0:T(8,128)(2,1)S(1)}, u32[]{:S(2)}, u32[]{:S(2)}) %collective-permute-start.68) | collective-permute-done | bytes 147488 | tf_op jit(solution)/shard_map/ppermute | solution.py:480
  965.8 8.3 collective-permute-done.87
  977.0 9.0 collective-permute-done.44
  986.5 7.8 collective-permute-done.45
  1002.6 6.9 collective-permute-done.47
  1031.9 6.6 copy.67
  1038.4 6.1 copy.65
  1044.6 6.6 copy.68
  (592 shorter events, 339.5 us)
Async XLA Ops:
  177.7 128.3 %collective-permute-start.5 = (bf16[384,1024]{1,0:T(8,128)(2,1)S(1)}, bf16[384,1024]{1,0:T(8,128)(2,1)}, u32[]{:S(2)}, u32[]{:S(2)}) collective-permute-start(bf16[384,1024]{1,0:T(8,128)(2,1)S(1)} %get-tuple-element.56), channel_id=1, source_target_pairs={{0,1},{1,2},{2,3},{3,0},{4,5},{5,6},{6,7},{7,4},{8,9},{9,10},{10,1... | collective-permute-start | bytes 2359304 | tf_op jit(solution)/shard_map/ppermute | solution.py:509
  179.0 131.3 %collective-permute-start.6 = (bf16[384,1024]{1,0:T(8,128)(2,1)S(1)}, bf16[384,1024]{1,0:T(8,128)(2,1)}, u32[]{:S(2)}, u32[]{:S(2)}) collective-permute-start(bf16[384,1024]{1,0:T(8,128)(2,1)S(1)} %get-tuple-element.56), channel_id=1, source_target_pairs={{0,2},{1,3},{2,0},{3,1},{4,6},{5,7},{6,4},{7,5},{8,10},{9,11},{10,... | collective-permute-start | bytes 2359304 | tf_op jit(solution)/shard_map/ppermute | solution.py:509
  179.6 110.9 %collective-permute-start.8 = (bf16[128,1536]{1,0:T(8,128)(2,1)S(1)}, bf16[128,1536]{1,0:T(8,128)(2,1)}, u32[]{:S(2)}, u32[]{:S(2)}) collective-permute-start(bf16[128,1536]{1,0:T(8,128)(2,1)S(1)} %get-tuple-element.57), channel_id=1, source_target_pairs={{0,1},{1,2},{2,3},{3,0},{4,5},{5,6},{6,7},{7,4},{8,9},{9,10},{10,1... | collective-permute-start | bytes 1179656 | tf_op jit(solution)/shard_map/ppermute | solution.py:509
  182.0 111.3 %collective-permute-start.9 = (bf16[128,1536]{1,0:T(8,128)(2,1)S(1)}, bf16[128,1536]{1,0:T(8,128)(2,1)}, u32[]{:S(2)}, u32[]{:S(2)}) collective-permute-start(bf16[128,1536]{1,0:T(8,128)(2,1)S(1)} %get-tuple-element.57), channel_id=1, source_target_pairs={{0,2},{1,3},{2,0},{3,1},{4,6},{5,7},{6,4},{7,5},{8,10},{9,11},{10,... | collective-permute-start | bytes 1179656 | tf_op jit(solution)/shard_map/ppermute | solution.py:509
  183.1 142.8 %collective-permute-start.12 = (bf16[2,256,1536]{2,1,0:T(8,128)(2,1)}, bf16[2,256,1536]{2,1,0:T(8,128)(2,1)}, u32[]{:S(2)}, u32[]{:S(2)}) collective-permute-start(bf16[2,256,1536]{2,1,0:T(8,128)(2,1)} %param.14), channel_id=1, source_target_pairs={{0,4},{4,0},{8,12},{12,8},{16,20},{20,16},{24,28},{28,24},{1,5},{5... | collective-permute-start | bytes 4718600 | tf_op jit(solution)/shard_map/ppermute | solution.py:476
  293.4 33.9 %collective-permute-start = (bf16[512,1536]{1,0:T(8,128)(2,1)S(1)}, bf16[512,1536]{1,0:T(8,128)(2,1)S(1)}, u32[]{:S(2)}, u32[]{:S(2)}) collective-permute-start(bf16[512,1536]{1,0:T(8,128)(2,1)S(1)} %multiply_convert_fusion), channel_id=1, source_target_pairs={{0,4},{4,0},{8,12},{12,8},{16,20},{20,16},{24,28},{28,24},{1,5},{5... | collective-permute-start | bytes 4718600 | tf_op jit(solution)/shard_map/ppermute | solution.py:476
  302.1 20.5 %collective-permute-start.7 = (bf16[384,1024]{1,0:T(8,128)(2,1)S(1)}, bf16[384,1024]{1,0:T(8,128)(2,1)S(1)}, u32[]{:S(2)}, u32[]{:S(2)}) collective-permute-start(bf16[384,1024]{1,0:T(8,128)(2,1)S(1)} %get-tuple-element.56), channel_id=1, source_target_pairs={{0,3},{1,0},{2,1},{3,2},{4,7},{5,4},{6,5},{7,6},{8,11},{9,8},{10,9... | collective-permute-start | bytes 2359304 | tf_op jit(solution)/shard_map/ppermute | solution.py:509
  306.0 116.1 %collective-permute-start.3 = (bf16[1536,1024]{1,0:T(8,128)(2,1)}, bf16[1536,1024]{1,0:T(8,128)(2,1)}, u32[]{:S(2)}, u32[]{:S(2)}) collective-permute-start(bf16[1536,1024]{1,0:T(8,128)(2,1)} %bitcast.6), channel_id=1, source_target_pairs={{0,16},{4,20},{8,24},{12,28},{16,0},{20,4},{24,8},{28,12},{1,17},{... | collective-permute-start | bytes 9437192 | tf_op jit(solution)/shard_map/ppermute | solution.py:480
  310.3 129.3 %collective-permute-start.1 = (bf16[1536,1024]{1,0:T(8,128)(2,1)}, bf16[1536,1024]{1,0:T(8,128)(2,1)}, u32[]{:S(2)}, u32[]{:S(2)}) collective-permute-start(bf16[1536,1024]{1,0:T(8,128)(2,1)} %bitcast.6), channel_id=1, source_target_pairs={{0,8},{4,12},{8,0},{12,4},{16,24},{20,28},{24,16},{28,20},{1,9},{5... | collective-permute-start | bytes 9437192 | tf_op jit(solution)/shard_map/ppermute | solution.py:480
  322.6 106.4 %collective-permute-start.4 = (bf16[512,1536]{1,0:T(8,128)(2,1)S(1)}, bf16[512,1536]{1,0:T(8,128)(2,1)}, u32[]{:S(2)}, u32[]{:S(2)}) collective-permute-start(bf16[512,1536]{1,0:T(8,128)(2,1)S(1)} %bitcast.315), channel_id=1, source_target_pairs={{0,16},{4,20},{8,24},{12,28},{16,0},{20,4},{24,8},{28,12},{1,17},{... | collective-permute-start | bytes 4718600 | tf_op jit(solution)/shard_map/ppermute | solution.py:480
  358.9 57.9 %collective-permute-start.82 = (bf16[384,1024]{0,1:T(8,128)(2,1)}, bf16[384,1024]{0,1:T(8,128)(2,1)}, u32[]{:S(2)}, u32[]{:S(2)}) collective-permute-start(bf16[384,1024]{0,1:T(8,128)(2,1)} %bitcast.377), channel_id=1, source_target_pairs={{0,1},{1,2},{2,3},{3,0},{4,5},{5,6},{6,7},{7,4},{8,9},{9,10},{10,1... | collective-permute-start | bytes 2359304 | tf_op jit(solution)/shard_map/ppermute | solution.py:485
  363.8 24.2 %collective-permute-start.95 = (bf16[128,1536]{1,0:T(8,128)(2,1)S(1)}, bf16[128,1536]{1,0:T(8,128)(2,1)S(1)}, u32[]{:S(2)}, u32[]{:S(2)}) collective-permute-start(bf16[128,1536]{1,0:T(8,128)(2,1)S(1)} %dynamic-slice_bitcast_fusion.11), channel_id=1, source_target_pairs={{0,1},{1,2},{2,3},{3,0},{4,5},{5,6},{6,7},{7,4},{8,9},{9,10},{10,1... | collective-permute-start | bytes 1179656 | tf_op jit(solution)/shard_map/ppermute | solution.py:485
  416.8 37.4 %collective-permute-start.2 = (bf16[512,1536]{1,0:T(8,128)(2,1)S(1)}, bf16[512,1536]{1,0:T(8,128)(2,1)S(1)}, u32[]{:S(2)}, u32[]{:S(2)}) collective-permute-start(bf16[512,1536]{1,0:T(8,128)(2,1)S(1)} %bitcast.318), channel_id=1, source_target_pairs={{0,8},{4,12},{8,0},{12,4},{16,24},{20,28},{24,16},{28,20},{1,9},{5... | collective-permute-start | bytes 4718600 | tf_op jit(solution)/shard_map/ppermute | solution.py:480
  420.2 82.9 %collective-permute-start.83 = (bf16[384,1024]{0,1:T(8,128)(2,1)}, bf16[384,1024]{0,1:T(8,128)(2,1)}, u32[]{:S(2)}, u32[]{:S(2)}) collective-permute-start(bf16[384,1024]{0,1:T(8,128)(2,1)} %fusion.34), channel_id=1, source_target_pairs={{0,1},{1,2},{2,3},{3,0},{4,5},{5,6},{6,7},{7,4},{8,9},{9,10},{10,1... | collective-permute-start | bytes 2359304 | tf_op jit(solution)/shard_map/ppermute | solution.py:485
  422.1 135.6 %collective-permute-start.98 = (bf16[128,1536]{1,0:T(8,128)(2,1)}, bf16[128,1536]{1,0:T(8,128)(2,1)}, u32[]{:S(2)}, u32[]{:S(2)}) collective-permute-start(bf16[128,1536]{1,0:T(8,128)(2,1)} %fusion.51), channel_id=1, source_target_pairs={{0,24},{4,28},{8,16},{12,20},{16,8},{20,12},{24,0},{28,4},{1,25},{... | collective-permute-start | bytes 1179656 | tf_op jit(solution)/shard_map/ppermute | solution.py:480
  438.4 56.7 %collective-permute-start.91 = (bf16[4,128,1536]{2,1,0:T(8,128)(2,1)}, bf16[4,128,1536]{2,1,0:T(8,128)(2,1)}, u32[]{:S(2)}, u32[]{:S(2)}) collective-permute-start(bf16[4,128,1536]{2,1,0:T(8,128)(2,1)} %bitcast.116), channel_id=1, source_target_pairs={{0,16},{4,20},{8,24},{12,28},{16,0},{20,4},{24,8},{28,12},{1,17},{... | collective-permute-start | bytes 4718600 | tf_op jit(solution)/shard_map/ppermute | solution.py:480
  462.1 33.1 %collective-permute-start.90 = (bf16[4,128,1536]{2,1,0:T(8,128)(2,1)}, bf16[4,128,1536]{2,1,0:T(8,128)(2,1)}, u32[]{:S(2)}, u32[]{:S(2)}) collective-permute-start(bf16[4,128,1536]{2,1,0:T(8,128)(2,1)} %bitcast.115), channel_id=1, source_target_pairs={{0,8},{4,12},{8,0},{12,4},{16,24},{20,28},{24,16},{28,20},{1,9},{5... | collective-permute-start | bytes 4718600 | tf_op jit(solution)/shard_map/ppermute | solution.py:480
  489.8 72.1 %collective-permute-start.13 = (f32[512,1536]{1,0:T(8,128)}, f32[512,1536]{1,0:T(8,128)S(1)}, u32[]{:S(2)}, u32[]{:S(2)}) collective-permute-start(f32[512,1536]{1,0:T(8,128)} %slice.219), channel_id=1, source_target_pairs={{0,4},{4,0},{8,12},{12,8},{16,20},{20,16},{24,28},{28,24},{1,5},{5... | collective-permute-start | bytes 9437192 | tf_op jit(solution)/shard_map/ppermute | solution.py:476
  508.8 45.0 %collective-permute-start.84 = (bf16[384,1024]{0,1:T(8,128)(2,1)}, bf16[384,1024]{0,1:T(8,128)(2,1)}, u32[]{:S(2)}, u32[]{:S(2)}) collective-permute-start(bf16[384,1024]{0,1:T(8,128)(2,1)} %fusion.33), channel_id=1, source_target_pairs={{0,1},{1,2},{2,3},{3,0},{4,5},{5,6},{6,7},{7,4},{8,9},{9,10},{10,1... | collective-permute-start | bytes 2359304 | tf_op jit(solution)/shard_map/ppermute | solution.py:485
  514.6 24.9 %collective-permute-start.93 = (bf16[128,1536]{1,0:T(8,128)(2,1)}, bf16[128,1536]{1,0:T(8,128)(2,1)S(1)}, u32[]{:S(2)}, u32[]{:S(2)}) collective-permute-start(bf16[128,1536]{1,0:T(8,128)(2,1)} %fusion.57), channel_id=1, source_target_pairs={{0,1},{1,2},{2,3},{3,0},{4,5},{5,6},{6,7},{7,4},{8,9},{9,10},{10,1... | collective-permute-start | bytes 1179656 | tf_op jit(solution)/shard_map/ppermute | solution.py:485
  525.4 155.9 %collective-permute-start.78 = (bf16[4,384,1024]{1,2,0:T(8,128)(2,1)}, bf16[4,384,1024]{1,2,0:T(8,128)(2,1)}, u32[]{:S(2)}, u32[]{:S(2)}) collective-permute-start(bf16[4,384,1024]{1,2,0:T(8,128)(2,1)} %copy.59), channel_id=1, source_target_pairs={{0,16},{4,20},{8,24},{12,28},{16,0},{20,4},{24,8},{28,12},{1,17},{... | collective-permute-start | bytes 9437192 | tf_op jit(solution)/shard_map/ppermute | solution.py:480
  553.8 128.2 %collective-permute-start.77 = (bf16[4,384,1024]{1,2,0:T(8,128)(2,1)}, bf16[4,384,1024]{1,2,0:T(8,128)(2,1)}, u32[]{:S(2)}, u32[]{:S(2)}) collective-permute-start(bf16[4,384,1024]{1,2,0:T(8,128)(2,1)} %copy.57), channel_id=1, source_target_pairs={{0,8},{4,12},{8,0},{12,4},{16,24},{20,28},{24,16},{28,20},{1,9},{5... | collective-permute-start | bytes 9437192 | tf_op jit(solution)/shard_map/ppermute | solution.py:480
  575.0 102.9 %collective-permute-start.73 = (f32[384]{0:T(512)S(1)}, f32[384]{0:T(512)S(1)}, u32[]{:S(2)}, u32[]{:S(2)}) collective-permute-start(f32[384]{0:T(512)S(1)} %get-tuple-element.100), channel_id=1, source_target_pairs={{0,3},{1,0},{2,1},{3,2},{4,7},{5,4},{6,5},{7,6},{8,11},{9,8},{10,9... | collective-permute-start | bytes 4616 | tf_op jit(solution)/shard_map/ppermute | solution.py:781
  578.6 100.7 %collective-permute-start.72 = (f32[384]{0:T(512)S(1)}, f32[384]{0:T(512)S(1)}, u32[]{:S(2)}, u32[]{:S(2)}) collective-permute-start(f32[384]{0:T(512)S(1)} %get-tuple-element.101), channel_id=1, source_target_pairs={{0,2},{1,3},{2,0},{3,1},{4,6},{5,7},{6,4},{7,5},{8,10},{9,11},{10,... | collective-permute-start | bytes 4616 | tf_op jit(solution)/shard_map/ppermute | solution.py:781
  578.8 101.2 %collective-permute-start.71 = (f32[384]{0:T(512)S(1)}, f32[384]{0:T(512)S(1)}, u32[]{:S(2)}, u32[]{:S(2)}) collective-permute-start(f32[384]{0:T(512)S(1)} %get-tuple-element.99), channel_id=1, source_target_pairs={{0,1},{1,2},{2,3},{3,0},{4,5},{5,6},{6,7},{7,4},{8,9},{9,10},{10,1... | collective-permute-start | bytes 4616 | tf_op jit(solution)/shard_map/ppermute | solution.py:781
  677.8 40.5 %collective-permute-start.101 = (bf16[128,1536]{1,0:T(8,128)(2,1)}, bf16[128,1536]{1,0:T(8,128)(2,1)S(1)}, u32[]{:S(2)}, u32[]{:S(2)}) collective-permute-start(bf16[128,1536]{1,0:T(8,128)(2,1)} %get-tuple-element.116), channel_id=1, source_target_pairs={{0,24},{4,28},{8,16},{12,20},{16,8},{20,12},{24,0},{28,4},{1,25},{... | collective-permute-start | bytes 1179656 | tf_op jit(solution)/shard_map/ppermute | solution.py:480
  679.4 39.9 %collective-permute-start.100 = (bf16[128,1536]{1,0:T(8,128)(2,1)}, bf16[128,1536]{1,0:T(8,128)(2,1)S(1)}, u32[]{:S(2)}, u32[]{:S(2)}) collective-permute-start(bf16[128,1536]{1,0:T(8,128)(2,1)} %get-tuple-element.116), channel_id=1, source_target_pairs={{0,16},{4,20},{8,24},{12,28},{16,0},{20,4},{24,8},{28,12},{1,17},{... | collective-permute-start | bytes 1179656 | tf_op jit(solution)/shard_map/ppermute | solution.py:480
  680.1 58.2 %collective-permute-start.17 = (bf16[768,512]{1,0:T(8,128)(2,1)}, bf16[768,512]{1,0:T(8,128)(2,1)}, u32[]{:S(2)}, u32[]{:S(2)}) collective-permute-start(bf16[768,512]{1,0:T(8,128)(2,1)} %get-tuple-element.67), channel_id=1, source_target_pairs={{0,8},{4,12},{8,0},{12,4},{16,24},{20,28},{24,16},{28,20},{1,9},{5... | collective-permute-start | bytes 2359304 | tf_op jit(solution)/shard_map/ppermute | solution.py:480
  681.3 32.7 %collective-permute-start.15 = (bf16[768,512]{1,0:T(8,128)(2,1)}, bf16[768,512]{1,0:T(8,128)(2,1)}, u32[]{:S(2)}, u32[]{:S(2)}) collective-permute-start(bf16[768,512]{1,0:T(8,128)(2,1)} %get-tuple-element.64), channel_id=1, source_target_pairs={{0,16},{4,20},{8,24},{12,28},{16,0},{20,4},{24,8},{28,12},{1,17},{... | collective-permute-start | bytes 2359304 | tf_op jit(solution)/shard_map/ppermute | solution.py:480
  714.0 26.4 %collective-permute-start.79 = (bf16[384,1024]{0,1:T(8,128)(2,1)S(1)}, bf16[384,1024]{0,1:T(8,128)(2,1)S(1)}, u32[]{:S(2)}, u32[]{:S(2)}) collective-permute-start(bf16[384,1024]{0,1:T(8,128)(2,1)S(1)} %dynamic-slice_bitcast_fusion), channel_id=1, source_target_pairs={{0,1},{1,2},{2,3},{3,0},{4,5},{5,6},{6,7},{7,4},{8,9},{9,10},{10,1... | collective-permute-start | bytes 2359304 | tf_op jit(solution)/shard_map/ppermute | solution.py:485
  718.3 24.4 %collective-permute-start.14 = (bf16[768,512]{1,0:T(8,128)(2,1)S(1)}, bf16[768,512]{1,0:T(8,128)(2,1)S(1)}, u32[]{:S(2)}, u32[]{:S(2)}) collective-permute-start(bf16[768,512]{1,0:T(8,128)(2,1)S(1)} %copy-done.80), channel_id=1, source_target_pairs={{0,16},{4,20},{8,24},{12,28},{16,0},{20,4},{24,8},{28,12},{1,17},{... | collective-permute-start | bytes 2359304 | tf_op jit(solution)/shard_map/ppermute | solution.py:480
  720.4 22.4 %collective-permute-start.16 = (bf16[768,512]{1,0:T(8,128)(2,1)S(1)}, bf16[768,512]{1,0:T(8,128)(2,1)S(1)}, u32[]{:S(2)}, u32[]{:S(2)}) collective-permute-start(bf16[768,512]{1,0:T(8,128)(2,1)S(1)} %add_convert_fusion.3), channel_id=1, source_target_pairs={{0,8},{4,12},{8,0},{12,4},{16,24},{20,28},{24,16},{28,20},{1,9},{5... | collective-permute-start | bytes 2359304 | tf_op jit(solution)/shard_map/ppermute | solution.py:480
  737.6 35.0 %collective-permute-start.27 = (bf16[768,512]{1,0:T(8,128)(2,1)}, bf16[768,512]{1,0:T(8,128)(2,1)}, u32[]{:S(2)}, u32[]{:S(2)}) collective-permute-start(bf16[768,512]{1,0:T(8,128)(2,1)} %bitcast.35), channel_id=1, source_target_pairs={{0,4},{4,0},{8,12},{12,8},{16,20},{20,16},{24,28},{28,24},{1,5},{5... | collective-permute-start | bytes 2359304 | tf_op jit(solution)/shard_map/ppermute | solution.py:476
  742.8 22.8 %collective-permute-start.56 = (bf16[768,512]{1,0:T(8,128)(2,1)S(1)}, bf16[768,512]{1,0:T(8,128)(2,1)S(1)}, u32[]{:S(2)}, u32[]{:S(2)}) collective-permute-start(bf16[768,512]{1,0:T(8,128)(2,1)S(1)} %bitcast.381), channel_id=1, source_target_pairs={{0,4},{4,0},{8,12},{12,8},{16,20},{20,16},{24,28},{28,24},{1,5},{5... | collective-permute-start | bytes 2359304 | tf_op jit(solution)/shard_map/ppermute | solution.py:476
  742.9 23.2 %collective-permute-start.57 = (bf16[512,1536]{1,0:T(8,128)(2,1)S(1)}, bf16[512,1536]{1,0:T(8,128)(2,1)S(1)}, u32[]{:S(2)}, u32[]{:S(2)}) collective-permute-start(bf16[512,1536]{1,0:T(8,128)(2,1)S(1)} %copy-done.37), channel_id=1, source_target_pairs={{0,4},{4,0},{8,12},{12,8},{16,20},{20,16},{24,28},{28,24},{1,5},{5... | collective-permute-start | bytes 4718600 | tf_op jit(solution)/shard_map/ppermute | solution.py:476
  758.2 139.9 %collective-permute-start.85 = (bf16[384,1024]{0,1:T(8,128)(2,1)}, bf16[384,1024]{0,1:T(8,128)(2,1)}, u32[]{:S(2)}, u32[]{:S(2)}) collective-permute-start(bf16[384,1024]{0,1:T(8,128)(2,1)} %fusion.32), channel_id=1, source_target_pairs={{0,24},{4,28},{8,16},{12,20},{16,8},{20,12},{24,0},{28,4},{1,25},{... | collective-permute-start | bytes 2359304 | tf_op jit(solution)/shard_map/ppermute | solution.py:480
  765.6 195.9 %collective-permute-start.11 = (f32[512,1536]{1,0:T(8,128)}, f32[512,1536]{1,0:T(8,128)}, u32[]{:S(2)}, u32[]{:S(2)}) collective-permute-start(f32[512,1536]{1,0:T(8,128)} %pad_maximum_fusion.1), channel_id=1, source_target_pairs={{0,4},{4,0},{8,12},{12,8},{16,20},{20,16},{24,28},{28,24},{1,5},{5... | collective-permute-start | bytes 9437192 | tf_op jit(solution)/shard_map/ppermute | solution.py:476
  766.1 21.7 %collective-permute-start.80 = (bf16[384,1024]{0,1:T(8,128)(2,1)}, bf16[384,1024]{0,1:T(8,128)(2,1)}, u32[]{:S(2)}, u32[]{:S(2)}) collective-permute-start(bf16[384,1024]{0,1:T(8,128)(2,1)} %fusion.38), channel_id=1, source_target_pairs={{0,1},{1,2},{2,3},{3,0},{4,5},{5,6},{6,7},{7,4},{8,9},{9,10},{10,1... | collective-permute-start | bytes 2359304 | tf_op jit(solution)/shard_map/ppermute | solution.py:485
  772.7 21.8 %collective-permute-start.23 = (f32[384]{0:T(512)S(1)}, f32[384]{0:T(512)S(1)}, u32[]{:S(2)}, u32[]{:S(2)}) collective-permute-start(f32[384]{0:T(512)S(1)} %get-tuple-element.104), channel_id=1, source_target_pairs={{0,3},{1,0},{2,1},{3,2},{4,7},{5,4},{6,5},{7,6},{8,11},{9,8},{10,9... | collective-permute-start | bytes 4616 | tf_op jit(solution)/shard_map/ppermute | solution.py:781
  798.1 53.1 %collective-permute-start.30 = (bf16[4,48,1536]{2,1,0:T(8,128)(2,1)S(1)}, bf16[4,48,1536]{2,1,0:T(8,128)(2,1)S(1)}, u32[]{:S(2)}, u32[]{:S(2)}) collective-permute-start(bf16[4,48,1536]{2,1,0:T(8,128)(2,1)S(1)} %get-tuple-element.159), channel_id=1, source_target_pairs={{0,16},{4,20},{8,24},{12,28},{16,0},{20,4},{24,8},{28,12},{1,17},{... | collective-permute-start | bytes 1769480 | tf_op jit(solution)/shard_map/ppermute | solution.py:480
  811.6 40.5 %collective-permute-start.29 = (bf16[4,48,1536]{2,1,0:T(8,128)(2,1)S(1)}, bf16[4,48,1536]{2,1,0:T(8,128)(2,1)S(1)}, u32[]{:S(2)}, u32[]{:S(2)}) collective-permute-start(bf16[4,48,1536]{2,1,0:T(8,128)(2,1)S(1)} %get-tuple-element.158), channel_id=1, source_target_pairs={{0,8},{4,12},{8,0},{12,4},{16,24},{20,28},{24,16},{28,20},{1,9},{5... | collective-permute-start | bytes 1769480 | tf_op jit(solution)/shard_map/ppermute | solution.py:480
  850.2 53.0 %collective-permute-start.20 = (bf16[256,1536]{1,0:T(8,128)(2,1)S(1)}, bf16[256,1536]{1,0:T(8,128)(2,1)S(1)}, u32[]{:S(2)}, u32[]{:S(2)}) collective-permute-start(bf16[256,1536]{1,0:T(8,128)(2,1)S(1)} %get-tuple-element.167), channel_id=1, source_target_pairs={{0,4},{4,0},{8,12},{12,8},{16,20},{20,16},{24,28},{28,24},{1,5},{5... | collective-permute-start | bytes 2359304 | tf_op jit(solution)/shard_map/ppermute | solution.py:476
  867.0 32.6 %collective-permute-start.81 = (bf16[384,1024]{0,1:T(8,128)(2,1)S(1)}, bf16[384,1024]{0,1:T(8,128)(2,1)S(1)}, u32[]{:S(2)}, u32[]{:S(2)}) collective-permute-start(bf16[384,1024]{0,1:T(8,128)(2,1)S(1)} %fusion.37), channel_id=1, source_target_pairs={{0,1},{1,2},{2,3},{3,0},{4,5},{5,6},{6,7},{7,4},{8,9},{9,10},{10,1... | collective-permute-start | bytes 2359304 | tf_op jit(solution)/shard_map/ppermute | solution.py:485
  867.6 23.5 %collective-permute-start.31 = (bf16[48,1536]{1,0:T(8,128)(2,1)S(1)}, bf16[48,1536]{1,0:T(8,128)(2,1)S(1)}, u32[]{:S(2)}, u32[]{:S(2)}) collective-permute-start(bf16[48,1536]{1,0:T(8,128)(2,1)S(1)} %dynamic-slice_bitcast_fusion.18), channel_id=1, source_target_pairs={{0,1},{1,2},{2,3},{3,0},{4,5},{5,6},{6,7},{7,4},{8,9},{9,10},{10,1... | collective-permute-start | bytes 442376 | tf_op jit(solution)/shard_map/ppermute | solution.py:485
  898.0 59.3 %collective-permute-start.42 = (bf16[1536,512]{1,0:T(8,128)(2,1)S(1)}, bf16[1536,512]{1,0:T(8,128)(2,1)S(1)}, u32[]{:S(2)}, u32[]{:S(2)}) collective-permute-start(bf16[1536,512]{1,0:T(8,128)(2,1)S(1)} %pad_maximum_fusion.8), channel_id=1, source_target_pairs={{0,4},{4,0},{8,12},{12,8},{16,20},{20,16},{24,28},{28,24},{1,5},{5... | collective-permute-start | bytes 4718600 | tf_op jit(solution)/shard_map/ppermute | solution.py:476
  899.6 26.8 %collective-permute-start.66 = (bf16[48,1536]{1,0:T(8,128)(2,1)S(1)}, bf16[48,1536]{1,0:T(8,128)(2,1)S(1)}, u32[]{:S(2)}, u32[]{:S(2)}) collective-permute-start(bf16[48,1536]{1,0:T(8,128)(2,1)S(1)} %fusion.58), channel_id=1, source_target_pairs={{0,24},{4,28},{8,16},{12,20},{16,8},{20,12},{24,0},{28,4},{1,25},{... | collective-permute-start | bytes 442376 | tf_op jit(solution)/shard_map/ppermute | solution.py:480
  939.7 26.1 %collective-permute-start.88 = (bf16[384,1024]{0,1:T(8,128)(2,1)S(1)}, bf16[384,1024]{0,1:T(8,128)(2,1)S(1)}, u32[]{:S(2)}, u32[]{:S(2)}) collective-permute-start(bf16[384,1024]{0,1:T(8,128)(2,1)S(1)} %get-tuple-element.118), channel_id=1, source_target_pairs={{0,24},{4,28},{8,16},{12,20},{16,8},{20,12},{24,0},{28,4},{1,25},{... | collective-permute-start | bytes 2359304 | tf_op jit(solution)/shard_map/ppermute | solution.py:480
  976.6 47.1 %collective-permute-start.89 = (bf16[4,384,1024]{1,2,0:T(8,128)(2,1)S(1)}, bf16[4,384,1024]{1,2,0:T(8,128)(2,1)S(1)}, u32[]{:S(2)}, u32[]{:S(2)}) collective-permute-start(bf16[4,384,1024]{1,2,0:T(8,128)(2,1)S(1)} %pad_maximum_fusion.3), channel_id=1, source_target_pairs={{0,4},{4,0},{8,12},{12,8},{16,20},{20,16},{24,28},{28,24},{1,5},{5... | collective-permute-start | bytes 9437192 | tf_op jit(solution)/shard_map/ppermute | solution.py:476
  (165 other events, 2791.5 us)

commit v3 on v2

--- a/solution.py
+++ b/solution.py
@@ -101,7 +101,7 @@
     )(ids, inv, qT, *ks, *vs)
 
 
-def bwd_kernel(nchip, scale, ids_ref, inv_ref, q_ref, o_ref, do_ref, lse_ref, *rest):
+def bwd_kernel(nchip, scale, ids_ref, inv_ref, q_ref, o_ref, do_ref, lse_ref, cos_ref, sin_ref, *rest):
     k_refs, v_refs = rest[:nchip], rest[nchip:2 * nchip]
     dq_ref = rest[2 * nchip]
     dk_refs, dv_refs = rest[2 * nchip + 1:3 * nchip + 1], rest[3 * nchip + 1:4 * nchip + 1]
@@ -146,8 +146,12 @@
     lax.fori_loop(0, nb + 1, step, 0)
     for qi in range(nq):
         lanes = slice(128 * qi, 128 * (qi + 1))
-        dq_ref[0:96, lanes] = dq_s[qi][:, :128] * scale
-        dq_ref[96:192, lanes] = dq_s[qi][:, 128:] * scale
+        cos, sin = cos_ref[:, lanes], sin_ref[:, lanes]
+        for h in range(2):
+            a = dq_s[qi, 0:48, 128 * h:128 * (h + 1)] * scale
+            b = dq_s[qi, 48:96, 128 * h:128 * (h + 1)] * scale
+            dq_ref[96 * h:96 * h + 48, lanes] = (a * cos + b * sin).astype(jnp.bfloat16)
+            dq_ref[96 * h + 48:96 * h + 96, lanes] = (b * cos - a * sin).astype(jnp.bfloat16)
     for r in range(nchip):
         for j in range(nq):
             n = r * nq + j
@@ -160,7 +164,7 @@
             dv_refs[r][:, 128 * j:128 * (j + 1)] = dv.astype(jnp.bfloat16)
 
 
-def attn_bwd(ids, inv, qT, oT, doT, lse, ks, vs, heads):
+def attn_bwd(ids, inv, qT, oT, doT, lse, cosine, sine, ks, vs, heads):
     nchip = len(ks)
     T = qT.shape[1]
     nq = T // 128
@@ -170,7 +174,8 @@
     grid_spec = pltpu.PrefetchScalarGridSpec(
         num_scalar_prefetch=2,
         grid=(heads,),
-        in_specs=[wide, wide, wide, pl.BlockSpec((None, nq, 1, 256), lambda g, *_: (g, 0, 0, 0))] + [slim] * (2 * nchip),
+        in_specs=[wide, wide, wide, pl.BlockSpec((None, nq, 1, 256), lambda g, *_: (g, 0, 0, 0))]
+        + [pl.BlockSpec((48, T), lambda g, *_: (0, 0))] * 2 + [slim] * (2 * nchip),
         out_specs=[wide] + [slim] * (2 * nchip),
         scratch_shapes=[
             pltpu.VMEM((nb, 128, 96), jnp.bfloat16),
@@ -188,10 +193,10 @@
     outs = pl.pallas_call(
         functools.partial(bwd_kernel, nchip, SCALE),
         grid_spec=grid_spec,
-        out_shape=[jax.ShapeDtypeStruct((heads * 192, T), jnp.float32)] + [slab] * (2 * nchip),
+        out_shape=[jax.ShapeDtypeStruct((heads * 192, T), jnp.bfloat16)] + [slab] * (2 * nchip),
         cost_estimate=pl.CostEstimate(flops=90 * 10**9, bytes_accessed=24 * 2**20, transcendentals=0),
         name="attention_backward",
-    )(ids, inv, qT, oT, doT, lse, *ks, *vs)
+    )(ids, inv, qT, oT, doT, lse, cosine, sine, *ks, *vs)
     return outs[0], outs[1:1 + nchip], outs[1 + nchip:]
 
 
@@ -468,6 +473,327 @@
     )(tokens, gains, cut(key_w), cut(value_w), cut(query_w), cut(out_w), gate_w, up_w, down_w, cosine, sine)
 
 
+def tail_kernel(zsize, *refs):
+    dk, dv = refs[0:4], refs[4:8]
+    dq, cos, sin, first_half, out_grad = refs[8:13]
+    wide_in, tall_in = refs[13:16], refs[16:19]
+    far_wide_in, far_tall_in = refs[19:19 + zsize], refs[19 + zsize:19 + 2 * zsize]
+    rest = refs[19 + 2 * zsize:]
+    o_all, q_all, kv_all, wide_all, tall_all, kv_low = rest[:6]
+    (got, held, dq_pair, kv_pair, half, grads, gl, gr, gx, gy, gz, piece, wide_s, tall_s, wide_0, tall_0, wide_z, tall_z,
+     wide_f, tall_f, wide_r, tall_r, wide_p, tall_p, ss, rs, ls) = rest[6:]
+    index, depth = lax.axis_index("ctx"), lax.axis_index("fsdp")
+    chip, core = index // 2, lax.rem(index, 2)
+    chip_x, chip_y, chip_d = chip + 1 - 2 * lax.rem(chip, 2), lax.rem(chip + 2, 4), 3 - chip
+    nxt, prv = lax.rem(depth + 1, zsize), lax.rem(depth + zsize - 1, zsize)
+    to_next, to_prev = (index, nxt), (index, prv)
+    to_x, to_y, to_core = (chip_x * 2 + core, depth), (chip_y * 2 + core, depth), (chip * 2 + 1 - core, depth)
+    to_far = (chip_d * 2 + core, depth)
+    last = zsize - 1
+    kv_rows = dk[0].shape[0]
+    width = first_half.shape[0] * 2
+    strip = piece.shape[1]
+    length = dq.shape[1]
+
+    barrier = pltpu.get_barrier_semaphore()
+    for target in (to_next, to_prev, to_x, to_y, to_core, to_far):
+        pl.semaphore_signal(barrier, inc=1, device_id=target, device_id_type=pl.DeviceIdType.MESH)
+    pl.semaphore_wait(barrier, 6)
+
+    count = [0, 0]
+    sent, kept = [], []
+
+    def send(src, dst, target):
+        k = count[0]
+        count[0] += 1
+        copy = pltpu.make_async_remote_copy(
+            src_ref=src, dst_ref=dst, send_sem=ss.at[k], recv_sem=rs.at[k], device_id=target, device_id_type=pl.DeviceIdType.MESH
+        )
+        copy.start()
+        sent.append(copy)
+        return copy
+
+    def local(src, dst):
+        k = count[1]
+        count[1] += 1
+        copy = pltpu.make_async_copy(src, dst, ls.at[k])
+        copy.start()
+        return copy
+
+    def wait_all(copies):
+        for copy in copies:
+            copy.wait()
+
+    def received(*copies):
+        for copy in copies:
+            copy.wait_recv()
+
+    def add_rows(target, sources, block):
+        def one(t, _):
+            part = pl.ds(pl.multiple_of(t * block, block), block)
+            total = target[part].astype(F32)
+            for source in sources:
+                total = total + source[part].astype(F32)
+            target[part] = total.astype(BF)
+            return 0
+
+        lax.fori_loop(0, target.shape[0] // block, one, 0)
+
+    def place_at(j):
+        return lax.rem(depth + 2 * zsize - 1 - j, zsize)
+
+    k3, v3 = send(dk[3], got.at[0], to_y), send(dv[3], got.at[1], to_x)
+    q_swap = send(dq, dq_pair.at[1], to_core)
+
+    def load_ffn(j):
+        slot = lax.rem(j, 2) if not isinstance(j, int) else j % 2
+        return [local(wide_in[n].at[place_at(j)], wide_s.at[slot, n]) for n in range(3)] + [
+            local(tall_in[n].at[place_at(j)], tall_s.at[slot, n]) for n in range(3)]
+
+    ffn_loads = {0: load_ffn(0)}
+    load_o = local(out_grad, grads.at[0])
+    load_q = [local(dq, dq_pair.at[0]), local(first_half, half)]
+    load_kv = [local(dk[0], held.at[0]), local(dk[1], held.at[1]), local(dv[0], held.at[2]), local(dv[2], held.at[3])]
+    load_far = [local(far_wide_in[0].at[depth], wide_f.at[0]), local(far_tall_in[0].at[depth], tall_f.at[0])]
+    for n in range(1, zsize):
+        load_far += [local(far_wide_in[n], wide_f.at[n]), local(far_tall_in[n], tall_f.at[n])]
+
+    moves = {}
+
+    def ffn_step(j):
+        if j + 1 <= last:
+            ffn_loads[j + 1] = load_ffn(j + 1)
+        wait_all(ffn_loads[j])
+        w = [wide_s.at[j % 2, n] for n in range(3)]
+        t = [tall_s.at[j % 2, n] for n in range(3)]
+        if j == 0:
+            sum_rows(wide_0, w, 64)
+            sum_rows(tall_0, t, 64)
+            moves["wide", 0], moves["tall", 0] = send(wide_0, wide_z.at[0], to_next), send(tall_0, tall_z.at[0], to_next)
+            return
+        received(moves["tall", j - 1])
+        add_rows(tall_z.at[j - 1], t, 64)
+        if j < last:
+            moves["tall", j] = send(tall_z.at[j - 1], tall_z.at[j], to_next)
+        received(moves["wide", j - 1])
+        add_rows(wide_z.at[j - 1], w, 64)
+        if j < last:
+            moves["wide", j] = send(wide_z.at[j - 1], wide_z.at[j], to_next)
+
+    def sum_rows(target, sources, block):
+        def one(t, _):
+            part = pl.ds(pl.multiple_of(t * block, block), block)
+            total = sources[0][part].astype(F32)
+            for source in sources[1:]:
+                total = total + source[part].astype(F32)
+            target[part] = total.astype(BF)
+            return 0
+
+        lax.fori_loop(0, target.shape[0] // block, one, 0)
+
+    mid = width // 2
+    tiles = 512
+
+    def stage_1(m):
+        moves["l", m] = send(grads.at[m, :, chip_d, :, pl.ds(0, mid)], gl.at[m], to_y)
+        moves["r", m] = send(grads.at[m, :, chip_d, :, pl.ds(mid, mid)], gr.at[m], to_x)
+
+    def stage_2(m):
+        received(moves["l", m])
+
+        def left(zz, _):
+            grads[m, zz, chip_x, :, 0:mid] = (grads[m, zz, chip_x, :, 0:mid].astype(F32) + gl[m, zz].astype(F32)).astype(BF)
+            return 0
+
+        lax.fori_loop(0, zsize, left, 0)
+        moves["x", m] = send(grads.at[m, :, chip_x], gx.at[m], to_x)
+        received(moves["r", m])
+
+        def right(zz, _):
+            grads[m, zz, chip_y, :, mid:] = (grads[m, zz, chip_y, :, mid:].astype(F32) + gr[m, zz].astype(F32)).astype(BF)
+            return 0
+
+        lax.fori_loop(0, zsize, right, 0)
+        moves["y", m] = send(grads.at[m, :, chip_y], gy.at[m], to_y)
+
+    def stage_3(m):
+        received(moves["x", m], moves["y", m])
+
+        def own(zz, _):
+            grads[m, zz, chip] = (grads[m, zz, chip].astype(F32) + gx[m, zz].astype(F32) + gy[m, zz].astype(F32)).astype(BF)
+            return 0
+
+        lax.fori_loop(0, zsize, own, 0)
+        moves["z", m, 0] = send(grads.at[m, place_at(0), chip], gz.at[m, 0], to_next)
+
+    def ring_step(m, j):
+        received(moves["z", m, j - 1])
+        total = gz[m, j - 1].astype(F32) + grads[m, place_at(j), chip].astype(F32)
+        if j < last:
+            gz[m, j - 1] = total.astype(BF)
+            moves["z", m, j] = send(gz.at[m, j - 1], gz.at[m, j], to_next)
+        else:
+            piece[m] = total.astype(BF)
+
+    def spread(name, source, target):
+        kept.append(local(source, target.at[chip, core]))
+        moves[name, "x"] = send(source, target.at[chip, core], to_x)
+        moves[name, "y"] = send(source, target.at[chip, core], to_y)
+
+    def forward(name, target):
+        middle = target.shape[3] // 2
+        received(moves[name, "x"])
+        left = target.at[chip_x, core, :, pl.ds(0, middle)]
+        moves[name, "fy"] = send(left, left, to_y)
+        received(moves[name, "y"])
+        right = target.at[chip_y, core, :, pl.ds(middle, middle)]
+        moves[name, "fx"] = send(right, right, to_x)
+
+    def cross(name, target):
+        received(moves[name, "fx"], moves[name, "fy"])
+        column = target.at[:, core]
+        moves[name, "core"] = send(column, column, to_core)
+
+    def product(m, pair):
+        per = width // tiles
+
+        def one(t, _):
+            zz = t // per
+            cols = pl.ds(pl.multiple_of(lax.rem(t, per) * tiles, tiles), tiles)
+            rows = pl.ds(pl.multiple_of(zz * (4 * strip), 4 * strip), 4 * strip)
+            nt = (((1,), (1,)), ((), ()))
+            r = lax.dot_general(half[rows, 0:length], pair[0, cols], nt, preferred_element_type=F32)
+            r = r + lax.dot_general(half[rows, length:], pair[1, cols], nt, preferred_element_type=F32)
+            grads[m, zz, :, :, cols] = r.astype(BF).reshape(4, strip, tiles)
+            return 0
+
+        lax.fori_loop(0, zsize * per, one, 0)
+
+    ffn_step(0)
+    load_o.wait()
+    stage_1(0)
+    received(q_swap)
+    wait_all(load_q)
+    product(1, dq_pair)
+    stage_1(1)
+
+    received(k3)
+    wait_all(load_kv)
+    add_rows(held.at[1], [got.at[0]], 96)
+    k1 = send(held.at[1], got.at[2], to_x)
+    received(v3)
+    add_rows(held.at[3], [got.at[1]], 96)
+    v2 = send(held.at[3], got.at[3], to_y)
+    k2, v1 = send(dk[2], got.at[4], to_y), send(dv[1], got.at[5], to_x)
+    if last > 1:
+        ffn_step(1)
+    received(k1, k2, v1, v2)
+
+    def finish_keys(h, _):
+        rows = pl.ds(pl.multiple_of(h * 96, 96), 96)
+        v = held[0, rows].astype(F32) + got[2, rows].astype(F32) + got[4, rows].astype(F32)
+        kv_pair[0, rows] = rotate_back(v, cos[...], sin[...]).astype(BF)
+        return 0
+
+    def finish_values(h, _):
+        rows = pl.ds(pl.multiple_of(h * 96, 96), 96)
+        v = held[2, rows].astype(F32) + got[3, rows].astype(F32) + got[5, rows].astype(F32)
+        kv_pair[0, pl.ds(pl.multiple_of(kv_rows + h * 96, 96), 96)] = v.astype(BF)
+        return 0
+
+    lax.fori_loop(0, kv_rows // 96, finish_keys, 0)
+    lax.fori_loop(0, kv_rows // 96, finish_values, 0)
+    kv_swap = send(kv_pair.at[0], kv_pair.at[1], to_core)
+    kept.append(local(kv_pair.at[0], kv_low))
+    stage_2(0)
+    stage_2(1)
+    if last > 2:
+        ffn_step(2)
+    wait_all(load_far)
+    add_rows(wide_f.at[0], [wide_f.at[n] for n in range(1, zsize)], 64)
+    add_rows(tall_f.at[0], [tall_f.at[n] for n in range(1, zsize)], 64)
+    far = send(wide_f.at[0], wide_r, to_far), send(tall_f.at[0], tall_r, to_far)
+    received(kv_swap)
+    product(2, kv_pair)
+    stage_1(2)
+    stage_3(0)
+    stage_3(1)
+    stage_2(2)
+    for j in range(3, last):
+        ffn_step(j)
+    ffn_step(last)
+    received(*far)
+
+    def whole_wide(t, _):
+        part = pl.ds(pl.multiple_of(t * 64, 64), 64)
+        wide_p[part] = (wide_z[last - 1, part].astype(F32) + wide_r[part].astype(F32)).astype(BF)
+        return 0
+
+    def whole_tall(t, _):
+        part = pl.ds(pl.multiple_of(t * 64, 64), 64)
+        tall_p[part] = (tall_z[last - 1, part].astype(F32) + tall_r[part].astype(F32)).astype(BF)
+        return 0
+
+    lax.fori_loop(0, tall_p.shape[0] // 64, whole_tall, 0)
+    spread("tall", tall_p, tall_all)
+    lax.fori_loop(0, wide_p.shape[0] // 64, whole_wide, 0)
+    spread("wide", wide_p, wide_all)
+    for j in range(1, zsize):
+        ring_step(0, j)
+        ring_step(1, j)
+        if j == 1:
+            stage_3(2)
+    spread(0, piece.at[0], o_all)
+    spread(1, piece.at[1], q_all)
+    for j in range(1, zsize):
+        ring_step(2, j)
+    spread(2, piece.at[2], kv_all)
+    targets = (("tall", tall_all), ("wide", wide_all), (0, o_all), (1, q_all), (2, kv_all))
+    for name, target in targets:
+        forward(name, target)
+    wait_all(kept)
+    for name, target in targets:
+        cross(name, target)
+    for name, target in targets:
+        received(moves[name, "core"])
+    for copy in sent:
+        copy.wait_send()
+
+
+def tail(dk, dv, dq, cosine, sine, first_half, out_grad, wide, tall, far_wide, far_tall, zsize, chips):
+    kv_rows, length = dk[0].shape
+    width = 2 * kv_rows
+    strip = out_grad.shape[2]
+    rows, two = wide[0].shape[1:]
+    fine = tall[0].shape[1]
+    hbm, vmem = pl.BlockSpec(memory_space=pl.ANY), pl.BlockSpec(memory_space=pltpu.VMEM)
+    shape = lambda *s: jax.ShapeDtypeStruct(s, BF)
+    store = lambda *s: pltpu.VMEM(s, BF)
+    copies = 6 + 2 + 1 + 2 * (zsize - 1) + 3 * (4 + zsize - 1) + 5 * 5 + 2
+    inputs = [*dk, *dv, dq, cosine, sine, first_half, out_grad, *wide, *tall, *far_wide, *far_tall]
+    last = zsize - 1
+    return pl.pallas_call(
+        functools.partial(tail_kernel, zsize),
+        out_shape=[shape(chips, 2, strip, width)] * 3 + [shape(chips, 2, rows, two), shape(chips, 2, fine, width), shape(width, length)],
+        in_specs=[hbm] * 9 + [vmem] * 2 + [hbm] * (len(inputs) - 11),
+        out_specs=[hbm] * 6,
+        scratch_shapes=[
+            store(6, kv_rows, length), store(4, kv_rows, length), store(2, width, length), store(2, width, length),
+            store(width // 2, 2 * length), store(3, zsize, chips, strip, width),
+            store(3, zsize, strip, width // 2), store(3, zsize, strip, width // 2),
+            store(3, zsize, strip, width), store(3, zsize, strip, width),
+            store(3, last, strip, width), store(3, strip, width),
+            store(2, 3, rows, two), store(2, 3, fine, width), store(rows, two), store(fine, width),
+            store(last, rows, two), store(last, fine, width),
+            store(zsize, rows, two), store(zsize, fine, width), store(rows, two), store(fine, width), store(rows, two), store(fine, width),
+            pltpu.SemaphoreType.DMA((copies,)), pltpu.SemaphoreType.DMA((copies,)),
+            pltpu.SemaphoreType.DMA((6 * zsize + 8 + 2 * zsize + 6,)),
+        ],
+        compiler_params=pltpu.CompilerParams(collective_id=1, has_side_effects=True, vmem_limit_bytes=60 * 2**20),
+        name="tail",
+    )(*inputs)
+
+
 def mm(left, right, left_dim, right_dim):
     return lax.dot_general(left, right, (((left_dim,), (right_dim,)), ((), ())), preferred_element_type=F32)
 
@@ -719,55 +1045,73 @@
     gain_second_part = jnp.sum(second_grad * unit_second, 0)
     middle_grad = cot[:length].astype(F32) + norm_back(second_grad, unit_second, inverse_second, gain_second)
 
-    def scatter(parts):
-        total = parts[0].astype(F32)
-        for r in near:
-            total = total + hop(parts[r], r).astype(F32)
-        far = hop(depth_scatter(parts[diag], depth).astype(BF), diag)
-        total = depth_scatter(total.astype(BF), depth) + far.astype(F32)
-        return total.astype(BF)
-
-    tall_piece = scatter({r: tall_grad[r].reshape(zsize, fine, width) for r in range(chips)})
-    wide_piece = scatter({r: wide_grad[r].reshape(zsize, rows, 2 * chunk) for r in range(chips)})
-    tall_all = plane_gather(tall_piece, index)
-    wide_all = plane_gather(wide_piece, index)
-    down_grad = jnp.transpose(tall_all.reshape(chips, 2, fine, width), (1, 0, 2, 3)).reshape(hidden_rows, width).astype(F32)
-    wide_all = wide_all.reshape(chips, 2, rows, 2, zsize, fine)
-    gate_grad = jnp.transpose(wide_all[:, :, :, 0], (2, 3, 1, 0, 4)).reshape(rows, -1).astype(F32)
-    up_grad = jnp.transpose(wide_all[:, :, :, 1], (2, 3, 1, 0, 4)).reshape(rows, -1).astype(F32)
-
-    middle_low = middle_grad.astype(BF)
-    attended_grad = mm(output_full, middle_low, 1, 1).astype(BF)
-    query_total, key_parts, value_parts = attn_bwd(
-        ids, order, query, attended, attended_grad, log_total, key_list, value_list, KEY_HEADS
-    )
-    key_sum = [part for part in key_parts]
-    value_sum = [part for part in value_parts]
-    for r in range(chips - 1, 0, -1):
-        high = 1 << (r.bit_length() - 1)
-        low = r & -r
-        key_sum[r ^ high] = key_sum[r ^ high].astype(F32) + hop(key_sum[r].astype(BF), high).astype(F32)
-        value_sum[r ^ low] = value_sum[r ^ low].astype(F32) + hop(value_sum[r].astype(BF), low).astype(F32)
-    query_low = rotate_back(query_total, cosine, sine).astype(BF)
-    key_low = rotate_back(key_sum[0], cosine, sine).astype(BF)
-    value_low = value_sum[0].astype(BF)
-    kv_low = jnp.concatenate([key_low, value_low])
-
     def halves(a):
         cut = a.reshape(zsize, chips, 2, strip, length)
         here = pick(cut, core, 2).reshape(-1, length)
         there = swap(pick(cut, 1 - core, 2).reshape(-1, length))
         return jnp.concatenate([here, there], 1)
 
-    def square_grad(product):
-        parts = product.astype(BF).reshape(zsize, chips, strip, width)
-        piece = scatter({r: pick(parts, chip ^ r, 1) for r in range(chips)})
-        return plane_gather(piece, index).reshape(rows, width).astype(F32)
-
     first_half = halves(first_t)
-    output_grad = square_grad(mm(halves(attended), jnp.concatenate([middle_low, swap(middle_low)]), 1, 0))
-    query_grad = square_grad(mm(first_half, jnp.concatenate([query_low, swap(query_low)], 1), 1, 1))
-    kv_grad = square_grad(mm(first_half, jnp.concatenate([kv_low, swap(kv_low)], 1), 1, 1))
+    middle_low = middle_grad.astype(BF)
+    out_part_grad = mm(halves(attended), jnp.concatenate([middle_low, swap(middle_low)]), 1, 0)
+    attended_grad = mm(output_full, middle_low, 1, 1).astype(BF)
+    query_low, key_parts, value_parts = attn_bwd(
+        ids, order, query, attended, attended_grad, log_total, cosine, sine, key_list, value_list, KEY_HEADS
+    )
+    wide_cut = {r: wide_grad[r].reshape(zsize, rows, 2 * chunk) for r in range(chips)}
+    tall_cut = {r: tall_grad[r].reshape(zsize, fine, width) for r in range(chips)}
+    if fast:
+        def shifted(parts):
+            return [parts] + [
+                lax.ppermute(pick(parts, lax.rem(depth + s, zsize)), "fsdp", [(k, (k + s) % zsize) for k in range(zsize)])
+                for s in range(1, zsize)
+            ]
+
+        o_all, q_all, kv_all, wide_all, tall_all, kv_low = tail(
+            key_parts, value_parts, query_low, cosine, sine, first_half,
+            out_part_grad.astype(BF).reshape(zsize, chips, strip, width),
+            [wide_cut[0], hop(wide_cut[1], 1), hop(wide_cut[2], 2)], [tall_cut[0], hop(tall_cut[1], 1), hop(tall_cut[2], 2)],
+            shifted(wide_cut[diag]), shifted(tall_cut[diag]), zsize, chips,
+        )
+        output_grad, query_grad, kv_grad = (a.reshape(rows, width).astype(F32) for a in (o_all, q_all, kv_all))
+    else:
+        key_sum = [part for part in key_parts]
+        value_sum = [part for part in value_parts]
+        for r in range(chips - 1, 0, -1):
+            high = 1 << (r.bit_length() - 1)
+            low = r & -r
+            key_sum[r ^ high] = key_sum[r ^ high].astype(F32) + hop(key_sum[r].astype(BF), high).astype(F32)
+            value_sum[r ^ low] = value_sum[r ^ low].astype(F32) + hop(value_sum[r].astype(BF), low).astype(F32)
+        key_low = rotate_back(key_sum[0], cosine, sine).astype(BF)
+        value_low = value_sum[0].astype(BF)
+        kv_low = jnp.concatenate([key_low, value_low])
+
+        def scatter(parts):
+            total = parts[0].astype(F32)
+            for r in near:
+                total = total + hop(parts[r], r).astype(F32)
+            far = hop(depth_scatter(parts[diag], depth).astype(BF), diag)
+            total = depth_scatter(total.astype(BF), depth) + far.astype(F32)
+            return total.astype(BF)
+
+        tall_piece = scatter(tall_cut)
+        wide_piece = scatter(wide_cut)
+        tall_all = plane_gather(tall_piece, index)
+        wide_all = plane_gather(wide_piece, index)
+        def square_grad(product):
+            parts = product.astype(BF).reshape(zsize, chips, strip, width)
+            piece = scatter({r: pick(parts, chip ^ r, 1) for r in range(chips)})
+            return plane_gather(piece, index).reshape(rows, width).astype(F32)
+
+        output_grad = square_grad(out_part_grad)
+        query_grad = square_grad(mm(first_half, jnp.concatenate([query_low, swap(query_low)], 1), 1, 1))
+        kv_grad = square_grad(mm(first_half, jnp.concatenate([kv_low, swap(kv_low)], 1), 1, 1))
+
+
+    down_grad = jnp.transpose(tall_all.reshape(chips, 2, fine, width), (1, 0, 2, 3)).reshape(hidden_rows, width).astype(F32)
+    wide_all = wide_all.reshape(chips, 2, rows, 2, zsize, fine)
+    gate_grad = jnp.transpose(wide_all[:, :, :, 0], (2, 3, 1, 0, 4)).reshape(rows, -1).astype(F32)
+    up_grad = jnp.transpose(wide_all[:, :, :, 1], (2, 3, 1, 0, 4)).reshape(rows, -1).astype(F32)
 
     first_grad = mm(query_low, query_full, 0, 1) + mm(kv_low, key_value_full, 0, 1)
     gain_first_part = jnp.sum(first_grad * unit_first, 0)

time: 1060 us -> 983 us (0.927)
  Pallas kernels: 332 us -> 534 us
  waiting for transfers between devices: 275 us -> 96.6 us
  other arithmetic: 78.5 us -> 37.8 us
  starting transfers between devices: 84.5 us -> 46.4 us
  matrix products: 169 us -> 156 us
    pallas_call x0 -> x1, Pallas kernels: none -> 203 us  [tail(): pl.pallas_call(functools.partial(tail_kernel, zsize), out_shape=[shape(ch...]
    ppermute x30 -> x6, waiting for transfers between devices: 137 us -> 42.3 us  [shifted(): lax.ppermute(pick(parts, lax.rem(depth + s, zsize)), 'fsdp', [(k, (k + s)...]
    ppermute x44 -> x12, waiting for transfers between devices: 120 us -> 36.3 us  [hop(): lax.ppermute(a, 'ctx', [(i, i ^ 2 * r) for i in range(lax.axis_size('ctx'...]
    ppermute x44 -> x12, starting transfers between devices: 51.3 us -> 12.2 us  [hop(): lax.ppermute(a, 'ctx', [(i, i ^ 2 * r) for i in range(lax.axis_size('ctx'...]
    convert_element_type x37 -> x2, other arithmetic: 38.4 us -> 4.53 us  [body(): a.reshape(rows, width).astype(F32)]
    unnamed x223 -> x184, local copies, waits for them, and re-layouts: 37.4 us -> 20.7 us
    dot_general x31 -> x29, matrix products: 169 us -> 156 us  [mm(): lax.dot_general(left, right, (((left_dim,), (right_dim,)), ((), ())), pre...]
    convert_element_type x1 -> x2, local copies, waits for them, and re-layouts: 3.13 us -> 14.6 us  [body(): jnp.transpose(wide_all[:, :, :, 0], (2, 3, 1, 0, 4)).reshape(rows, -1)]
  transfers between devices with their start and end apart: 103 -> 40, of which waited for: 42 -> 9; matrix products, arithmetic and copies ran while one was open for 29% -> 27% of each run, Pallas kernels for 16% -> 38%
where the time goes in v3:
time: 983 us; the launch traced here: 975 us
  Pallas kernels  534 us (54%)
  matrix products  156 us (16%)
  local copies, waits for them, and re-layouts  102 us (10%)
  waiting for transfers between devices  96.6 us (10%)
  starting transfers between devices  46.4 us (5%)
  other arithmetic  37.8 us (4%)
    pallas_call x1, Pallas kernels, tail(): pl.pallas_call(functools.partial(tail_kernel, zsize), out_shape=[shape(ch...  203 us
    pallas_call x1, Pallas kernels, front(): pl.pallas_call(functools.partial(front_kernel, zsize), out_shape=[square,...  160 us
    dot_general x29, matrix products, mm(): lax.dot_general(left, right, (((left_dim,), (right_dim,)), ((), ())), pre...  156 us
    pallas_call x1, Pallas kernels, attn_bwd(): pl.pallas_call(functools.partial(bwd_kernel, nchip, SCALE), grid_spec=gri...  87.5 us
    pallas_call x1, Pallas kernels, attn_fwd(): pl.pallas_call(functools.partial(fwd_kernel, nchip, SCALE), grid_spec=gri...  84.2 us
    ppermute x6, waiting for transfers between devices, shifted(): lax.ppermute(pick(parts, lax.rem(depth + s, zsize)), 'fsdp', [(k, (k + s)...  42.3 us
    ppermute x12, waiting for transfers between devices, hop(): lax.ppermute(a, 'ctx', [(i, i ^ 2 * r) for i in range(lax.axis_size('ctx'...  36.3 us
    unnamed x184, local copies, waits for them, and re-layouts  20.7 us
  transfers between devices with their start and end apart: 40, of which 9 were waited for; matrix products, arithmetic and copies ran while one was open for 27% of the time, Pallas kernels for 38%

profile of v3, /device:TPU:0, one launch (start us, length us, event | category | flops | bytes accessed | tf_op | source)
XLA Modules:
  0.0 974.7 jit_solution(16723335076704174563)
XLA Ops:
  9.2 159.7 %front.1 = (bf16[4,4,2,48,1536]{4,3,2,1,0:T(8,128)(2,1)}, bf16[4,4,2,48,1536]{4,3,2,1,0:T(8,128)(2,1)}, bf16[4,4,2,48,1536]{4,3,2,1,0:T(8,128)(2,1)}, bf16[4,384...) custom-call(bf16[2,256,1536]{2,1,0:T(8,128)(2,1)} %refs_0_.1, ...), custom_call_target="tpu_custom_call" | custom-call | tf_op jit(solution)/shard_map/front/pallas_call | solution.py:444
  185.2 84.2 %attention_forward.1 = (bf16[1536,512]{1,0:T(8,128)(2,1)}, f32[8,4,1,256]{3,2,1,0:T(1,128)}) custom-call(s32[4]{0:T(128)} %get-tuple-element.108.ids_ref, s32[16]{0:T(128)} %select_reduce_fusion.inv_ref, bf16[1536,512]{1,0:T(8,128)(2,1)} %get-tuple-element.48.q_ref, bf16[768,512]{1,0:T(8,128)(2,1)} %copy-done.10, bf16[768,512]{1,0:T(8,128)(2,1)} %copy-done.11, ...), custom_call_target="tpu_custom_call" | custom-call | flops 89999998976 | bytes 16777216 | tf_op jit(solution)/shard_map/attention_forward/pallas_call | solution.py:95
  269.5 7.3 multiply_reduce_fusion.2
  295.3 8.6 collective-permute-done.10
  303.9 3.3 collective-permute-start.7
  314.9 8.3 collective-permute-done.7
  327.8 3.6 fusion.56
  331.4 4.8 multiply_convert_fusion.8
  336.2 6.2 fusion.53
  342.5 4.8 multiply_convert_fusion.2
  350.4 4.5 fusion.63
  355.0 5.3 convolution_convert_fusion.3
  360.3 3.7 convolution_convert_fusion
  369.3 3.5 fusion.25
  372.8 6.8 collective-permute-done.3
  379.6 5.2 fusion.54
  384.8 28.1 %collective-permute-done.4 = bf16[512,1536]{1,0:T(8,128)(2,1)S(1)} collective-permute-done((bf16[512,1536]{1,0:T(8,128)(2,1)S(1)}, bf16[512,1536]{1,0:T(8,128)(2,1)S(1)}, u32[]{:S(2)}, u32[]{:S(2)}) %collective-permute-start.4) | collective-permute-done | bytes 1572896 | tf_op jit(solution)/shard_map/ppermute | solution.py:806
  412.9 7.6 multiply_convert_fusion.4
  420.5 5.4 fusion.23
  425.9 5.0 fusion.55
  431.0 7.5 multiply_convert_fusion.6
  439.8 5.6 fusion.24
  445.4 9.8 %add_add_fusion = f32[1024,1536]{1,0:T(8,128)S(1)} fusion(f32[1024,1536]{1,0:T(8,128)} %fusion.23, f32[1024,1536]{1,0:T(8,128)S(1)} %fusion.25, f32[1024,1536]{1,0:T(8,128)} %fusion.24, bf16[1536,1024]{1,0:T(8,128)(2,1)} %bitcast.12, bf16[1024,512]{0,1:T(8,128)(2,1)} %copy-done.46, bf16[1024,512]{0,1:T(8,128)(2,1)S(1)} %get-tuple-element.111), kind=kOutput, calls=%fused_computation.3 | convolution fusion | flops 3230138368 | bytes 30408704 | tf_op jit(solution)/shard_map/dot_general | solution.py:798
  460.7 6.1 fusion.64
  466.8 4.9 convolution_convert_fusion.2
  474.7 3.4 convolution_convert_fusion.6
  478.2 8.3 add_add_fusion.1
  490.4 7.8 convolution_convert_fusion.1
  498.2 3.0 collective-permute-start.22
  503.9 5.1 fusion.61
  512.9 16.3 %collective-permute-done.24.refs_24_ = bf16[128,1536]{1,0:T(8,128)(2,1)S(1)} collective-permute-done((bf16[128,1536]{1,0:T(8,128)(2,1)S(1)}, bf16[128,1536]{1,0:T(8,128)(2,1)S(1)}, u32[]{:S(2)}, u32[]{:S(2)}) %collective-permute-start.24) | collective-permute-done | bytes 393248 | tf_op jit(solution)/shard_map/ppermute | solution.py:1066
  530.5 5.1 convolution_convert_fusion.9.do_ref
  535.6 25.5 %collective-permute-done.25.refs_25_ = bf16[128,1536]{1,0:T(8,128)(2,1)S(1)} collective-permute-done((bf16[128,1536]{1,0:T(8,128)(2,1)S(1)}, bf16[128,1536]{1,0:T(8,128)(2,1)S(1)}, u32[]{:S(2)}, u32[]{:S(2)}) %collective-permute-start.25) | collective-permute-done | bytes 393248 | tf_op jit(solution)/shard_map/ppermute | solution.py:1066
  566.2 87.5 %attention_backward.1 = (bf16[1536,512]{1,0:T(8,128)(2,1)}, bf16[768,512]{1,0:T(8,128)(2,1)}, bf16[768,512]{1,0:T(8,128)(2,1)}, bf16[768,512]{1,0:T(8,128)(2,1)}...) custom-call(s32[4]{0:T(128)} %get-tuple-element.108.ids_ref, ...), custom_call_target="tpu_custom_call" | custom-call | flops 89999998976 | bytes 25165824 | tf_op jit(solution)/shard_map/attention_backward/pallas_call | solution.py:193
  653.7 9.9 %collective-permute-start.23 = (bf16[384,1024]{1,0:T(8,128)(2,1)}, bf16[384,1024]{1,0:T(8,128)(2,1)S(1)}, u32[]{:S(2)}, u32[]{:S(2)}) collective-permute-start(bf16[384,1024]{1,0:T(8,128)(2,1)} %get-tuple-element.123), channel_id=1, source_target_pairs={{0,3},{1,0},{2,1},{3,2},{4,7},{5,4},{6,5},{7,6},{8,11},{9,8},{10,9... | collective-permute-start | bytes 2359304 | tf_op jit(solution)/shard_map/ppermute | solution.py:1066
  663.5 7.3 fusion.66
  674.7 6.1 convolution_convert_fusion.4
  683.2 202.7 %tail.1 = (bf16[4,2,48,1536]{3,2,1,0:T(8,128)(2,1)}, bf16[4,2,48,1536]{3,2,1,0:T(8,128)(2,1)}, bf16[4,2,48,1536]{3,2,1,0:T(8,128)(2,1)}, bf16[4,2,384,1024]{3,2,...) custom-call(bf16[768,512]{1,0:T(8,128)(2,1)} %get-tuple-element.67.refs_0_, ...), custom_call_target="tpu_custom_call" | custom-call | tf_op jit(solution)/shard_map/tail/pallas_call | solution.py:775
  885.9 7.4 fusion.8
  898.7 3.5 convert_bitcast_fusion.2
  905.2 11.2 %reshape.227 = bf16[4,2,384,2,4,128]{5,4,3,2,1,0:T(4,128)(2,1)} reshape(bf16[4,2,384,1024]{3,2,1,0:T(8,128)(2,1)} %get-tuple-element.81) | data formatting | bytes 12582912 | tf_op jit(solution)/shard_map/reshape | solution.py:1112
  916.4 6.4 convert_bitcast_fusion
  928.6 6.7 copy.32
  935.4 7.9 reshape.231
  943.3 9.5 copy.33
  952.8 8.0 reshape.232
  960.8 6.1 copy.34
  967.5 3.1 maximum_select_fusion.1
  (322 shorter events, 115.0 us)
Async XLA Ops:
  4.4 164.5 %copy-start.4 = (f32[48,512]{1,0:T(8,128)}, f32[48,512]{1,0:T(8,128)S(1)}, u32[]{:S(2)}) copy-start(f32[48,512]{1,0:T(8,128)S(1)} %get-tuple-element.144.refs_10_.sin_ref) | copy-start | bytes 294916
  4.4 164.5 %copy-start.5 = (f32[48,512]{1,0:T(8,128)}, f32[48,512]{1,0:T(8,128)S(1)}, u32[]{:S(2)}) copy-start(f32[48,512]{1,0:T(8,128)S(1)} %get-tuple-element.145.refs_9_.cos_ref) | copy-start | bytes 294916
  177.3 131.4 %collective-permute-start.5 = (bf16[384,1024]{1,0:T(8,128)(2,1)S(1)}, bf16[384,1024]{1,0:T(8,128)(2,1)}, u32[]{:S(2)}, u32[]{:S(2)}) collective-permute-start(bf16[384,1024]{1,0:T(8,128)(2,1)S(1)} %get-tuple-element.62), channel_id=1, source_target_pairs={{0,1},{1,2},{2,3},{3,0},{4,5},{5,6},{6,7},{7,4},{8,9},{9,10},{10,1... | collective-permute-start | bytes 2359304 | tf_op jit(solution)/shard_map/ppermute | solution.py:835
  179.6 132.6 %collective-permute-start.6 = (bf16[384,1024]{1,0:T(8,128)(2,1)S(1)}, bf16[384,1024]{1,0:T(8,128)(2,1)}, u32[]{:S(2)}, u32[]{:S(2)}) collective-permute-start(bf16[384,1024]{1,0:T(8,128)(2,1)S(1)} %get-tuple-element.62), channel_id=1, source_target_pairs={{0,2},{1,3},{2,0},{3,1},{4,6},{5,7},{6,4},{7,5},{8,10},{9,11},{10,... | collective-permute-start | bytes 2359304 | tf_op jit(solution)/shard_map/ppermute | solution.py:835
  180.6 109.9 %collective-permute-start.8 = (bf16[128,1536]{1,0:T(8,128)(2,1)S(1)}, bf16[128,1536]{1,0:T(8,128)(2,1)}, u32[]{:S(2)}, u32[]{:S(2)}) collective-permute-start(bf16[128,1536]{1,0:T(8,128)(2,1)S(1)} %get-tuple-element.63), channel_id=1, source_target_pairs={{0,1},{1,2},{2,3},{3,0},{4,5},{5,6},{6,7},{7,4},{8,9},{9,10},{10,1... | collective-permute-start | bytes 1179656 | tf_op jit(solution)/shard_map/ppermute | solution.py:835
  181.7 111.2 %collective-permute-start.9 = (bf16[128,1536]{1,0:T(8,128)(2,1)S(1)}, bf16[128,1536]{1,0:T(8,128)(2,1)}, u32[]{:S(2)}, u32[]{:S(2)}) collective-permute-start(bf16[128,1536]{1,0:T(8,128)(2,1)S(1)} %get-tuple-element.63), channel_id=1, source_target_pairs={{0,2},{1,3},{2,0},{3,1},{4,6},{5,7},{6,4},{7,5},{8,10},{9,11},{10,... | collective-permute-start | bytes 1179656 | tf_op jit(solution)/shard_map/ppermute | solution.py:835
  184.1 141.4 %collective-permute-start.12 = (bf16[2,256,1536]{2,1,0:T(8,128)(2,1)}, bf16[2,256,1536]{2,1,0:T(8,128)(2,1)}, u32[]{:S(2)}, u32[]{:S(2)}) collective-permute-start(bf16[2,256,1536]{2,1,0:T(8,128)(2,1)} %param.14), channel_id=1, source_target_pairs={{0,4},{4,0},{8,12},{12,8},{16,20},{20,16},{24,28},{28,24},{1,5},{5... | collective-permute-start | bytes 4718600 | tf_op jit(solution)/shard_map/ppermute | solution.py:802
  282.2 192.5 %copy-start.31 = (bf16[256,1536]{1,0:T(8,128)(2,1)}, bf16[256,1536]{1,0:T(8,128)(2,1)S(1)}, u32[]{:S(2)}) copy-start(bf16[256,1536]{1,0:T(8,128)(2,1)S(1)} %get-tuple-element.140) | copy-start | bytes 2359300
  290.2 135.7 %copy-start.40 = (bf16[512,1536]{1,0:T(8,128)(2,1)}, bf16[512,1536]{1,0:T(8,128)(2,1)S(1)}, u32[]{:S(2)}) copy-start(bf16[512,1536]{1,0:T(8,128)(2,1)S(1)} %multiply_convert_fusion) | copy-start | bytes 4718596
  290.5 16.8 %collective-permute-start.14 = (bf16[768,512]{1,0:T(8,128)(2,1)S(1)}, bf16[768,512]{1,0:T(8,128)(2,1)S(1)}, u32[]{:S(2)}, u32[]{:S(2)}) collective-permute-start(bf16[768,512]{1,0:T(8,128)(2,1)S(1)} %bitcast.159), channel_id=1, source_target_pairs={{0,4},{4,0},{8,12},{12,8},{16,20},{20,16},{24,28},{28,24},{1,5},{5... | collective-permute-start | bytes 2359304 | tf_op jit(solution)/shard_map/ppermute | solution.py:802
  292.9 11.0 %collective-permute-start.10 = (bf16[128,1536]{1,0:T(8,128)(2,1)S(1)}, bf16[128,1536]{1,0:T(8,128)(2,1)S(1)}, u32[]{:S(2)}, u32[]{:S(2)}) collective-permute-start(bf16[128,1536]{1,0:T(8,128)(2,1)S(1)} %get-tuple-element.63), channel_id=1, source_target_pairs={{0,3},{1,0},{2,1},{3,2},{4,7},{5,4},{6,5},{7,6},{8,11},{9,8},{10,9... | collective-permute-start | bytes 1179656 | tf_op jit(solution)/shard_map/ppermute | solution.py:835
  303.9 19.4 %collective-permute-start.7 = (bf16[384,1024]{1,0:T(8,128)(2,1)S(1)}, bf16[384,1024]{1,0:T(8,128)(2,1)S(1)}, u32[]{:S(2)}, u32[]{:S(2)}) collective-permute-start(bf16[384,1024]{1,0:T(8,128)(2,1)S(1)} %get-tuple-element.62), channel_id=1, source_target_pairs={{0,3},{1,0},{2,1},{3,2},{4,7},{5,4},{6,5},{7,6},{8,11},{9,8},{10,9... | collective-permute-start | bytes 2359304 | tf_op jit(solution)/shard_map/ppermute | solution.py:835
  307.2 20.5 %collective-permute-start = (bf16[512,1536]{1,0:T(8,128)(2,1)S(1)}, bf16[512,1536]{1,0:T(8,128)(2,1)S(1)}, u32[]{:S(2)}, u32[]{:S(2)}) collective-permute-start(bf16[512,1536]{1,0:T(8,128)(2,1)S(1)} %multiply_convert_fusion), channel_id=1, source_target_pairs={{0,4},{4,0},{8,12},{12,8},{16,20},{20,16},{24,28},{28,24},{1,5},{5... | collective-permute-start | bytes 4718600 | tf_op jit(solution)/shard_map/ppermute | solution.py:802
  308.7 70.9 %collective-permute-start.3 = (bf16[1536,1024]{1,0:T(8,128)(2,1)S(1)}, bf16[1536,1024]{1,0:T(8,128)(2,1)S(1)}, u32[]{:S(2)}, u32[]{:S(2)}) collective-permute-start(bf16[1536,1024]{1,0:T(8,128)(2,1)S(1)} %bitcast.166), channel_id=1, source_target_pairs={{0,16},{4,20},{8,24},{12,28},{16,0},{20,4},{24,8},{28,12},{1,17},{... | collective-permute-start | bytes 9437192 | tf_op jit(solution)/shard_map/ppermute | solution.py:806
  312.1 113.8 %collective-permute-start.1 = (bf16[1536,1024]{1,0:T(8,128)(2,1)S(1)}, bf16[1536,1024]{1,0:T(8,128)(2,1)S(1)}, u32[]{:S(2)}, u32[]{:S(2)}) collective-permute-start(bf16[1536,1024]{1,0:T(8,128)(2,1)S(1)} %bitcast.167), channel_id=1, source_target_pairs={{0,8},{4,12},{8,0},{12,4},{16,24},{20,28},{24,16},{28,20},{1,9},{5... | collective-permute-start | bytes 9437192 | tf_op jit(solution)/shard_map/ppermute | solution.py:806
  323.2 89.7 %collective-permute-start.4 = (bf16[512,1536]{1,0:T(8,128)(2,1)S(1)}, bf16[512,1536]{1,0:T(8,128)(2,1)S(1)}, u32[]{:S(2)}, u32[]{:S(2)}) collective-permute-start(bf16[512,1536]{1,0:T(8,128)(2,1)S(1)} %bitcast.136), channel_id=1, source_target_pairs={{0,16},{4,20},{8,24},{12,28},{16,0},{20,4},{24,8},{28,12},{1,17},{... | collective-permute-start | bytes 4718600 | tf_op jit(solution)/shard_map/ppermute | solution.py:806
  325.5 105.5 %collective-permute-start.2 = (bf16[512,1536]{1,0:T(8,128)(2,1)S(1)}, bf16[512,1536]{1,0:T(8,128)(2,1)}, u32[]{:S(2)}, u32[]{:S(2)}) collective-permute-start(bf16[512,1536]{1,0:T(8,128)(2,1)S(1)} %bitcast.137), channel_id=1, source_target_pairs={{0,8},{4,12},{8,0},{12,4},{16,24},{20,28},{24,16},{28,20},{1,9},{5... | collective-permute-start | bytes 4718600 | tf_op jit(solution)/shard_map/ppermute | solution.py:806
  327.7 147.0 %copy-start.33 = (bf16[256,1536]{1,0:T(8,128)(2,1)}, bf16[256,1536]{1,0:T(8,128)(2,1)S(1)}, u32[]{:S(2)}) copy-start(bf16[256,1536]{1,0:T(8,128)(2,1)S(1)} %get-tuple-element.142) | copy-start | bytes 2359300
  327.7 182.8 %collective-permute-start.15 = (bf16[768,512]{1,0:T(8,128)(2,1)}, bf16[768,512]{1,0:T(8,128)(2,1)}, u32[]{:S(2)}, u32[]{:S(2)}) collective-permute-start(bf16[768,512]{1,0:T(8,128)(2,1)} %bitcast.31), channel_id=1, source_target_pairs={{0,4},{4,0},{8,12},{12,8},{16,20},{20,16},{24,28},{28,24},{1,5},{5... | collective-permute-start | bytes 2359304 | tf_op jit(solution)/shard_map/ppermute | solution.py:802
  379.6 183.6 %collective-permute-start.21 = (bf16[384,1024]{1,0:T(8,128)(2,1)}, bf16[384,1024]{1,0:T(8,128)(2,1)}, u32[]{:S(2)}, u32[]{:S(2)}) collective-permute-start(bf16[384,1024]{1,0:T(8,128)(2,1)} %get-tuple-element.125), channel_id=1, source_target_pairs={{0,1},{1,2},{2,3},{3,0},{4,5},{5,6},{6,7},{7,4},{8,9},{9,10},{10,1... | collective-permute-start | bytes 2359304 | tf_op jit(solution)/shard_map/ppermute | solution.py:1066
  457.1 29.4 %collective-permute-start.13 = (f32[512,1536]{1,0:T(8,128)}, f32[512,1536]{1,0:T(8,128)S(1)}, u32[]{:S(2)}, u32[]{:S(2)}) collective-permute-start(f32[512,1536]{1,0:T(8,128)} %slice.123), channel_id=1, source_target_pairs={{0,4},{4,0},{8,12},{12,8},{16,20},{20,16},{24,28},{28,24},{1,5},{5... | collective-permute-start | bytes 9437192 | tf_op jit(solution)/shard_map/ppermute | solution.py:802
  488.3 9.9 %collective-permute-start.36 = (f32[384]{0:T(512)S(1)}, f32[384]{0:T(512)S(1)}, u32[]{:S(2)}, u32[]{:S(2)}) collective-permute-start(f32[384]{0:T(512)S(1)} %get-tuple-element.90), channel_id=1, source_target_pairs={{0,3},{1,0},{2,1},{3,2},{4,7},{5,4},{6,5},{7,6},{8,11},{9,8},{10,9... | collective-permute-start | bytes 4616 | tf_op jit(solution)/shard_map/ppermute | solution.py:1125
  488.4 12.8 %collective-permute-start.35 = (f32[384]{0:T(512)S(1)}, f32[384]{0:T(512)S(1)}, u32[]{:S(2)}, u32[]{:S(2)}) collective-permute-start(f32[384]{0:T(512)S(1)} %get-tuple-element.91), channel_id=1, source_target_pairs={{0,2},{1,3},{2,0},{3,1},{4,6},{5,7},{6,4},{7,5},{8,10},{9,11},{10,... | collective-permute-start | bytes 4616 | tf_op jit(solution)/shard_map/ppermute | solution.py:1125
  488.6 12.6 %collective-permute-start.34 = (f32[384]{0:T(512)S(1)}, f32[384]{0:T(512)S(1)}, u32[]{:S(2)}, u32[]{:S(2)}) collective-permute-start(f32[384]{0:T(512)S(1)} %get-tuple-element.89), channel_id=1, source_target_pairs={{0,1},{1,2},{2,3},{3,0},{4,5},{5,6},{6,7},{7,4},{8,9},{9,10},{10,1... | collective-permute-start | bytes 4616 | tf_op jit(solution)/shard_map/ppermute | solution.py:1125
  498.2 66.4 %collective-permute-start.22 = (bf16[384,1024]{1,0:T(8,128)(2,1)S(1)}, bf16[384,1024]{1,0:T(8,128)(2,1)S(1)}, u32[]{:S(2)}, u32[]{:S(2)}) collective-permute-start(bf16[384,1024]{1,0:T(8,128)(2,1)S(1)} %copy-done.53), channel_id=1, source_target_pairs={{0,2},{1,3},{2,0},{3,1},{4,6},{5,7},{6,4},{7,5},{8,10},{9,11},{10,... | collective-permute-start | bytes 2359304 | tf_op jit(solution)/shard_map/ppermute | solution.py:1066
  501.2 28.0 %collective-permute-start.24 = (bf16[128,1536]{1,0:T(8,128)(2,1)S(1)}, bf16[128,1536]{1,0:T(8,128)(2,1)S(1)}, u32[]{:S(2)}, u32[]{:S(2)}) collective-permute-start(bf16[128,1536]{1,0:T(8,128)(2,1)S(1)} %copy-done.61), channel_id=1, source_target_pairs={{0,1},{1,2},{2,3},{3,0},{4,5},{5,6},{6,7},{7,4},{8,9},{9,10},{10,1... | collective-permute-start | bytes 1179656 | tf_op jit(solution)/shard_map/ppermute | solution.py:1066
  501.2 1.2 collective-permute-start.37
  502.5 6.5 collective-permute-start.38
  509.0 52.2 %collective-permute-start.25 = (bf16[128,1536]{1,0:T(8,128)(2,1)S(1)}, bf16[128,1536]{1,0:T(8,128)(2,1)S(1)}, u32[]{:S(2)}, u32[]{:S(2)}) collective-permute-start(bf16[128,1536]{1,0:T(8,128)(2,1)S(1)} %copy-done.60), channel_id=1, source_target_pairs={{0,2},{1,3},{2,0},{3,1},{4,6},{5,7},{6,4},{7,5},{8,10},{9,11},{10,... | collective-permute-start | bytes 1179656 | tf_op jit(solution)/shard_map/ppermute | solution.py:1066
  510.5 52.0 %collective-permute-start.26 = (bf16[128,1536]{1,0:T(8,128)(2,1)S(1)}, bf16[128,1536]{1,0:T(8,128)(2,1)S(1)}, u32[]{:S(2)}, u32[]{:S(2)}) collective-permute-start(bf16[128,1536]{1,0:T(8,128)(2,1)S(1)} %copy-done.59), channel_id=1, source_target_pairs={{0,3},{1,0},{2,1},{3,2},{4,7},{5,4},{6,5},{7,6},{8,11},{9,8},{10,9... | collective-permute-start | bytes 1179656 | tf_op jit(solution)/shard_map/ppermute | solution.py:1066
  529.1 37.0 %collective-permute-start.39 = (f32[384]{0:T(512)S(1)}, f32[384]{0:T(512)S(1)}, u32[]{:S(2)}, u32[]{:S(2)}) collective-permute-start(f32[384]{0:T(512)S(1)} %add.288), channel_id=1, source_target_pairs={{0,16},{4,20},{8,24},{12,28},{16,0},{20,4},{24,8},{28,12},{1,17},{... | collective-permute-start | bytes 4616 | tf_op jit(solution)/shard_map/ppermute | solution.py:806
  561.2 120.1 %collective-permute-start.17 = (bf16[4,384,1024]{2,1,0:T(8,128)(2,1)}, bf16[4,384,1024]{2,1,0:T(8,128)(2,1)S(1)}, u32[]{:S(2)}, u32[]{:S(2)}) collective-permute-start(bf16[4,384,1024]{2,1,0:T(8,128)(2,1)} %bitcast.34), channel_id=1, source_target_pairs={{0,8},{4,12},{8,0},{12,4},{16,24},{20,28},{24,16},{28,20},{1,9},{5... | collective-permute-start | bytes 9437192 | tf_op jit(solution)/shard_map/ppermute | solution.py:806
  562.5 118.8 %collective-permute-start.18 = (bf16[4,384,1024]{2,1,0:T(8,128)(2,1)}, bf16[4,384,1024]{2,1,0:T(8,128)(2,1)}, u32[]{:S(2)}, u32[]{:S(2)}) collective-permute-start(bf16[4,384,1024]{2,1,0:T(8,128)(2,1)} %bitcast.35), channel_id=1, source_target_pairs={{0,16},{4,20},{8,24},{12,28},{16,0},{20,4},{24,8},{28,12},{1,17},{... | collective-permute-start | bytes 9437192 | tf_op jit(solution)/shard_map/ppermute | solution.py:806
  563.2 118.0 %collective-permute-start.19 = (bf16[4,128,1536]{2,1,0:T(8,128)(2,1)}, bf16[4,128,1536]{2,1,0:T(8,128)(2,1)}, u32[]{:S(2)}, u32[]{:S(2)}) collective-permute-start(bf16[4,128,1536]{2,1,0:T(8,128)(2,1)} %bitcast.37), channel_id=1, source_target_pairs={{0,8},{4,12},{8,0},{12,4},{16,24},{20,28},{24,16},{28,20},{1,9},{5... | collective-permute-start | bytes 4718600 | tf_op jit(solution)/shard_map/ppermute | solution.py:806
  565.5 115.8 %collective-permute-start.20 = (bf16[4,128,1536]{2,1,0:T(8,128)(2,1)}, bf16[4,128,1536]{2,1,0:T(8,128)(2,1)}, u32[]{:S(2)}, u32[]{:S(2)}) collective-permute-start(bf16[4,128,1536]{2,1,0:T(8,128)(2,1)} %bitcast.38), channel_id=1, source_target_pairs={{0,16},{4,20},{8,24},{12,28},{16,0},{20,4},{24,8},{28,12},{1,17},{... | collective-permute-start | bytes 4718600 | tf_op jit(solution)/shard_map/ppermute | solution.py:806
  566.1 87.5 %collective-permute-start.16 = (bf16[512,1536]{1,0:T(8,128)(2,1)}, bf16[512,1536]{1,0:T(8,128)(2,1)}, u32[]{:S(2)}, u32[]{:S(2)}) collective-permute-start(bf16[512,1536]{1,0:T(8,128)(2,1)} %get-tuple-element.105), channel_id=1, source_target_pairs={{0,4},{4,0},{8,12},{12,8},{16,20},{20,16},{24,28},{28,24},{1,5},{5... | collective-permute-start | bytes 4718600 | tf_op jit(solution)/shard_map/ppermute | solution.py:802
  653.7 27.6 %collective-permute-start.23 = (bf16[384,1024]{1,0:T(8,128)(2,1)}, bf16[384,1024]{1,0:T(8,128)(2,1)S(1)}, u32[]{:S(2)}, u32[]{:S(2)}) collective-permute-start(bf16[384,1024]{1,0:T(8,128)(2,1)} %get-tuple-element.123), channel_id=1, source_target_pairs={{0,3},{1,0},{2,1},{3,2},{4,7},{5,4},{6,5},{7,6},{8,11},{9,8},{10,9... | collective-permute-start | bytes 2359304 | tf_op jit(solution)/shard_map/ppermute | solution.py:1066
  681.3 289.3 %collective-permute-start.11 = (f32[512,1536]{1,0:T(8,128)}, f32[512,1536]{1,0:T(8,128)}, u32[]{:S(2)}, u32[]{:S(2)}) collective-permute-start(f32[512,1536]{1,0:T(8,128)} %pad_maximum_fusion.1), channel_id=1, source_target_pairs={{0,4},{4,0},{8,12},{12,8},{16,20},{20,16},{24,28},{28,24},{1,5},{5... | collective-permute-start | bytes 9437192 | tf_op jit(solution)/shard_map/ppermute | solution.py:802
  683.2 202.7 %copy-start.1 = (bf16[512,1536]{1,0:T(8,128)(2,1)S(1)}, bf16[512,1536]{1,0:T(8,128)(2,1)}, u32[]{:S(2)}) copy-start(bf16[512,1536]{1,0:T(8,128)(2,1)} %copy-done) | copy-start | bytes 4718596
  683.2 202.7 %copy-start.66 = (f32[1536]{0:T(1024)S(1)}, f32[1536]{0:T(1024)}, u32[]{:S(2)}) copy-start(f32[1536]{0:T(1024)} %get-tuple-element.87) | copy-start | bytes 18436
  683.2 202.7 %copy-start.67 = (f32[512]{0:T(512)S(1)}, f32[512]{0:T(512)}, u32[]{:S(2)}) copy-start(f32[512]{0:T(512)} %add_rsqrt_fusion) | copy-start | bytes 6148
  895.5 72.0 %collective-permute-start.27 = (bf16[256,1536]{1,0:T(8,128)(2,1)}, bf16[256,1536]{1,0:T(8,128)(2,1)}, u32[]{:S(2)}, u32[]{:S(2)}) collective-permute-start(bf16[256,1536]{1,0:T(8,128)(2,1)} %get-tuple-element.132), channel_id=1, source_target_pairs={{0,4},{4,0},{8,12},{12,8},{16,20},{20,16},{24,28},{28,24},{1,5},{5... | collective-permute-start | bytes 2359304 | tf_op jit(solution)/shard_map/ppermute | solution.py:802
  896.0 20.3 %collective-permute-start.30 = (f32[384]{0:T(512)S(1)}, f32[384]{0:T(512)S(1)}, u32[]{:S(2)}, u32[]{:S(2)}) collective-permute-start(f32[384]{0:T(512)S(1)} %get-tuple-element.94), channel_id=1, source_target_pairs={{0,3},{1,0},{2,1},{3,2},{4,7},{5,4},{6,5},{7,6},{8,11},{9,8},{10,9... | collective-permute-start | bytes 4616 | tf_op jit(solution)/shard_map/ppermute | solution.py:1125
  897.6 18.8 %collective-permute-start.29 = (f32[384]{0:T(512)S(1)}, f32[384]{0:T(512)S(1)}, u32[]{:S(2)}, u32[]{:S(2)}) collective-permute-start(f32[384]{0:T(512)S(1)} %get-tuple-element.95), channel_id=1, source_target_pairs={{0,2},{1,3},{2,0},{3,1},{4,6},{5,7},{6,4},{7,5},{8,10},{9,11},{10,... | collective-permute-start | bytes 4616 | tf_op jit(solution)/shard_map/ppermute | solution.py:1125
  897.6 18.8 %collective-permute-start.28 = (f32[384]{0:T(512)S(1)}, f32[384]{0:T(512)S(1)}, u32[]{:S(2)}, u32[]{:S(2)}) collective-permute-start(f32[384]{0:T(512)S(1)} %get-tuple-element.93), channel_id=1, source_target_pairs={{0,1},{1,2},{2,3},{3,0},{4,5},{5,6},{6,7},{7,4},{8,9},{9,10},{10,1... | collective-permute-start | bytes 4616 | tf_op jit(solution)/shard_map/ppermute | solution.py:1125
  916.3 6.5 collective-permute-start.31
  922.8 3.6 collective-permute-start.32
  926.4 40.5 %collective-permute-start.33 = (f32[384]{0:T(512)S(1)}, f32[384]{0:T(512)S(1)}, u32[]{:S(2)}, u32[]{:S(2)}) collective-permute-start(f32[384]{0:T(512)S(1)} %add.282), channel_id=1, source_target_pairs={{0,16},{4,20},{8,24},{12,28},{16,0},{20,4},{24,8},{28,12},{1,17},{... | collective-permute-start | bytes 4616 | tf_op jit(solution)/shard_map/ppermute | solution.py:806
  (85 other events, 874.2 us)

commit v4 on v3

--- a/solution.py
+++ b/solution.py
@@ -17,198 +17,239 @@
 BF = jnp.bfloat16
 F32 = jnp.float32
 
+ATT_COST = 8
 LOG2E = 1.4426950408889634
-
-def attn_setup(nchip, g_refs, nat, tr):
-    for r in range(nchip):
-        for j in range(g_refs[r].shape[1] // 128):
-            n = r * (g_refs[r].shape[1] // 128) + j
-            block = g_refs[r][:, 128 * j:128 * (j + 1)]
-            if nat is not None:
-                nat[n] = block.T
-            if tr is not None:
-                tr[n] = block
-
-
-def fwd_kernel(nchip, scale, ids_ref, inv_ref, q_ref, *rest):
+NT = (((1,), (1,)), ((), ()))
+
+
+def block_tasks(ids_ref, inv_ref, slices, t):
+    tasks = []
+    for sl in range(slices):
+        first = ids_ref[2 * sl]
+        late = (t > first).astype(jnp.int32)
+        kpos = t - late * (first + 1)
+        tasks.append((sl, late, inv_ref[kpos], (ids_ref[2 * sl + late] - kpos) * BLK))
+    return tasks
+
+
+def causal_difference():
+    return lax.broadcasted_iota(jnp.int32, (BLK, 2 * BLK), 0) - lax.rem(lax.broadcasted_iota(jnp.int32, (BLK, 2 * BLK), 1), BLK)
+
+
+def fwd_kernel(nchip, heads, ids_ref, inv_ref, q_ref, *rest):
     k_refs, v_refs = rest[:nchip], rest[nchip:2 * nchip]
-    o_ref, lse_ref, knat, vtr, qs, m_s, l_s, acc = rest[2 * nchip:]
-    nq = q_ref.shape[1] // 128
-    nb = knat.shape[0]
-    c = scale * LOG2E
-    attn_setup(nchip, k_refs, knat, None)
-    attn_setup(nchip, v_refs, None, vtr)
-    for qi in range(nq):
-        qs[qi] = jnp.concatenate([q_ref[0:96, 128 * qi:128 * (qi + 1)], q_ref[96:192, 128 * qi:128 * (qi + 1)]], axis=1)
-    m_s[...] = jnp.full(m_s.shape, -1e30, jnp.float32)
-    l_s[...] = jnp.zeros(l_s.shape, jnp.float32)
-    acc[...] = jnp.zeros(acc.shape, jnp.float32)
-    diff = lax.broadcasted_iota(jnp.int32, (128, 256), 0) - lax.rem(lax.broadcasted_iota(jnp.int32, (128, 256), 1), 128)
+    o_ref, lse_ref, knat, vtr = rest[2 * nchip:2 * nchip + 4]
+    state = rest[2 * nchip + 4:]
+    nq = q_ref.shape[1] // BLK
+    slices = nq // 2
+    nb = nchip * nq
+    c = SCALE * LOG2E
+    chains = [(h, sl) for h in range(heads) for sl in range(slices)]
+    qs, m_s, l_s, acc = ({chain: state[4 * n + k] for n, chain in enumerate(chains)} for k in range(4))
+    for h in range(heads):
+        for n in range(nb):
+            r, lanes = n // nq, slice(BLK * (n % nq), BLK * (n % nq + 1))
+            knat[h, n] = k_refs[r][96 * h:96 * (h + 1), lanes].T
+            vtr[h, n] = v_refs[r][96 * h:96 * (h + 1), lanes]
+        for sl in range(slices):
+            for half in range(2):
+                lanes = slice(BLK * (2 * sl + half), BLK * (2 * sl + half + 1))
+                qs[h, sl][half] = jnp.concatenate([q_ref[192 * h:192 * h + 96, lanes], q_ref[192 * h + 96:192 * h + 192, lanes]], axis=1)
+            m_s[h, sl][...] = jnp.full((2, 1, 2 * BLK), -1e30, F32)
+            l_s[h, sl][...] = jnp.zeros((2, 1, 2 * BLK), F32)
+            acc[h, sl][...] = jnp.zeros((2, 96, 2 * BLK), F32)
+    diff = causal_difference()
 
     def step(t, _):
-        for sl in range(nq // 2):
-            first = ids_ref[2 * sl]
-            late = (t > first).astype(jnp.int32)
-            qi = 2 * sl + late
-            kpos = t - late * (first + 1)
-            qid = ids_ref[qi]
-            n = inv_ref[kpos]
-            s = jnp.dot(knat[n], qs[qi], preferred_element_type=jnp.float32)
-            s = jnp.where(diff <= (qid - kpos) * 128, s, -jnp.inf)
-            m_old = m_s[qi]
-            m_new = jnp.maximum(m_old, jnp.max(s, axis=0, keepdims=True))
-            p = jnp.exp2((s - m_new) * c)
-            alpha = jnp.exp2((m_old - m_new) * c)
-            l_s[qi] = l_s[qi] * alpha + jnp.sum(p, axis=0, keepdims=True)
-            m_s[qi] = m_new
-            acc[qi] = acc[qi] * alpha + jnp.dot(vtr[n], p.astype(jnp.bfloat16), preferred_element_type=jnp.float32)
+        tasks = block_tasks(ids_ref, inv_ref, slices, t)
+        todo = [(h, *task) for h in range(heads) for task in tasks]
+        scores = [
+            jnp.where(diff <= offset, jnp.dot(knat[h, n], qs[h, sl][late], preferred_element_type=F32), -jnp.inf)
+            for h, sl, late, n, offset in todo
+        ]
+        old = [(m_s[h, sl][late], l_s[h, sl][late], acc[h, sl][late]) for h, sl, late, n, offset in todo]
+        peaks = [jnp.maximum(m, jnp.max(s, axis=0, keepdims=True)) for s, (m, _l, _a) in zip(scores, old)]
+        weights = [jnp.exp2((s - peak) * c) for s, peak in zip(scores, peaks)]
+        shrink = [jnp.exp2((m - peak) * c) for peak, (m, _l, _a) in zip(peaks, old)]
+        totals = [l * a + jnp.sum(p, axis=0, keepdims=True) for (_m, l, _a), a, p in zip(old, shrink, weights)]
+        mixed = [
+            o * a + jnp.dot(vtr[h, n], p.astype(BF), preferred_element_type=F32)
+            for (h, sl, late, n, offset), (_m, _l, o), a, p in zip(todo, old, shrink, weights)
+        ]
+        for (h, sl, late, n, offset), peak, total, o in zip(todo, peaks, totals, mixed):
+            m_s[h, sl][late] = peak
+            l_s[h, sl][late] = total
+            acc[h, sl][late] = o
         return 0
 
     lax.fori_loop(0, nb + 1, step, 0)
-    for qi in range(nq):
-        l = l_s[qi]
-        o = acc[qi] / l
-        lse_ref[qi] = m_s[qi] * c + jnp.log2(l)
-        o_ref[0:96, 128 * qi:128 * (qi + 1)] = o[:, :128].astype(jnp.bfloat16)
-        o_ref[96:192, 128 * qi:128 * (qi + 1)] = o[:, 128:].astype(jnp.bfloat16)
+    for h, sl in chains:
+        for half in range(2):
+            lanes = slice(BLK * (2 * sl + half), BLK * (2 * sl + half + 1))
+            l = l_s[h, sl][half]
+            o = acc[h, sl][half] / l
+            lse_ref[h, 2 * sl + half] = m_s[h, sl][half] * c + jnp.log2(l)
+            o_ref[192 * h:192 * h + 96, lanes] = o[:, :BLK].astype(BF)
+            o_ref[192 * h + 96:192 * h + 192, lanes] = o[:, BLK:].astype(BF)
 
 
 def attn_fwd(ids, inv, qT, ks, vs, heads):
     nchip = len(ks)
     T = qT.shape[1]
-    nq = T // 128
+    nq = T // BLK
     nb = nchip * nq
+    per = 4 if nb <= 16 else 2
+    wide = pl.BlockSpec((192 * per, T), lambda g, *_: (g, 0))
+    slim = pl.BlockSpec((96 * per, T), lambda g, *_: (g, 0))
+    chain = [
+        pltpu.VMEM((2, 96, 2 * BLK), BF),
+        pltpu.VMEM((2, 1, 2 * BLK), F32),
+        pltpu.VMEM((2, 1, 2 * BLK), F32),
+        pltpu.VMEM((2, 96, 2 * BLK), F32),
+    ]
     grid_spec = pltpu.PrefetchScalarGridSpec(
         num_scalar_prefetch=2,
-        grid=(heads,),
-        in_specs=[pl.BlockSpec((192, T), lambda g, *_: (g, 0))] + [pl.BlockSpec((96, T), lambda g, *_: (g, 0))] * (2 * nchip),
-        out_specs=[pl.BlockSpec((192, T), lambda g, *_: (g, 0)), pl.BlockSpec((None, nq, 1, 256), lambda g, *_: (g, 0, 0, 0))],
-        scratch_shapes=[
-            pltpu.VMEM((nb, 128, 96), jnp.bfloat16),
-            pltpu.VMEM((nb, 96, 128), jnp.bfloat16),
-            pltpu.VMEM((nq, 96, 256), jnp.bfloat16),
-            pltpu.VMEM((nq, 1, 256), jnp.float32),
-            pltpu.VMEM((nq, 1, 256), jnp.float32),
-            pltpu.VMEM((nq, 96, 256), jnp.float32),
-        ],
+        grid=(heads // per,),
+        in_specs=[wide] + [slim] * (2 * nchip),
+        out_specs=[wide, pl.BlockSpec((per, nq, 1, 2 * BLK), lambda g, *_: (g, 0, 0, 0))],
+        scratch_shapes=[pltpu.VMEM((per, nb, BLK, 96), BF), pltpu.VMEM((per, nb, 96, BLK), BF)] + chain * (per * nq // 2),
     )
     return pl.pallas_call(
-        functools.partial(fwd_kernel, nchip, SCALE),
+        functools.partial(fwd_kernel, nchip, per),
         grid_spec=grid_spec,
-        out_shape=[jax.ShapeDtypeStruct((heads * 192, T), jnp.bfloat16), jax.ShapeDtypeStruct((heads, nq, 1, 256), jnp.float32)],
-        cost_estimate=pl.CostEstimate(flops=90 * 10**9, bytes_accessed=16 * 2**20, transcendentals=0),
+        out_shape=[jax.ShapeDtypeStruct((heads * 192, T), BF), jax.ShapeDtypeStruct((heads, nq, 1, 2 * BLK), F32)],
+        cost_estimate=pl.CostEstimate(flops=ATT_COST * 10**9, bytes_accessed=16 * 2**20, transcendentals=0),
+        compiler_params=pltpu.CompilerParams(vmem_limit_bytes=48 * 2**20),
         name="attention_forward",
     )(ids, inv, qT, *ks, *vs)
 
 
-def bwd_kernel(nchip, scale, ids_ref, inv_ref, q_ref, o_ref, do_ref, lse_ref, cos_ref, sin_ref, *rest):
+def bwd_kernel(nchip, heads, ids_ref, inv_ref, q_ref, o_ref, do_ref, lse_ref, cos_ref, sin_ref, *rest):
     k_refs, v_refs = rest[:nchip], rest[nchip:2 * nchip]
     dq_ref = rest[2 * nchip]
     dk_refs, dv_refs = rest[2 * nchip + 1:3 * nchip + 1], rest[3 * nchip + 1:4 * nchip + 1]
-    knat, ktr, vnat, qs, dos, delta, dq_s, dk_s, dv_s = rest[4 * nchip + 1:]
-    nq = q_ref.shape[1] // 128
-    nb = knat.shape[0]
-    nsl = nq // 2
-    c = scale * LOG2E
-    attn_setup(nchip, k_refs, knat, ktr)
-    attn_setup(nchip, v_refs, vnat, None)
-    for qi in range(nq):
-        lanes = slice(128 * qi, 128 * (qi + 1))
-        qs[qi] = jnp.concatenate([q_ref[0:96, lanes], q_ref[96:192, lanes]], axis=1)
-        do = jnp.concatenate([do_ref[0:96, lanes], do_ref[96:192, lanes]], axis=1)
-        dos[qi] = do
-        o = jnp.concatenate([o_ref[0:96, lanes], o_ref[96:192, lanes]], axis=1)
-        delta[qi] = jnp.sum(o.astype(jnp.float32) * do.astype(jnp.float32), axis=0, keepdims=True)
-    dq_s[...] = jnp.zeros(dq_s.shape, jnp.float32)
-    dk_s[...] = jnp.zeros(dk_s.shape, jnp.float32)
-    dv_s[...] = jnp.zeros(dv_s.shape, jnp.float32)
-    diff = lax.broadcasted_iota(jnp.int32, (128, 256), 0) - lax.rem(lax.broadcasted_iota(jnp.int32, (128, 256), 1), 128)
-    nt = (((1,), (1,)), ((), ()))
+    knat, ktr, vnat = rest[4 * nchip + 1:4 * nchip + 4]
+    state = rest[4 * nchip + 4:]
+    nq = q_ref.shape[1] // BLK
+    slices = nq // 2
+    nb = nchip * nq
+    c = SCALE * LOG2E
+    chains = [(h, sl) for h in range(heads) for sl in range(slices)]
+    qs, dos, stat, dq_s, dk_s, dv_s = ({chain: state[6 * n + k] for n, chain in enumerate(chains)} for k in range(6))
+    for h in range(heads):
+        for n in range(nb):
+            r, lanes = n // nq, slice(BLK * (n % nq), BLK * (n % nq + 1))
+            block = k_refs[r][96 * h:96 * (h + 1), lanes]
+            knat[h, n] = block.T
+            ktr[h, n] = block
+            vnat[h, n] = v_refs[r][96 * h:96 * (h + 1), lanes].T
+    for h, sl in chains:
+        for half in range(2):
+            lanes = slice(BLK * (2 * sl + half), BLK * (2 * sl + half + 1))
+            pair = lambda ref: jnp.concatenate([ref[192 * h:192 * h + 96, lanes], ref[192 * h + 96:192 * h + 192, lanes]], axis=1)
+            do = pair(do_ref)
+            qs[h, sl][half] = pair(q_ref)
+            dos[h, sl][half] = do
+            stat[h, sl][half, 0:1] = lse_ref[h, 2 * sl + half]
+            stat[h, sl][half, 1:2] = jnp.sum(pair(o_ref).astype(F32) * do.astype(F32), axis=0, keepdims=True)
+        dq_s[h, sl][...] = jnp.zeros((2, 96, 2 * BLK), F32)
+        dk_s[h, sl][...] = jnp.zeros((nb, 96, BLK), F32)
+        dv_s[h, sl][...] = jnp.zeros((nb, 96, BLK), F32)
+    diff = causal_difference()
 
     def step(t, _):
-        for sl in range(nsl):
-            first = ids_ref[2 * sl]
-            late = (t > first).astype(jnp.int32)
-            qi = 2 * sl + late
-            kpos = t - late * (first + 1)
-            qid = ids_ref[qi]
-            n = inv_ref[kpos]
-            q, do = qs[qi], dos[qi]
-            s = jnp.dot(knat[n], q, preferred_element_type=jnp.float32)
-            p = jnp.exp2(jnp.where(diff <= (qid - kpos) * 128, s * c - lse_ref[qi], -jnp.inf))
-            dp = jnp.dot(vnat[n], do, preferred_element_type=jnp.float32)
-            ds = (p * (dp - delta[qi])).astype(jnp.bfloat16)
-            dv_s[sl, n] += lax.dot_general(do, p.astype(jnp.bfloat16), nt, preferred_element_type=jnp.float32)
-            dk_s[sl, n] += lax.dot_general(q, ds, nt, preferred_element_type=jnp.float32)
-            dq_s[qi] += jnp.dot(ktr[n], ds, preferred_element_type=jnp.float32)
+        tasks = block_tasks(ids_ref, inv_ref, slices, t)
+        todo = [(h, *task) for h in range(heads) for task in tasks]
+        q = [qs[h, sl][late] for h, sl, late, n, offset in todo]
+        do = [dos[h, sl][late] for h, sl, late, n, offset in todo]
+        scores = [jnp.dot(knat[h, n], x, preferred_element_type=F32) for (h, sl, late, n, offset), x in zip(todo, q)]
+        grads = [jnp.dot(vnat[h, n], x, preferred_element_type=F32) for (h, sl, late, n, offset), x in zip(todo, do)]
+        weights = [
+            jnp.exp2(jnp.where(diff <= offset, s * c - stat[h, sl][late, 0:1], -jnp.inf))
+            for (h, sl, late, n, offset), s in zip(todo, scores)
+        ]
+        low = [(p * (g - stat[h, sl][late, 1:2])).astype(BF) for (h, sl, late, n, offset), p, g in zip(todo, weights, grads)]
+        dv = [lax.dot_general(x, p.astype(BF), NT, preferred_element_type=F32) for x, p in zip(do, weights)]
+        dk = [lax.dot_general(x, ds, NT, preferred_element_type=F32) for x, ds in zip(q, low)]
+        dq = [jnp.dot(ktr[h, n], ds, preferred_element_type=F32) for (h, sl, late, n, offset), ds in zip(todo, low)]
+        for (h, sl, late, n, offset), a, b, d in zip(todo, dv, dk, dq):
+            dv_s[h, sl][n] += a
+            dk_s[h, sl][n] += b
+            dq_s[h, sl][late] += d
         return 0
 
     lax.fori_loop(0, nb + 1, step, 0)
-    for qi in range(nq):
-        lanes = slice(128 * qi, 128 * (qi + 1))
-        cos, sin = cos_ref[:, lanes], sin_ref[:, lanes]
-        for h in range(2):
-            a = dq_s[qi, 0:48, 128 * h:128 * (h + 1)] * scale
-            b = dq_s[qi, 48:96, 128 * h:128 * (h + 1)] * scale
-            dq_ref[96 * h:96 * h + 48, lanes] = (a * cos + b * sin).astype(jnp.bfloat16)
-            dq_ref[96 * h + 48:96 * h + 96, lanes] = (b * cos - a * sin).astype(jnp.bfloat16)
-    for r in range(nchip):
-        for j in range(nq):
-            n = r * nq + j
-            dk = dk_s[0, n]
-            dv = dv_s[0, n]
-            for sl in range(1, nsl):
-                dk = dk + dk_s[sl, n]
-                dv = dv + dv_s[sl, n]
-            dk_refs[r][:, 128 * j:128 * (j + 1)] = (dk * scale).astype(jnp.bfloat16)
-            dv_refs[r][:, 128 * j:128 * (j + 1)] = dv.astype(jnp.bfloat16)
+    for h, sl in chains:
+        for half in range(2):
+            lanes = slice(BLK * (2 * sl + half), BLK * (2 * sl + half + 1))
+            cos, sin = cos_ref[:, lanes], sin_ref[:, lanes]
+            for e in range(2):
+                a = dq_s[h, sl][half, 0:48, BLK * e:BLK * (e + 1)] * SCALE
+                b = dq_s[h, sl][half, 48:96, BLK * e:BLK * (e + 1)] * SCALE
+                at = 192 * h + 96 * e
+                dq_ref[at:at + 48, lanes] = (a * cos + b * sin).astype(BF)
+                dq_ref[at + 48:at + 96, lanes] = (b * cos - a * sin).astype(BF)
+    for h in range(heads):
+        for n in range(nb):
+            r, lanes = n // nq, slice(BLK * (n % nq), BLK * (n % nq + 1))
+            dk = sum(dk_s[h, sl][n] for sl in range(slices))
+            dv = sum(dv_s[h, sl][n] for sl in range(slices))
+            dk_refs[r][96 * h:96 * (h + 1), lanes] = (dk * SCALE).astype(BF)
+            dv_refs[r][96 * h:96 * (h + 1), lanes] = dv.astype(BF)
 
 
 def attn_bwd(ids, inv, qT, oT, doT, lse, cosine, sine, ks, vs, heads):
     nchip = len(ks)
     T = qT.shape[1]
-    nq = T // 128
+    nq = T // BLK
     nb = nchip * nq
-    wide = pl.BlockSpec((192, T), lambda g, *_: (g, 0))
-    slim = pl.BlockSpec((96, T), lambda g, *_: (g, 0))
+    per = 4 if nb <= 16 else 2
+    wide = pl.BlockSpec((192 * per, T), lambda g, *_: (g, 0))
+    slim = pl.BlockSpec((96 * per, T), lambda g, *_: (g, 0))
+    chain = [
+        pltpu.VMEM((2, 96, 2 * BLK), BF),
+        pltpu.VMEM((2, 96, 2 * BLK), BF),
+        pltpu.VMEM((2, 2, 2 * BLK), F32),
+        pltpu.VMEM((2, 96, 2 * BLK), F32),
+        pltpu.VMEM((nb, 96, BLK), F32),
+        pltpu.VMEM((nb, 96, BLK), F32),
+    ]
     grid_spec = pltpu.PrefetchScalarGridSpec(
         num_scalar_prefetch=2,
-        grid=(heads,),
-        in_specs=[wide, wide, wide, pl.BlockSpec((None, nq, 1, 256), lambda g, *_: (g, 0, 0, 0))]
+        grid=(heads // per,),
+        in_specs=[wide, wide, wide, pl.BlockSpec((per, nq, 1, 2 * BLK), lambda g, *_: (g, 0, 0, 0))]
         + [pl.BlockSpec((48, T), lambda g, *_: (0, 0))] * 2 + [slim] * (2 * nchip),
         out_specs=[wide] + [slim] * (2 * nchip),
-        scratch_shapes=[
-            pltpu.VMEM((nb, 128, 96), jnp.bfloat16),
-            pltpu.VMEM((nb, 96, 128), jnp.bfloat16),
-            pltpu.VMEM((nb, 128, 96), jnp.bfloat16),
-            pltpu.VMEM((nq, 96, 256), jnp.bfloat16),
-            pltpu.VMEM((nq, 96, 256), jnp.bfloat16),
-            pltpu.VMEM((nq, 1, 256), jnp.float32),
-            pltpu.VMEM((nq, 96, 256), jnp.float32),
-            pltpu.VMEM((nq // 2, nb, 96, 128), jnp.float32),
-            pltpu.VMEM((nq // 2, nb, 96, 128), jnp.float32),
-        ],
+        scratch_shapes=[pltpu.VMEM((per, nb, BLK, 96), BF), pltpu.VMEM((per, nb, 96, BLK), BF), pltpu.VMEM((per, nb, BLK, 96), BF)]
+        + chain * (per * nq // 2),
     )
-    slab = jax.ShapeDtypeStruct((heads * 96, T), jnp.bfloat16)
+    slab = jax.ShapeDtypeStruct((heads * 96, T), BF)
     outs = pl.pallas_call(
-        functools.partial(bwd_kernel, nchip, SCALE),
+        functools.partial(bwd_kernel, nchip, per),
         grid_spec=grid_spec,
-        out_shape=[jax.ShapeDtypeStruct((heads * 192, T), jnp.bfloat16)] + [slab] * (2 * nchip),
-        cost_estimate=pl.CostEstimate(flops=90 * 10**9, bytes_accessed=24 * 2**20, transcendentals=0),
+        out_shape=[jax.ShapeDtypeStruct((heads * 192, T), BF)] + [slab] * (2 * nchip),
+        cost_estimate=pl.CostEstimate(flops=ATT_COST * 10**9, bytes_accessed=24 * 2**20, transcendentals=0),
+        compiler_params=pltpu.CompilerParams(vmem_limit_bytes=48 * 2**20),
         name="attention_backward",
     )(ids, inv, qT, oT, doT, lse, cosine, sine, *ks, *vs)
     return outs[0], outs[1:1 + nchip], outs[1 + nchip:]
 
 
+def pack_width(rows, fine, zsize, width):
+    return 2 * fine * zsize + width * fine // rows
+
+
 def front_kernel(zsize, *refs):
     (tok, gains, key_w, value_w, query_w, out_w, gate_w, up_w, down_w, cos, sin) = refs[:11]
-    (full_kv, full_q, full_o, wide, tall, far_wide, far_tall, x_out, first, q_out, gains_out, k0, k1, k2, k3, v0, v1, v2, v3) = refs[11:30]
-    x_s, gain_s, kv_w, q_w, kv_s, ss, rs, ls, gs, gr = refs[30:]
+    (full_kv, full_q, full_o, pack, far_pack, x_out, first, q_out, gains_out, k0, k1, k2, k3, v0, v1, v2, v3) = refs[11:28]
+    x_s, gain_s, kv_w, q_w, kv_s, ss, rs, ls, gs, gr = refs[28:]
     ks, vs = (k0, k1, k2, k3), (v0, v1, v2, v3)
     index, depth = lax.axis_index("ctx"), lax.axis_index("fsdp")
     chip, core = index // 2, lax.rem(index, 2)
-    fine = tall.shape[1]
+    fine = down_w.shape[0] // 8
     chunk = fine * zsize
+    folds = pack.shape[1] // fine
+    fold = first.shape[1] // folds
     width = first.shape[1]
     length = first.shape[0]
     kv_rows = k0.shape[0]
@@ -295,16 +336,19 @@
     ring_step("kv", 1)
     gain_step(1)
     own_late = [local(query_w, full_q.at[depth]), local(out_w, full_o.at[depth])]
-    own_ffn = [local(down_w.at[pl.ds(pl.multiple_of(core * (4 * fine) + chip * fine, fine), fine)], tall.at[depth])]
-    for part in range(zsize):
-        column = pl.multiple_of(part * (8 * fine) + core * (4 * fine) + chip * fine, fine)
-        own_ffn.append(local(gate_w.at[:, pl.ds(column, fine)], wide.at[depth, :, pl.ds(part * fine, fine)]))
-        own_ffn.append(local(up_w.at[:, pl.ds(column, fine)], wide.at[depth, :, pl.ds(chunk + part * fine, fine)]))
-    far_ffn = [local(down_w.at[pl.ds(pl.multiple_of(core * (4 * fine) + chip_d * fine, fine), fine)], far_tall)]
-    for part in range(zsize):
-        column = pl.multiple_of(part * (8 * fine) + core * (4 * fine) + chip_d * fine, fine)
-        far_ffn.append(local(gate_w.at[:, pl.ds(column, fine)], far_wide.at[:, pl.ds(part * fine, fine)]))
-        far_ffn.append(local(up_w.at[:, pl.ds(column, fine)], far_wide.at[:, pl.ds(chunk + part * fine, fine)]))
+    def cut_pack(which, target):
+        copies = []
+        for part in range(zsize):
+            column = pl.multiple_of(part * (8 * fine) + core * (4 * fine) + which * fine, fine)
+            copies.append(local(gate_w.at[:, pl.ds(column, fine)], target.at[:, pl.ds(part * fine, fine)]))
+            copies.append(local(up_w.at[:, pl.ds(column, fine)], target.at[:, pl.ds(chunk + part * fine, fine)]))
+        row = pl.multiple_of(core * (4 * fine) + which * fine, fine)
+        for n in range(folds):
+            copies.append(local(down_w.at[pl.ds(row, fine), pl.ds(n * fold, fold)], target.at[pl.ds(n * fine, fine), pl.ds(2 * chunk, fold)]))
+        return copies
+
+    own_ffn = cut_pack(chip, pack.at[depth])
+    far_ffn = cut_pack(chip_d, far_pack)
 
     for s in steps:
         moves["kv", "ring", s].wait_recv()
@@ -385,8 +429,8 @@
         copy.wait()
 
     def ffn_step(s):
-        a, b = wide.at[slot(s - 1)], tall.at[slot(s - 1)]
-        moves["ffn", s] = (send(a, a, to_next), send(b, b, to_next))
+        a = pack.at[slot(s - 1)]
+        moves["ffn", s] = send(a, a, to_next)
 
     ffn_step(1)
     for s in steps:
@@ -413,8 +457,7 @@
     v_y.wait_recv()
     v_d = send(v2, v3, to_x)
     for s in steps:
-        for copy in moves["ffn", s]:
-            copy.wait_recv()
+        moves["ffn", s].wait_recv()
         if s < last:
             ffn_step(s + 1)
     for s in steps:
@@ -433,29 +476,27 @@
     rows = width // zsize
     strip = rows // ctx
     fine = down_w.shape[0] // ctx
-    chunk = fine * zsize
+    packed = pack_width(rows, fine, zsize, width)
     kv_rows = key_w.shape[1]
     chips = ctx // 2
     cut = lambda w: w.reshape(chips, 2, strip, w.shape[1])
     square = jax.ShapeDtypeStruct((zsize, chips, 2, strip, width), BF)
     flat = jax.ShapeDtypeStruct((kv_rows, length), BF)
     hbm, vmem = pl.BlockSpec(memory_space=pl.ANY), pl.BlockSpec(memory_space=pltpu.VMEM)
-    copies = 18 * (zsize - 1) + 2 * (zsize - 1) + 8
+    copies = 19 * (zsize - 1) + 8
     return pl.pallas_call(
         functools.partial(front_kernel, zsize),
         out_shape=[
             square, square, square,
-            jax.ShapeDtypeStruct((zsize, rows, 2 * chunk), BF),
-            jax.ShapeDtypeStruct((zsize, fine, width), BF),
-            jax.ShapeDtypeStruct((rows, 2 * chunk), BF),
-            jax.ShapeDtypeStruct((fine, width), BF),
+            jax.ShapeDtypeStruct((zsize, rows, packed), BF),
+            jax.ShapeDtypeStruct((rows, packed), BF),
             jax.ShapeDtypeStruct((length, width), BF),
             jax.ShapeDtypeStruct((length, width), BF),
             jax.ShapeDtypeStruct((width, length), BF),
             jax.ShapeDtypeStruct((2, width), F32),
         ] + [flat] * 8,
         in_specs=[vmem, vmem] + [hbm] * 7 + [vmem] * 2,
-        out_specs=[hbm] * 7 + [vmem] * 4 + [hbm] * 8,
+        out_specs=[hbm] * 5 + [vmem] * 4 + [hbm] * 8,
         scratch_shapes=[
             pltpu.VMEM((2, length // 2, width), BF),
             pltpu.VMEM((zsize, 2, rows), F32),
@@ -464,7 +505,7 @@
             pltpu.VMEM((2 * kv_rows, length), BF),
             pltpu.SemaphoreType.DMA((copies,)),
             pltpu.SemaphoreType.DMA((copies,)),
-            pltpu.SemaphoreType.DMA((10 + 4 * zsize,)),
+            pltpu.SemaphoreType.DMA((8 + 4 * zsize + 2 * (rows // fine),)),
             pltpu.SemaphoreType.DMA((zsize,)),
             pltpu.SemaphoreType.DMA((zsize,)),
         ],
@@ -476,12 +517,11 @@
 def tail_kernel(zsize, *refs):
     dk, dv = refs[0:4], refs[4:8]
     dq, cos, sin, first_half, out_grad = refs[8:13]
-    wide_in, tall_in = refs[13:16], refs[16:19]
-    far_wide_in, far_tall_in = refs[19:19 + zsize], refs[19 + zsize:19 + 2 * zsize]
-    rest = refs[19 + 2 * zsize:]
-    o_all, q_all, kv_all, wide_all, tall_all, kv_low = rest[:6]
-    (got, held, dq_pair, kv_pair, half, grads, gl, gr, gx, gy, gz, piece, wide_s, tall_s, wide_0, tall_0, wide_z, tall_z,
-     wide_f, tall_f, wide_r, tall_r, wide_p, tall_p, ss, rs, ls) = rest[6:]
+    pack_in, far_in = refs[13:16], refs[16:16 + zsize]
+    rest = refs[16 + zsize:]
+    o_all, q_all, kv_all, pack_all, kv_low = rest[:5]
+    (got, held, dq_pair, kv_pair, half, grads, gl, gr, gx, gy, gz, piece,
+     pack_s, pack_0, pack_z, far_s, far_r, pack_p, ss, rs, ls) = rest[5:]
     index, depth = lax.axis_index("ctx"), lax.axis_index("fsdp")
     chip, core = index // 2, lax.rem(index, 2)
     chip_x, chip_y, chip_d = chip + 1 - 2 * lax.rem(chip, 2), lax.rem(chip + 2, 4), 3 - chip
@@ -545,18 +585,17 @@
     k3, v3 = send(dk[3], got.at[0], to_y), send(dv[3], got.at[1], to_x)
     q_swap = send(dq, dq_pair.at[1], to_core)
 
+    part = pack_0.shape[0] // 2
+    parts = [pl.ds(h * part, part) for h in range(2)]
+
     def load_ffn(j):
-        slot = lax.rem(j, 2) if not isinstance(j, int) else j % 2
-        return [local(wide_in[n].at[place_at(j)], wide_s.at[slot, n]) for n in range(3)] + [
-            local(tall_in[n].at[place_at(j)], tall_s.at[slot, n]) for n in range(3)]
+        return [local(pack_in[n].at[place_at(j)], pack_s.at[j % 2, n]) for n in range(3)]
 
     ffn_loads = {0: load_ffn(0)}
     load_o = local(out_grad, grads.at[0])
     load_q = [local(dq, dq_pair.at[0]), local(first_half, half)]
     load_kv = [local(dk[0], held.at[0]), local(dk[1], held.at[1]), local(dv[0], held.at[2]), local(dv[2], held.at[3])]
-    load_far = [local(far_wide_in[0].at[depth], wide_f.at[0]), local(far_tall_in[0].at[depth], tall_f.at[0])]
-    for n in range(1, zsize):
-        load_far += [local(far_wide_in[n], wide_f.at[n]), local(far_tall_in[n], tall_f.at[n])]
+    load_far = [local(far_in[n], far_s.at[n]) for n in range(zsize)]
 
     moves = {}
 
@@ -564,21 +603,17 @@
         if j + 1 <= last:
             ffn_loads[j + 1] = load_ffn(j + 1)
         wait_all(ffn_loads[j])
-        w = [wide_s.at[j % 2, n] for n in range(3)]
-        t = [tall_s.at[j % 2, n] for n in range(3)]
-        if j == 0:
-            sum_rows(wide_0, w, 64)
-            sum_rows(tall_0, t, 64)
-            moves["wide", 0], moves["tall", 0] = send(wide_0, wide_z.at[0], to_next), send(tall_0, tall_z.at[0], to_next)
-            return
-        received(moves["tall", j - 1])
-        add_rows(tall_z.at[j - 1], t, 64)
-        if j < last:
-            moves["tall", j] = send(tall_z.at[j - 1], tall_z.at[j], to_next)
-        received(moves["wide", j - 1])
-        add_rows(wide_z.at[j - 1], w, 64)
-        if j < last:
-            moves["wide", j] = send(wide_z.at[j - 1], wide_z.at[j], to_next)
+        for h in range(2):
+            mine = [pack_s.at[j % 2, n, parts[h]] for n in range(3)]
+            if j == 0:
+                sum_rows(pack_0.at[parts[h]], mine, 64)
+                moves["pack", h, 0] = send(pack_0.at[parts[h]], pack_z.at[0, parts[h]], to_next)
+                continue
+            received(moves["pack", h, j - 1])
+            here = pack_z.at[j - 1, parts[h]]
+            add_rows(here, mine, 64)
+            if j < last:
+                moves["pack", h, j] = send(here, pack_z.at[j, parts[h]], to_next)
 
     def sum_rows(target, sources, block):
         def one(t, _):
@@ -636,23 +671,34 @@
             piece[m] = total.astype(BF)
 
     def spread(name, source, target):
-        kept.append(local(source, target.at[chip, core]))
-        moves[name, "x"] = send(source, target.at[chip, core], to_x)
-        moves[name, "y"] = send(source, target.at[chip, core], to_y)
+        kept.append(local(source, target(chip, core)))
+        moves[name, "x"] = send(source, target(chip, core), to_x)
+        moves[name, "y"] = send(source, target(chip, core), to_y)
 
     def forward(name, target):
-        middle = target.shape[3] // 2
         received(moves[name, "x"])
-        left = target.at[chip_x, core, :, pl.ds(0, middle)]
+        left = target(chip_x, core, pl.ds(0, mid))
         moves[name, "fy"] = send(left, left, to_y)
         received(moves[name, "y"])
-        right = target.at[chip_y, core, :, pl.ds(middle, middle)]
+        right = target(chip_y, core, pl.ds(mid, mid))
         moves[name, "fx"] = send(right, right, to_x)
 
     def cross(name, target):
         received(moves[name, "fx"], moves[name, "fy"])
-        column = target.at[:, core]
+        column = target(slice(None), core)
         moves[name, "core"] = send(column, column, to_core)
+
+    def whole(ref):
+        def at(p, c, cols=None):
+            return ref.at[p, c] if cols is None else ref.at[p, c, :, cols]
+
+        return at
+
+    def half_rows(ref, h):
+        def at(p, c, cols=None):
+            return ref.at[p, c, parts[h]] if cols is None else ref.at[p, c, parts[h], cols]
+
+        return at
 
     def product(m, pair):
         per = width // tiles
@@ -710,9 +756,8 @@
     if last > 2:
         ffn_step(2)
     wait_all(load_far)
-    add_rows(wide_f.at[0], [wide_f.at[n] for n in range(1, zsize)], 64)
-    add_rows(tall_f.at[0], [tall_f.at[n] for n in range(1, zsize)], 64)
-    far = send(wide_f.at[0], wide_r, to_far), send(tall_f.at[0], tall_r, to_far)
+    add_rows(far_s.at[0], [far_s.at[n] for n in range(1, zsize)], 64)
+    far = send(far_s.at[0], far_r, to_far)
     received(kv_swap)
     product(2, kv_pair)
     stage_1(2)
@@ -722,33 +767,22 @@
     for j in range(3, last):
         ffn_step(j)
     ffn_step(last)
-    received(*far)
-
-    def whole_wide(t, _):
-        part = pl.ds(pl.multiple_of(t * 64, 64), 64)
-        wide_p[part] = (wide_z[last - 1, part].astype(F32) + wide_r[part].astype(F32)).astype(BF)
-        return 0
-
-    def whole_tall(t, _):
-        part = pl.ds(pl.multiple_of(t * 64, 64), 64)
-        tall_p[part] = (tall_z[last - 1, part].astype(F32) + tall_r[part].astype(F32)).astype(BF)
-        return 0
-
-    lax.fori_loop(0, tall_p.shape[0] // 64, whole_tall, 0)
-    spread("tall", tall_p, tall_all)
-    lax.fori_loop(0, wide_p.shape[0] // 64, whole_wide, 0)
-    spread("wide", wide_p, wide_all)
+    received(far)
+    for h in range(2):
+        sum_rows(pack_p.at[parts[h]], [pack_z.at[last - 1, parts[h]], far_r.at[parts[h]]], 64)
+        spread(("pack", h), pack_p.at[parts[h]], half_rows(pack_all, h))
     for j in range(1, zsize):
         ring_step(0, j)
         ring_step(1, j)
         if j == 1:
             stage_3(2)
-    spread(0, piece.at[0], o_all)
-    spread(1, piece.at[1], q_all)
+    spread(0, piece.at[0], whole(o_all))
+    spread(1, piece.at[1], whole(q_all))
     for j in range(1, zsize):
         ring_step(2, j)
-    spread(2, piece.at[2], kv_all)
-    targets = (("tall", tall_all), ("wide", wide_all), (0, o_all), (1, q_all), (2, kv_all))
+    spread(2, piece.at[2], whole(kv_all))
+    targets = [(("pack", h), half_rows(pack_all, h)) for h in range(2)]
+    targets += [(m, whole(ref)) for m, ref in enumerate((o_all, q_all, kv_all))]
     for name, target in targets:
         forward(name, target)
     wait_all(kept)
@@ -760,40 +794,277 @@
         copy.wait_send()
 
 
-def tail(dk, dv, dq, cosine, sine, first_half, out_grad, wide, tall, far_wide, far_tall, zsize, chips):
+def tail(dk, dv, dq, cosine, sine, first_half, out_grad, packs, far_packs, zsize, chips):
     kv_rows, length = dk[0].shape
     width = 2 * kv_rows
     strip = out_grad.shape[2]
-    rows, two = wide[0].shape[1:]
-    fine = tall[0].shape[1]
+    rows, packed = packs[0].shape[1:]
     hbm, vmem = pl.BlockSpec(memory_space=pl.ANY), pl.BlockSpec(memory_space=pltpu.VMEM)
     shape = lambda *s: jax.ShapeDtypeStruct(s, BF)
     store = lambda *s: pltpu.VMEM(s, BF)
-    copies = 6 + 2 + 1 + 2 * (zsize - 1) + 3 * (4 + zsize - 1) + 5 * 5 + 2
-    inputs = [*dk, *dv, dq, cosine, sine, first_half, out_grad, *wide, *tall, *far_wide, *far_tall]
+    copies = 9 + 2 * (zsize - 1) + 3 * (4 + zsize - 1) + 5 * 5
+    inputs = [*dk, *dv, dq, cosine, sine, first_half, out_grad, *packs, *far_packs]
     last = zsize - 1
     return pl.pallas_call(
         functools.partial(tail_kernel, zsize),
-        out_shape=[shape(chips, 2, strip, width)] * 3 + [shape(chips, 2, rows, two), shape(chips, 2, fine, width), shape(width, length)],
+        out_shape=[shape(chips, 2, strip, width)] * 3 + [shape(chips, 2, rows, packed), shape(width, length)],
         in_specs=[hbm] * 9 + [vmem] * 2 + [hbm] * (len(inputs) - 11),
-        out_specs=[hbm] * 6,
+        out_specs=[hbm] * 5,
         scratch_shapes=[
             store(6, kv_rows, length), store(4, kv_rows, length), store(2, width, length), store(2, width, length),
             store(width // 2, 2 * length), store(3, zsize, chips, strip, width),
             store(3, zsize, strip, width // 2), store(3, zsize, strip, width // 2),
             store(3, zsize, strip, width), store(3, zsize, strip, width),
             store(3, last, strip, width), store(3, strip, width),
-            store(2, 3, rows, two), store(2, 3, fine, width), store(rows, two), store(fine, width),
-            store(last, rows, two), store(last, fine, width),
-            store(zsize, rows, two), store(zsize, fine, width), store(rows, two), store(fine, width), store(rows, two), store(fine, width),
+            store(2, 3, rows, packed), store(rows, packed), store(last, rows, packed),
+            store(zsize, rows, packed), store(rows, packed), store(rows, packed),
             pltpu.SemaphoreType.DMA((copies,)), pltpu.SemaphoreType.DMA((copies,)),
-            pltpu.SemaphoreType.DMA((6 * zsize + 8 + 2 * zsize + 6,)),
+            pltpu.SemaphoreType.DMA((4 * zsize + 13,)),
         ],
         compiler_params=pltpu.CompilerParams(collective_id=1, has_side_effects=True, vmem_limit_bytes=60 * 2**20),
         name="tail",
     )(*inputs)
 
 
+def unfold(refs, wide, tall, start):
+    zsize, fine = tall.shape[0], tall.shape[1]
+    folds = wide.shape[1] // fine
+    fold = tall.shape[2] // folds
+    two = wide.shape[2]
+    whole = len(refs) == 1
+    depth = 0 if whole else lax.axis_index("fsdp")
+    for s in range(1 if whole else zsize):
+        at = slice(None) if whole else lax.rem(depth + zsize - s, zsize)
+        lead = (slice(None),) if whole else ()
+        start(refs[s].at[(*lead, slice(None), pl.ds(0, two))], wide.at[at])
+        for n in range(folds):
+            cols = pl.ds(n * fold, fold)
+            start(refs[s].at[(*lead, pl.ds(n * fine, fine), pl.ds(two, fold))], tall.at[at, :, cols])
+
+
+def ffn_kernel(pieces, second, second_t, cot, *refs):
+    weights, (hidden_o, low_o), grads = refs[:pieces], refs[pieces:pieces + 2], refs[pieces + 2:2 * pieces + 2]
+    s_v, st_v, c_v, wi_v, wo_v, h_v, ht_v, l_v, w_v, t_v, sem = refs[2 * pieces + 2:]
+    tokens, width = second.shape
+    zsize, fine = wo_v.shape[:2]
+    rows = wi_v.shape[1]
+    chunk = zsize * fine
+    loads = []
+
+    def load(src, dst):
+        copy = pltpu.make_async_copy(src, dst, sem.at[len(loads)])
+        copy.start()
+        loads.append(copy)
+
+    unfold(weights, wi_v, wo_v, load)
+    load(second, s_v)
+    load(cot, c_v)
+    load(second_t, st_v)
+    for copy in loads[:-1]:
+        copy.wait()
+    nt = (((1,), (1,)), ((), ()))
+    tile = 256
+
+    def one(t, _):
+        part = pl.ds(pl.multiple_of(t * tile, tile), tile)
+        pre = jnp.dot(s_v[part], wi_v[...].reshape(width, 2 * chunk), preferred_element_type=F32)
+        hidden_grad = lax.dot_general(c_v[part], wo_v[...].reshape(chunk, width), nt, preferred_element_type=F32)
+        gate, up = pre[:, :chunk], pre[:, chunk:]
+        sigmoid = jax.nn.sigmoid(gate)
+        silu = gate * sigmoid
+        hidden = silu * up
+        h_v[part] = hidden.astype(BF)
+        ht_v[:, part] = hidden.T.astype(BF)
+        l_v[part, 0:chunk] = (hidden_grad * up * sigmoid * (1.0 + gate * (1.0 - sigmoid))).astype(BF)
+        l_v[part, chunk:] = (hidden_grad * silu).astype(BF)
+        return 0
+
+    lax.fori_loop(0, tokens // tile, one, 0)
+    stores = []
+
+    def store(src, dst):
+        copy = pltpu.make_async_copy(src, dst, sem.at[len(loads) + len(stores)])
+        copy.start()
+        stores.append(copy)
+
+    store(h_v, hidden_o)
+    store(l_v, low_o)
+    loads[-1].wait()
+    depth = 0 if pieces == 1 else lax.axis_index("fsdp")
+    grad_at = lambda n: grads[0].at[n] if pieces == 1 else grads[n]
+
+    def place(n):
+        return n if pieces == 1 else lax.rem(depth + n, zsize)
+
+    for n in range(zsize):
+        z = place(n)
+        part = pl.ds(pl.multiple_of(z * rows, rows), rows)
+        w_v[z] = jnp.dot(st_v[part], l_v[...], preferred_element_type=F32).astype(BF)
+        store(w_v.at[z], grad_at(n).at[:, pl.ds(0, 2 * chunk)])
+    folds = rows // fine
+    fold = width // folds
+    for n in range(folds):
+        cols = slice(fold * n, fold * (n + 1))
+        t_v[:, :, cols] = jnp.dot(ht_v[...], c_v[:, cols], preferred_element_type=F32).astype(BF).reshape(zsize, fine, fold)
+        if pieces == 1:
+            store(t_v.at[:, :, cols], grads[0].at[:, pl.ds(n * fine, fine), pl.ds(2 * chunk, fold)])
+        else:
+            for k in range(zsize):
+                store(t_v.at[place(k), :, cols], grads[k].at[pl.ds(n * fine, fine), pl.ds(2 * chunk, fold)])
+    for copy in stores:
+        copy.wait()
+
+
+def ffn_chunk(second, second_t, cot, weights, zsize, fine):
+    pieces = len(weights)
+    tokens, width = second.shape
+    chunk = zsize * fine
+    rows = width // zsize
+    folds = rows // fine
+    shape = lambda *s: jax.ShapeDtypeStruct(s, BF)
+    store = lambda *s: pltpu.VMEM(s, BF)
+    hbm = pl.BlockSpec(memory_space=pl.ANY)
+    out = pl.pallas_call(
+        functools.partial(ffn_kernel, pieces),
+        out_shape=[shape(tokens, chunk), shape(tokens, 2 * chunk)] + [shape(*w.shape) for w in weights],
+        in_specs=[hbm] * (3 + pieces),
+        out_specs=[hbm] * (2 + pieces),
+        scratch_shapes=[
+            store(tokens, width), store(width, tokens), store(tokens, width), store(zsize, rows, 2 * chunk), store(zsize, fine, width),
+            store(tokens, chunk), store(chunk, tokens), store(tokens, 2 * chunk), store(zsize, rows, 2 * chunk), store(zsize, fine, width),
+            pltpu.SemaphoreType.DMA((5 + zsize + pieces * (2 * folds + 1),)),
+        ],
+        cost_estimate=pl.CostEstimate(flops=16 * 10**9, bytes_accessed=24 * 2**20, transcendentals=0),
+        compiler_params=pltpu.CompilerParams(vmem_limit_bytes=50 * 2**20),
+        name="ffn_chunk",
+    )(second, second_t, cot, *weights)
+    return out[0], out[1], out[2:]
+
+def combine_kernel(counts, *refs):
+    count = len(counts)
+    hidden, low = refs[:count], refs[count:2 * count]
+    weights, at = [], 2 * count
+    for n in counts:
+        weights.append(refs[at:at + n])
+        at += n
+    out, grad, h_v, l_v, wi_v, wo_v, o_v, g_v, sem = refs[at:]
+    tokens, chunk = hidden[0].shape
+    width = out.shape[1]
+    loads = []
+
+    def load(src, dst):
+        copy = pltpu.make_async_copy(src, dst, sem.at[len(loads)])
+        copy.start()
+        loads.append(copy)
+
+    for r in range(count):
+        load(hidden[r], h_v.at[:, pl.ds(r * chunk, chunk)])
+        unfold(weights[r], wi_v.at[:, :, pl.ds(2 * r * chunk, 2 * chunk)], wo_v.at[r], load)
+    for r in range(count):
+        load(low[r], l_v.at[:, pl.ds(2 * r * chunk, 2 * chunk)])
+    nt = (((1,), (1,)), ((), ()))
+    tile = 256
+    steps = tokens // tile
+    stores = []
+
+    def store(src, dst):
+        copy = pltpu.make_async_copy(src, dst, sem.at[len(loads) + len(stores)])
+        copy.start()
+        stores.append(copy)
+
+    for copy in loads[:-count]:
+        copy.wait()
+    for t in range(steps):
+        rows = slice(tile * t, tile * (t + 1))
+        if t >= 2:
+            stores[t - 2].wait()
+        o_v[t % 2] = jnp.dot(h_v[rows], wo_v[...].reshape(count * chunk, width), preferred_element_type=F32)
+        store(o_v.at[t % 2], out.at[rows])
+    for copy in loads[-count:]:
+        copy.wait()
+    for t in range(steps):
+        rows = slice(tile * t, tile * (t + 1))
+        if t >= 2:
+            stores[steps + t - 2].wait()
+        g_v[t % 2] = lax.dot_general(l_v[rows], wi_v[...].reshape(width, 2 * count * chunk), nt, preferred_element_type=F32)
+        store(g_v.at[t % 2], grad.at[rows])
+    for t in range(max(steps - 2, 0), steps):
+        stores[t].wait()
+        stores[steps + t].wait()
+
+
+def combine(hidden, low, weights, zsize, fine):
+    counts = tuple(len(w) for w in weights)
+    count = len(counts)
+    tokens, chunk = hidden[0].shape
+    rows = weights[0][0].shape[-2]
+    width = rows * zsize
+    hbm = pl.BlockSpec(memory_space=pl.ANY)
+    shape = jax.ShapeDtypeStruct((tokens, width), F32)
+    inputs = [*hidden, *low] + [piece for w in weights for piece in w]
+    return pl.pallas_call(
+        functools.partial(combine_kernel, counts),
+        out_shape=[shape, shape],
+        in_specs=[hbm] * len(inputs),
+        out_specs=[hbm] * 2,
+        scratch_shapes=[
+            pltpu.VMEM((tokens, count * chunk), BF), pltpu.VMEM((tokens, 2 * count * chunk), BF),
+            pltpu.VMEM((zsize, rows, 2 * count * chunk), BF), pltpu.VMEM((count, zsize, fine, width), BF),
+            pltpu.VMEM((2, 256, width), F32), pltpu.VMEM((2, 256, width), F32),
+            pltpu.SemaphoreType.DMA((2 * count + sum(counts) * (1 + rows // fine) + 2 * (tokens // 256),)),
+        ],
+        cost_estimate=pl.CostEstimate(flops=26 * 10**9, bytes_accessed=48 * 2**20, transcendentals=0),
+        compiler_params=pltpu.CompilerParams(vmem_limit_bytes=56 * 2**20),
+        name="ffn_combine",
+    )(*inputs)
+
+
+def assemble_kernel(zsize, wide, tall, o, q, kv, gate_o, up_o, down_o, o_o, q_o, k_o, v_o):
+    fold = tall.shape[3]
+    folds = down_o.shape[1] // fold
+    fine = tall.shape[2] // folds
+    kv_rows = k_o.shape[1]
+    for p in range(4):
+        for c in range(2):
+            for part in range(zsize):
+                at = slice((part * 8 + c * 4 + p) * fine, (part * 8 + c * 4 + p + 1) * fine)
+                gate_o[:, at] = wide[p, c, :, part * fine:(part + 1) * fine].astype(F32)
+                up_o[:, at] = wide[p, c, :, (zsize + part) * fine:(zsize + part + 1) * fine].astype(F32)
+    for p in range(2):
+        for n in range(folds):
+            down_o[p * fine:(p + 1) * fine, n * fold:(n + 1) * fold] = tall[p, 0, n * fine:(n + 1) * fine].astype(F32)
+    o_o[...] = o[...].astype(F32)
+    q_o[...] = q[...].astype(F32)
+    k_o[...] = kv[:, 0:kv_rows].astype(F32)
+    v_o[...] = kv[:, kv_rows:].astype(F32)
+
+
+def assemble(packs, o, q, kv, zsize, fine):
+    chips, cores, rows, packed = packs.shape
+    width = o.shape[1]
+    steps = 4
+    block = rows // steps
+    two = 2 * fine * zsize
+    fold = packed - two
+    flat = lambda n: pl.BlockSpec((block, n), lambda i: (i, 0))
+    out = lambda r, c: jax.ShapeDtypeStruct((r, c), F32)
+    ff = fine * chips * cores
+    return pl.pallas_call(
+        functools.partial(assemble_kernel, zsize),
+        grid=(steps,),
+        out_shape=[out(rows, ff * zsize), out(rows, ff * zsize), out(ff, width), out(rows, width), out(rows, width), out(rows, width // 2), out(rows, width // 2)],
+        in_specs=[
+            pl.BlockSpec((chips, cores, block, two), lambda i: (0, 0, i, 0)),
+            pl.BlockSpec((2, 1, rows, fold), lambda i: (i % 2, i // 2, 0, two // fold)),
+            flat(width), flat(width), flat(width),
+        ],
+        out_specs=[flat(ff * zsize), flat(ff * zsize), pl.BlockSpec((ff // steps, width), lambda i: (i, 0)), flat(width), flat(width), flat(width // 2), flat(width // 2)],
+        cost_estimate=pl.CostEstimate(flops=0, bytes_accessed=39 * 2**20, transcendentals=0),
+        compiler_params=pltpu.CompilerParams(vmem_limit_bytes=40 * 2**20),
+        name="assemble",
+    )(packs, packs, o, q, kv)
+
+
 def mm(left, right, left_dim, right_dim):
     return lax.dot_general(left, right, (((left_dim,), (right_dim,)), ((), ())), preferred_element_type=F32)
 
@@ -817,6 +1088,11 @@
 
 def place(buffer, piece, index, axis=0):
     return lax.dynamic_update_slice_in_dim(buffer, jnp.expand_dims(piece, axis), index, axis)
+
+
+def shift(a, s):
+    n = lax.axis_size("fsdp")
+    return lax.ppermute(a, "fsdp", [(i, (i + s) % n) for i in range(n)])
 
 
 def depth_gather(piece, depth):
@@ -825,15 +1101,6 @@
     for s in range(1, n):
         piece = ring(piece)
         buffer = place(buffer, piece, lax.rem(depth + n - s, n))
-    return buffer
-
-
-def depth_gather_direct(piece, depth):
-    n = lax.axis_size("fsdp")
-    buffer = place(jnp.zeros((n,) + piece.shape, piece.dtype), piece, depth)
-    for s in range(1, n):
-        moved = lax.ppermute(piece, "fsdp", [(k, (k + s) % n) for k in range(n)])
-        buffer = place(buffer, moved, lax.rem(depth + n - s, n))
     return buffer
 
 
@@ -923,15 +1190,16 @@
     angles = frequency[:, None] * positions.astype(F32)[None, :]
     cosine, sine = jnp.cos(angles), jnp.sin(angles)
 
-    gate_up, down, keys, values = {}, {}, {}, {}
+    packs, keys, values = {}, {}, {}
+    folds = rows // fine
     fast = chips == 4 and strip % 16 == 0 and fine % 128 == 0
     if fast:
-        (key_value_full, query_full, output_full, wide, tall, far_wide, far_tall, x, first, query, gains_full, *kv) = front(
+        (key_value_full, query_full, output_full, pack, far_pack, x, first, query, gains_full, *kv) = front(
             tokens, jnp.stack([attention_gain, feedforward_gain]).astype(F32), key_matrix, value_matrix, query_weight,
             output_weight, gate_weight, up_weight, down_weight, cosine, sine, zsize, ctx,
         )
         key_value_full, query_full, output_full = (w.reshape(width, width) for w in (key_value_full, query_full, output_full))
-        gate_up[0], down[0] = wide.reshape(width, 2 * chunk), tall.reshape(chunk, width)
+        packs[0] = [pack]
         for r in range(chips):
             keys[r], values[r] = kv[r], kv[chips + r]
         x = x.astype(F32)
@@ -939,8 +1207,7 @@
         inverse_first = lax.rsqrt(jnp.mean(x * x, -1, keepdims=True) + EPS)
         unit_first = x * inverse_first
         first_t = jnp.transpose(first)
-        gate_up[diag] = depth_gather_direct(far_wide, depth).reshape(width, 2 * chunk)
-        down[diag] = depth_gather_direct(far_tall, depth).reshape(chunk, width)
+        packs[diag] = [far_pack] + [shift(far_pack, s) for s in range(1, zsize)]
     else:
         gate_cut = gate_weight.reshape(rows, zsize, 2, chips, fine)
         up_cut = up_weight.reshape(rows, zsize, 2, chips, fine)
@@ -950,7 +1217,8 @@
             gate = pick(pick(gate_cut, core, 2), chip ^ r, 2).reshape(rows, chunk)
             up = pick(pick(up_cut, core, 2), chip ^ r, 2).reshape(rows, chunk)
             down = pick(pick(down_cut, core), chip ^ r)
-            return jnp.concatenate([gate, up], 1), down
+            folded = jnp.transpose(down.reshape(fine, folds, width // folds), (1, 0, 2)).reshape(rows, width // folds)
+            return jnp.concatenate([gate, up, folded], 1)
 
         gains = jnp.stack([attention_gain, feedforward_gain])
         gain_buffer = place(jnp.zeros((zsize, 2, rows), BF), gains, depth)
@@ -979,9 +1247,7 @@
         output_full = gather_square(output_weight)
 
         x = jnp.concatenate([pick(tokens, core), swap(pick(tokens, 1 - core))]).astype(F32)
-        wide, tall = own_piece(0)
-        gate_up[0] = depth_gather(wide, depth).reshape(width, 2 * chunk)
-        down[0] = depth_gather(tall, depth).reshape(chunk, width)
+        packs[0] = [depth_gather(own_piece(0), depth)]
         inverse_first = lax.rsqrt(jnp.mean(x * x, -1, keepdims=True) + EPS)
         unit_first = x * inverse_first
         first = (unit_first * gain_first).astype(BF)
@@ -995,13 +1261,10 @@
             keys[r] = hop(keys[r ^ high], high)
             values[r] = hop(values[r ^ low], low)
         query = rotate(mm(query_full, first_t, 0, 0), cosine, sine).astype(BF)
-        wide, tall = own_piece(diag)
-        gate_up[diag] = depth_gather(wide, depth).reshape(width, 2 * chunk)
-        down[diag] = depth_gather(tall, depth).reshape(chunk, width)
+        packs[diag] = [depth_gather(own_piece(diag), depth)]
 
     for r in near:
-        gate_up[r] = hop(gate_up[0], r)
-        down[r] = hop(down[0], r)
+        packs[r] = [hop(packs[0][0], r)]
 
     key_list = [keys[r] for r in range(chips)]
     value_list = [values[r] for r in range(chips)]
@@ -1012,23 +1275,12 @@
     unit_second = middle * inverse_second
     second = (unit_second * gain_second).astype(BF)
     second = jnp.concatenate([second, swap(second)])
-    out_part = 0.0
-    second_grad = 0.0
-    wide_grad, tall_grad = {}, {}
+    second_t = jnp.transpose(second)
+    grads, hidden, low = {}, {}, {}
     for r in [0] + list(near) + [diag]:
-        pre = mm(second, gate_up[r], 1, 0)
-        gate_pre, up_pre = pre[:, :chunk], pre[:, chunk:]
-        hidden_grad = mm(cot, down[r], 1, 1)
-        sigmoid = jax.nn.sigmoid(gate_pre)
-        silu = gate_pre * sigmoid
-        hidden = (silu * up_pre).astype(BF)
-        gate_low = (hidden_grad * up_pre * sigmoid * (1.0 + gate_pre * (1.0 - sigmoid))).astype(BF)
-        up_low = (hidden_grad * silu).astype(BF)
-        both_low = jnp.concatenate([gate_low, up_low], 1)
-        tall_grad[r] = mm(hidden, cot, 0, 0).astype(BF)
-        wide_grad[r] = mm(second, both_low, 0, 0).astype(BF)
-        out_part = out_part + mm(hidden, down[r], 1, 0)
-        second_grad = second_grad + mm(both_low, gate_up[r], 1, 1)
+        hidden[r], low[r], grads[r] = ffn_chunk(second, second_t, cot, packs[r], zsize, fine)
+    every = range(chips)
+    out_part, second_grad = combine([hidden[r] for r in every], [low[r] for r in every], [packs[r] for r in every], zsize, fine)
 
     q = slice_len
     out_part = jnp.concatenate([out_part[:length] + middle, out_part[length:]])
@@ -1058,22 +1310,16 @@
     query_low, key_parts, value_parts = attn_bwd(
         ids, order, query, attended, attended_grad, log_total, cosine, sine, key_list, value_list, KEY_HEADS
     )
-    wide_cut = {r: wide_grad[r].reshape(zsize, rows, 2 * chunk) for r in range(chips)}
-    tall_cut = {r: tall_grad[r].reshape(zsize, fine, width) for r in range(chips)}
     if fast:
-        def shifted(parts):
-            return [parts] + [
-                lax.ppermute(pick(parts, lax.rem(depth + s, zsize)), "fsdp", [(k, (k + s) % zsize) for k in range(zsize)])
-                for s in range(1, zsize)
-            ]
-
-        o_all, q_all, kv_all, wide_all, tall_all, kv_low = tail(
+        o_all, q_all, kv_all, pack_all, kv_low = tail(
             key_parts, value_parts, query_low, cosine, sine, first_half,
             out_part_grad.astype(BF).reshape(zsize, chips, strip, width),
-            [wide_cut[0], hop(wide_cut[1], 1), hop(wide_cut[2], 2)], [tall_cut[0], hop(tall_cut[1], 1), hop(tall_cut[2], 2)],
-            shifted(wide_cut[diag]), shifted(tall_cut[diag]), zsize, chips,
+            [grads[0][0], hop(grads[1][0], 1), hop(grads[2][0], 2)],
+            [grads[diag][0]] + [shift(grads[diag][s], s) for s in range(1, zsize)], zsize, chips,
         )
-        output_grad, query_grad, kv_grad = (a.reshape(rows, width).astype(F32) for a in (o_all, q_all, kv_all))
+        gate_grad, up_grad, down_grad, output_grad, query_grad, key_grad, value_grad = assemble(
+            pack_all, *(a.reshape(rows, width) for a in (o_all, q_all, kv_all)), zsize, fine
+        )
     else:
         key_sum = [part for part in key_parts]
         value_sum = [part for part in value_parts]
@@ -1094,10 +1340,9 @@
             total = depth_scatter(total.astype(BF), depth) + far.astype(F32)
             return total.astype(BF)
 
-        tall_piece = scatter(tall_cut)
-        wide_piece = scatter(wide_cut)
-        tall_all = plane_gather(tall_piece, index)
-        wide_all = plane_gather(wide_piece, index)
+        pack_all = plane_gather(scatter({r: grads[r][0] for r in range(chips)}), index)
+        wide_all = pack_all[:, :, :2 * chunk]
+        tall_all = jnp.transpose(pack_all[:, :, 2 * chunk:].reshape(ctx, folds, fine, width // folds), (0, 2, 1, 3))
         def square_grad(product):
             parts = product.astype(BF).reshape(zsize, chips, strip, width)
             piece = scatter({r: pick(parts, chip ^ r, 1) for r in range(chips)})
@@ -1106,12 +1351,11 @@
         output_grad = square_grad(out_part_grad)
         query_grad = square_grad(mm(first_half, jnp.concatenate([query_low, swap(query_low)], 1), 1, 1))
         kv_grad = square_grad(mm(first_half, jnp.concatenate([kv_low, swap(kv_low)], 1), 1, 1))
-
-
-    down_grad = jnp.transpose(tall_all.reshape(chips, 2, fine, width), (1, 0, 2, 3)).reshape(hidden_rows, width).astype(F32)
-    wide_all = wide_all.reshape(chips, 2, rows, 2, zsize, fine)
-    gate_grad = jnp.transpose(wide_all[:, :, :, 0], (2, 3, 1, 0, 4)).reshape(rows, -1).astype(F32)
-    up_grad = jnp.transpose(wide_all[:, :, :, 1], (2, 3, 1, 0, 4)).reshape(rows, -1).astype(F32)
+        down_grad = jnp.transpose(tall_all.reshape(chips, 2, fine, width), (1, 0, 2, 3)).reshape(hidden_rows, width).astype(F32)
+        wide_all = wide_all.reshape(chips, 2, rows, 2, zsize, fine)
+        gate_grad = jnp.transpose(wide_all[:, :, :, 0], (2, 3, 1, 0, 4)).reshape(rows, -1).astype(F32)
+        up_grad = jnp.transpose(wide_all[:, :, :, 1], (2, 3, 1, 0, 4)).reshape(rows, -1).astype(F32)
+        key_grad, value_grad = kv_grad[:, :kv_rows], kv_grad[:, kv_rows:]
 
     first_grad = mm(query_low, query_full, 0, 1) + mm(kv_low, key_value_full, 0, 1)
     gain_first_part = jnp.sum(first_grad * unit_first, 0)
@@ -1137,8 +1381,8 @@
         tokens_grad,
         gain_total(gain_first_part),
         query_grad,
-        kv_grad[:, :kv_rows],
-        kv_grad[:, kv_rows:],
+        key_grad,
+        value_grad,
         output_grad,
         gain_total(gain_second_part),
         gate_grad,

time: 983 us -> 815 us (0.83)
  matrix products: 156 us -> 31.7 us
  local copies, waits for them, and re-layouts: 102 us -> 49.1 us
  Pallas kernels: 534 us -> 558 us
  waiting for transfers between devices: 96.6 us -> 83.7 us
    dot_general x29 -> x5, matrix products: 156 us -> 31.7 us  [mm(): lax.dot_general(left, right, (((left_dim,), (right_dim,)), ((), ())), pre...]
    convert_element_type x5 -> x0, local copies, waits for them, and re-layouts: 38.3 us -> none  [the longest x2 17.6 us: body(): jnp.transpose(wide_all[:, :, :, 1], (2, 3, 1, 0, 4)).reshape(rows, -1)]
    ppermute x12 -> x8, waiting for transfers between devices: 36.3 us -> 4.92 us  [hop(): lax.ppermute(a, 'ctx', [(i, i ^ 2 * r) for i in range(lax.axis_size('ctx'...]
    pallas_call x1, Pallas kernels: 203 us -> 220 us  [tail(): pl.pallas_call(functools.partial(tail_kernel, zsize), out_shape=[shape(ch...]
    ppermute x12 -> x6, waiting for transfers between devices: 59.2 us -> 76.3 us  [shift(): return lax.ppermute(a, 'fsdp', [(i, (i + s) % n) for i in range(n)])]
    convert_element_type x4 -> x0, other arithmetic: 14.4 us -> none  [the longest x1 6.39 us: body(): jnp.transpose(wide_all[:, :, :, 1], (2, 3, 1, 0, 4)).reshape(rows, -1)]
    reshape x1 -> x0, local copies, waits for them, and re-layouts: 11.2 us -> none  [body(): wide_all = wide_all.reshape(chips, 2, rows, 2, zsize, fine)]
    pallas_call x2 -> x8, Pallas kernels: 172 us -> 179 us  [the longest x4 67.3 us: ffn_chunk(): pl.pallas_call(functools.partial(ffn_kernel, pieces), out_shape=[shape(to...]
  transfers between devices with their start and end apart: 40 -> 30, of which waited for: 9 -> 11; matrix products, arithmetic and copies ran while one was open for 27% -> 9% of each run, Pallas kernels for 38% -> 40%
where the time goes in v4:
time: 815 us; the launch traced here: 808 us
  Pallas kernels  558 us (68%)
  waiting for transfers between devices  83.7 us (10%)
  starting transfers between devices  50 us (6%)
  local copies, waits for them, and re-layouts  49.1 us (6%)
  other arithmetic  33.4 us (4%)
  matrix products  31.7 us (4%)
    pallas_call x1, Pallas kernels, tail(): pl.pallas_call(functools.partial(tail_kernel, zsize), out_shape=[shape(ch...  220 us
    pallas_call x1, Pallas kernels, front(): pl.pallas_call(functools.partial(front_kernel, zsize), out_shape=[square,...  160 us
    ppermute x6, waiting for transfers between devices, shift(): return lax.ppermute(a, 'fsdp', [(i, (i + s) % n) for i in range(n)])  76.3 us
    pallas_call x4, Pallas kernels, ffn_chunk(): pl.pallas_call(functools.partial(ffn_kernel, pieces), out_shape=[shape(to...  67.3 us
    pallas_call x1, Pallas kernels, attn_bwd(): pl.pallas_call(functools.partial(bwd_kernel, nchip, per), grid_spec=grid_...  43.5 us
    ppermute x6, starting transfers between devices, shift(): return lax.ppermute(a, 'fsdp', [(i, (i + s) % n) for i in range(n)])  32.4 us
    dot_general x5, matrix products, mm(): lax.dot_general(left, right, (((left_dim,), (right_dim,)), ((), ())), pre...  31.7 us
    pallas_call x1, Pallas kernels, combine(): pl.pallas_call(functools.partial(combine_kernel, counts), out_shape=[shap...  29.9 us
  transfers between devices with their start and end apart: 30, of which 11 were waited for; matrix products, arithmetic and copies ran while one was open for 9% of the time, Pallas kernels for 40%

profile of v4, /device:TPU:0, one launch (start us, length us, event | category | flops | bytes accessed | tf_op | source)
XLA Modules:
  0.0 807.8 jit_solution(13461235489612737608)
XLA Ops:
  8.9 159.7 %front.1 = (bf16[4,4,2,48,1536]{4,3,2,1,0:T(8,128)(2,1)}, bf16[4,4,2,48,1536]{4,3,2,1,0:T(8,128)(2,1)}, bf16[4,4,2,48,1536]{4,3,2,1,0:T(8,128)(2,1)}, bf16[4,384...) custom-call(bf16[2,256,1536]{2,1,0:T(8,128)(2,1)} %refs_0_.1, ...), custom_call_target="tpu_custom_call" | custom-call | tf_op jit(solution)/shard_map/front/pallas_call | solution.py:487
  169.6 28.6 %attention_forward.1 = (bf16[1536,512]{1,0:T(8,128)(2,1)}, f32[8,4,1,256]{3,2,1,0:T(1,128)S(1)}) custom-call(s32[4]{0:T(128)S(1)} %get-tuple-element.150.ids_ref, s32[16]{0:T(128)S(1)} %select_reduce_fusion.inv_ref, bf16[1536,512]{1,0:T(8,128)(2,1)} %get-tuple-element.69.q_ref, bf16[768,512]{1,0:T(8,128)(2,1)S(1)} %get-tuple-element.70.rest_0_, ...), custom_call_target="tpu_custom_call" | custom-call | flops 8000000000 | bytes 16777216 | tf_op jit(solution)/shard_map/attention_forward/pallas_call | solution.py:117
  198.3 5.3 multiply_reduce_fusion.2
  205.3 1.5 multiply_convert_fusion
  208.9 4.2 collective-permute-start.5
  213.0 2.6 dynamic-slice_bitcast_fusion.3
  216.9 5.0 fusion.37
  221.9 4.7 copy.34.second_t
  227.2 1.5 dynamic-slice_bitcast_fusion.2
  228.7 2.0 pad_maximum_fusion.1.cot
  230.6 16.6 %ffn_chunk.4 = (bf16[1024,512]{1,0:T(8,128)(2,1)S(1)}, bf16[1024,1024]{1,0:T(8,128)(2,1)S(1)}, bf16[4,384,1536]{2,1,0:T(8,128)(2,1)}) custom-call(bf16[1024,1536]{1,0:T(8,128)(2,1)} %get-tuple-element.155.second, bf16[1536,1024]{1,0:T(8,128)(2,1)} %copy.34.second_t, bf16[1024,1536]{1,0:T(8,128)(2,1)} %pad_maximum_fusion.1.cot, ...), custom_call_target="tpu_custom_call" | custom-call | flops 16000000000 | bytes 25165824 | tf_op jit(solution)/shard_map/ffn_chunk/pallas_call | solution.py:927
  249.6 39.8 %collective-permute-done.5.refs_2_.refs_13_ = bf16[384,1536]{1,0:T(8,128)(2,1)} collective-permute-done((bf16[384,1536]{1,0:T(8,128)(2,1)}, bf16[384,1536]{1,0:T(8,128)(2,1)}, u32[]{:S(2)}, u32[]{:S(2)}) %collective-permute-start.5) | collective-permute-done | bytes 1179680 | tf_op jit(solution)/shard_map/ppermute | solution.py:1095
  289.3 17.1 %ffn_chunk.7 = (bf16[1024,512]{1,0:T(8,128)(2,1)S(1)}, bf16[1024,1024]{1,0:T(8,128)(2,1)}, bf16[384,1536]{1,0:T(8,128)(2,1)S(1)}, bf16[384,1536]{1,0:T(8,128)(2,...) custom-call(bf16[1024,1536]{1,0:T(8,128)(2,1)} %get-tuple-element.155.second, ...), custom_call_target="tpu_custom_call" | custom-call | flops 16000000000 | bytes 25165824 | tf_op jit(solution)/shard_map/ffn_chunk/pallas_call | solution.py:927
  309.5 1.8 collective-permute-done.3.refs_0_.refs_10_
  311.3 16.7 %ffn_chunk.6 = (bf16[1024,512]{1,0:T(8,128)(2,1)S(1)}, bf16[1024,1024]{1,0:T(8,128)(2,1)S(1)}, bf16[4,384,1536]{2,1,0:T(8,128)(2,1)}) custom-call(bf16[1024,1536]{1,0:T(8,128)(2,1)} %get-tuple-element.155.second, bf16[1536,1024]{1,0:T(8,128)(2,1)} %copy.34.second_t, bf16[1024,1536]{1,0:T(8,128)(2,1)} %pad_maximum_fusion.1.cot, ...), custom_call_target="tpu_custom_call" | custom-call | flops 16000000000 | bytes 25165824 | tf_op jit(solution)/shard_map/ffn_chunk/pallas_call | solution.py:927
  330.3 2.2 copy-done.51
  332.5 16.9 %ffn_chunk.5 = (bf16[1024,512]{1,0:T(8,128)(2,1)S(1)}, bf16[1024,1024]{1,0:T(8,128)(2,1)S(1)}, bf16[4,384,1536]{2,1,0:T(8,128)(2,1)}) custom-call(bf16[1024,1536]{1,0:T(8,128)(2,1)} %get-tuple-element.155.second, bf16[1536,1024]{1,0:T(8,128)(2,1)} %copy.34.second_t, bf16[1024,1536]{1,0:T(8,128)(2,1)} %pad_maximum_fusion.1.cot, bf16[4,384,1536]{2,1,0:T(8,128)(2,1)} %copy-done.51), custom_call_target="tpu_custom_call" | custom-call | flops 16000000000 | bytes 25165824 | tf_op jit(solution)/shard_map/ffn_chunk/pallas_call | solution.py:927
  351.7 29.9 %ffn_combine.1 = (f32[1024,1536]{1,0:T(8,128)}, f32[1024,1536]{1,0:T(8,128)}) custom-call(bf16[1024,512]{1,0:T(8,128)(2,1)} %copy-done.31, bf16[1024,512]{1,0:T(8,128)(2,1)} %copy-done.34, bf16[1024,512]{1,0:T(8,128)(2,1)} %copy-done.33, bf16[1024,512]{1,0:T(8,128)(2,1)} %copy-done.32, bf16[1024,1024]{1,0:T(8,128)(2,1)} %copy-done.28, ...), custom_call_target="tpu_custom_call" | custom-call | flops 25999998976 | bytes 50331648 | tf_op jit(solution)/shard_map/ffn_combine/pallas_call | solution.py:1005
  381.5 3.9 slice.55
  385.4 1.3 constant_dynamic-slice_fusion.9
  387.3 1.6 copy.38
  388.8 1.7 constant_dynamic-slice_fusion.11
  393.1 4.0 multiply_reduce_fusion
  397.2 6.6 fusion.38
  403.9 1.4 pad_maximum_fusion.3.refs_11_
  405.9 24.0 %collective-permute-start.14 = (bf16[384,1536]{1,0:T(8,128)(2,1)S(1)}, bf16[384,1536]{1,0:T(8,128)(2,1)}, u32[]{:S(2)}, u32[]{:S(2)}) collective-permute-start(bf16[384,1536]{1,0:T(8,128)(2,1)S(1)} %copy-done.19), channel_id=1, source_target_pairs={{0,1},{1,2},{2,3},{3,0},{4,5},{5,6},{6,7},{7,4},{8,9},{9,10},{10,1... | collective-permute-start | bytes 3538952 | tf_op jit(solution)/shard_map/ppermute | solution.py:1095
  429.9 1.5 slice.49
  431.4 5.6 convolution_convert_fusion.1.do_ref
  437.1 43.5 %attention_backward.1 = (bf16[1536,512]{1,0:T(8,128)(2,1)}, bf16[768,512]{1,0:T(8,128)(2,1)S(1)}, bf16[768,512]{1,0:T(8,128)(2,1)S(1)}, bf16[768,512]{1,0:T(8,12...) custom-call(s32[4]{0:T(128)S(1)} %get-tuple-element.150.ids_ref, ...), custom_call_target="tpu_custom_call" | custom-call | flops 8000000000 | bytes 25165824 | tf_op jit(solution)/shard_map/attention_backward/pallas_call | solution.py:227
  481.8 1.4 collective-permute-start.16
  483.1 1.8 pad_maximum_fusion.2
  485.0 6.7 fusion.39
  491.8 6.1 convolution_convert_fusion
  497.9 36.5 %collective-permute-done.15.refs_18_ = bf16[384,1536]{1,0:T(8,128)(2,1)S(1)} collective-permute-done((bf16[384,1536]{1,0:T(8,128)(2,1)}, bf16[384,1536]{1,0:T(8,128)(2,1)S(1)}, u32[]{:S(2)}, u32[]{:S(2)}) %collective-permute-start.15) | collective-permute-done | bytes 1179680 | tf_op jit(solution)/shard_map/ppermute | solution.py:1095
  535.5 220.0 %tail.1 = (bf16[4,2,48,1536]{3,2,1,0:T(8,128)(2,1)}, bf16[4,2,48,1536]{3,2,1,0:T(8,128)(2,1)}, bf16[4,2,48,1536]{3,2,1,0:T(8,128)(2,1)}, bf16[4,2,384,1536]{3,2,1,0:T(8,128)(2,1)}, bf16[1536,512]{1,0:T(8,128)(2,1)}) custom-call(bf16[768,512]{1,0:T(8,128)(2,1)} %copy-done.9, bf16[768,512]{1,0:T(8,128)(2,1)} %copy-done.10, bf16[768,512]{1,0:T(8,128)(2,1)} %copy-done.11, ...), custom_call_target="tpu_custom_call" | custom-call | tf_op jit(solution)/shard_map/tail/pallas_call | solution.py:808
  755.5 8.0 fusion.8
  766.7 2.1 collective-permute-start.24
  769.1 2.1 collective-permute-start.26
  774.6 2.3 collective-permute-start.20
  778.9 1.4 collective-permute-start.28
  780.9 1.6 collective-permute-done.28
  782.5 1.4 collective-permute-start.29
  784.5 1.6 collective-permute-done.29
  786.7 3.7 copy-done
  790.3 9.4 %assemble.1 = (f32[384,4096]{1,0:T(8,128)}, f32[384,4096]{1,0:T(8,128)}, f32[1024,1536]{1,0:T(8,128)}, f32[384,1536]{1,0:T(8,128)}, f32[384,1536]{1,0:T(8,128)}, /*index=5*/f32[384,768]{1,0:T(8,128)}, f32[384,768]{1,0:T(8,128)}) custom-call(bf16[4,2,384,1536]{3,2,1,0:T(8,128)(2,1)S(1)} %copy-done, bf16[4,2,384,1536]{3,2,1,0:T(8,128)(2,1)S(1)} %copy-done, ...), custom_call_target="tpu_custom_call" | custom-call | bytes 40894464 | tf_op jit(solution)/shard_map/assemble/pallas_call | solution.py:1052
  800.4 3.1 maximum_select_fusion.1
  803.4 2.8 fusion.18
  806.2 1.4 maximum_select_fusion
  (187 shorter events, 42.1 us)
Async XLA Ops:
  4.2 432.9 %copy-start.7 = (f32[48,512]{1,0:T(8,128)}, f32[48,512]{1,0:T(8,128)S(1)}, u32[]{:S(2)}) copy-start(f32[48,512]{1,0:T(8,128)S(1)} %get-tuple-element.166.refs_10_.sin_ref) | copy-start | bytes 294916
  4.2 432.9 %copy-start.8 = (f32[48,512]{1,0:T(8,128)}, f32[48,512]{1,0:T(8,128)S(1)}, u32[]{:S(2)}) copy-start(f32[48,512]{1,0:T(8,128)S(1)} %get-tuple-element.167.refs_9_.cos_ref) | copy-start | bytes 294916
  169.6 28.7 %copy-start.20 = (bf16[768,512]{1,0:T(8,128)(2,1)}, bf16[768,512]{1,0:T(8,128)(2,1)S(1)}, u32[]{:S(2)}) copy-start(bf16[768,512]{1,0:T(8,128)(2,1)S(1)} %get-tuple-element.70.rest_0_) | copy-start | bytes 2359300
  169.6 28.7 %copy-start.21 = (bf16[768,512]{1,0:T(8,128)(2,1)}, bf16[768,512]{1,0:T(8,128)(2,1)S(1)}, u32[]{:S(2)}) copy-start(bf16[768,512]{1,0:T(8,128)(2,1)S(1)} %get-tuple-element.71.rest_1_) | copy-start | bytes 2359300
  169.6 28.7 %copy-start.22 = (bf16[768,512]{1,0:T(8,128)(2,1)}, bf16[768,512]{1,0:T(8,128)(2,1)S(1)}, u32[]{:S(2)}) copy-start(bf16[768,512]{1,0:T(8,128)(2,1)S(1)} %get-tuple-element.72.rest_2_) | copy-start | bytes 2359300
  169.6 28.7 %copy-start.23 = (bf16[768,512]{1,0:T(8,128)(2,1)}, bf16[768,512]{1,0:T(8,128)(2,1)S(1)}, u32[]{:S(2)}) copy-start(bf16[768,512]{1,0:T(8,128)(2,1)S(1)} %get-tuple-element.73.rest_3_) | copy-start | bytes 2359300
  169.6 28.7 %copy-start.24 = (bf16[768,512]{1,0:T(8,128)(2,1)}, bf16[768,512]{1,0:T(8,128)(2,1)S(1)}, u32[]{:S(2)}) copy-start(bf16[768,512]{1,0:T(8,128)(2,1)S(1)} %get-tuple-element.74.rest_4_) | copy-start | bytes 2359300
  169.6 28.7 %copy-start.25 = (bf16[768,512]{1,0:T(8,128)(2,1)}, bf16[768,512]{1,0:T(8,128)(2,1)S(1)}, u32[]{:S(2)}) copy-start(bf16[768,512]{1,0:T(8,128)(2,1)S(1)} %get-tuple-element.75.rest_5_) | copy-start | bytes 2359300
  169.6 28.7 %copy-start.26 = (bf16[768,512]{1,0:T(8,128)(2,1)}, bf16[768,512]{1,0:T(8,128)(2,1)S(1)}, u32[]{:S(2)}) copy-start(bf16[768,512]{1,0:T(8,128)(2,1)S(1)} %get-tuple-element.76.rest_6_) | copy-start | bytes 2359300
  206.8 8.9 %collective-permute-start = (bf16[512,1536]{1,0:T(8,128)(2,1)}, bf16[512,1536]{1,0:T(8,128)(2,1)}, u32[]{:S(2)}, u32[]{:S(2)}) collective-permute-start(bf16[512,1536]{1,0:T(8,128)(2,1)} %multiply_convert_fusion), channel_id=1, source_target_pairs={{0,4},{4,0},{8,12},{12,8},{16,20},{20,16},{24,28},{28,24},{1,5},{5... | collective-permute-start | bytes 4718600 | tf_op jit(solution)/shard_map/ppermute | solution.py:1073
  206.8 19.8 %collective-permute-start.1 = (bf16[2,256,1536]{2,1,0:T(8,128)(2,1)}, bf16[2,256,1536]{2,1,0:T(8,128)(2,1)}, u32[]{:S(2)}, u32[]{:S(2)}) collective-permute-start(bf16[2,256,1536]{2,1,0:T(8,128)(2,1)} %param.14), channel_id=1, source_target_pairs={{0,4},{4,0},{8,12},{12,8},{16,20},{20,16},{24,28},{28,24},{1,5},{5... | collective-permute-start | bytes 4718600 | tf_op jit(solution)/shard_map/ppermute | solution.py:1073
  207.3 104.0 %collective-permute-start.3 = (bf16[4,384,1536]{2,1,0:T(8,128)(2,1)}, bf16[4,384,1536]{2,1,0:T(8,128)(2,1)}, u32[]{:S(2)}, u32[]{:S(2)}) collective-permute-start(bf16[4,384,1536]{2,1,0:T(8,128)(2,1)} %get-tuple-element.81.refs_0_.refs_8_), channel_id=1, source_target_pairs={{0,16},{4,20},{8,24},{12,28},{16,0},{20,4},{24,8},{28,12},{1,17},{... | collective-permute-start | bytes 14155784 | tf_op jit(solution)/shard_map/ppermute | solution.py:1077
  208.3 41.3 %collective-permute-start.4 = (bf16[384,1536]{1,0:T(8,128)(2,1)}, bf16[384,1536]{1,0:T(8,128)(2,1)}, u32[]{:S(2)}, u32[]{:S(2)}) collective-permute-start(bf16[384,1536]{1,0:T(8,128)(2,1)} %get-tuple-element.85.refs_0_.refs_11_), channel_id=1, source_target_pairs={{0,1},{1,2},{2,3},{3,0},{4,5},{5,6},{6,7},{7,4},{8,9},{9,10},{10,1... | collective-permute-start | bytes 3538952 | tf_op jit(solution)/shard_map/ppermute | solution.py:1095
  208.9 80.5 %collective-permute-start.5 = (bf16[384,1536]{1,0:T(8,128)(2,1)}, bf16[384,1536]{1,0:T(8,128)(2,1)}, u32[]{:S(2)}, u32[]{:S(2)}) collective-permute-start(bf16[384,1536]{1,0:T(8,128)(2,1)} %get-tuple-element.85.refs_0_.refs_11_), channel_id=1, source_target_pairs={{0,2},{1,3},{2,0},{3,1},{4,6},{5,7},{6,4},{7,5},{8,10},{9,11},{10,... | collective-permute-start | bytes 3538952 | tf_op jit(solution)/shard_map/ppermute | solution.py:1095
  215.6 73.7 %collective-permute-start.6 = (bf16[384,1536]{1,0:T(8,128)(2,1)}, bf16[384,1536]{1,0:T(8,128)(2,1)}, u32[]{:S(2)}, u32[]{:S(2)}) collective-permute-start(bf16[384,1536]{1,0:T(8,128)(2,1)} %get-tuple-element.85.refs_0_.refs_11_), channel_id=1, source_target_pairs={{0,3},{1,0},{2,1},{3,2},{4,7},{5,4},{6,5},{7,6},{8,11},{9,8},{10,9... | collective-permute-start | bytes 3538952 | tf_op jit(solution)/shard_map/ppermute | solution.py:1095
  226.6 103.6 %collective-permute-start.2 = (bf16[4,384,1536]{2,1,0:T(8,128)(2,1)}, bf16[4,384,1536]{2,1,0:T(8,128)(2,1)S(1)}, u32[]{:S(2)}, u32[]{:S(2)}) collective-permute-start(bf16[4,384,1536]{2,1,0:T(8,128)(2,1)} %get-tuple-element.81.refs_0_.refs_8_), channel_id=1, source_target_pairs={{0,8},{4,12},{8,0},{12,4},{16,24},{20,28},{24,16},{28,20},{1,9},{5... | collective-permute-start | bytes 14155784 | tf_op jit(solution)/shard_map/ppermute | solution.py:1077
  385.4 7.7 collective-permute-start.8
  386.7 93.9 %collective-permute-start.10 = (bf16[768,512]{1,0:T(8,128)(2,1)}, bf16[768,512]{1,0:T(8,128)(2,1)}, u32[]{:S(2)}, u32[]{:S(2)}) collective-permute-start(bf16[768,512]{1,0:T(8,128)(2,1)} %bitcast.20), channel_id=1, source_target_pairs={{0,4},{4,0},{8,12},{12,8},{16,20},{20,16},{24,28},{28,24},{1,5},{5... | collective-permute-start | bytes 2359304 | tf_op jit(solution)/shard_map/ppermute | solution.py:1073
  390.5 13.3 %collective-permute-start.9 = (bf16[768,512]{1,0:T(8,128)(2,1)S(1)}, bf16[768,512]{1,0:T(8,128)(2,1)S(1)}, u32[]{:S(2)}, u32[]{:S(2)}) collective-permute-start(bf16[768,512]{1,0:T(8,128)(2,1)S(1)} %bitcast.58), channel_id=1, source_target_pairs={{0,4},{4,0},{8,12},{12,8},{16,20},{20,16},{24,28},{28,24},{1,5},{5... | collective-permute-start | bytes 2359304 | tf_op jit(solution)/shard_map/ppermute | solution.py:1073
  391.0 143.5 %collective-permute-start.13 = (bf16[4,384,1536]{2,1,0:T(8,128)(2,1)}, bf16[4,384,1536]{2,1,0:T(8,128)(2,1)}, u32[]{:S(2)}, u32[]{:S(2)}) collective-permute-start(bf16[4,384,1536]{2,1,0:T(8,128)(2,1)} %get-tuple-element.107), channel_id=1, source_target_pairs={{0,16},{4,20},{8,24},{12,28},{16,0},{20,4},{24,8},{28,12},{1,17},{... | collective-permute-start | bytes 14155784 | tf_op jit(solution)/shard_map/ppermute | solution.py:1077
  392.1 142.4 %collective-permute-start.12 = (bf16[4,384,1536]{2,1,0:T(8,128)(2,1)}, bf16[4,384,1536]{2,1,0:T(8,128)(2,1)}, u32[]{:S(2)}, u32[]{:S(2)}) collective-permute-start(bf16[4,384,1536]{2,1,0:T(8,128)(2,1)} %get-tuple-element.106), channel_id=1, source_target_pairs={{0,8},{4,12},{8,0},{12,4},{16,24},{20,28},{24,16},{28,20},{1,9},{5... | collective-permute-start | bytes 14155784 | tf_op jit(solution)/shard_map/ppermute | solution.py:1077
  393.1 38.3 %slice-start = ((s8[4718592]{0:T(1024)(128)(4,1)}), s8[4194304]{0:T(1024)(128)(4,1)S(1)}, s32[]{:S(2)}) async-start(s8[4718592]{0:T(1024)(128)(4,1)} %bitcast.62), calls=%async_computation | async-start | bytes 8388608
  397.2 34.2 %slice-start.1 = ((s8[4718592]{0:T(1024)(128)(4,1)}), s8[524288]{0:T(1024)(128)(4,1)S(1)}, s32[]{:S(2)}) async-start(s8[4718592]{0:T(1024)(128)(4,1)} %bitcast.62), calls=%async_computation.1 | async-start | bytes 1048576
  403.8 33.2 %copy-start.38 = (f32[512,1536]{1,0:T(8,128)}, f32[512,1536]{1,0:T(8,128)S(1)}, u32[]{:S(2)}) copy-start(f32[512,1536]{1,0:T(8,128)S(1)} %get-tuple-element.151) | copy-start | bytes 9437188
  403.8 78.0 %collective-permute-start.11 = (bf16[512,1536]{1,0:T(8,128)(2,1)}, bf16[512,1536]{1,0:T(8,128)(2,1)}, u32[]{:S(2)}, u32[]{:S(2)}) collective-permute-start(bf16[512,1536]{1,0:T(8,128)(2,1)} %get-tuple-element.147), channel_id=1, source_target_pairs={{0,4},{4,0},{8,12},{12,8},{16,20},{20,16},{24,28},{28,24},{1,5},{5... | collective-permute-start | bytes 4718600 | tf_op jit(solution)/shard_map/ppermute | solution.py:1073
  405.9 92.0 %collective-permute-start.14 = (bf16[384,1536]{1,0:T(8,128)(2,1)S(1)}, bf16[384,1536]{1,0:T(8,128)(2,1)}, u32[]{:S(2)}, u32[]{:S(2)}) collective-permute-start(bf16[384,1536]{1,0:T(8,128)(2,1)S(1)} %copy-done.19), channel_id=1, source_target_pairs={{0,1},{1,2},{2,3},{3,0},{4,5},{5,6},{6,7},{7,4},{8,9},{9,10},{10,1... | collective-permute-start | bytes 3538952 | tf_op jit(solution)/shard_map/ppermute | solution.py:1095
  437.1 44.7 %copy-start.52 = (bf16[384,1536]{1,0:T(8,128)(2,1)S(1)}, bf16[384,1536]{1,0:T(8,128)(2,1)}, u32[]{:S(2)}) copy-start(bf16[384,1536]{1,0:T(8,128)(2,1)} %get-tuple-element.111) | copy-start | bytes 3538948
  480.7 53.8 %collective-permute-start.15 = (bf16[384,1536]{1,0:T(8,128)(2,1)}, bf16[384,1536]{1,0:T(8,128)(2,1)S(1)}, u32[]{:S(2)}, u32[]{:S(2)}) collective-permute-start(bf16[384,1536]{1,0:T(8,128)(2,1)} %get-tuple-element.110), channel_id=1, source_target_pairs={{0,2},{1,3},{2,0},{3,1},{4,6},{5,7},{6,4},{7,5},{8,10},{9,11},{10,... | collective-permute-start | bytes 3538952 | tf_op jit(solution)/shard_map/ppermute | solution.py:1095
  481.8 52.7 %collective-permute-start.16 = (bf16[384,1536]{1,0:T(8,128)(2,1)S(1)}, bf16[384,1536]{1,0:T(8,128)(2,1)}, u32[]{:S(2)}, u32[]{:S(2)}) collective-permute-start(bf16[384,1536]{1,0:T(8,128)(2,1)S(1)} %copy-done.52), channel_id=1, source_target_pairs={{0,3},{1,0},{2,1},{3,2},{4,7},{5,4},{6,5},{7,6},{8,11},{9,8},{10,9... | collective-permute-start | bytes 3538952 | tf_op jit(solution)/shard_map/ppermute | solution.py:1095
  497.9 305.5 %collective-permute-start.7 = (f32[512,1536]{1,0:T(8,128)}, f32[512,1536]{1,0:T(8,128)}, u32[]{:S(2)}, u32[]{:S(2)}) collective-permute-start(f32[512,1536]{1,0:T(8,128)} %pad_maximum_fusion.2), channel_id=1, source_target_pairs={{0,4},{4,0},{8,12},{12,8},{16,20},{20,16},{24,28},{28,24},{1,5},{5... | collective-permute-start | bytes 9437192 | tf_op jit(solution)/shard_map/ppermute | solution.py:1073
  535.5 220.0 %copy-start.50 = (f32[1536]{0:T(1024)S(1)}, f32[1536]{0:T(1024)}, u32[]{:S(2)}) copy-start(f32[1536]{0:T(1024)} %get-tuple-element.129) | copy-start | bytes 18436
  763.4 23.2 %copy-start.3 = (bf16[4,2,48,1536]{3,2,1,0:T(8,128)(2,1)S(1)}, bf16[4,2,48,1536]{3,2,1,0:T(8,128)(2,1)}, u32[]{:S(2)}) copy-start(bf16[4,2,48,1536]{3,2,1,0:T(8,128)(2,1)} %get-tuple-element.117) | copy-start | bytes 3538948
  764.4 22.3 %copy-start.1 = (bf16[4,2,48,1536]{3,2,1,0:T(8,128)(2,1)S(1)}, bf16[4,2,48,1536]{3,2,1,0:T(8,128)(2,1)}, u32[]{:S(2)}) copy-start(bf16[4,2,48,1536]{3,2,1,0:T(8,128)(2,1)} %get-tuple-element.115) | copy-start | bytes 3538948
  764.4 22.2 %copy-start.2 = (bf16[4,2,48,1536]{3,2,1,0:T(8,128)(2,1)S(1)}, bf16[4,2,48,1536]{3,2,1,0:T(8,128)(2,1)}, u32[]{:S(2)}) copy-start(bf16[4,2,48,1536]{3,2,1,0:T(8,128)(2,1)} %get-tuple-element.116) | copy-start | bytes 3538948
  765.7 34.7 %collective-permute-start.17 = (bf16[256,1536]{1,0:T(8,128)(2,1)}, bf16[256,1536]{1,0:T(8,128)(2,1)}, u32[]{:S(2)}, u32[]{:S(2)}) collective-permute-start(bf16[256,1536]{1,0:T(8,128)(2,1)} %get-tuple-element.157), channel_id=1, source_target_pairs={{0,4},{4,0},{8,12},{12,8},{16,20},{20,16},{24,28},{28,24},{1,5},{5... | collective-permute-start | bytes 2359304 | tf_op jit(solution)/shard_map/ppermute | solution.py:1073
  766.7 5.6 collective-permute-start.24
  768.9 4.7 collective-permute-start.25
  769.1 5.5 collective-permute-start.26
  772.3 5.4 collective-permute-start.18
  773.6 4.5 collective-permute-start.19
  774.6 3.7 collective-permute-start.20
  777.7 1.2 collective-permute-start.27
  778.3 2.0 collective-permute-start.21
  778.9 3.6 collective-permute-start.28
  780.3 3.6 collective-permute-start.22
  782.5 3.6 collective-permute-start.29
  783.9 15.9 %collective-permute-start.23 = (f32[384]{0:T(512)S(1)}, f32[384]{0:T(512)S(1)}, u32[]{:S(2)}, u32[]{:S(2)}) collective-permute-start(f32[384]{0:T(512)S(1)} %add.198), channel_id=1, source_target_pairs={{0,16},{4,20},{8,24},{12,28},{16,0},{20,4},{24,8},{28,12},{1,17},{... | collective-permute-start | bytes 4616 | tf_op jit(solution)/shard_map/ppermute | solution.py:1077
  790.3 10.0 %copy-start.45 = (bf16[1,256,1536]{2,1,0:T(8,128)(2,1)S(1)}, bf16[1,256,1536]{2,1,0:T(8,128)(2,1)}, u32[]{:S(2)}) copy-start(bf16[1,256,1536]{2,1,0:T(8,128)(2,1)} %get-tuple-element.156) | copy-start | bytes 2359300
  (37 other events, 103.0 us)

commit v5 on v4

--- a/solution.py
+++ b/solution.py
@@ -16,8 +16,9 @@
 SCALE = HEAD_WIDTH ** -0.5
 BF = jnp.bfloat16
 F32 = jnp.float32
-
-ATT_COST = 8
+NO_COST = pl.CostEstimate(flops=0, bytes_accessed=0, transcendentals=0)
+LONG = pl.CostEstimate(flops=200 * 10**9, bytes_accessed=0, transcendentals=0)
+
 LOG2E = 1.4426950408889634
 NT = (((1,), (1,)), ((), ()))
 
@@ -36,10 +37,22 @@
     return lax.broadcasted_iota(jnp.int32, (BLK, 2 * BLK), 0) - lax.rem(lax.broadcasted_iota(jnp.int32, (BLK, 2 * BLK), 1), BLK)
 
 
+def load_keys(refs, scratch, sem):
+    copies = [pltpu.make_async_copy(ref, scratch.at[n], sem.at[n]) for n, ref in enumerate(refs)]
+
+    @pl.when(pl.program_id(0) == 0)
+    def _():
+        for copy in copies:
+            copy.start()
+        for copy in copies:
+            copy.wait()
+
+
 def fwd_kernel(nchip, heads, ids_ref, inv_ref, q_ref, *rest):
-    k_refs, v_refs = rest[:nchip], rest[nchip:2 * nchip]
-    o_ref, lse_ref, knat, vtr = rest[2 * nchip:2 * nchip + 4]
-    state = rest[2 * nchip + 4:]
+    o_ref, lse_ref, kv_s, sem, knat, vtr = rest[2 * nchip:2 * nchip + 6]
+    state = rest[2 * nchip + 6:]
+    load_keys(rest[:2 * nchip], kv_s, sem)
+    base = pl.program_id(0) * (96 * heads)
     nq = q_ref.shape[1] // BLK
     slices = nq // 2
     nb = nchip * nq
@@ -49,8 +62,9 @@
     for h in range(heads):
         for n in range(nb):
             r, lanes = n // nq, slice(BLK * (n % nq), BLK * (n % nq + 1))
-            knat[h, n] = k_refs[r][96 * h:96 * (h + 1), lanes].T
-            vtr[h, n] = v_refs[r][96 * h:96 * (h + 1), lanes]
+            part = pl.ds(pl.multiple_of(base + 96 * h, 96), 96)
+            knat[h, n] = kv_s[r, part, lanes].T
+            vtr[h, n] = kv_s[nchip + r, part, lanes]
         for sl in range(slices):
             for half in range(2):
                 lanes = slice(BLK * (2 * sl + half), BLK * (2 * sl + half + 1))
@@ -110,26 +124,30 @@
     grid_spec = pltpu.PrefetchScalarGridSpec(
         num_scalar_prefetch=2,
         grid=(heads // per,),
-        in_specs=[wide] + [slim] * (2 * nchip),
+        in_specs=[wide] + [pl.BlockSpec(memory_space=pltpu.HBM)] * (2 * nchip),
         out_specs=[wide, pl.BlockSpec((per, nq, 1, 2 * BLK), lambda g, *_: (g, 0, 0, 0))],
-        scratch_shapes=[pltpu.VMEM((per, nb, BLK, 96), BF), pltpu.VMEM((per, nb, 96, BLK), BF)] + chain * (per * nq // 2),
+        scratch_shapes=[
+            pltpu.VMEM((2 * nchip, heads * 96, T), BF), pltpu.SemaphoreType.DMA((2 * nchip,)),
+            pltpu.VMEM((per, nb, BLK, 96), BF), pltpu.VMEM((per, nb, 96, BLK), BF),
+        ] + chain * (per * nq // 2),
     )
     return pl.pallas_call(
         functools.partial(fwd_kernel, nchip, per),
         grid_spec=grid_spec,
         out_shape=[jax.ShapeDtypeStruct((heads * 192, T), BF), jax.ShapeDtypeStruct((heads, nq, 1, 2 * BLK), F32)],
-        cost_estimate=pl.CostEstimate(flops=ATT_COST * 10**9, bytes_accessed=16 * 2**20, transcendentals=0),
-        compiler_params=pltpu.CompilerParams(vmem_limit_bytes=48 * 2**20),
+        cost_estimate=NO_COST,
+        compiler_params=pltpu.CompilerParams(vmem_limit_bytes=56 * 2**20),
         name="attention_forward",
     )(ids, inv, qT, *ks, *vs)
 
 
 def bwd_kernel(nchip, heads, ids_ref, inv_ref, q_ref, o_ref, do_ref, lse_ref, cos_ref, sin_ref, *rest):
-    k_refs, v_refs = rest[:nchip], rest[nchip:2 * nchip]
     dq_ref = rest[2 * nchip]
     dk_refs, dv_refs = rest[2 * nchip + 1:3 * nchip + 1], rest[3 * nchip + 1:4 * nchip + 1]
-    knat, ktr, vnat = rest[4 * nchip + 1:4 * nchip + 4]
-    state = rest[4 * nchip + 4:]
+    kv_s, sem, knat, ktr, vnat = rest[4 * nchip + 1:4 * nchip + 6]
+    state = rest[4 * nchip + 6:]
+    load_keys(rest[:2 * nchip], kv_s, sem)
+    base = pl.program_id(0) * (96 * heads)
     nq = q_ref.shape[1] // BLK
     slices = nq // 2
     nb = nchip * nq
@@ -139,10 +157,11 @@
     for h in range(heads):
         for n in range(nb):
             r, lanes = n // nq, slice(BLK * (n % nq), BLK * (n % nq + 1))
-            block = k_refs[r][96 * h:96 * (h + 1), lanes]
+            part = pl.ds(pl.multiple_of(base + 96 * h, 96), 96)
+            block = kv_s[r, part, lanes]
             knat[h, n] = block.T
             ktr[h, n] = block
-            vnat[h, n] = v_refs[r][96 * h:96 * (h + 1), lanes].T
+            vnat[h, n] = kv_s[nchip + r, part, lanes].T
     for h, sl in chains:
         for half in range(2):
             lanes = slice(BLK * (2 * sl + half), BLK * (2 * sl + half + 1))
@@ -218,9 +237,12 @@
         num_scalar_prefetch=2,
         grid=(heads // per,),
         in_specs=[wide, wide, wide, pl.BlockSpec((per, nq, 1, 2 * BLK), lambda g, *_: (g, 0, 0, 0))]
-        + [pl.BlockSpec((48, T), lambda g, *_: (0, 0))] * 2 + [slim] * (2 * nchip),
+        + [pl.BlockSpec((48, T), lambda g, *_: (0, 0))] * 2 + [pl.BlockSpec(memory_space=pltpu.HBM)] * (2 * nchip),
         out_specs=[wide] + [slim] * (2 * nchip),
-        scratch_shapes=[pltpu.VMEM((per, nb, BLK, 96), BF), pltpu.VMEM((per, nb, 96, BLK), BF), pltpu.VMEM((per, nb, BLK, 96), BF)]
+        scratch_shapes=[
+            pltpu.VMEM((2 * nchip, heads * 96, T), BF), pltpu.SemaphoreType.DMA((2 * nchip,)),
+            pltpu.VMEM((per, nb, BLK, 96), BF), pltpu.VMEM((per, nb, 96, BLK), BF), pltpu.VMEM((per, nb, BLK, 96), BF),
+        ]
         + chain * (per * nq // 2),
     )
     slab = jax.ShapeDtypeStruct((heads * 96, T), BF)
@@ -228,8 +250,8 @@
         functools.partial(bwd_kernel, nchip, per),
         grid_spec=grid_spec,
         out_shape=[jax.ShapeDtypeStruct((heads * 192, T), BF)] + [slab] * (2 * nchip),
-        cost_estimate=pl.CostEstimate(flops=ATT_COST * 10**9, bytes_accessed=24 * 2**20, transcendentals=0),
-        compiler_params=pltpu.CompilerParams(vmem_limit_bytes=48 * 2**20),
+        cost_estimate=LONG,
+        compiler_params=pltpu.CompilerParams(vmem_limit_bytes=56 * 2**20),
         name="attention_backward",
     )(ids, inv, qT, oT, doT, lse, cosine, sine, *ks, *vs)
     return outs[0], outs[1:1 + nchip], outs[1 + nchip:]
@@ -240,15 +262,16 @@
 
 
 def front_kernel(zsize, *refs):
-    (tok, gains, key_w, value_w, query_w, out_w, gate_w, up_w, down_w, cos, sin) = refs[:11]
-    (full_kv, full_q, full_o, pack, far_pack, x_out, first, q_out, gains_out, k0, k1, k2, k3, v0, v1, v2, v3) = refs[11:28]
-    x_s, gain_s, kv_w, q_w, kv_s, ss, rs, ls, gs, gr = refs[28:]
+    (tok, cot_in, gains, key_w, value_w, query_w, out_w, gate_w, up_w, down_w, cos, sin) = refs[:12]
+    (kv_all, q_all, o_all, pack, rest, pack_x, pack_y, far_pack, cot, first_half, x_out, first, q_out, gains_out) = refs[12:26]
+    (k0, k1, k2, k3, v0, v1, v2, v3) = refs[26:34]
+    x_s, gain_s, full_kv, full_q, full_o, kv_s, first_s, pack_s, cot_s, ss, rs, ls, gs, gr = refs[34:]
     ks, vs = (k0, k1, k2, k3), (v0, v1, v2, v3)
     index, depth = lax.axis_index("ctx"), lax.axis_index("fsdp")
     chip, core = index // 2, lax.rem(index, 2)
     fine = down_w.shape[0] // 8
     chunk = fine * zsize
-    folds = pack.shape[1] // fine
+    folds = pack.shape[0] // fine
     fold = first.shape[1] // folds
     width = first.shape[1]
     length = first.shape[0]
@@ -332,6 +355,9 @@
         copy.start()
         sent.append(copy)
         moves["gain", s] = copy
+
+    def ffn_step(s):
+        moves["ffn", s] = send(pack_s.at[0] if s == 1 else rest.at[s - 2], rest.at[s - 1], to_next)
 
     ring_step("kv", 1)
     gain_step(1)
@@ -347,8 +373,10 @@
             copies.append(local(down_w.at[pl.ds(row, fine), pl.ds(n * fold, fold)], target.at[pl.ds(n * fine, fine), pl.ds(2 * chunk, fold)]))
         return copies
 
-    own_ffn = cut_pack(chip, pack.at[depth])
-    far_ffn = cut_pack(chip_d, far_pack)
+    own_ffn = cut_pack(chip, pack_s.at[0])
+    far_ffn = cut_pack(chip_d, pack_s.at[1]) + cut_pack(chip_x, pack_s.at[2]) + cut_pack(chip_y, pack_s.at[3])
+    far_ffn += [local(cot_in.at[core], cot_s.at[0]), local(cot_in.at[1 - core], cot_s.at[1])]
+    cot_moves = [send(cot_in.at[1 - core], cot.at[1], to_core), send(cot_in.at[core], cot.at[2], to_core)]
 
     for s in steps:
         moves["kv", "ring", s].wait_recv()
@@ -357,7 +385,10 @@
             ring_step("kv", s + 1)
             gain_step(s + 1)
         else:
+            for copy in own_ffn:
+                copy.wait()
             ring_step("q", 1)
+            ffn_step(1)
         spread("kv", s)
     for s in steps:
         forward("kv", s)
@@ -390,14 +421,10 @@
         ring_step("o", 2)
     spread("o", 1)
     for s in steps:
+        forward("q", s)
+    for s in steps:
         moves["kv", "core", s].wait_recv()
-    load_kv = local(full_kv, kv_w)
-    if last > 1:
-        moves["o", "ring", 2].wait_recv()
-        if last > 2:
-            ring_step("o", 3)
-        spread("o", 2)
-    load_kv.wait()
+    keep = [local(full_kv, kv_all)]
     tile = 384
 
     def project(weight, t, turn):
@@ -409,68 +436,75 @@
         return r.astype(BF)
 
     def project_kv(t, turn):
-        kv_s[pl.ds(pl.multiple_of(t * tile, tile), tile)] = project(kv_w, t, turn)
+        kv_s[pl.ds(pl.multiple_of(t * tile, tile), tile)] = project(full_kv, t, turn)
         return 0
 
     per = kv_rows // tile
     lax.fori_loop(0, per, lambda t, _: project_kv(t, True), 0)
     k_here, v_here = kv_s.at[pl.ds(0, kv_rows)], kv_s.at[pl.ds(kv_rows, kv_rows)]
     k_x, k_y = send(k_here, k1, to_x), send(k_here, k2, to_y)
+    if last > 1:
+        moves["o", "ring", 2].wait_recv()
+        if last > 2:
+            ring_step("o", 3)
+        spread("o", 2)
     lax.fori_loop(per, 2 * per, lambda t, _: project_kv(t, False), 0)
     v_y, v_x = send(v_here, v2, to_y), send(v_here, v1, to_x)
-    keep = [local(k_here, k0), local(v_here, v0)]
-
     for s in range(3, zsize):
         moves["o", "ring", s].wait_recv()
         if s < last:
             ring_step("o", s + 1)
         spread("o", s)
-    for copy in own_ffn:
+    keep += [local(k_here, k0), local(v_here, v0)]
+    for copy in far_ffn:
         copy.wait()
-
-    def ffn_step(s):
-        a = pack.at[slot(s - 1)]
-        moves["ffn", s] = send(a, a, to_next)
-
-    ffn_step(1)
-    for s in steps:
-        forward("q", s)
+    keep += [local(pack_s.at[n], out) for n, out in enumerate((pack, far_pack, pack_x, pack_y))]
+    keep += [local(cot_s.at[0], cot.at[0]), local(cot_s.at[1], cot.at[3])]
     for s in steps:
         cross("q", s)
-    for s in steps:
-        forward("o", s)
-    for s in steps:
-        cross("o", s)
+    if last > 1:
+        moves["ffn", 1].wait_recv()
+        ffn_step(2)
+    for z in range(zsize):
+        strips = first[:, z * tile:(z + 1) * tile].astype(F32).T.astype(BF)
+        first_s[z] = strips.reshape(4, 2, strips.shape[0] // 8, length)
+    keep.append(local(first_s.at[:, :, core], first_half.at[:, :, :, pl.ds(0, length)]))
+    half_move = send(first_s.at[:, :, 1 - core], first_half.at[:, :, :, pl.ds(length, length)], to_core)
     for s in steps:
         moves["q", "core", s].wait_recv()
     for copy in own_late:
         copy.wait()
-    local(full_q, q_w).wait()
+    keep.append(local(full_q, q_all))
 
     def project_q(t, _):
-        q_out[pl.ds(pl.multiple_of(t * tile, tile), tile)] = project(q_w, t, True)
+        q_out[pl.ds(pl.multiple_of(t * tile, tile), tile)] = project(full_q, t, True)
         return 0
 
     lax.fori_loop(0, width // tile, project_q, 0)
+    for s in steps:
+        forward("o", s)
     k_x.wait_recv()
     k_d = send(k1, k3, to_y)
     v_y.wait_recv()
     v_d = send(v2, v3, to_x)
+    for s in range(2, last):
+        moves["ffn", s].wait_recv()
+        ffn_step(s + 1)
     for s in steps:
-        moves["ffn", s].wait_recv()
-        if s < last:
-            ffn_step(s + 1)
+        cross("o", s)
     for s in steps:
         moves["o", "core", s].wait_recv()
-    for copy in (k_y, v_x, k_d, v_d):
+    keep.append(local(full_o, o_all))
+    moves["ffn", last].wait_recv()
+    for copy in (k_y, v_x, k_d, v_d, half_move, *cot_moves):
         copy.wait_recv()
-    for copy in keep + far_ffn:
+    for copy in keep:
         copy.wait()
     for copy in sent:
         copy.wait_send()
 
 
-def front(tokens, gains, key_w, value_w, query_w, out_w, gate_w, up_w, down_w, cosine, sine, zsize, ctx):
+def front(tokens, cotangent, gains, key_w, value_w, query_w, out_w, gate_w, up_w, down_w, cosine, sine, zsize, ctx):
     width = tokens.shape[2]
     length = 2 * tokens.shape[1]
     rows = width // zsize
@@ -482,46 +516,56 @@
     cut = lambda w: w.reshape(chips, 2, strip, w.shape[1])
     square = jax.ShapeDtypeStruct((zsize, chips, 2, strip, width), BF)
     flat = jax.ShapeDtypeStruct((kv_rows, length), BF)
-    hbm, vmem = pl.BlockSpec(memory_space=pl.ANY), pl.BlockSpec(memory_space=pltpu.VMEM)
-    copies = 19 * (zsize - 1) + 8
+    hbm, vmem = pl.BlockSpec(memory_space=pltpu.HBM), pl.BlockSpec(memory_space=pltpu.VMEM)
+    copies = 19 * (zsize - 1) + 12
     return pl.pallas_call(
         functools.partial(front_kernel, zsize),
         out_shape=[
             square, square, square,
-            jax.ShapeDtypeStruct((zsize, rows, packed), BF),
             jax.ShapeDtypeStruct((rows, packed), BF),
+            jax.ShapeDtypeStruct((zsize - 1, rows, packed), BF),
+            jax.ShapeDtypeStruct((rows, packed), BF),
+            jax.ShapeDtypeStruct((rows, packed), BF),
+            jax.ShapeDtypeStruct((rows, packed), BF),
+            jax.ShapeDtypeStruct((4, length // 2, width), BF),
+            jax.ShapeDtypeStruct((zsize, chips, strip, 2 * length), BF),
             jax.ShapeDtypeStruct((length, width), BF),
             jax.ShapeDtypeStruct((length, width), BF),
             jax.ShapeDtypeStruct((width, length), BF),
             jax.ShapeDtypeStruct((2, width), F32),
         ] + [flat] * 8,
-        in_specs=[vmem, vmem] + [hbm] * 7 + [vmem] * 2,
-        out_specs=[hbm] * 5 + [vmem] * 4 + [hbm] * 8,
+        in_specs=[vmem, hbm, vmem] + [hbm] * 7 + [vmem] * 2,
+        out_specs=[hbm] * 10 + [vmem] * 4 + [hbm] * 8,
         scratch_shapes=[
             pltpu.VMEM((2, length // 2, width), BF),
             pltpu.VMEM((zsize, 2, rows), F32),
             pltpu.VMEM(square.shape, BF),
             pltpu.VMEM(square.shape, BF),
+            pltpu.VMEM(square.shape, BF),
             pltpu.VMEM((2 * kv_rows, length), BF),
+            pltpu.VMEM((zsize, chips, 2, strip, length), BF),
+            pltpu.VMEM((4, rows, packed), BF),
+            pltpu.VMEM((2, length // 2, width), BF),
             pltpu.SemaphoreType.DMA((copies,)),
             pltpu.SemaphoreType.DMA((copies,)),
-            pltpu.SemaphoreType.DMA((8 + 4 * zsize + 2 * (rows // fine),)),
+            pltpu.SemaphoreType.DMA((20 + 8 * zsize + 4 * (rows // fine),)),
             pltpu.SemaphoreType.DMA((zsize,)),
             pltpu.SemaphoreType.DMA((zsize,)),
         ],
-        compiler_params=pltpu.CompilerParams(collective_id=0, has_side_effects=True, vmem_limit_bytes=40 * 2**20),
+        compiler_params=pltpu.CompilerParams(collective_id=0, has_side_effects=True, vmem_limit_bytes=50 * 2**20),
         name="front",
-    )(tokens, gains, cut(key_w), cut(value_w), cut(query_w), cut(out_w), gate_w, up_w, down_w, cosine, sine)
+    )(tokens, cotangent, gains, cut(key_w), cut(value_w), cut(query_w), cut(out_w), gate_w, up_w, down_w, cosine, sine)
 
 
 def tail_kernel(zsize, *refs):
     dk, dv = refs[0:4], refs[4:8]
-    dq, cos, sin, first_half, out_grad = refs[8:13]
+    dq, cos, sin, first_half, att_half = refs[8:13]
     pack_in, far_in = refs[13:16], refs[16:16 + zsize]
-    rest = refs[16 + zsize:]
-    o_all, q_all, kv_all, pack_all, kv_low = rest[:5]
+    mid_t, query_w, kv_w, x_in, middle, gain, second_part = refs[16 + zsize:23 + zsize]
+    rest = refs[23 + zsize:]
+    o_all, q_all, kv_all, pack_all, tokens_out, gains_out = rest[:6]
     (got, held, dq_pair, kv_pair, half, grads, gl, gr, gx, gy, gz, piece,
-     pack_s, pack_0, pack_z, far_s, far_r, pack_p, ss, rs, ls) = rest[5:]
+     pack_s, pack_0, pack_z, far_s, far_r, pack_p, first_grad, tokens_s, gain_s, gain_r, ss, rs, ls) = rest[6:]
     index, depth = lax.axis_index("ctx"), lax.axis_index("fsdp")
     chip, core = index // 2, lax.rem(index, 2)
     chip_x, chip_y, chip_d = chip + 1 - 2 * lax.rem(chip, 2), lax.rem(chip + 2, 4), 3 - chip
@@ -531,7 +575,7 @@
     to_far = (chip_d * 2 + core, depth)
     last = zsize - 1
     kv_rows = dk[0].shape[0]
-    width = first_half.shape[0] * 2
+    width = kv_w.shape[2]
     strip = piece.shape[1]
     length = dq.shape[1]
 
@@ -553,6 +597,10 @@
         sent.append(copy)
         return copy
 
+    def settle(copy):
+        copy.wait_send()
+        sent[:] = [other for other in sent if other is not copy]
+
     def local(src, dst):
         k = count[1]
         count[1] += 1
@@ -583,6 +631,7 @@
         return lax.rem(depth + 2 * zsize - 1 - j, zsize)
 
     k3, v3 = send(dk[3], got.at[0], to_y), send(dv[3], got.at[1], to_x)
+    mid_swap = send(mid_t, held.at[1], to_core)
     q_swap = send(dq, dq_pair.at[1], to_core)
 
     part = pack_0.shape[0] // 2
@@ -592,9 +641,8 @@
         return [local(pack_in[n].at[place_at(j)], pack_s.at[j % 2, n]) for n in range(3)]
 
     ffn_loads = {0: load_ffn(0)}
-    load_o = local(out_grad, grads.at[0])
-    load_q = [local(dq, dq_pair.at[0]), local(first_half, half)]
-    load_kv = [local(dk[0], held.at[0]), local(dk[1], held.at[1]), local(dv[0], held.at[2]), local(dv[2], held.at[3])]
+    load_o = [local(mid_t, held.at[0]), local(att_half, half.at[0])]
+    load_q = [local(dq, dq_pair.at[0]), local(first_half, half.at[1])]
     load_far = [local(far_in[n], far_s.at[n]) for n in range(zsize)]
 
     moves = {}
@@ -700,36 +748,41 @@
 
         return at
 
-    def product(m, pair):
+    def product(m, pair, which):
         per = width // tiles
 
         def one(t, _):
             zz = t // per
             cols = pl.ds(pl.multiple_of(lax.rem(t, per) * tiles, tiles), tiles)
-            rows = pl.ds(pl.multiple_of(zz * (4 * strip), 4 * strip), 4 * strip)
             nt = (((1,), (1,)), ((), ()))
-            r = lax.dot_general(half[rows, 0:length], pair[0, cols], nt, preferred_element_type=F32)
-            r = r + lax.dot_general(half[rows, length:], pair[1, cols], nt, preferred_element_type=F32)
+            left = half[which, zz].reshape(4 * strip, 2 * length)
+            r = lax.dot_general(left[:, 0:length], pair[0, cols], nt, preferred_element_type=F32)
+            r = r + lax.dot_general(left[:, length:], pair[1, cols], nt, preferred_element_type=F32)
             grads[m, zz, :, :, cols] = r.astype(BF).reshape(4, strip, tiles)
             return 0
 
         lax.fori_loop(0, zsize * per, one, 0)
 
     ffn_step(0)
-    load_o.wait()
+    received(mid_swap)
+    wait_all(load_o)
+    product(0, held, 0)
     stage_1(0)
+    keys_0, keys_1 = held.at[0, pl.ds(0, kv_rows)], held.at[0, pl.ds(kv_rows, kv_rows)]
+    values_0, values_2 = held.at[1, pl.ds(0, kv_rows)], held.at[1, pl.ds(kv_rows, kv_rows)]
+    load_kv = [local(dk[0], keys_0), local(dk[1], keys_1), local(dv[0], values_0), local(dv[2], values_2)]
     received(q_swap)
     wait_all(load_q)
-    product(1, dq_pair)
+    product(1, dq_pair, 1)
     stage_1(1)
 
     received(k3)
     wait_all(load_kv)
-    add_rows(held.at[1], [got.at[0]], 96)
-    k1 = send(held.at[1], got.at[2], to_x)
+    add_rows(keys_1, [got.at[0]], 96)
+    k1 = send(keys_1, got.at[2], to_x)
     received(v3)
-    add_rows(held.at[3], [got.at[1]], 96)
-    v2 = send(held.at[3], got.at[3], to_y)
+    add_rows(values_2, [got.at[1]], 96)
+    v2 = send(values_2, got.at[3], to_y)
     k2, v1 = send(dk[2], got.at[4], to_y), send(dv[1], got.at[5], to_x)
     if last > 1:
         ffn_step(1)
@@ -737,20 +790,19 @@
 
     def finish_keys(h, _):
         rows = pl.ds(pl.multiple_of(h * 96, 96), 96)
-        v = held[0, rows].astype(F32) + got[2, rows].astype(F32) + got[4, rows].astype(F32)
+        v = keys_0[rows].astype(F32) + got[2, rows].astype(F32) + got[4, rows].astype(F32)
         kv_pair[0, rows] = rotate_back(v, cos[...], sin[...]).astype(BF)
         return 0
 
     def finish_values(h, _):
         rows = pl.ds(pl.multiple_of(h * 96, 96), 96)
-        v = held[2, rows].astype(F32) + got[3, rows].astype(F32) + got[5, rows].astype(F32)
+        v = values_0[rows].astype(F32) + got[3, rows].astype(F32) + got[5, rows].astype(F32)
         kv_pair[0, pl.ds(pl.multiple_of(kv_rows + h * 96, 96), 96)] = v.astype(BF)
         return 0
 
     lax.fori_loop(0, kv_rows // 96, finish_keys, 0)
     lax.fori_loop(0, kv_rows // 96, finish_values, 0)
     kv_swap = send(kv_pair.at[0], kv_pair.at[1], to_core)
-    kept.append(local(kv_pair.at[0], kv_low))
     stage_2(0)
     stage_2(1)
     if last > 2:
@@ -759,7 +811,7 @@
     add_rows(far_s.at[0], [far_s.at[n] for n in range(1, zsize)], 64)
     far = send(far_s.at[0], far_r, to_far)
     received(kv_swap)
-    product(2, kv_pair)
+    product(2, kv_pair, 1)
     stage_1(2)
     stage_3(0)
     stage_3(1)
@@ -781,47 +833,97 @@
     for j in range(1, zsize):
         ring_step(2, j)
     spread(2, piece.at[2], whole(kv_all))
+    settle(far)
+    weight_at = [(pack_s.at[k // 3, k % 3], far_s.at[k]) for k in range(zsize)]
+    loads = [(local(query_w.at[k], a), local(kv_w.at[k], b)) for k, (a, b) in enumerate(weight_at)]
+    rows = width // zsize
+    for k, (a, b) in enumerate(weight_at):
+        wait_all(loads[k])
+        r = jnp.dot(a[...], dq_pair[0], preferred_element_type=F32) + jnp.dot(b[...], kv_pair[0], preferred_element_type=F32)
+        first_grad[:, k * rows:(k + 1) * rows] = r.T
+    gain_s[...] = jnp.zeros(gain_s.shape, F32)
+    gain_s[1:2] = second_part[...]
+
+    def finish_tokens(t, _):
+        at = pl.ds(pl.multiple_of(t * 64, 64), 64)
+        v = x_in[at].astype(F32)
+        inverse = lax.rsqrt(jnp.mean(v * v, -1, keepdims=True) + EPS)
+        unit = v * inverse
+        d = first_grad[at]
+        gain_s[0:1] += jnp.sum(d * unit, axis=0, keepdims=True)
+        scaled = d * gain[...]
+        tokens_s[at] = (middle[at] + inverse * (scaled - unit * jnp.mean(scaled * unit, -1, keepdims=True))).astype(BF)
+        return 0
+
+    lax.fori_loop(0, length // 64, finish_tokens, 0)
+    near_half = pl.ds(0, length // 2)
+    kept.append(local(tokens_s.at[near_half], tokens_out.at[core]))
+    tokens_swap = send(tokens_s.at[pl.ds(length // 2, length // 2)], tokens_out.at[core], to_core)
+    gain_swap = send(gain_s, gain_r.at[0], to_core)
+
     targets = [(("pack", h), half_rows(pack_all, h)) for h in range(2)]
     targets += [(m, whole(ref)) for m, ref in enumerate((o_all, q_all, kv_all))]
-    for name, target in targets:
+    for name, target in targets[:2]:
         forward(name, target)
+    received(gain_swap)
+    settle(gain_swap)
+    gain_s[...] += gain_r[0]
+    for n, target in ((1, to_x), (2, to_y)):
+        copy = send(gain_s, gain_r.at[n], target)
+        for name, at in targets[2 * n:2 * n + 2]:
+            forward(name, at)
+        received(copy)
+        settle(copy)
+        gain_s[...] += gain_r[n]
+    copy = send(gain_s, gain_r.at[3], to_next)
     wait_all(kept)
     for name, target in targets:
         cross(name, target)
+    total = gain_s[...]
+    for s in range(1, zsize):
+        received(copy)
+        total = total + gain_r[2 + s]
+        if s < last:
+            copy = send(gain_r.at[2 + s], gain_r.at[3 + s], to_next)
+    gains_out[...] = total
+    received(tokens_swap)
     for name, target in targets:
         received(moves[name, "core"])
     for copy in sent:
         copy.wait_send()
 
 
-def tail(dk, dv, dq, cosine, sine, first_half, out_grad, packs, far_packs, zsize, chips):
+def tail(dk, dv, dq, cosine, sine, first_half, att_half, packs, far_packs, mid_t, query_w, kv_w, x, middle, gain, second_part, zsize, chips):
     kv_rows, length = dk[0].shape
     width = 2 * kv_rows
-    strip = out_grad.shape[2]
+    strip = att_half.shape[2]
     rows, packed = packs[0].shape[1:]
-    hbm, vmem = pl.BlockSpec(memory_space=pl.ANY), pl.BlockSpec(memory_space=pltpu.VMEM)
+    hbm, vmem = pl.BlockSpec(memory_space=pltpu.HBM), pl.BlockSpec(memory_space=pltpu.VMEM)
     shape = lambda *s: jax.ShapeDtypeStruct(s, BF)
     store = lambda *s: pltpu.VMEM(s, BF)
-    copies = 9 + 2 * (zsize - 1) + 3 * (4 + zsize - 1) + 5 * 5
-    inputs = [*dk, *dv, dq, cosine, sine, first_half, out_grad, *packs, *far_packs]
+    copies = 15 + 3 * (zsize - 1) + 3 * (4 + zsize - 1) + 5 * 5
+    cut = lambda w: w.reshape(zsize, rows, width)
+    inputs = [*dk, *dv, dq, cosine, sine, first_half, att_half, *packs, *far_packs, mid_t, cut(query_w), cut(kv_w), x, middle, gain, second_part]
     last = zsize - 1
     return pl.pallas_call(
         functools.partial(tail_kernel, zsize),
-        out_shape=[shape(chips, 2, strip, width)] * 3 + [shape(chips, 2, rows, packed), shape(width, length)],
-        in_specs=[hbm] * 9 + [vmem] * 2 + [hbm] * (len(inputs) - 11),
-        out_specs=[hbm] * 5,
+        out_shape=[shape(chips, 2, strip, width)] * 3 + [
+            shape(chips, 2, rows, packed), shape(2, length // 2, width), jax.ShapeDtypeStruct((8, width), F32)],
+        in_specs=[hbm] * 9 + [vmem] * 2 + [hbm] * (len(inputs) - 15) + [vmem] * 4,
+        out_specs=[hbm] * 5 + [vmem],
         scratch_shapes=[
-            store(6, kv_rows, length), store(4, kv_rows, length), store(2, width, length), store(2, width, length),
-            store(width // 2, 2 * length), store(3, zsize, chips, strip, width),
+            store(6, kv_rows, length), store(2, width, length), store(2, width, length), store(2, width, length),
+            store(2, zsize, chips, strip, 2 * length), store(3, zsize, chips, strip, width),
             store(3, zsize, strip, width // 2), store(3, zsize, strip, width // 2),
             store(3, zsize, strip, width), store(3, zsize, strip, width),
             store(3, last, strip, width), store(3, strip, width),
             store(2, 3, rows, packed), store(rows, packed), store(last, rows, packed),
             store(zsize, rows, packed), store(rows, packed), store(rows, packed),
+            pltpu.VMEM((length, width), F32), store(length, width), pltpu.VMEM((8, width), F32), pltpu.VMEM((zsize + 2, 8, width), F32),
             pltpu.SemaphoreType.DMA((copies,)), pltpu.SemaphoreType.DMA((copies,)),
-            pltpu.SemaphoreType.DMA((4 * zsize + 13,)),
+            pltpu.SemaphoreType.DMA((6 * zsize + 14,)),
         ],
-        compiler_params=pltpu.CompilerParams(collective_id=1, has_side_effects=True, vmem_limit_bytes=60 * 2**20),
+        compiler_params=pltpu.CompilerParams(collective_id=1, has_side_effects=True, vmem_limit_bytes=62 * 2**20),
         name="tail",
     )(*inputs)
 
@@ -831,20 +933,22 @@
     folds = wide.shape[1] // fine
     fold = tall.shape[2] // folds
     two = wide.shape[2]
-    whole = len(refs) == 1
-    depth = 0 if whole else lax.axis_index("fsdp")
-    for s in range(1 if whole else zsize):
-        at = slice(None) if whole else lax.rem(depth + zsize - s, zsize)
-        lead = (slice(None),) if whole else ()
-        start(refs[s].at[(*lead, slice(None), pl.ds(0, two))], wide.at[at])
+    if len(refs) == 1:
+        sources = [(refs[0], slice(None), (slice(None),))]
+    else:
+        depth = lax.axis_index("fsdp")
+        pieces = [refs[0]] + ([refs[1].at[s] for s in range(zsize - 1)] if len(refs) == 2 else list(refs[1:]))
+        sources = [(piece, lax.rem(depth + zsize - s, zsize), ()) for s, piece in enumerate(pieces)]
+    for source, at, lead in sources:
+        start(source.at[(*lead, slice(None), pl.ds(0, two))], wide.at[at])
         for n in range(folds):
             cols = pl.ds(n * fold, fold)
-            start(refs[s].at[(*lead, pl.ds(n * fine, fine), pl.ds(two, fold))], tall.at[at, :, cols])
-
-
-def ffn_kernel(pieces, second, second_t, cot, *refs):
-    weights, (hidden_o, low_o), grads = refs[:pieces], refs[pieces:pieces + 2], refs[pieces + 2:2 * pieces + 2]
-    s_v, st_v, c_v, wi_v, wo_v, h_v, ht_v, l_v, w_v, t_v, sem = refs[2 * pieces + 2:]
+            start(source.at[(*lead, pl.ds(n * fine, fine), pl.ds(two, fold))], tall.at[at, :, cols])
+
+
+def ffn_kernel(given, pieces, before, second, second_t, cot, *refs):
+    weights, (hidden_o, low_o), grads = refs[:given], refs[given:given + 2], refs[given + 2:given + pieces + 2]
+    s_v, st_v, c_v, wi_v, wo_v, h_v, ht_v, l_v, w_v, t_v, sem = refs[given + pieces + 2:]
     tokens, width = second.shape
     zsize, fine = wo_v.shape[:2]
     rows = wi_v.shape[1]
@@ -915,29 +1019,31 @@
         copy.wait()
 
 
-def ffn_chunk(second, second_t, cot, weights, zsize, fine):
-    pieces = len(weights)
+def ffn_chunk(before, second, second_t, cot, weights, split, zsize, fine):
+    pieces = zsize if split else 1
     tokens, width = second.shape
     chunk = zsize * fine
     rows = width // zsize
     folds = rows // fine
     shape = lambda *s: jax.ShapeDtypeStruct(s, BF)
     store = lambda *s: pltpu.VMEM(s, BF)
-    hbm = pl.BlockSpec(memory_space=pl.ANY)
+    hbm = pl.BlockSpec(memory_space=pltpu.HBM)
+    packed = weights[0].shape[-1]
+    piece = (rows, packed) if split else (zsize, rows, packed)
     out = pl.pallas_call(
-        functools.partial(ffn_kernel, pieces),
-        out_shape=[shape(tokens, chunk), shape(tokens, 2 * chunk)] + [shape(*w.shape) for w in weights],
-        in_specs=[hbm] * (3 + pieces),
+        functools.partial(ffn_kernel, len(weights), pieces),
+        out_shape=[shape(tokens, chunk), shape(tokens, 2 * chunk)] + [shape(*piece)] * pieces,
+        in_specs=[hbm] * (4 + len(weights)),
         out_specs=[hbm] * (2 + pieces),
         scratch_shapes=[
             store(tokens, width), store(width, tokens), store(tokens, width), store(zsize, rows, 2 * chunk), store(zsize, fine, width),
             store(tokens, chunk), store(chunk, tokens), store(tokens, 2 * chunk), store(zsize, rows, 2 * chunk), store(zsize, fine, width),
-            pltpu.SemaphoreType.DMA((5 + zsize + pieces * (2 * folds + 1),)),
+            pltpu.SemaphoreType.DMA((5 + zsize + 2 * zsize * (folds + 1),)),
         ],
-        cost_estimate=pl.CostEstimate(flops=16 * 10**9, bytes_accessed=24 * 2**20, transcendentals=0),
+        cost_estimate=NO_COST,
         compiler_params=pltpu.CompilerParams(vmem_limit_bytes=50 * 2**20),
         name="ffn_chunk",
-    )(second, second_t, cot, *weights)
+    )(before, second, second_t, cot, *weights)
     return out[0], out[1], out[2:]
 
 def combine_kernel(counts, *refs):
@@ -999,7 +1105,7 @@
     tokens, chunk = hidden[0].shape
     rows = weights[0][0].shape[-2]
     width = rows * zsize
-    hbm = pl.BlockSpec(memory_space=pl.ANY)
+    hbm = pl.BlockSpec(memory_space=pltpu.HBM)
     shape = jax.ShapeDtypeStruct((tokens, width), F32)
     inputs = [*hidden, *low] + [piece for w in weights for piece in w]
     return pl.pallas_call(
@@ -1013,7 +1119,7 @@
             pltpu.VMEM((2, 256, width), F32), pltpu.VMEM((2, 256, width), F32),
             pltpu.SemaphoreType.DMA((2 * count + sum(counts) * (1 + rows // fine) + 2 * (tokens // 256),)),
         ],
-        cost_estimate=pl.CostEstimate(flops=26 * 10**9, bytes_accessed=48 * 2**20, transcendentals=0),
+        cost_estimate=NO_COST,
         compiler_params=pltpu.CompilerParams(vmem_limit_bytes=56 * 2**20),
         name="ffn_combine",
     )(*inputs)
@@ -1059,10 +1165,222 @@
             flat(width), flat(width), flat(width),
         ],
         out_specs=[flat(ff * zsize), flat(ff * zsize), pl.BlockSpec((ff // steps, width), lambda i: (i, 0)), flat(width), flat(width), flat(width // 2), flat(width // 2)],
-        cost_estimate=pl.CostEstimate(flops=0, bytes_accessed=39 * 2**20, transcendentals=0),
+        cost_estimate=NO_COST,
         compiler_params=pltpu.CompilerParams(vmem_limit_bytes=40 * 2**20),
         name="assemble",
     )(packs, packs, o, q, kv)
+
+
+MESH = pl.DeviceIdType.MESH
+
+
+class Mover:
+    def __init__(self, send_sems, recv_sems, local_sems):
+        self.sems = send_sems, recv_sems, local_sems
+        self.sent, self.kept, self.counts = [], [], [0, 0]
+
+    def send(self, src, dst, target):
+        k = self.counts[0]
+        self.counts[0] += 1
+        copy = pltpu.make_async_remote_copy(
+            src_ref=src, dst_ref=dst, send_sem=self.sems[0].at[k], recv_sem=self.sems[1].at[k], device_id=target, device_id_type=MESH
+        )
+        copy.start()
+        self.sent.append(copy)
+        return copy
+
+    def local(self, src, dst):
+        k = self.counts[1]
+        self.counts[1] += 1
+        copy = pltpu.make_async_copy(src, dst, self.sems[2].at[k])
+        copy.start()
+        return copy
+
+    def settle(self, copy):
+        copy.wait_send()
+        self.sent = [other for other in self.sent if other is not copy]
+
+    def finish(self):
+        for copy in self.sent:
+            copy.wait_send()
+        for copy in self.kept:
+            copy.wait()
+
+
+def greet_other_core():
+    index, depth = lax.axis_index("ctx"), lax.axis_index("fsdp")
+    core = lax.rem(index, 2)
+    other = (index + 1 - 2 * core, depth)
+    barrier = pltpu.get_barrier_semaphore()
+    pl.semaphore_signal(barrier, inc=1, device_id=other, device_id_type=MESH)
+    pl.semaphore_wait(barrier, 1)
+    return core, other
+
+
+def bridge_kernel(att, weight, x, gain, middle, second, second_t, att_half, att_s, w_s, low_s, low_t, ss, rs, ls):
+    core, other = greet_other_core()
+    move = Mover(ss, rs, ls)
+    zsize, chips, _, strip, length = att.shape
+    width = x.shape[1]
+    loads = [move.local(att, att_s), move.local(weight, w_s)]
+    arrive = [move.send(att.at[:, :, 1 - core], att_half.at[:, :, :, pl.ds(length, length)], other)]
+    for copy in loads:
+        copy.wait()
+    move.kept.append(move.local(att_s.at[:, :, core], att_half.at[:, :, :, pl.ds(0, length)]))
+    tile = 128
+    for t in range(length // tile):
+        rows = slice(tile * t, tile * (t + 1))
+        left = att_s[:, :, :, :, rows].reshape(width, tile).astype(F32).T.astype(BF)
+        y = x[rows].astype(F32) + jnp.dot(left, w_s[...], preferred_element_type=F32)
+        middle[rows] = y
+        inverse = lax.rsqrt(jnp.mean(y * y, -1, keepdims=True) + EPS)
+        normed = y * inverse * gain[...]
+        low_s[rows] = normed.astype(BF)
+        low_t[:, rows] = normed.T.astype(BF)
+        here, there = pl.ds(tile * t, tile), pl.ds(length + tile * t, tile)
+        arrive.append(move.send(low_s.at[here], second.at[there], other))
+        arrive.append(move.send(low_t.at[:, here], second_t.at[:, there], other))
+    move.kept.append(move.local(low_s, second.at[pl.ds(0, length)]))
+    move.kept.append(move.local(low_t, second_t.at[:, pl.ds(0, length)]))
+    for copy in arrive:
+        copy.wait_recv()
+    move.finish()
+
+
+def bridge(attended, weight, x, gain, zsize, chips):
+    width, length = attended.shape
+    strip = width // (zsize * chips * 2)
+    hbm, vmem = pl.BlockSpec(memory_space=pltpu.HBM), pl.BlockSpec(memory_space=pltpu.VMEM)
+    steps = length // 128
+    return pl.pallas_call(
+        bridge_kernel,
+        out_shape=[
+            jax.ShapeDtypeStruct((length, width), F32), jax.ShapeDtypeStruct((2 * length, width), BF),
+            jax.ShapeDtypeStruct((width, 2 * length), BF), jax.ShapeDtypeStruct((zsize, chips, strip, 2 * length), BF),
+        ],
+        in_specs=[hbm, hbm, vmem, vmem],
+        out_specs=[vmem, hbm, hbm, hbm],
+        scratch_shapes=[
+            pltpu.VMEM((zsize, chips, 2, strip, length), BF), pltpu.VMEM((width, width), BF),
+            pltpu.VMEM((length, width), BF), pltpu.VMEM((width, length), BF),
+            pltpu.SemaphoreType.DMA((1 + 2 * steps,)), pltpu.SemaphoreType.DMA((1 + 2 * steps,)), pltpu.SemaphoreType.DMA((5,)),
+        ],
+        compiler_params=pltpu.CompilerParams(collective_id=2, has_side_effects=True, vmem_limit_bytes=40 * 2**20),
+        cost_estimate=NO_COST,
+        name="bridge",
+    )(attended.reshape(zsize, chips, 2, strip, length), weight, x, gain)
+
+
+def middle_kernel(counts, *refs):
+    count = len(counts)
+    hidden, low = refs[:count], refs[count:2 * count]
+    weights, at = [], 2 * count
+    for n in counts:
+        weights.append(refs[at:at + n])
+        at += n
+    y_in, cot_in, gain, out_w = refs[at:at + 4]
+    layer_out, middle_grad, low_t, att_grad, gain_part = refs[at + 4:at + 9]
+    h_v, l_v, wi_v, wo_v, send_s, got, own, out_s, ss, rs, ls = refs[at + 9:]
+    core, other = greet_other_core()
+    move = Mover(ss, rs, ls)
+    tokens, chunk = hidden[0].shape
+    length, width = y_in.shape
+    loads = []
+    load = lambda src, dst: loads.append(move.local(src, dst))
+    late = []
+    for r in range(count):
+        load(low[r], l_v.at[:, pl.ds(2 * r * chunk, 2 * chunk)])
+    for r in range(count):
+        unfold(weights[r], wi_v.at[:, :, pl.ds(2 * r * chunk, 2 * chunk)], wo_v.at[r], load)
+    for r in range(count):
+        late.append(move.local(hidden[r], h_v.at[:, pl.ds(r * chunk, chunk)]))
+    nt = (((1,), (1,)), ((), ()))
+    tile = tokens // 4
+
+    def grad_tile(t):
+        return lax.dot_general(
+            l_v[tile * t:tile * (t + 1)], wi_v[...].reshape(width, 2 * count * chunk), nt, preferred_element_type=F32
+        )
+
+    def out_tile(t):
+        return jnp.dot(h_v[tile * t:tile * (t + 1)], wo_v[...].reshape(count * chunk, width), preferred_element_type=F32)
+
+    for copy in loads:
+        copy.wait()
+    there = []
+    for n in range(2):
+        send_s[n] = grad_tile(2 + n)
+        there.append(move.send(send_s.at[n], got.at[n], other))
+    for n in range(2):
+        own[tile * n:tile * (n + 1)] = grad_tile(n)
+    load_out = move.local(out_w, wi_v.at[:, :, pl.ds(0, width)])
+    for copy in late:
+        copy.wait()
+    for n in range(2):
+        move.settle(there[n])
+        send_s[n] = out_tile(2) if n == 0 else out_tile(1) + y_in[tile:2 * tile]
+        there.append(move.send(send_s.at[n], got.at[2 + n], other))
+    there[0].wait_recv()
+    there[1].wait_recv()
+    gain_part[...] = jnp.zeros(gain_part.shape, F32)
+    step = 128
+
+    for t in range(length // step):
+        part = slice(step * t, step * (t + 1))
+        y = y_in[part]
+        inverse = lax.rsqrt(jnp.mean(y * y, -1, keepdims=True) + EPS)
+        unit = y * inverse
+        d = own[part] + got[step * t // tile, step * t % tile:step * t % tile + step]
+        gain_part[...] += jnp.sum(d * unit, axis=0, keepdims=True)
+        scaled = d * gain[...]
+        g = cot_in[step * t // tile, step * t % tile:step * t % tile + step].astype(F32)
+        g = g + inverse * (scaled - unit * jnp.mean(scaled * unit, -1, keepdims=True))
+        middle_grad[part] = g
+        low_t[:, part] = g.T.astype(BF)
+    load_out.wait()
+    rows = wi_v.shape[1]
+    for z in range(wi_v.shape[0]):
+        att_grad[z * rows:(z + 1) * rows] = jnp.dot(wi_v[z, :, 0:width], low_t[...], preferred_element_type=F32).astype(BF)
+    first, last = out_tile(0) + y_in[0:tile], out_tile(3)
+    there[2].wait_recv()
+    out_s[0] = (first + got[2]).astype(BF)
+    there[3].wait_recv()
+    out_s[1] = (last + got[3]).astype(BF)
+    move.kept.append(move.local(out_s.at[0], layer_out.at[core]))
+    move.kept.append(move.local(out_s.at[1], layer_out.at[1 - core]))
+    move.finish()
+
+
+def middle_part(hidden, low, weights, y, cot, gain, out_w, zsize, fine):
+    counts = tuple(len(w) for w in weights)
+    count = len(counts)
+    tokens, chunk = hidden[0].shape
+    length, width = y.shape
+    rows = width // zsize
+    hbm, vmem = pl.BlockSpec(memory_space=pltpu.HBM), pl.BlockSpec(memory_space=pltpu.VMEM)
+    inputs = [*hidden, *low] + [piece for w in weights for piece in w]
+    tile = tokens // 4
+    return pl.pallas_call(
+        functools.partial(middle_kernel, counts),
+        out_shape=[
+            jax.ShapeDtypeStruct((2, length // 2, width), BF), jax.ShapeDtypeStruct((length, width), F32),
+            jax.ShapeDtypeStruct((width, length), BF), jax.ShapeDtypeStruct((width, length), BF),
+            jax.ShapeDtypeStruct((1, width), F32),
+        ],
+        in_specs=[hbm] * len(inputs) + [vmem, vmem, vmem, hbm],
+        out_specs=[hbm] + [vmem] * 4,
+        scratch_shapes=[
+            pltpu.VMEM((tokens, count * chunk), BF), pltpu.VMEM((tokens, 2 * count * chunk), BF),
+            pltpu.VMEM((zsize, rows, 2 * count * chunk), BF), pltpu.VMEM((count, zsize, fine, width), BF),
+            pltpu.VMEM((2, tile, width), F32), pltpu.VMEM((4, tile, width), F32),
+            pltpu.VMEM((length, width), F32), pltpu.VMEM((2, tile, width), BF),
+            pltpu.SemaphoreType.DMA((4,)), pltpu.SemaphoreType.DMA((4,)),
+            pltpu.SemaphoreType.DMA((2 * count + count * zsize * (1 + rows // fine) + 3,)),
+        ],
+        compiler_params=pltpu.CompilerParams(collective_id=3, has_side_effects=True, vmem_limit_bytes=61 * 2**20),
+        cost_estimate=LONG,
+        name="middle",
+    )(*inputs, y, cot[:2], gain, out_w.reshape(zsize, rows, width))
 
 
 def mm(left, right, left_dim, right_dim):
@@ -1172,10 +1490,6 @@
     chunk = fine * zsize
     kv_rows = KEY_HEADS * HEAD_WIDTH
 
-    cot_there = swap(cotangent)
-    cot = jnp.concatenate(
-        [pick(cotangent, core), pick(cot_there, core), pick(cot_there, 1 - core), pick(cotangent, 1 - core)]
-    )
     length = 2 * slice_len
 
     ids_all = jnp.concatenate([pick(block_pairs, index ^ r) for r in range(ctx)])
@@ -1192,21 +1506,17 @@
 
     packs, keys, values = {}, {}, {}
     folds = rows // fine
-    fast = chips == 4 and strip % 16 == 0 and fine % 128 == 0
+    fast = chips == 4 and strip % 16 == 0 and fine % 128 == 0 and pack_width(rows, fine, zsize, width) == width
     if fast:
-        (key_value_full, query_full, output_full, pack, far_pack, x, first, query, gains_full, *kv) = front(
-            tokens, jnp.stack([attention_gain, feedforward_gain]).astype(F32), key_matrix, value_matrix, query_weight,
+        (key_value_full, query_full, output_full, pack, rest, pack_x, pack_y, far_pack, cot, first_half, x_low, first, query, gains_full, *kv) = front(
+            tokens, cotangent, jnp.stack([attention_gain, feedforward_gain]).astype(F32), key_matrix, value_matrix, query_weight,
             output_weight, gate_weight, up_weight, down_weight, cosine, sine, zsize, ctx,
         )
         key_value_full, query_full, output_full = (w.reshape(width, width) for w in (key_value_full, query_full, output_full))
-        packs[0] = [pack]
+        packs[0], packs[1], packs[2] = [pack, rest], [pack_x, hop(rest, 1)], [pack_y, hop(rest, 2)]
         for r in range(chips):
             keys[r], values[r] = kv[r], kv[chips + r]
-        x = x.astype(F32)
         gain_first, gain_second = gains_full[0], gains_full[1]
-        inverse_first = lax.rsqrt(jnp.mean(x * x, -1, keepdims=True) + EPS)
-        unit_first = x * inverse_first
-        first_t = jnp.transpose(first)
         packs[diag] = [far_pack] + [shift(far_pack, s) for s in range(1, zsize)]
     else:
         gate_cut = gate_weight.reshape(rows, zsize, 2, chips, fine)
@@ -1263,59 +1573,82 @@
         query = rotate(mm(query_full, first_t, 0, 0), cosine, sine).astype(BF)
         packs[diag] = [depth_gather(own_piece(diag), depth)]
 
-    for r in near:
-        packs[r] = [hop(packs[0][0], r)]
+        for r in near:
+            packs[r] = [hop(packs[0][0], r)]
+        cot_there = swap(cotangent)
+        cot = jnp.concatenate(
+            [pick(cotangent, core), pick(cot_there, core), pick(cot_there, 1 - core), pick(cotangent, 1 - core)]
+        )
 
     key_list = [keys[r] for r in range(chips)]
     value_list = [values[r] for r in range(chips)]
     attended, log_total = attn_fwd(ids, order, query, key_list, value_list, KEY_HEADS)
 
-    middle = x + mm(attended, output_full, 0, 0)
-    inverse_second = lax.rsqrt(jnp.mean(middle * middle, -1, keepdims=True) + EPS)
-    unit_second = middle * inverse_second
-    second = (unit_second * gain_second).astype(BF)
-    second = jnp.concatenate([second, swap(second)])
-    second_t = jnp.transpose(second)
+    if fast:
+        middle, second, second_t, att_half = bridge(attended, output_full, x_low, gain_second[None], zsize, chips)
+    else:
+        middle = x + mm(attended, output_full, 0, 0)
+        inverse_second = lax.rsqrt(jnp.mean(middle * middle, -1, keepdims=True) + EPS)
+        unit_second = middle * inverse_second
+        second = (unit_second * gain_second).astype(BF)
+        second = jnp.concatenate([second, swap(second)])
+        second_t = jnp.transpose(second)
     grads, hidden, low = {}, {}, {}
+    before = second
     for r in [0] + list(near) + [diag]:
-        hidden[r], low[r], grads[r] = ffn_chunk(second, second_t, cot, packs[r], zsize, fine)
+        before, low[r], grads[r] = ffn_chunk(
+            before, second, second_t, cot.reshape(2 * length, width), packs[r], fast and r == diag, zsize, fine
+        )
+        hidden[r] = before
     every = range(chips)
-    out_part, second_grad = combine([hidden[r] for r in every], [low[r] for r in every], [packs[r] for r in every], zsize, fine)
-
-    q = slice_len
-    out_part = jnp.concatenate([out_part[:length] + middle, out_part[length:]])
-    came = swap(jnp.concatenate([out_part[2 * q:3 * q], out_part[q:2 * q]]))
-    out_here = (out_part[:q] + came[:q]).astype(BF)
-    out_there = (out_part[3 * q:] + came[q:]).astype(BF)
-
-    def stored(here, there):
-        return jnp.where(core == 0, jnp.stack([here, there]), jnp.stack([there, here]))
-
-    layer_out = stored(out_here, out_there)
-
-    second_grad = second_grad[:length] + swap(second_grad[length:])
-    gain_second_part = jnp.sum(second_grad * unit_second, 0)
-    middle_grad = cot[:length].astype(F32) + norm_back(second_grad, unit_second, inverse_second, gain_second)
-
-    def halves(a):
-        cut = a.reshape(zsize, chips, 2, strip, length)
-        here = pick(cut, core, 2).reshape(-1, length)
-        there = swap(pick(cut, 1 - core, 2).reshape(-1, length))
-        return jnp.concatenate([here, there], 1)
-
-    first_half = halves(first_t)
-    middle_low = middle_grad.astype(BF)
-    out_part_grad = mm(halves(attended), jnp.concatenate([middle_low, swap(middle_low)]), 1, 0)
-    attended_grad = mm(output_full, middle_low, 1, 1).astype(BF)
+    hidden, low, packs = ([a[r] for r in every] for a in (hidden, low, packs))
+
+    if fast:
+        layer_out, middle_grad, middle_t, attended_grad, gain_second_part = middle_part(
+            hidden, low, packs, middle, cot, gain_second[None], output_full, zsize, fine
+        )
+    else:
+        out_part, second_grad = combine(hidden, low, packs, zsize, fine)
+
+        q = slice_len
+        out_part = jnp.concatenate([out_part[:length] + middle, out_part[length:]])
+        came = swap(jnp.concatenate([out_part[2 * q:3 * q], out_part[q:2 * q]]))
+        out_here = (out_part[:q] + came[:q]).astype(BF)
+        out_there = (out_part[3 * q:] + came[q:]).astype(BF)
+
+        def stored(here, there):
+            return jnp.where(core == 0, jnp.stack([here, there]), jnp.stack([there, here]))
+
+        layer_out = stored(out_here, out_there)
+
+        second_grad = second_grad[:length] + swap(second_grad[length:])
+        gain_second_part = jnp.sum(second_grad * unit_second, 0)
+        middle_grad = cot[:length].astype(F32) + norm_back(second_grad, unit_second, inverse_second, gain_second)
+
+        def halves(a):
+            cut = a.reshape(zsize, chips, 2, strip, length)
+            here = pick(cut, core, 2).reshape(-1, length)
+            there = swap(pick(cut, 1 - core, 2).reshape(-1, length))
+            return jnp.concatenate([here, there], 1)
+
+        first_half = halves(first_t)
+        middle_low = middle_grad.astype(BF)
+        out_part_grad = mm(halves(attended), jnp.concatenate([middle_low, swap(middle_low)]), 1, 0)
+        attended_grad = mm(output_full, middle_low, 1, 1).astype(BF)
+
     query_low, key_parts, value_parts = attn_bwd(
         ids, order, query, attended, attended_grad, log_total, cosine, sine, key_list, value_list, KEY_HEADS
     )
     if fast:
-        o_all, q_all, kv_all, pack_all, kv_low = tail(
+        o_all, q_all, kv_all, pack_all, tokens_grad, gain_sums = tail(
             key_parts, value_parts, query_low, cosine, sine, first_half,
-            out_part_grad.astype(BF).reshape(zsize, chips, strip, width),
+            att_half,
             [grads[0][0], hop(grads[1][0], 1), hop(grads[2][0], 2)],
-            [grads[diag][0]] + [shift(grads[diag][s], s) for s in range(1, zsize)], zsize, chips,
+            [grads[diag][0]] + [shift(grads[diag][s], s) for s in range(1, zsize)],
+            middle_t, query_full, key_value_full, x_low, middle_grad, gain_first[None], gain_second_part, zsize, chips,
+        )
+        gain_first_grad, gain_second_grad = (
+            lax.dynamic_slice_in_dim(gain_sums[n], depth * rows, rows) for n in range(2)
         )
         gate_grad, up_grad, down_grad, output_grad, query_grad, key_grad, value_grad = assemble(
             pack_all, *(a.reshape(rows, width) for a in (o_all, q_all, kv_all)), zsize, fine
@@ -1357,34 +1690,35 @@
         up_grad = jnp.transpose(wide_all[:, :, :, 1], (2, 3, 1, 0, 4)).reshape(rows, -1).astype(F32)
         key_grad, value_grad = kv_grad[:, :kv_rows], kv_grad[:, kv_rows:]
 
-    first_grad = mm(query_low, query_full, 0, 1) + mm(kv_low, key_value_full, 0, 1)
-    gain_first_part = jnp.sum(first_grad * unit_first, 0)
-    tokens_part = (middle_grad + norm_back(first_grad, unit_first, inverse_first, gain_first)).astype(BF)
-    tokens_grad = stored(tokens_part[:q], swap(tokens_part[q:]))
-
-    def gain_total(part):
-        cut = part.reshape(zsize, rows)
-        total = pick(cut, depth)
-        for s in range(1, zsize):
-            total = total + lax.ppermute(
-                pick(cut, lax.rem(depth + s, zsize)), "fsdp", [(k, (k + s) % zsize) for k in range(zsize)]
-            )
-        total = total + swap(total)
-        bit = 1
-        while bit < chips:
-            total = total + hop(total, bit)
-            bit *= 2
-        return total
+        def gain_total(part):
+            cut = part.reshape(zsize, rows)
+            total = pick(cut, depth)
+            for s in range(1, zsize):
+                total = total + lax.ppermute(
+                    pick(cut, lax.rem(depth + s, zsize)), "fsdp", [(k, (k + s) % zsize) for k in range(zsize)]
+                )
+            total = total + swap(total)
+            bit = 1
+            while bit < chips:
+                total = total + hop(total, bit)
+                bit *= 2
+            return total
+
+        first_grad = mm(query_low, query_full, 0, 1) + mm(kv_low, key_value_full, 0, 1)
+        gain_first_part = jnp.sum(first_grad * unit_first, 0)
+        tokens_part = (middle_grad + norm_back(first_grad, unit_first, inverse_first, gain_first)).astype(BF)
+        tokens_grad = stored(tokens_part[:q], swap(tokens_part[q:]))
+        gain_first_grad, gain_second_grad = gain_total(gain_first_part), gain_total(gain_second_part)
 
     return (
         layer_out,
         tokens_grad,
-        gain_total(gain_first_part),
+        gain_first_grad,
         query_grad,
         key_grad,
         value_grad,
         output_grad,
-        gain_total(gain_second_part),
+        gain_second_grad,
         gate_grad,
         up_grad,
         down_grad,

time: 815 us -> 617 us (0.76)
  waiting for transfers between devices: 83.7 us -> 13.4 us
  starting transfers between devices: 50 us -> 13.2 us
  matrix products: 31.7 us -> 0 us
  other arithmetic: 33.4 us -> 1.74 us
  local copies, waits for them, and re-layouts: 49.1 us -> 32.7 us
    ppermute x6, waiting for transfers between devices: 76.3 us -> 0.02 us  [shift(): return lax.ppermute(a, 'fsdp', [(i, (i + s) % n) for i in range(n)])]
    dot_general x5 -> x0, matrix products: 31.7 us -> none  [mm(): lax.dot_general(left, right, (((left_dim,), (right_dim,)), ((), ())), pre...]
    ppermute x6, starting transfers between devices: 32.4 us -> 9.12 us  [shift(): return lax.ppermute(a, 'fsdp', [(i, (i + s) % n) for i in range(n)])]
    pallas_call x1, Pallas kernels: 160 us -> 138 us  [front(): pl.pallas_call(functools.partial(front_kernel, zsize), out_shape=[square,...]
    pallas_call x5 -> x6, Pallas kernels: 97.2 us -> 119 us  [the longest x4 67.8 us: ffn_chunk(): pl.pallas_call(functools.partial(ffn_kernel, len(weights), pieces), out_s...]
    pallas_call x1, Pallas kernels: 220 us -> 205 us  [tail(): pl.pallas_call(functools.partial(tail_kernel, zsize), out_shape=[shape(ch...]
    ppermute x16 -> x0, starting transfers between devices: 9.84 us -> none  [the longest x6 8.2 us: gain_total(): lax.ppermute(pick(cut, lax.rem(depth + s, zsize)), 'fsdp', [(k, (k + s) %...]
    convert_element_type x3 -> x0, other arithmetic: 9.01 us -> none  [the longest x1 6.6 us: body(): middle_low = middle_grad.astype(BF)]
  transfers between devices with their start and end apart: 30 -> 10, of which waited for: 11 -> 2; matrix products, arithmetic and copies ran while one was open for 9% -> 1% of each run, Pallas kernels for 40% -> 29%
where the time goes in v5:
time: 617 us; the launch traced here: 612 us
  Pallas kernels  550 us (89%)
  local copies, waits for them, and re-layouts  32.7 us (5%)
  waiting for transfers between devices  13.4 us (2%)
  starting transfers between devices  13.2 us (2%)
    pallas_call x1, Pallas kernels, tail(): pl.pallas_call(functools.partial(tail_kernel, zsize), out_shape=[shape(ch...  205 us
    pallas_call x1, Pallas kernels, front(): pl.pallas_call(functools.partial(front_kernel, zsize), out_shape=[square,...  138 us
    pallas_call x4, Pallas kernels, ffn_chunk(): pl.pallas_call(functools.partial(ffn_kernel, len(weights), pieces), out_s...  67.8 us
    pallas_call x1, Pallas kernels, attn_bwd(): pl.pallas_call(functools.partial(bwd_kernel, nchip, per), grid_spec=grid_...  47.6 us
    pallas_call x1, Pallas kernels, middle_part(): pl.pallas_call(functools.partial(middle_kernel, counts), out_shape=[jax.S...  41.2 us
    pallas_call x1, Pallas kernels, attn_fwd(): pl.pallas_call(functools.partial(fwd_kernel, nchip, per), grid_spec=grid_...  30.8 us
    unnamed x58, local copies, waits for them, and re-layouts  25.2 us
    ppermute x4, waiting for transfers between devices, hop(): lax.ppermute(a, 'ctx', [(i, i ^ 2 * r) for i in range(lax.axis_size('ctx'...  13.4 us
  transfers between devices with their start and end apart: 10, of which 2 were waited for; matrix products, arithmetic and copies ran while one was open for 1% of the time, Pallas kernels for 29%

profile of v5, /device:TPU:0, one launch (start us, length us, event | category | flops | bytes accessed | tf_op | source)
XLA Modules:
  0.0 612.5 jit_solution(13173911148553365350)
XLA Ops:
  0.7 1.3 fusion.9
  2.7 0.7 stack.10
  3.4 0.7 stack.9
  4.5 1.1 copy-done.21
  5.6 1.1 copy-done.22
  6.7 138.3 %front.1 = (bf16[4,4,2,48,1536]{4,3,2,1,0:T(8,128)(2,1)}, bf16[4,4,2,48,1536]{4,3,2,1,0:T(8,128)(2,1)}, bf16[4,4,2,48,1536]{4,3,2,1,0:T(8,128)(2,1)}, bf16[384,1...) custom-call(bf16[2,256,1536]{2,1,0:T(8,128)(2,1)} %refs_0_.1, ...), custom_call_target="tpu_custom_call" | custom-call | tf_op jit(solution)/shard_map/front/pallas_call | solution.py:521
  145.0 0.9 copy-done.18
  145.9 0.9 copy-done.19
  146.8 1.0 copy-done.20
  147.8 0.9 collective-permute-start
  148.7 1.2 collective-permute-start.1
  149.8 1.9 collective-permute-start.2
  152.2 2.2 collective-permute-start.4
  154.3 2.7 slice.18.refs_19_
  157.1 0.6 select_reduce_fusion.inv_ref
  157.7 30.8 %attention_forward.1 = (bf16[1536,512]{1,0:T(8,128)(2,1)}, f32[8,4,1,256]{3,2,1,0:T(1,128)}) custom-call(s32[4]{0:T(128)} %get-tuple-element.158.ids_ref, s32[16]{0:T(128)} %select_reduce_fusion.inv_ref, bf16[1536,512]{1,0:T(8,128)(2,1)} %get-tuple-element.80.q_ref, bf16[768,512]{1,0:T(8,128)(2,1)} %copy-done.18, bf16[768,512]{1,0:T(8,128)(2,1)} %copy-done.19, ...), custom_call_target="tpu_custom_call" | custom-call | tf_op jit(solution)/shard_map/attention_forward/pallas_call | solution.py:134
  188.5 0.6 fusion.11
  189.1 1.4 copy-done.5
  190.5 9.5 %bridge.1 = (f32[512,1536]{1,0:T(8,128)S(1)}, bf16[1024,1536]{1,0:T(8,128)(2,1)S(1)}, bf16[1536,1024]{1,0:T(8,128)(2,1)S(1)}, bf16[4,4,48,1024]{3,2,1,0:T(8,128)(2,1)S(1)}) custom-call(bf16[4,4,2,48,512]{4,3,2,1,0:T(8,128)(2,1)S(1)} %bitcast.15, bf16[1536,1536]{1,0:T(8,128)(2,1)} %bitcast.27, bf16[512,1536]{1,0:T(8,128)(2,1)S(1)} %copy-done.3, ...), custom_call_target="tpu_custom_call" | custom-call | tf_op jit(solution)/shard_map/bridge/pallas_call | solution.py:1255
  200.0 1.7 copy-done
  201.7 1.7 copy-done.1
  203.4 1.2 copy-done.4
  204.6 1.6 copy-done.24
  206.3 16.5 %ffn_chunk.4 = (bf16[1024,512]{1,0:T(8,128)(2,1)S(1)}, bf16[1024,1024]{1,0:T(8,128)(2,1)}, bf16[4,384,1536]{2,1,0:T(8,128)(2,1)}) custom-call(bf16[1024,1536]{1,0:T(8,128)(2,1)} %copy-done, bf16[1024,1536]{1,0:T(8,128)(2,1)} %copy-done, bf16[1536,1024]{1,0:T(8,128)(2,1)} %copy-done.1, bf16[1024,1536]{1,0:T(8,128)(2,1)} %bitcast.21, ...), custom_call_target="tpu_custom_call" | custom-call | tf_op jit(solution)/shard_map/ffn_chunk/pallas_call | solution.py:1033
  222.9 17.3 %ffn_chunk.5 = (bf16[1024,512]{1,0:T(8,128)(2,1)S(1)}, bf16[1024,1024]{1,0:T(8,128)(2,1)}, bf16[4,384,1536]{2,1,0:T(8,128)(2,1)}) custom-call(bf16[1024,512]{1,0:T(8,128)(2,1)S(1)} %get-tuple-element.98.before.refs_0_, bf16[1024,1536]{1,0:T(8,128)(2,1)} %copy-done, bf16[1536,1024]{1,0:T(8,128)(2,1)} %copy-done.1, bf16[1024,1536]{1,0:T(8,128)(2,1)} %bitcast.22, ...), custom_call_target="tpu_custom_call" | custom-call | tf_op jit(solution)/shard_map/ffn_chunk/pallas_call | solution.py:1033
  240.2 16.7 %ffn_chunk.6 = (bf16[1024,512]{1,0:T(8,128)(2,1)S(1)}, bf16[1024,1024]{1,0:T(8,128)(2,1)}, bf16[4,384,1536]{2,1,0:T(8,128)(2,1)}) custom-call(bf16[1024,512]{1,0:T(8,128)(2,1)S(1)} %get-tuple-element.100.before.refs_1_, bf16[1024,1536]{1,0:T(8,128)(2,1)} %copy-done, bf16[1536,1024]{1,0:T(8,128)(2,1)} %copy-done.1, bf16[1024,1536]{1,0:T(8,128)(2,1)} %bitcast.23, ...), custom_call_target="tpu_custom_call" | custom-call | tf_op jit(solution)/shard_map/ffn_chunk/pallas_call | solution.py:1033
  257.0 17.2 %ffn_chunk.7 = (bf16[1024,512]{1,0:T(8,128)(2,1)S(1)}, bf16[1024,1024]{1,0:T(8,128)(2,1)}, bf16[384,1536]{1,0:T(8,128)(2,1)S(1)}, bf16[384,1536]{1,0:T(8,128)(2,...) custom-call(bf16[1024,512]{1,0:T(8,128)(2,1)S(1)} %get-tuple-element.102.before.refs_2_, ...), custom_call_target="tpu_custom_call" | custom-call | tf_op jit(solution)/shard_map/ffn_chunk/pallas_call | solution.py:1033
  274.3 1.0 copy-done.7
  275.3 1.0 copy-done.25
  276.4 2.4 collective-permute-start.8
  278.8 2.1 collective-permute-start.9
  280.9 0.9 collective-permute-start.6
  281.8 1.1 collective-permute-start.5
  282.9 41.2 %middle.1 = (bf16[2,256,1536]{2,1,0:T(8,128)(2,1)}, f32[512,1536]{1,0:T(8,128)}, bf16[1536,512]{1,0:T(8,128)(2,1)}, bf16[1536,512]{1,0:T(8,128)(2,1)}, f32[1,1536]{1,0:T(1,128)}) custom-call(bf16[1024,512]{1,0:T(8,128)(2,1)} %copy-done.13, bf16[1024,512]{1,0:T(8,128)(2,1)} %copy-done.14, bf16[1024,512]{1,0:T(8,128)(2,1)} %copy-done.15, ...), custom_call_target="tpu_custom_call" | custom-call | flops 199999995904 | tf_op jit(solution)/shard_map/middle/pallas_call | solution.py:1363
  324.1 47.6 %attention_backward.1 = (bf16[1536,512]{1,0:T(8,128)(2,1)}, bf16[768,512]{1,0:T(8,128)(2,1)}, bf16[768,512]{1,0:T(8,128)(2,1)}, bf16[768,512]{1,0:T(8,128)(2,1)}...) custom-call(s32[4]{0:T(128)} %get-tuple-element.158.ids_ref, ...), custom_call_target="tpu_custom_call" | custom-call | flops 199999995904 | tf_op jit(solution)/shard_map/attention_backward/pallas_call | solution.py:249
  371.7 12.5 %collective-permute-done.6.refs_15_ = bf16[4,384,1536]{2,1,0:T(8,128)(2,1)} collective-permute-done((bf16[4,384,1536]{2,1,0:T(8,128)(2,1)}, bf16[4,384,1536]{2,1,0:T(8,128)(2,1)}, u32[]{:S(2)}, u32[]{:S(2)}) %collective-permute-start.6) | collective-permute-done | bytes 4718624 | tf_op jit(solution)/shard_map/ppermute | solution.py:1395
  384.2 0.9 collective-permute-done.5.refs_14_
  385.1 205.4 %tail.1 = (bf16[4,2,48,1536]{3,2,1,0:T(8,128)(2,1)}, bf16[4,2,48,1536]{3,2,1,0:T(8,128)(2,1)}, bf16[4,2,48,1536]{3,2,1,0:T(8,128)(2,1)}, bf16[4,2,384,1536]{3,2,...) custom-call(bf16[768,512]{1,0:T(8,128)(2,1)} %get-tuple-element.113.refs_0_, ...), custom_call_target="tpu_custom_call" | custom-call | tf_op jit(solution)/shard_map/tail/pallas_call | solution.py:908
  590.5 0.9 fusion.10
  591.4 0.6 fusion
  592.0 3.7 copy-done.2
  595.7 1.3 copy-done.8
  596.9 1.3 copy-done.9
  598.2 1.3 copy-done.10
  599.5 9.4 %assemble.1 = (f32[384,4096]{1,0:T(8,128)}, f32[384,4096]{1,0:T(8,128)}, f32[1024,1536]{1,0:T(8,128)}, f32[384,1536]{1,0:T(8,128)}, f32[384,1536]{1,0:T(8,128)}, /*index=5*/f32[384,768]{1,0:T(8,128)}, f32[384,768]{1,0:T(8,128)}) custom-call(bf16[4,2,384,1536]{3,2,1,0:T(8,128)(2,1)S(1)} %copy-done.2, bf16[4,2,384,1536]{3,2,1,0:T(8,128)(2,1)S(1)} %copy-done.2, ...), custom_call_target="tpu_custom_call" | custom-call | tf_op jit(solution)/shard_map/assemble/pallas_call | solution.py:1158
  608.9 1.1 copy.25
  610.1 0.8 copy-done.27
  610.9 1.1 copy.26
  (55 shorter events, 1.8 us)
Async XLA Ops:
  4.5 140.5 %copy-start.16 = (f32[48,512]{1,0:T(8,128)}, f32[48,512]{1,0:T(8,128)S(1)}, u32[]{:S(2)}) copy-start(f32[48,512]{1,0:T(8,128)S(1)} %get-tuple-element.163.refs_11_.sin_ref.refs_10_) | copy-start | bytes 294916
  4.5 140.5 %copy-start.17 = (f32[48,512]{1,0:T(8,128)}, f32[48,512]{1,0:T(8,128)S(1)}, u32[]{:S(2)}) copy-start(f32[48,512]{1,0:T(8,128)S(1)} %get-tuple-element.164.refs_10_.cos_ref.refs_9_) | copy-start | bytes 294916
  4.5 1.1 copy-start.21
  5.6 1.1 copy-start.22
  145.0 0.9 copy-start.18
  145.9 0.9 copy-start.19
  146.8 1.0 copy-start.20
  147.8 75.0 %collective-permute-start = (bf16[3,384,1536]{2,1,0:T(8,128)(2,1)}, bf16[3,384,1536]{2,1,0:T(8,128)(2,1)}, u32[]{:S(2)}, u32[]{:S(2)}) collective-permute-start(bf16[3,384,1536]{2,1,0:T(8,128)(2,1)} %get-tuple-element.97.refs_1_.refs_9_), channel_id=1, source_target_pairs={{0,8},{4,12},{8,0},{12,4},{16,24},{20,28},{24,16},{28,20},{1,9},{5... | collective-permute-start | bytes 10616840 | tf_op jit(solution)/shard_map/ppermute | solution.py:1395
  148.7 91.5 %collective-permute-start.1 = (bf16[3,384,1536]{2,1,0:T(8,128)(2,1)}, bf16[3,384,1536]{2,1,0:T(8,128)(2,1)}, u32[]{:S(2)}, u32[]{:S(2)}) collective-permute-start(bf16[3,384,1536]{2,1,0:T(8,128)(2,1)} %get-tuple-element.97.refs_1_.refs_9_), channel_id=1, source_target_pairs={{0,16},{4,20},{8,24},{12,28},{16,0},{20,4},{24,8},{28,12},{1,17},{... | collective-permute-start | bytes 10616840 | tf_op jit(solution)/shard_map/ppermute | solution.py:1395
  149.8 107.1 %collective-permute-start.2 = (bf16[384,1536]{1,0:T(8,128)(2,1)}, bf16[384,1536]{1,0:T(8,128)(2,1)}, u32[]{:S(2)}, u32[]{:S(2)}) collective-permute-start(bf16[384,1536]{1,0:T(8,128)(2,1)} %get-tuple-element.103.refs_0_.refs_14_), channel_id=1, source_target_pairs={{0,1},{1,2},{2,3},{3,0},{4,5},{5,6},{6,7},{7,4},{8,9},{9,10},{10,1... | collective-permute-start | bytes 3538952 | tf_op jit(solution)/shard_map/ppermute | solution.py:1413
  151.7 105.3 %collective-permute-start.3 = (bf16[384,1536]{1,0:T(8,128)(2,1)}, bf16[384,1536]{1,0:T(8,128)(2,1)}, u32[]{:S(2)}, u32[]{:S(2)}) collective-permute-start(bf16[384,1536]{1,0:T(8,128)(2,1)} %get-tuple-element.103.refs_0_.refs_14_), channel_id=1, source_target_pairs={{0,2},{1,3},{2,0},{3,1},{4,6},{5,7},{6,4},{7,5},{8,10},{9,11},{10,... | collective-permute-start | bytes 3538952 | tf_op jit(solution)/shard_map/ppermute | solution.py:1413
  152.2 104.8 %collective-permute-start.4 = (bf16[384,1536]{1,0:T(8,128)(2,1)}, bf16[384,1536]{1,0:T(8,128)(2,1)}, u32[]{:S(2)}, u32[]{:S(2)}) collective-permute-start(bf16[384,1536]{1,0:T(8,128)(2,1)} %get-tuple-element.103.refs_0_.refs_14_), channel_id=1, source_target_pairs={{0,3},{1,0},{2,1},{3,2},{4,7},{5,4},{6,5},{7,6},{8,11},{9,8},{10,9... | collective-permute-start | bytes 3538952 | tf_op jit(solution)/shard_map/ppermute | solution.py:1413
  157.7 31.4 %copy-start.3 = (bf16[512,1536]{1,0:T(8,128)(2,1)S(1)}, bf16[512,1536]{1,0:T(8,128)(2,1)}, u32[]{:S(2)}) copy-start(bf16[512,1536]{1,0:T(8,128)(2,1)} %get-tuple-element.91.x.refs_23_) | copy-start | bytes 4718596
  189.1 10.9 %copy-start.23 = (f32[1,1536]{1,0:T(1,128)}, f32[1,1536]{1,0:T(1,128)S(1)}, u32[]{:S(2)}) copy-start(f32[1,1536]{1,0:T(1,128)S(1)} %get-tuple-element.162.gain.refs_20_) | copy-start | bytes 18436
  189.1 1.4 copy-start.5
  190.5 15.8 %copy-start.6 = (bf16[384,1536]{1,0:T(8,128)(2,1)S(1)}, bf16[384,1536]{1,0:T(8,128)(2,1)}, u32[]{:S(2)}) copy-start(bf16[384,1536]{1,0:T(8,128)(2,1)} %get-tuple-element.96.refs_0_.refs_8_) | copy-start | bytes 3538948
  200.0 1.7 copy-start
  201.7 1.7 copy-start.1
  203.4 1.2 copy-start.4
  204.6 1.6 copy-start.24
  206.3 16.6 %copy-start.11 = (bf16[384,1536]{1,0:T(8,128)(2,1)S(1)}, bf16[384,1536]{1,0:T(8,128)(2,1)}, u32[]{:S(2)}) copy-start(bf16[384,1536]{1,0:T(8,128)(2,1)} %get-tuple-element.99.refs_0_.refs_10_) | copy-start | bytes 3538948
  222.8 17.4 %copy-start.13 = (bf16[1024,512]{1,0:T(8,128)(2,1)}, bf16[1024,512]{1,0:T(8,128)(2,1)S(1)}, u32[]{:S(2)}) copy-start(bf16[1024,512]{1,0:T(8,128)(2,1)S(1)} %get-tuple-element.98.before.refs_0_) | copy-start | bytes 3145732
  222.8 17.4 %copy-start.12 = (bf16[384,1536]{1,0:T(8,128)(2,1)S(1)}, bf16[384,1536]{1,0:T(8,128)(2,1)}, u32[]{:S(2)}) copy-start(bf16[384,1536]{1,0:T(8,128)(2,1)} %get-tuple-element.101.refs_0_.refs_12_) | copy-start | bytes 3538948
  240.2 16.7 %copy-start.14 = (bf16[1024,512]{1,0:T(8,128)(2,1)}, bf16[1024,512]{1,0:T(8,128)(2,1)S(1)}, u32[]{:S(2)}) copy-start(bf16[1024,512]{1,0:T(8,128)(2,1)S(1)} %get-tuple-element.100.before.refs_1_) | copy-start | bytes 3145732
  257.0 17.3 %copy-start.15 = (bf16[1024,512]{1,0:T(8,128)(2,1)}, bf16[1024,512]{1,0:T(8,128)(2,1)S(1)}, u32[]{:S(2)}) copy-start(bf16[1024,512]{1,0:T(8,128)(2,1)S(1)} %get-tuple-element.102.before.refs_2_) | copy-start | bytes 3145732
  274.3 1.0 copy-start.7
  275.3 1.0 copy-start.25
  276.3 95.4 %collective-permute-start.7 = (bf16[384,1536]{1,0:T(8,128)(2,1)}, bf16[384,1536]{1,0:T(8,128)(2,1)}, u32[]{:S(2)}, u32[]{:S(2)}) collective-permute-start(bf16[384,1536]{1,0:T(8,128)(2,1)} %get-tuple-element.128), channel_id=1, source_target_pairs={{0,1},{1,2},{2,3},{3,0},{4,5},{5,6},{6,7},{7,4},{8,9},{9,10},{10,1... | collective-permute-start | bytes 3538952 | tf_op jit(solution)/shard_map/ppermute | solution.py:1413
  276.4 95.3 %collective-permute-start.8 = (bf16[384,1536]{1,0:T(8,128)(2,1)}, bf16[384,1536]{1,0:T(8,128)(2,1)}, u32[]{:S(2)}, u32[]{:S(2)}) collective-permute-start(bf16[384,1536]{1,0:T(8,128)(2,1)} %get-tuple-element.129), channel_id=1, source_target_pairs={{0,2},{1,3},{2,0},{3,1},{4,6},{5,7},{6,4},{7,5},{8,10},{9,11},{10,... | collective-permute-start | bytes 3538952 | tf_op jit(solution)/shard_map/ppermute | solution.py:1413
  278.8 92.9 %collective-permute-start.9 = (bf16[384,1536]{1,0:T(8,128)(2,1)}, bf16[384,1536]{1,0:T(8,128)(2,1)}, u32[]{:S(2)}, u32[]{:S(2)}) collective-permute-start(bf16[384,1536]{1,0:T(8,128)(2,1)} %get-tuple-element.130), channel_id=1, source_target_pairs={{0,3},{1,0},{2,1},{3,2},{4,7},{5,4},{6,5},{7,6},{8,11},{9,8},{10,9... | collective-permute-start | bytes 3538952 | tf_op jit(solution)/shard_map/ppermute | solution.py:1413
  280.9 103.3 %collective-permute-start.6 = (bf16[4,384,1536]{2,1,0:T(8,128)(2,1)}, bf16[4,384,1536]{2,1,0:T(8,128)(2,1)}, u32[]{:S(2)}, u32[]{:S(2)}) collective-permute-start(bf16[4,384,1536]{2,1,0:T(8,128)(2,1)} %get-tuple-element.126), channel_id=1, source_target_pairs={{0,16},{4,20},{8,24},{12,28},{16,0},{20,4},{24,8},{28,12},{1,17},{... | collective-permute-start | bytes 14155784 | tf_op jit(solution)/shard_map/ppermute | solution.py:1395
  281.8 103.3 %collective-permute-start.5 = (bf16[4,384,1536]{2,1,0:T(8,128)(2,1)}, bf16[4,384,1536]{2,1,0:T(8,128)(2,1)}, u32[]{:S(2)}, u32[]{:S(2)}) collective-permute-start(bf16[4,384,1536]{2,1,0:T(8,128)(2,1)} %get-tuple-element.125), channel_id=1, source_target_pairs={{0,8},{4,12},{8,0},{12,4},{16,24},{20,28},{24,16},{28,20},{1,9},{5... | collective-permute-start | bytes 14155784 | tf_op jit(solution)/shard_map/ppermute | solution.py:1395
  592.0 3.7 copy-start.2
  595.7 1.3 copy-start.8
  596.9 1.3 copy-start.9
  598.2 1.3 copy-start.10
  599.5 9.4 %copy-start.26 = (bf16[2,256,1536]{2,1,0:T(8,128)(2,1)S(1)}, bf16[2,256,1536]{2,1,0:T(8,128)(2,1)}, u32[]{:S(2)}) copy-start(bf16[2,256,1536]{2,1,0:T(8,128)(2,1)} %get-tuple-element.178) | copy-start | bytes 4718596
  608.9 2.0 copy-start.27

commit v6 on v5

--- a/solution.py
+++ b/solution.py
@@ -17,7 +17,7 @@
 BF = jnp.bfloat16
 F32 = jnp.float32
 NO_COST = pl.CostEstimate(flops=0, bytes_accessed=0, transcendentals=0)
-LONG = pl.CostEstimate(flops=200 * 10**9, bytes_accessed=0, transcendentals=0)
+LONG = pl.CostEstimate(flops=52 * 10**9, bytes_accessed=0, transcendentals=0)
 
 LOG2E = 1.4426950408889634
 NT = (((1,), (1,)), ((), ()))
@@ -141,7 +141,7 @@
     )(ids, inv, qT, *ks, *vs)
 
 
-def bwd_kernel(nchip, heads, ids_ref, inv_ref, q_ref, o_ref, do_ref, lse_ref, cos_ref, sin_ref, *rest):
+def bwd_kernel(nchip, heads, ids_ref, inv_ref, q_ref, o_ref, do_ref, lse_ref, cos_ref, sin_ref, before, *rest):
     dq_ref = rest[2 * nchip]
     dk_refs, dv_refs = rest[2 * nchip + 1:3 * nchip + 1], rest[3 * nchip + 1:4 * nchip + 1]
     kv_s, sem, knat, ktr, vnat = rest[4 * nchip + 1:4 * nchip + 6]
@@ -217,7 +217,7 @@
             dv_refs[r][96 * h:96 * (h + 1), lanes] = dv.astype(BF)
 
 
-def attn_bwd(ids, inv, qT, oT, doT, lse, cosine, sine, ks, vs, heads):
+def attn_bwd(before, ids, inv, qT, oT, doT, lse, cosine, sine, ks, vs, heads):
     nchip = len(ks)
     T = qT.shape[1]
     nq = T // BLK
@@ -237,7 +237,7 @@
         num_scalar_prefetch=2,
         grid=(heads // per,),
         in_specs=[wide, wide, wide, pl.BlockSpec((per, nq, 1, 2 * BLK), lambda g, *_: (g, 0, 0, 0))]
-        + [pl.BlockSpec((48, T), lambda g, *_: (0, 0))] * 2 + [pl.BlockSpec(memory_space=pltpu.HBM)] * (2 * nchip),
+        + [pl.BlockSpec((48, T), lambda g, *_: (0, 0))] * 2 + [pl.BlockSpec(memory_space=pltpu.HBM)] * (1 + 2 * nchip),
         out_specs=[wide] + [slim] * (2 * nchip),
         scratch_shapes=[
             pltpu.VMEM((2 * nchip, heads * 96, T), BF), pltpu.SemaphoreType.DMA((2 * nchip,)),
@@ -250,10 +250,10 @@
         functools.partial(bwd_kernel, nchip, per),
         grid_spec=grid_spec,
         out_shape=[jax.ShapeDtypeStruct((heads * 192, T), BF)] + [slab] * (2 * nchip),
-        cost_estimate=LONG,
+        cost_estimate=NO_COST,
         compiler_params=pltpu.CompilerParams(vmem_limit_bytes=56 * 2**20),
         name="attention_backward",
-    )(ids, inv, qT, oT, doT, lse, cosine, sine, *ks, *vs)
+    )(ids, inv, qT, oT, doT, lse, cosine, sine, before, *ks, *vs)
     return outs[0], outs[1:1 + nchip], outs[1 + nchip:]
 
 
@@ -314,8 +314,6 @@
     tokens_there = send(tok.at[1 - core], x_s.at[1], to_core)
     own_kv = [local(key_w, full_kv.at[depth, :, :, :, pl.ds(0, kv_rows)]), local(value_w, full_kv.at[depth, :, :, :, pl.ds(kv_rows, kv_rows)])]
     gain_s[depth] = gains[...]
-    for copy in own_kv:
-        copy.wait()
 
     weights = {"kv": full_kv, "q": full_q, "o": full_o}
     shards = {"q": query_w, "o": out_w}
@@ -324,8 +322,12 @@
     def ring_step(name, s):
         full = weights[name]
         place = full.at[slot(s - 1), chip, core]
-        source = shards[name].at[chip, core] if name in shards and s == 1 else place
-        moves[name, "ring", s] = send(source, place, to_next)
+        if name == "kv" and s == 1:
+            halves = ((key_w, pl.ds(0, kv_rows)), (value_w, pl.ds(kv_rows, kv_rows)))
+            moves[name, "ring", s] = [send(ref.at[chip, core], full.at[slot(0), chip, core, :, cols], to_next) for ref, cols in halves]
+        else:
+            source = shards[name].at[chip, core] if name in shards and s == 1 else place
+            moves[name, "ring", s] = [send(source, place, to_next)]
 
     def spread(name, s):
         place = weights[name].at[slot(s), chip, core]
@@ -378,22 +380,28 @@
     far_ffn += [local(cot_in.at[core], cot_s.at[0]), local(cot_in.at[1 - core], cot_s.at[1])]
     cot_moves = [send(cot_in.at[1 - core], cot.at[1], to_core), send(cot_in.at[core], cot.at[2], to_core)]
 
+    def around(name, s):
+        for copy in moves[name, "ring", s]:
+            copy.wait_recv()
+        if s < last:
+            ring_step(name, s + 1)
+
+    ring_step("q", 1)
+    ring_step("o", 1)
     for s in steps:
-        moves["kv", "ring", s].wait_recv()
         moves["gain", s].wait_recv()
         if s < last:
-            ring_step("kv", s + 1)
             gain_step(s + 1)
-        else:
-            for copy in own_ffn:
-                copy.wait()
-            ring_step("q", 1)
-            ffn_step(1)
+        around("kv", s)
         spread("kv", s)
+        around("q", s)
+        around("o", s)
+    for copy in own_ffn:
+        copy.wait()
+    ffn_step(1)
     for s in steps:
         forward("kv", s)
-        moves["q", "ring", s].wait_recv()
-        ring_step("q", s + 1) if s < last else ring_step("o", 1)
+    for s in steps:
         spread("q", s)
     for s in steps:
         cross("kv", s)
@@ -416,14 +424,12 @@
 
     lax.fori_loop(0, length // rows, normalize, 0)
 
-    moves["o", "ring", 1].wait_recv()
-    if last > 1:
-        ring_step("o", 2)
-    spread("o", 1)
     for s in steps:
-        forward("q", s)
+        spread("o", s)
     for s in steps:
         moves["kv", "core", s].wait_recv()
+    for copy in own_kv:
+        copy.wait()
     keep = [local(full_kv, kv_all)]
     tile = 384
 
@@ -443,34 +449,35 @@
     lax.fori_loop(0, per, lambda t, _: project_kv(t, True), 0)
     k_here, v_here = kv_s.at[pl.ds(0, kv_rows)], kv_s.at[pl.ds(kv_rows, kv_rows)]
     k_x, k_y = send(k_here, k1, to_x), send(k_here, k2, to_y)
-    if last > 1:
-        moves["o", "ring", 2].wait_recv()
-        if last > 2:
-            ring_step("o", 3)
-        spread("o", 2)
     lax.fori_loop(per, 2 * per, lambda t, _: project_kv(t, False), 0)
     v_y, v_x = send(v_here, v2, to_y), send(v_here, v1, to_x)
-    for s in range(3, zsize):
-        moves["o", "ring", s].wait_recv()
-        if s < last:
-            ring_step("o", s + 1)
-        spread("o", s)
+    if last > 1:
+        moves["ffn", 1].wait_recv()
+        ffn_step(2)
+    for s in steps:
+        forward("q", s)
     keep += [local(k_here, k0), local(v_here, v0)]
     for copy in far_ffn:
         copy.wait()
     keep += [local(pack_s.at[n], out) for n, out in enumerate((pack, far_pack, pack_x, pack_y))]
     keep += [local(cot_s.at[0], cot.at[0]), local(cot_s.at[1], cot.at[3])]
-    for s in steps:
-        cross("q", s)
-    if last > 1:
-        moves["ffn", 1].wait_recv()
-        ffn_step(2)
     for z in range(zsize):
         strips = first[:, z * tile:(z + 1) * tile].astype(F32).T.astype(BF)
         first_s[z] = strips.reshape(4, 2, strips.shape[0] // 8, length)
     keep.append(local(first_s.at[:, :, core], first_half.at[:, :, :, pl.ds(0, length)]))
     half_move = send(first_s.at[:, :, 1 - core], first_half.at[:, :, :, pl.ds(length, length)], to_core)
     for s in steps:
+        cross("q", s)
+    for s in steps:
+        forward("o", s)
+    for s in range(2, last):
+        moves["ffn", s].wait_recv()
+        ffn_step(s + 1)
+    k_x.wait_recv()
+    k_d = send(k1, k3, to_y)
+    v_y.wait_recv()
+    v_d = send(v2, v3, to_x)
+    for s in steps:
         moves["q", "core", s].wait_recv()
     for copy in own_late:
         copy.wait()
@@ -481,15 +488,6 @@
         return 0
 
     lax.fori_loop(0, width // tile, project_q, 0)
-    for s in steps:
-        forward("o", s)
-    k_x.wait_recv()
-    k_d = send(k1, k3, to_y)
-    v_y.wait_recv()
-    v_d = send(v2, v3, to_x)
-    for s in range(2, last):
-        moves["ffn", s].wait_recv()
-        ffn_step(s + 1)
     for s in steps:
         cross("o", s)
     for s in steps:
@@ -517,7 +515,7 @@
     square = jax.ShapeDtypeStruct((zsize, chips, 2, strip, width), BF)
     flat = jax.ShapeDtypeStruct((kv_rows, length), BF)
     hbm, vmem = pl.BlockSpec(memory_space=pltpu.HBM), pl.BlockSpec(memory_space=pltpu.VMEM)
-    copies = 19 * (zsize - 1) + 12
+    copies = 19 * (zsize - 1) + 13
     return pl.pallas_call(
         functools.partial(front_kernel, zsize),
         out_shape=[
@@ -560,9 +558,9 @@
 def tail_kernel(zsize, *refs):
     dk, dv = refs[0:4], refs[4:8]
     dq, cos, sin, first_half, att_half = refs[8:13]
-    pack_in, far_in = refs[13:16], refs[16:16 + zsize]
-    mid_t, query_w, kv_w, x_in, middle, gain, second_part = refs[16 + zsize:23 + zsize]
-    rest = refs[23 + zsize:]
+    pack_in, far_in = refs[13:16], refs[16:19]
+    mid_t, query_w, kv_w, x_in, middle, gain, second_part = refs[19:26]
+    rest = refs[26:]
     o_all, q_all, kv_all, pack_all, tokens_out, gains_out = rest[:6]
     (got, held, dq_pair, kv_pair, half, grads, gl, gr, gx, gy, gz, piece,
      pack_s, pack_0, pack_z, far_s, far_r, pack_p, first_grad, tokens_s, gain_s, gain_r, ss, rs, ls) = rest[6:]
@@ -643,7 +641,7 @@
     ffn_loads = {0: load_ffn(0)}
     load_o = [local(mid_t, held.at[0]), local(att_half, half.at[0])]
     load_q = [local(dq, dq_pair.at[0]), local(first_half, half.at[1])]
-    load_far = [local(far_in[n], far_s.at[n]) for n in range(zsize)]
+    load_far = [local(far_in[n], far_s.at[n]) for n in range(3)]
 
     moves = {}
 
@@ -764,6 +762,9 @@
         lax.fori_loop(0, zsize * per, one, 0)
 
     ffn_step(0)
+    wait_all(load_far)
+    add_rows(far_s.at[0], [far_s.at[1]], 64)
+    far_ring = send(far_s.at[0], far_s.at[3], to_next)
     received(mid_swap)
     wait_all(load_o)
     product(0, held, 0)
@@ -807,9 +808,9 @@
     stage_2(1)
     if last > 2:
         ffn_step(2)
-    wait_all(load_far)
-    add_rows(far_s.at[0], [far_s.at[n] for n in range(1, zsize)], 64)
-    far = send(far_s.at[0], far_r, to_far)
+    received(far_ring)
+    add_rows(far_s.at[2], [far_s.at[3]], 64)
+    far = send(far_s.at[2], far_r, to_far)
     received(kv_swap)
     product(2, kv_pair, 1)
     stage_1(2)
@@ -834,6 +835,7 @@
         ring_step(2, j)
     spread(2, piece.at[2], whole(kv_all))
     settle(far)
+    settle(far_ring)
     weight_at = [(pack_s.at[k // 3, k % 3], far_s.at[k]) for k in range(zsize)]
     loads = [(local(query_w.at[k], a), local(kv_w.at[k], b)) for k, (a, b) in enumerate(weight_at)]
     rows = width // zsize
@@ -901,7 +903,7 @@
     hbm, vmem = pl.BlockSpec(memory_space=pltpu.HBM), pl.BlockSpec(memory_space=pltpu.VMEM)
     shape = lambda *s: jax.ShapeDtypeStruct(s, BF)
     store = lambda *s: pltpu.VMEM(s, BF)
-    copies = 15 + 3 * (zsize - 1) + 3 * (4 + zsize - 1) + 5 * 5
+    copies = 16 + 3 * (zsize - 1) + 3 * (4 + zsize - 1) + 5 * 5
     cut = lambda w: w.reshape(zsize, rows, width)
     inputs = [*dk, *dv, dq, cosine, sine, first_half, att_half, *packs, *far_packs, mid_t, cut(query_w), cut(kv_w), x, middle, gain, second_part]
     last = zsize - 1
@@ -918,7 +920,7 @@
             store(3, zsize, strip, width), store(3, zsize, strip, width),
             store(3, last, strip, width), store(3, strip, width),
             store(2, 3, rows, packed), store(rows, packed), store(last, rows, packed),
-            store(zsize, rows, packed), store(rows, packed), store(rows, packed),
+            store(max(4, zsize), rows, packed), store(rows, packed), store(rows, packed),
             pltpu.VMEM((length, width), F32), store(length, width), pltpu.VMEM((8, width), F32), pltpu.VMEM((zsize + 2, 8, width), F32),
             pltpu.SemaphoreType.DMA((copies,)), pltpu.SemaphoreType.DMA((copies,)),
             pltpu.SemaphoreType.DMA((6 * zsize + 14,)),
@@ -960,17 +962,21 @@
         copy.start()
         loads.append(copy)
 
+    tile = 256
+    steps = tokens // tile
     unfold(weights, wi_v, wo_v, load)
-    load(second, s_v)
-    load(cot, c_v)
+    first = len(loads)
+    for t in range(steps):
+        part = pl.ds(t * tile, tile)
+        load(second.at[part], s_v.at[part])
+        load(cot.at[part], c_v.at[part])
     load(second_t, st_v)
-    for copy in loads[:-1]:
+    for copy in loads[:first]:
         copy.wait()
     nt = (((1,), (1,)), ((), ()))
-    tile = 256
 
     def one(t, _):
-        part = pl.ds(pl.multiple_of(t * tile, tile), tile)
+        part = pl.ds(t * tile, tile)
         pre = jnp.dot(s_v[part], wi_v[...].reshape(width, 2 * chunk), preferred_element_type=F32)
         hidden_grad = lax.dot_general(c_v[part], wo_v[...].reshape(chunk, width), nt, preferred_element_type=F32)
         gate, up = pre[:, :chunk], pre[:, chunk:]
@@ -983,7 +989,10 @@
         l_v[part, chunk:] = (hidden_grad * silu).astype(BF)
         return 0
 
-    lax.fori_loop(0, tokens // tile, one, 0)
+    for t in range(steps):
+        loads[first + 2 * t].wait()
+        loads[first + 2 * t + 1].wait()
+        one(t, 0)
     stores = []
 
     def store(src, dst):
@@ -1019,7 +1028,7 @@
         copy.wait()
 
 
-def ffn_chunk(before, second, second_t, cot, weights, split, zsize, fine):
+def ffn_chunk(before, second, second_t, cot, weights, split, cost, zsize, fine):
     pieces = zsize if split else 1
     tokens, width = second.shape
     chunk = zsize * fine
@@ -1038,9 +1047,9 @@
         scratch_shapes=[
             store(tokens, width), store(width, tokens), store(tokens, width), store(zsize, rows, 2 * chunk), store(zsize, fine, width),
             store(tokens, chunk), store(chunk, tokens), store(tokens, 2 * chunk), store(zsize, rows, 2 * chunk), store(zsize, fine, width),
-            pltpu.SemaphoreType.DMA((5 + zsize + 2 * zsize * (folds + 1),)),
+            pltpu.SemaphoreType.DMA((5 + zsize + 2 * zsize * (folds + 1) + 2 * (tokens // 256),)),
         ],
-        cost_estimate=NO_COST,
+        cost_estimate=cost,
         compiler_params=pltpu.CompilerParams(vmem_limit_bytes=50 * 2**20),
         name="ffn_chunk",
     )(before, second, second_t, cot, *weights)
@@ -1155,20 +1164,28 @@
     flat = lambda n: pl.BlockSpec((block, n), lambda i: (i, 0))
     out = lambda r, c: jax.ShapeDtypeStruct((r, c), F32)
     ff = fine * chips * cores
+    hbm = pl.BlockSpec(memory_space=pltpu.HBM)
+
+    def kernel(pack, o_in, q_in, kv_in, *outs):
+        pltpu.emit_pipeline(
+            functools.partial(assemble_kernel, zsize),
+            grid=(steps,),
+            in_specs=[
+                pl.BlockSpec((chips, cores, block, two), lambda i: (0, 0, i, 0)),
+                pl.BlockSpec((2, 1, rows, fold), lambda i: (i % 2, i // 2, 0, two // fold)),
+                flat(width), flat(width), flat(width),
+            ],
+            out_specs=[flat(ff * zsize), flat(ff * zsize), pl.BlockSpec((ff // steps, width), lambda i: (i, 0)), flat(width), flat(width), flat(width // 2), flat(width // 2)],
+        )(pack, pack, o_in, q_in, kv_in, *outs)
+
     return pl.pallas_call(
-        functools.partial(assemble_kernel, zsize),
-        grid=(steps,),
+        kernel,
         out_shape=[out(rows, ff * zsize), out(rows, ff * zsize), out(ff, width), out(rows, width), out(rows, width), out(rows, width // 2), out(rows, width // 2)],
-        in_specs=[
-            pl.BlockSpec((chips, cores, block, two), lambda i: (0, 0, i, 0)),
-            pl.BlockSpec((2, 1, rows, fold), lambda i: (i % 2, i // 2, 0, two // fold)),
-            flat(width), flat(width), flat(width),
-        ],
-        out_specs=[flat(ff * zsize), flat(ff * zsize), pl.BlockSpec((ff // steps, width), lambda i: (i, 0)), flat(width), flat(width), flat(width // 2), flat(width // 2)],
-        cost_estimate=NO_COST,
+        in_specs=[hbm] * 4,
+        out_specs=[hbm] * 7,
         compiler_params=pltpu.CompilerParams(vmem_limit_bytes=40 * 2**20),
         name="assemble",
-    )(packs, packs, o, q, kv)
+    )(packs, o, q, kv)
 
 
 MESH = pl.DeviceIdType.MESH
@@ -1217,7 +1234,7 @@
     return core, other
 
 
-def bridge_kernel(att, weight, x, gain, middle, second, second_t, att_half, att_s, w_s, low_s, low_t, ss, rs, ls):
+def bridge_kernel(att, weight, x, gain, middle_o, second, second_t, att_half, att_s, w_s, low_s, low_t, middle, ss, rs, ls):
     core, other = greet_other_core()
     move = Mover(ss, rs, ls)
     zsize, chips, _, strip, length = att.shape
@@ -1240,6 +1257,7 @@
         here, there = pl.ds(tile * t, tile), pl.ds(length + tile * t, tile)
         arrive.append(move.send(low_s.at[here], second.at[there], other))
         arrive.append(move.send(low_t.at[:, here], second_t.at[:, there], other))
+    move.kept.append(move.local(middle, middle_o))
     move.kept.append(move.local(low_s, second.at[pl.ds(0, length)]))
     move.kept.append(move.local(low_t, second_t.at[:, pl.ds(0, length)]))
     for copy in arrive:
@@ -1259,11 +1277,11 @@
             jax.ShapeDtypeStruct((width, 2 * length), BF), jax.ShapeDtypeStruct((zsize, chips, strip, 2 * length), BF),
         ],
         in_specs=[hbm, hbm, vmem, vmem],
-        out_specs=[vmem, hbm, hbm, hbm],
+        out_specs=[hbm, hbm, hbm, hbm],
         scratch_shapes=[
             pltpu.VMEM((zsize, chips, 2, strip, length), BF), pltpu.VMEM((width, width), BF),
-            pltpu.VMEM((length, width), BF), pltpu.VMEM((width, length), BF),
-            pltpu.SemaphoreType.DMA((1 + 2 * steps,)), pltpu.SemaphoreType.DMA((1 + 2 * steps,)), pltpu.SemaphoreType.DMA((5,)),
+            pltpu.VMEM((length, width), BF), pltpu.VMEM((width, length), BF), pltpu.VMEM((length, width), F32),
+            pltpu.SemaphoreType.DMA((1 + 2 * steps,)), pltpu.SemaphoreType.DMA((1 + 2 * steps,)), pltpu.SemaphoreType.DMA((6,)),
         ],
         compiler_params=pltpu.CompilerParams(collective_id=2, has_side_effects=True, vmem_limit_bytes=40 * 2**20),
         cost_estimate=NO_COST,
@@ -1280,45 +1298,48 @@
         at += n
     y_in, cot_in, gain, out_w = refs[at:at + 4]
     layer_out, middle_grad, low_t, att_grad, gain_part = refs[at + 4:at + 9]
-    h_v, l_v, wi_v, wo_v, send_s, got, own, out_s, ss, rs, ls = refs[at + 9:]
+    h_v, l_v, wi_v, wo_v, send_s, got, own, out_s, y_s, cot_s, ss, rs, ls = refs[at + 9:]
     core, other = greet_other_core()
     move = Mover(ss, rs, ls)
     tokens, chunk = hidden[0].shape
     length, width = y_in.shape
-    loads = []
-    load = lambda src, dst: loads.append(move.local(src, dst))
-    late = []
+    late, loads = [], []
     for r in range(count):
-        load(low[r], l_v.at[:, pl.ds(2 * r * chunk, 2 * chunk)])
-    for r in range(count):
+        chunk_loads = []
+        load = lambda src, dst: chunk_loads.append(move.local(src, dst))
+        load(low[r], l_v.at[r])
         unfold(weights[r], wi_v.at[:, :, pl.ds(2 * r * chunk, 2 * chunk)], wo_v.at[r], load)
+        loads.append(chunk_loads)
+    inputs = [move.local(y_in, y_s), move.local(cot_in.at[pl.ds(0, 2)], cot_s)]
     for r in range(count):
         late.append(move.local(hidden[r], h_v.at[:, pl.ds(r * chunk, chunk)]))
     nt = (((1,), (1,)), ((), ()))
     tile = tokens // 4
 
-    def grad_tile(t):
-        return lax.dot_general(
-            l_v[tile * t:tile * (t + 1)], wi_v[...].reshape(width, 2 * count * chunk), nt, preferred_element_type=F32
-        )
-
     def out_tile(t):
         return jnp.dot(h_v[tile * t:tile * (t + 1)], wo_v[...].reshape(count * chunk, width), preferred_element_type=F32)
 
-    for copy in loads:
+    targets = (own.at[pl.ds(0, tile)], own.at[pl.ds(tile, tile)], send_s.at[0], send_s.at[1])
+    there = []
+    for r in range(count):
+        for copy in loads[r]:
+            copy.wait()
+        for t in (2, 3, 0, 1):
+            part = lax.dot_general(
+                l_v[r, tile * t:tile * (t + 1)], wi_v[:, :, 2 * r * chunk:2 * (r + 1) * chunk].reshape(width, 2 * chunk), nt,
+                preferred_element_type=F32,
+            )
+            targets[t][...] = part if r == 0 else targets[t][...] + part
+            if r == count - 1 and t >= 2:
+                there.append(move.send(send_s.at[t - 2], got.at[t - 2], other))
+    for copy in inputs:
         copy.wait()
-    there = []
-    for n in range(2):
-        send_s[n] = grad_tile(2 + n)
-        there.append(move.send(send_s.at[n], got.at[n], other))
-    for n in range(2):
-        own[tile * n:tile * (n + 1)] = grad_tile(n)
     load_out = move.local(out_w, wi_v.at[:, :, pl.ds(0, width)])
     for copy in late:
         copy.wait()
     for n in range(2):
         move.settle(there[n])
-        send_s[n] = out_tile(2) if n == 0 else out_tile(1) + y_in[tile:2 * tile]
+        send_s[n] = out_tile(2) if n == 0 else out_tile(1) + y_s[tile:2 * tile]
         there.append(move.send(send_s.at[n], got.at[2 + n], other))
     there[0].wait_recv()
     there[1].wait_recv()
@@ -1327,13 +1348,13 @@
 
     for t in range(length // step):
         part = slice(step * t, step * (t + 1))
-        y = y_in[part]
+        y = y_s[part]
         inverse = lax.rsqrt(jnp.mean(y * y, -1, keepdims=True) + EPS)
         unit = y * inverse
         d = own[part] + got[step * t // tile, step * t % tile:step * t % tile + step]
         gain_part[...] += jnp.sum(d * unit, axis=0, keepdims=True)
         scaled = d * gain[...]
-        g = cot_in[step * t // tile, step * t % tile:step * t % tile + step].astype(F32)
+        g = cot_s[step * t // tile, step * t % tile:step * t % tile + step].astype(F32)
         g = g + inverse * (scaled - unit * jnp.mean(scaled * unit, -1, keepdims=True))
         middle_grad[part] = g
         low_t[:, part] = g.T.astype(BF)
@@ -1341,7 +1362,7 @@
     rows = wi_v.shape[1]
     for z in range(wi_v.shape[0]):
         att_grad[z * rows:(z + 1) * rows] = jnp.dot(wi_v[z, :, 0:width], low_t[...], preferred_element_type=F32).astype(BF)
-    first, last = out_tile(0) + y_in[0:tile], out_tile(3)
+    first, last = out_tile(0) + y_s[0:tile], out_tile(3)
     there[2].wait_recv()
     out_s[0] = (first + got[2]).astype(BF)
     there[3].wait_recv()
@@ -1367,20 +1388,21 @@
             jax.ShapeDtypeStruct((width, length), BF), jax.ShapeDtypeStruct((width, length), BF),
             jax.ShapeDtypeStruct((1, width), F32),
         ],
-        in_specs=[hbm] * len(inputs) + [vmem, vmem, vmem, hbm],
+        in_specs=[hbm] * len(inputs) + [hbm, hbm, vmem, hbm],
         out_specs=[hbm] + [vmem] * 4,
         scratch_shapes=[
-            pltpu.VMEM((tokens, count * chunk), BF), pltpu.VMEM((tokens, 2 * count * chunk), BF),
+            pltpu.VMEM((tokens, count * chunk), BF), pltpu.VMEM((count, tokens, 2 * chunk), BF),
             pltpu.VMEM((zsize, rows, 2 * count * chunk), BF), pltpu.VMEM((count, zsize, fine, width), BF),
             pltpu.VMEM((2, tile, width), F32), pltpu.VMEM((4, tile, width), F32),
             pltpu.VMEM((length, width), F32), pltpu.VMEM((2, tile, width), BF),
+            pltpu.VMEM((length, width), F32), pltpu.VMEM((2, tile, width), BF),
             pltpu.SemaphoreType.DMA((4,)), pltpu.SemaphoreType.DMA((4,)),
-            pltpu.SemaphoreType.DMA((2 * count + count * zsize * (1 + rows // fine) + 3,)),
+            pltpu.SemaphoreType.DMA((2 * count + count * zsize * (1 + rows // fine) + 5,)),
         ],
         compiler_params=pltpu.CompilerParams(collective_id=3, has_side_effects=True, vmem_limit_bytes=61 * 2**20),
-        cost_estimate=LONG,
+        cost_estimate=NO_COST,
         name="middle",
-    )(*inputs, y, cot[:2], gain, out_w.reshape(zsize, rows, width))
+    )(*inputs, y, cot, gain, out_w.reshape(zsize, rows, width))
 
 
 def mm(left, right, left_dim, right_dim):
@@ -1597,7 +1619,7 @@
     before = second
     for r in [0] + list(near) + [diag]:
         before, low[r], grads[r] = ffn_chunk(
-            before, second, second_t, cot.reshape(2 * length, width), packs[r], fast and r == diag, zsize, fine
+            before, second, second_t, cot.reshape(2 * length, width), packs[r], fast and r == diag, LONG if r == diag else NO_COST, zsize, fine
         )
         hidden[r] = before
     every = range(chips)
@@ -1636,15 +1658,24 @@
         out_part_grad = mm(halves(attended), jnp.concatenate([middle_low, swap(middle_low)]), 1, 0)
         attended_grad = mm(output_full, middle_low, 1, 1).astype(BF)
 
+    far_sum = middle_grad
+    if fast:
+        far_sum = grads[diag][zsize - 1]
+        for s in range(zsize - 2, 0, -1):
+            far_moved = shift(far_sum, 1)
+            if s > 1:
+                share, middle_t = lax.optimization_barrier((grads[diag][s], middle_t))
+                far_sum = (far_moved.astype(F32) + share.astype(F32)).astype(BF)
+
     query_low, key_parts, value_parts = attn_bwd(
-        ids, order, query, attended, attended_grad, log_total, cosine, sine, key_list, value_list, KEY_HEADS
+        far_sum, ids, order, query, attended, attended_grad, log_total, cosine, sine, key_list, value_list, KEY_HEADS
     )
     if fast:
         o_all, q_all, kv_all, pack_all, tokens_grad, gain_sums = tail(
             key_parts, value_parts, query_low, cosine, sine, first_half,
             att_half,
             [grads[0][0], hop(grads[1][0], 1), hop(grads[2][0], 2)],
-            [grads[diag][0]] + [shift(grads[diag][s], s) for s in range(1, zsize)],
+            [far_moved, grads[diag][1], grads[diag][0]],
             middle_t, query_full, key_value_full, x_low, middle_grad, gain_first[None], gain_second_part, zsize, chips,
         )
         gain_first_grad, gain_second_grad = (

time: 617 us -> 590 us (0.956)
  Pallas kernels: 550 us -> 534 us
  waiting for transfers between devices: 13.4 us -> 5.77 us
    pallas_call x1, Pallas kernels: 138 us -> 130 us  [front(): pl.pallas_call(functools.partial(front_kernel, zsize), out_shape=[square,...]
    ppermute x4, waiting for transfers between devices: 13.4 us -> 5.76 us  [hop(): lax.ppermute(a, 'ctx', [(i, i ^ 2 * r) for i in range(lax.axis_size('ctx'...]
    pallas_call x1, Pallas kernels: 41.2 us -> 35 us  [middle_part(): pl.pallas_call(functools.partial(middle_kernel, counts), out_shape=[jax.S...]
    unnamed x58 -> x64, local copies, waits for them, and re-layouts: 25.2 us -> 27 us
  transfers between devices with their start and end apart: 10 -> 9, of which waited for: 2 -> 1; matrix products, arithmetic and copies ran while one was open for 1% -> 0% of each run, Pallas kernels for 29% -> 32%
where the time goes in v6:
time: 590 us; the launch traced here: 585 us
  Pallas kernels  534 us (91%)
  local copies, waits for them, and re-layouts  31.8 us (5%)
  starting transfers between devices  10.2 us (2%)
    pallas_call x1, Pallas kernels, tail(): pl.pallas_call(functools.partial(tail_kernel, zsize), out_shape=[shape(ch...  209 us
    pallas_call x1, Pallas kernels, front(): pl.pallas_call(functools.partial(front_kernel, zsize), out_shape=[square,...  130 us
    pallas_call x4, Pallas kernels, ffn_chunk(): pl.pallas_call(functools.partial(ffn_kernel, len(weights), pieces), out_s...  61.7 us
    pallas_call x1, Pallas kernels, attn_bwd(): pl.pallas_call(functools.partial(bwd_kernel, nchip, per), grid_spec=grid_...  47.4 us
    pallas_call x1, Pallas kernels, middle_part(): pl.pallas_call(functools.partial(middle_kernel, counts), out_shape=[jax.S...  35 us
    pallas_call x1, Pallas kernels, attn_fwd(): pl.pallas_call(functools.partial(fwd_kernel, nchip, per), grid_spec=grid_...  30.8 us
    unnamed x64, local copies, waits for them, and re-layouts  27 us
  transfers between devices with their start and end apart: 9, of which 1 were waited for; matrix products, arithmetic and copies ran while one was open for 0% of the time, Pallas kernels for 32%

profile of v6, /device:TPU:0, one launch (start us, length us, event | category | flops | bytes accessed | tf_op | source)
XLA Modules:
  0.0 585.0 jit_solution(1331128806492207675)
XLA Ops:
  0.7 1.3 fusion.9
  2.0 0.6 broadcast_multiply_fusion
  2.7 0.7 stack.9
  3.4 0.7 stack.10
  4.5 1.1 copy-done.23
  5.6 1.1 copy-done.24
  6.7 130.1 %front.1 = (bf16[4,4,2,48,1536]{4,3,2,1,0:T(8,128)(2,1)}, bf16[4,4,2,48,1536]{4,3,2,1,0:T(8,128)(2,1)}, bf16[4,4,2,48,1536]{4,3,2,1,0:T(8,128)(2,1)}, bf16[384,1...) custom-call(bf16[2,256,1536]{2,1,0:T(8,128)(2,1)} %refs_0_.1, ...), custom_call_target="tpu_custom_call" | custom-call | tf_op jit(solution)/shard_map/front/pallas_call | solution.py:519
  136.9 0.9 copy-done.11
  137.7 0.9 copy-done.12
  138.6 0.9 copy-done.13
  139.5 1.5 collective-permute-start
  141.0 0.5 collective-permute-start.1
  142.0 2.5 collective-permute-start.3
  144.5 0.7 collective-permute-start.2
  145.3 0.6 select_reduce_fusion.inv_ref
  146.0 30.8 %attention_forward.1 = (bf16[1536,512]{1,0:T(8,128)(2,1)}, f32[8,4,1,256]{3,2,1,0:T(1,128)}) custom-call(s32[4]{0:T(128)} %get-tuple-element.162.ids_ref, s32[16]{0:T(128)} %select_reduce_fusion.inv_ref, bf16[1536,512]{1,0:T(8,128)(2,1)} %get-tuple-element.82.q_ref, bf16[768,512]{1,0:T(8,128)(2,1)} %copy-done.11, bf16[768,512]{1,0:T(8,128)(2,1)} %copy-done.12, ...), custom_call_target="tpu_custom_call" | custom-call | tf_op jit(solution)/shard_map/attention_forward/pallas_call | solution.py:134
  176.8 0.6 fusion.11
  177.4 1.4 copy-done.4
  178.8 9.5 %bridge.1 = (f32[512,1536]{1,0:T(8,128)S(1)}, bf16[1024,1536]{1,0:T(8,128)(2,1)S(1)}, bf16[1536,1024]{1,0:T(8,128)(2,1)S(1)}, bf16[4,4,48,1024]{3,2,1,0:T(8,128)(2,1)S(1)}) custom-call(bf16[4,4,2,48,512]{4,3,2,1,0:T(8,128)(2,1)S(1)} %bitcast.15, bf16[1536,1536]{1,0:T(8,128)(2,1)} %bitcast.25, bf16[512,1536]{1,0:T(8,128)(2,1)S(1)} %copy-done.3, ...), custom_call_target="tpu_custom_call" | custom-call | tf_op jit(solution)/shard_map/bridge/pallas_call | solution.py:1273
  188.3 1.7 copy-done
  190.0 1.7 copy-done.1
  191.7 1.6 copy-done.10
  193.4 1.1 copy-done.16
  194.5 15.6 %ffn_chunk.4 = (bf16[1024,512]{1,0:T(8,128)(2,1)S(1)}, bf16[1024,1024]{1,0:T(8,128)(2,1)}, bf16[4,384,1536]{2,1,0:T(8,128)(2,1)}) custom-call(bf16[1024,1536]{1,0:T(8,128)(2,1)} %copy-done, bf16[1024,1536]{1,0:T(8,128)(2,1)} %copy-done, bf16[1536,1024]{1,0:T(8,128)(2,1)} %copy-done.1, bf16[1024,1536]{1,0:T(8,128)(2,1)} %bitcast.21, ...), custom_call_target="tpu_custom_call" | custom-call | tf_op jit(solution)/shard_map/ffn_chunk/pallas_call | solution.py:1042
  210.2 5.7 collective-permute-done.refs_1_.refs_11_
  216.0 15.2 %ffn_chunk.5 = (bf16[1024,512]{1,0:T(8,128)(2,1)S(1)}, bf16[1024,1024]{1,0:T(8,128)(2,1)}, bf16[4,384,1536]{2,1,0:T(8,128)(2,1)}) custom-call(bf16[1024,512]{1,0:T(8,128)(2,1)S(1)} %get-tuple-element.100.before.refs_0_, bf16[1024,1536]{1,0:T(8,128)(2,1)} %copy-done, bf16[1536,1024]{1,0:T(8,128)(2,1)} %copy-done.1, bf16[1024,1536]{1,0:T(8,128)(2,1)} %bitcast.22, ...), custom_call_target="tpu_custom_call" | custom-call | tf_op jit(solution)/shard_map/ffn_chunk/pallas_call | solution.py:1042
  231.2 1.3 collective-permute-start.6
  232.5 15.3 %ffn_chunk.6 = (bf16[1024,512]{1,0:T(8,128)(2,1)S(1)}, bf16[1024,1024]{1,0:T(8,128)(2,1)}, bf16[4,384,1536]{2,1,0:T(8,128)(2,1)}) custom-call(bf16[1024,512]{1,0:T(8,128)(2,1)S(1)} %get-tuple-element.102.before.refs_1_, bf16[1024,1536]{1,0:T(8,128)(2,1)} %copy-done, bf16[1536,1024]{1,0:T(8,128)(2,1)} %copy-done.1, bf16[1024,1536]{1,0:T(8,128)(2,1)} %bitcast.23, ...), custom_call_target="tpu_custom_call" | custom-call | tf_op jit(solution)/shard_map/ffn_chunk/pallas_call | solution.py:1042
  247.8 0.8 collective-permute-start.7
  248.7 15.6 %ffn_chunk.7 = (bf16[1024,512]{1,0:T(8,128)(2,1)S(1)}, bf16[1024,1024]{1,0:T(8,128)(2,1)}, bf16[384,1536]{1,0:T(8,128)(2,1)S(1)}, bf16[384,1536]{1,0:T(8,128)(2,...) custom-call(bf16[1024,512]{1,0:T(8,128)(2,1)S(1)} %get-tuple-element.104.before.refs_2_, ...), custom_call_target="tpu_custom_call" | custom-call | flops 51999997952 | tf_op jit(solution)/shard_map/ffn_chunk/pallas_call | solution.py:1042
  264.3 1.0 copy-done.17
  265.3 1.0 copy-done.22
  266.2 2.2 collective-permute-start.5
  268.5 35.0 %middle.1 = (bf16[2,256,1536]{2,1,0:T(8,128)(2,1)}, f32[512,1536]{1,0:T(8,128)}, bf16[1536,512]{1,0:T(8,128)(2,1)}, bf16[1536,512]{1,0:T(8,128)(2,1)}, f32[1,1536]{1,0:T(1,128)}) custom-call(bf16[1024,512]{1,0:T(8,128)(2,1)} %copy-done.8, bf16[1024,512]{1,0:T(8,128)(2,1)} %copy-done.9, bf16[1024,512]{1,0:T(8,128)(2,1)} %copy-done.21, ...), custom_call_target="tpu_custom_call" | custom-call | tf_op jit(solution)/shard_map/middle/pallas_call | solution.py:1384
  303.9 0.9 copy-done.26
  304.8 47.4 %attention_backward.1 = (bf16[1536,512]{1,0:T(8,128)(2,1)}, bf16[768,512]{1,0:T(8,128)(2,1)}, bf16[768,512]{1,0:T(8,128)(2,1)}, bf16[768,512]{1,0:T(8,128)(2,1)}...) custom-call(s32[4]{0:T(128)} %get-tuple-element.162.ids_ref, ...), custom_call_target="tpu_custom_call" | custom-call | tf_op jit(solution)/shard_map/attention_backward/pallas_call | solution.py:249
  352.2 1.0 copy-done.29
  353.2 209.3 %tail.1 = (bf16[4,2,48,1536]{3,2,1,0:T(8,128)(2,1)}, bf16[4,2,48,1536]{3,2,1,0:T(8,128)(2,1)}, bf16[4,2,48,1536]{3,2,1,0:T(8,128)(2,1)}, bf16[4,2,384,1536]{3,2,...) custom-call(bf16[768,512]{1,0:T(8,128)(2,1)} %get-tuple-element.119.refs_0_, ...), custom_call_target="tpu_custom_call" | custom-call | tf_op jit(solution)/shard_map/tail/pallas_call | solution.py:910
  562.5 0.9 fusion.10
  563.4 0.6 fusion
  564.0 3.7 copy-done.2
  567.7 1.3 copy-done.18
  568.9 1.3 copy-done.19
  570.2 1.3 copy-done.20
  571.5 10.2 %assemble.1 = (f32[384,4096]{1,0:T(8,128)}, f32[384,4096]{1,0:T(8,128)}, f32[1024,1536]{1,0:T(8,128)}, f32[384,1536]{1,0:T(8,128)}, f32[384,1536]{1,0:T(8,128)}, /*index=5*/f32[384,768]{1,0:T(8,128)}, f32[384,768]{1,0:T(8,128)}) custom-call(bf16[4,2,384,1536]{3,2,1,0:T(8,128)(2,1)S(1)} %copy-done.2, bf16[384,1536]{1,0:T(8,128)(2,1)S(1)} %bitcast.16, ...), custom_call_target="tpu_custom_call" | custom-call | tf_op jit(solution)/shard_map/assemble/pallas_call | solution.py:1181
  581.7 1.1 copy.25
  582.8 0.8 copy-done.28
  583.6 1.1 copy.26
  (59 shorter events, 1.5 us)
Async XLA Ops:
  4.5 132.3 %copy-start.14 = (f32[48,512]{1,0:T(8,128)}, f32[48,512]{1,0:T(8,128)S(1)}, u32[]{:S(2)}) copy-start(f32[48,512]{1,0:T(8,128)S(1)} %get-tuple-element.167.refs_11_.sin_ref.refs_10_) | copy-start | bytes 294916
  4.5 132.3 %copy-start.15 = (f32[48,512]{1,0:T(8,128)}, f32[48,512]{1,0:T(8,128)S(1)}, u32[]{:S(2)}) copy-start(f32[48,512]{1,0:T(8,128)S(1)} %get-tuple-element.168.refs_10_.cos_ref.refs_9_) | copy-start | bytes 294916
  4.5 1.1 copy-start.23
  5.6 1.1 copy-start.24
  136.8 0.9 copy-start.11
  137.7 0.9 copy-start.12
  138.6 0.9 copy-start.13
  139.5 76.4 %collective-permute-start = (bf16[3,384,1536]{2,1,0:T(8,128)(2,1)}, bf16[3,384,1536]{2,1,0:T(8,128)(2,1)}, u32[]{:S(2)}, u32[]{:S(2)}) collective-permute-start(bf16[3,384,1536]{2,1,0:T(8,128)(2,1)} %get-tuple-element.99.refs_1_.refs_9_), channel_id=1, source_target_pairs={{0,8},{4,12},{8,0},{12,4},{16,24},{20,28},{24,16},{28,20},{1,9},{5... | collective-permute-start | bytes 10616840 | tf_op jit(solution)/shard_map/ppermute | solution.py:1417
  141.0 91.5 %collective-permute-start.1 = (bf16[3,384,1536]{2,1,0:T(8,128)(2,1)}, bf16[3,384,1536]{2,1,0:T(8,128)(2,1)}, u32[]{:S(2)}, u32[]{:S(2)}) collective-permute-start(bf16[3,384,1536]{2,1,0:T(8,128)(2,1)} %get-tuple-element.99.refs_1_.refs_9_), channel_id=1, source_target_pairs={{0,16},{4,20},{8,24},{12,28},{16,0},{20,4},{24,8},{28,12},{1,17},{... | collective-permute-start | bytes 10616840 | tf_op jit(solution)/shard_map/ppermute | solution.py:1417
  141.6 107.1 %collective-permute-start.4 = (bf16[384,1536]{1,0:T(8,128)(2,1)}, bf16[384,1536]{1,0:T(8,128)(2,1)}, u32[]{:S(2)}, u32[]{:S(2)}) collective-permute-start(bf16[384,1536]{1,0:T(8,128)(2,1)} %get-tuple-element.105.refs_0_.refs_14_), channel_id=1, source_target_pairs={{0,3},{1,0},{2,1},{3,2},{4,7},{5,4},{6,5},{7,6},{8,11},{9,8},{10,9... | collective-permute-start | bytes 3538952 | tf_op jit(solution)/shard_map/ppermute | solution.py:1435
  142.0 106.6 %collective-permute-start.3 = (bf16[384,1536]{1,0:T(8,128)(2,1)}, bf16[384,1536]{1,0:T(8,128)(2,1)}, u32[]{:S(2)}, u32[]{:S(2)}) collective-permute-start(bf16[384,1536]{1,0:T(8,128)(2,1)} %get-tuple-element.105.refs_0_.refs_14_), channel_id=1, source_target_pairs={{0,2},{1,3},{2,0},{3,1},{4,6},{5,7},{6,4},{7,5},{8,10},{9,11},{10,... | collective-permute-start | bytes 3538952 | tf_op jit(solution)/shard_map/ppermute | solution.py:1435
  144.5 104.1 %collective-permute-start.2 = (bf16[384,1536]{1,0:T(8,128)(2,1)}, bf16[384,1536]{1,0:T(8,128)(2,1)}, u32[]{:S(2)}, u32[]{:S(2)}) collective-permute-start(bf16[384,1536]{1,0:T(8,128)(2,1)} %get-tuple-element.105.refs_0_.refs_14_), channel_id=1, source_target_pairs={{0,1},{1,2},{2,3},{3,0},{4,5},{5,6},{6,7},{7,4},{8,9},{9,10},{10,1... | collective-permute-start | bytes 3538952 | tf_op jit(solution)/shard_map/ppermute | solution.py:1435
  146.0 31.4 %copy-start.3 = (bf16[512,1536]{1,0:T(8,128)(2,1)S(1)}, bf16[512,1536]{1,0:T(8,128)(2,1)}, u32[]{:S(2)}) copy-start(bf16[512,1536]{1,0:T(8,128)(2,1)} %get-tuple-element.93.x.refs_22_) | copy-start | bytes 4718596
  177.4 10.9 %copy-start.25 = (f32[1,1536]{1,0:T(1,128)}, f32[1,1536]{1,0:T(1,128)S(1)}, u32[]{:S(2)}) copy-start(f32[1,1536]{1,0:T(1,128)S(1)} %get-tuple-element.166.gain.refs_20_) | copy-start | bytes 18436
  177.4 1.4 copy-start.4
  178.8 15.7 %copy-start.5 = (bf16[384,1536]{1,0:T(8,128)(2,1)S(1)}, bf16[384,1536]{1,0:T(8,128)(2,1)}, u32[]{:S(2)}) copy-start(bf16[384,1536]{1,0:T(8,128)(2,1)} %get-tuple-element.98.refs_0_.refs_8_) | copy-start | bytes 3538948
  188.3 1.7 copy-start
  190.0 1.7 copy-start.1
  191.7 1.6 copy-start.10
  193.4 1.1 copy-start.16
  194.5 21.4 %copy-start.6 = (bf16[384,1536]{1,0:T(8,128)(2,1)S(1)}, bf16[384,1536]{1,0:T(8,128)(2,1)}, u32[]{:S(2)}) copy-start(bf16[384,1536]{1,0:T(8,128)(2,1)} %get-tuple-element.101.refs_0_.refs_10_) | copy-start | bytes 3538948
  210.2 21.0 %copy-start.8 = (bf16[1024,512]{1,0:T(8,128)(2,1)}, bf16[1024,512]{1,0:T(8,128)(2,1)S(1)}, u32[]{:S(2)}) copy-start(bf16[1024,512]{1,0:T(8,128)(2,1)S(1)} %get-tuple-element.100.before.refs_0_) | copy-start | bytes 3145732
  216.0 16.6 %copy-start.7 = (bf16[384,1536]{1,0:T(8,128)(2,1)S(1)}, bf16[384,1536]{1,0:T(8,128)(2,1)}, u32[]{:S(2)}) copy-start(bf16[384,1536]{1,0:T(8,128)(2,1)} %get-tuple-element.103.refs_0_.refs_12_) | copy-start | bytes 3538948
  231.2 16.6 %copy-start.9 = (bf16[1024,512]{1,0:T(8,128)(2,1)}, bf16[1024,512]{1,0:T(8,128)(2,1)S(1)}, u32[]{:S(2)}) copy-start(bf16[1024,512]{1,0:T(8,128)(2,1)S(1)} %get-tuple-element.102.before.refs_1_) | copy-start | bytes 3145732
  231.2 121.0 %collective-permute-start.6 = (bf16[4,384,1536]{2,1,0:T(8,128)(2,1)}, bf16[4,384,1536]{2,1,0:T(8,128)(2,1)}, u32[]{:S(2)}, u32[]{:S(2)}) collective-permute-start(bf16[4,384,1536]{2,1,0:T(8,128)(2,1)} %get-tuple-element.131), channel_id=1, source_target_pairs={{0,8},{4,12},{8,0},{12,4},{16,24},{20,28},{24,16},{28,20},{1,9},{5... | collective-permute-start | bytes 14155784 | tf_op jit(solution)/shard_map/ppermute | solution.py:1417
  247.8 16.4 %copy-start.21 = (bf16[1024,512]{1,0:T(8,128)(2,1)}, bf16[1024,512]{1,0:T(8,128)(2,1)S(1)}, u32[]{:S(2)}) copy-start(bf16[1024,512]{1,0:T(8,128)(2,1)S(1)} %get-tuple-element.104.before.refs_2_) | copy-start | bytes 3145732
  247.8 104.4 %collective-permute-start.7 = (bf16[4,384,1536]{2,1,0:T(8,128)(2,1)}, bf16[4,384,1536]{2,1,0:T(8,128)(2,1)}, u32[]{:S(2)}, u32[]{:S(2)}) collective-permute-start(bf16[4,384,1536]{2,1,0:T(8,128)(2,1)} %get-tuple-element.132), channel_id=1, source_target_pairs={{0,16},{4,20},{8,24},{12,28},{16,0},{20,4},{24,8},{28,12},{1,17},{... | collective-permute-start | bytes 14155784 | tf_op jit(solution)/shard_map/ppermute | solution.py:1417
  264.3 1.0 copy-start.17
  265.3 1.0 copy-start.22
  266.2 37.2 %collective-permute-start.5 = (bf16[384,1536]{1,0:T(8,128)(2,1)}, bf16[384,1536]{1,0:T(8,128)(2,1)S(1)}, u32[]{:S(2)}, u32[]{:S(2)}) collective-permute-start(bf16[384,1536]{1,0:T(8,128)(2,1)} %get-tuple-element.115), channel_id=1, source_target_pairs={{0,1},{1,2},{2,3},{3,0},{4,5},{5,6},{6,7},{7,4},{8,9},{9,10},{10,1... | collective-permute-start | bytes 3538952 | tf_op jit(solution)/shard_map/ppermute | solution.py:1435
  268.5 35.0 %copy-start.30 = (bf16[384,1536]{1,0:T(8,128)(2,1)S(1)}, bf16[384,1536]{1,0:T(8,128)(2,1)}, u32[]{:S(2)}) copy-start(bf16[384,1536]{1,0:T(8,128)(2,1)} %get-tuple-element.118) | copy-start | bytes 3538948
  303.8 1.0 copy-start.26
  303.8 48.4 %collective-permute-start.8 = (bf16[384,1536]{1,0:T(8,128)(2,1)S(1)}, bf16[384,1536]{1,0:T(8,128)(2,1)S(1)}, u32[]{:S(2)}, u32[]{:S(2)}) collective-permute-start(bf16[384,1536]{1,0:T(8,128)(2,1)S(1)} %add_convert_fusion.before), channel_id=1, source_target_pairs={{0,1},{1,2},{2,3},{3,0},{4,5},{5,6},{6,7},{7,4},{8,9},{9,10},{10,1... | collective-permute-start | bytes 3538952 | tf_op jit(solution)/shard_map/ppermute | solution.py:1435
  352.2 1.0 copy-start.29
  564.0 3.7 copy-start.2
  567.7 1.3 copy-start.18
  568.9 1.3 copy-start.19
  570.2 1.3 copy-start.20
  571.5 10.2 %copy-start.27 = (bf16[2,256,1536]{2,1,0:T(8,128)(2,1)S(1)}, bf16[2,256,1536]{2,1,0:T(8,128)(2,1)}, u32[]{:S(2)}) copy-start(bf16[2,256,1536]{2,1,0:T(8,128)(2,1)} %get-tuple-element.182) | copy-start | bytes 4718596
  581.7 2.0 copy-start.28

commit v7 on v6

--- a/solution.py
+++ b/solution.py
@@ -18,6 +18,7 @@
 F32 = jnp.float32
 NO_COST = pl.CostEstimate(flops=0, bytes_accessed=0, transcendentals=0)
 LONG = pl.CostEstimate(flops=52 * 10**9, bytes_accessed=0, transcendentals=0)
+ALL_VMEM = 62 * 2**20
 
 LOG2E = 1.4426950408889634
 NT = (((1,), (1,)), ((), ()))
@@ -136,7 +137,7 @@
         grid_spec=grid_spec,
         out_shape=[jax.ShapeDtypeStruct((heads * 192, T), BF), jax.ShapeDtypeStruct((heads, nq, 1, 2 * BLK), F32)],
         cost_estimate=NO_COST,
-        compiler_params=pltpu.CompilerParams(vmem_limit_bytes=56 * 2**20),
+        compiler_params=pltpu.CompilerParams(vmem_limit_bytes=ALL_VMEM),
         name="attention_forward",
     )(ids, inv, qT, *ks, *vs)
 
@@ -251,7 +252,7 @@
         grid_spec=grid_spec,
         out_shape=[jax.ShapeDtypeStruct((heads * 192, T), BF)] + [slab] * (2 * nchip),
         cost_estimate=NO_COST,
-        compiler_params=pltpu.CompilerParams(vmem_limit_bytes=56 * 2**20),
+        compiler_params=pltpu.CompilerParams(vmem_limit_bytes=ALL_VMEM),
         name="attention_backward",
     )(ids, inv, qT, oT, doT, lse, cosine, sine, before, *ks, *vs)
     return outs[0], outs[1:1 + nchip], outs[1 + nchip:]
@@ -550,7 +551,7 @@
             pltpu.SemaphoreType.DMA((zsize,)),
             pltpu.SemaphoreType.DMA((zsize,)),
         ],
-        compiler_params=pltpu.CompilerParams(collective_id=0, has_side_effects=True, vmem_limit_bytes=50 * 2**20),
+        compiler_params=pltpu.CompilerParams(collective_id=0, has_side_effects=True, vmem_limit_bytes=ALL_VMEM),
         name="front",
     )(tokens, cotangent, gains, cut(key_w), cut(value_w), cut(query_w), cut(out_w), gate_w, up_w, down_w, cosine, sine)
 
@@ -787,6 +788,9 @@
     k2, v1 = send(dk[2], got.at[4], to_y), send(dv[1], got.at[5], to_x)
     if last > 1:
         ffn_step(1)
+    received(far_ring)
+    add_rows(far_s.at[2], [far_s.at[3]], 64)
+    far = send(far_s.at[2], far_r, to_far)
     received(k1, k2, v1, v2)
 
     def finish_keys(h, _):
@@ -808,18 +812,15 @@
     stage_2(1)
     if last > 2:
         ffn_step(2)
-    received(far_ring)
-    add_rows(far_s.at[2], [far_s.at[3]], 64)
-    far = send(far_s.at[2], far_r, to_far)
     received(kv_swap)
     product(2, kv_pair, 1)
     stage_1(2)
+    for j in range(3, last):
+        ffn_step(j)
+    ffn_step(last)
     stage_3(0)
     stage_3(1)
     stage_2(2)
-    for j in range(3, last):
-        ffn_step(j)
-    ffn_step(last)
     received(far)
     for h in range(2):
         sum_rows(pack_p.at[parts[h]], [pack_z.at[last - 1, parts[h]], far_r.at[parts[h]]], 64)
@@ -925,7 +926,7 @@
             pltpu.SemaphoreType.DMA((copies,)), pltpu.SemaphoreType.DMA((copies,)),
             pltpu.SemaphoreType.DMA((6 * zsize + 14,)),
         ],
-        compiler_params=pltpu.CompilerParams(collective_id=1, has_side_effects=True, vmem_limit_bytes=62 * 2**20),
+        compiler_params=pltpu.CompilerParams(collective_id=1, has_side_effects=True, vmem_limit_bytes=ALL_VMEM),
         name="tail",
     )(*inputs)
 
@@ -1050,7 +1051,7 @@
             pltpu.SemaphoreType.DMA((5 + zsize + 2 * zsize * (folds + 1) + 2 * (tokens // 256),)),
         ],
         cost_estimate=cost,
-        compiler_params=pltpu.CompilerParams(vmem_limit_bytes=50 * 2**20),
+        compiler_params=pltpu.CompilerParams(vmem_limit_bytes=ALL_VMEM),
         name="ffn_chunk",
     )(before, second, second_t, cot, *weights)
     return out[0], out[1], out[2:]
@@ -1129,7 +1130,7 @@
             pltpu.SemaphoreType.DMA((2 * count + sum(counts) * (1 + rows // fine) + 2 * (tokens // 256),)),
         ],
         cost_estimate=NO_COST,
-        compiler_params=pltpu.CompilerParams(vmem_limit_bytes=56 * 2**20),
+        compiler_params=pltpu.CompilerParams(vmem_limit_bytes=ALL_VMEM),
         name="ffn_combine",
     )(*inputs)
 
@@ -1183,7 +1184,7 @@
         out_shape=[out(rows, ff * zsize), out(rows, ff * zsize), out(ff, width), out(rows, width), out(rows, width), out(rows, width // 2), out(rows, width // 2)],
         in_specs=[hbm] * 4,
         out_specs=[hbm] * 7,
-        compiler_params=pltpu.CompilerParams(vmem_limit_bytes=40 * 2**20),
+        compiler_params=pltpu.CompilerParams(vmem_limit_bytes=ALL_VMEM),
         name="assemble",
     )(packs, o, q, kv)
 
@@ -1283,7 +1284,7 @@
             pltpu.VMEM((length, width), BF), pltpu.VMEM((width, length), BF), pltpu.VMEM((length, width), F32),
             pltpu.SemaphoreType.DMA((1 + 2 * steps,)), pltpu.SemaphoreType.DMA((1 + 2 * steps,)), pltpu.SemaphoreType.DMA((6,)),
         ],
-        compiler_params=pltpu.CompilerParams(collective_id=2, has_side_effects=True, vmem_limit_bytes=40 * 2**20),
+        compiler_params=pltpu.CompilerParams(collective_id=2, has_side_effects=True, vmem_limit_bytes=ALL_VMEM),
         cost_estimate=NO_COST,
         name="bridge",
     )(attended.reshape(zsize, chips, 2, strip, length), weight, x, gain)
@@ -1399,7 +1400,7 @@
             pltpu.SemaphoreType.DMA((4,)), pltpu.SemaphoreType.DMA((4,)),
             pltpu.SemaphoreType.DMA((2 * count + count * zsize * (1 + rows // fine) + 5,)),
         ],
-        compiler_params=pltpu.CompilerParams(collective_id=3, has_side_effects=True, vmem_limit_bytes=61 * 2**20),
+        compiler_params=pltpu.CompilerParams(collective_id=3, has_side_effects=True, vmem_limit_bytes=ALL_VMEM),
         cost_estimate=NO_COST,
         name="middle",
     )(*inputs, y, cot, gain, out_w.reshape(zsize, rows, width))

time: 590 us -> 582 us (0.986)
  local copies, waits for them, and re-layouts: 31.8 us -> 9.59 us
  waiting for transfers between devices: 5.77 us -> 12 us
    unnamed x64 -> x12, local copies, waits for them, and re-layouts: 27 us -> 4.77 us
    ppermute x4, waiting for transfers between devices: 5.76 us -> 12 us  [hop(): lax.ppermute(a, 'ctx', [(i, i ^ 2 * r) for i in range(lax.axis_size('ctx'...]
  transfers between devices with their start and end apart: 9 -> 9, of which waited for: 1 -> 1; matrix products, arithmetic and copies ran while one was open for 0% -> 1% of each run, Pallas kernels for 32% -> 32%
where the time goes in v7:
time: 582 us; the launch traced here: 576 us
  Pallas kernels  538 us (92%)
  waiting for transfers between devices  12 us (2%)
  starting transfers between devices  10.4 us (2%)
  local copies, waits for them, and re-layouts  9.59 us (2%)
    pallas_call x1, Pallas kernels, tail(): pl.pallas_call(functools.partial(tail_kernel, zsize), out_shape=[shape(ch...  208 us
    pallas_call x1, Pallas kernels, front(): pl.pallas_call(functools.partial(front_kernel, zsize), out_shape=[square,...  130 us
    pallas_call x4, Pallas kernels, ffn_chunk(): pl.pallas_call(functools.partial(ffn_kernel, len(weights), pieces), out_s...  61.5 us
    pallas_call x1, Pallas kernels, attn_bwd(): pl.pallas_call(functools.partial(bwd_kernel, nchip, per), grid_spec=grid_...  47.2 us
    pallas_call x1, Pallas kernels, middle_part(): pl.pallas_call(functools.partial(middle_kernel, counts), out_shape=[jax.S...  34.9 us
    pallas_call x1, Pallas kernels, attn_fwd(): pl.pallas_call(functools.partial(fwd_kernel, nchip, per), grid_spec=grid_...  30.9 us
    pallas_call x1, Pallas kernels, assemble(): pl.pallas_call(kernel, out_shape=[out(rows, ff * zsize), out(rows, ff * z...  13.4 us
    ppermute x4, waiting for transfers between devices, hop(): lax.ppermute(a, 'ctx', [(i, i ^ 2 * r) for i in range(lax.axis_size('ctx'...  12 us
  transfers between devices with their start and end apart: 9, of which 1 were waited for; matrix products, arithmetic and copies ran while one was open for 1% of the time, Pallas kernels for 32%

profile of v7, /device:TPU:0, one launch (start us, length us, event | category | flops | bytes accessed | tf_op | source)
XLA Modules:
  0.0 575.7 jit_solution(15630735491880961704)
XLA Ops:
  0.7 1.3 fusion.9
  2.0 0.6 broadcast_multiply_fusion
  2.6 0.1 convert_bitcast_fusion
  2.7 0.7 stack.9
  3.4 0.7 stack.10
  4.0 0.6 maximum_convert_fusion.refs_2_
  4.6 1.1 multiply_sine_fusion
  5.7 130.4 %front.1 = (bf16[4,4,2,48,1536]{4,3,2,1,0:T(8,128)(2,1)}, bf16[4,4,2,48,1536]{4,3,2,1,0:T(8,128)(2,1)}, bf16[4,4,2,48,1536]{4,3,2,1,0:T(8,128)(2,1)}, bf16[384,1...) custom-call(bf16[2,256,1536]{2,1,0:T(8,128)(2,1)} %refs_0_.1, ...), custom_call_target="tpu_custom_call" | custom-call | tf_op jit(solution)/shard_map/front/pallas_call | solution.py:520
  136.1 1.6 collective-permute-start
  137.7 0.5 collective-permute-start.1
  138.2 0.4 collective-permute-start.4
  138.7 2.5 collective-permute-start.3
  141.2 0.5 collective-permute-start.2
  141.7 0.1 concatenate.11
  141.8 0.6 select_reduce_fusion.inv_ref
  142.4 30.9 %attention_forward.1 = (bf16[1536,512]{1,0:T(8,128)(2,1)}, f32[8,4,1,256]{3,2,1,0:T(1,128)}) custom-call(s32[4]{0:T(128)} %get-tuple-element.162.ids_ref, s32[16]{0:T(128)} %select_reduce_fusion.inv_ref, bf16[1536,512]{1,0:T(8,128)(2,1)} %get-tuple-element.82.q_ref, bf16[768,512]{1,0:T(8,128)(2,1)} %get-tuple-element.83.rest_0_, ...), custom_call_target="tpu_custom_call" | custom-call | tf_op jit(solution)/shard_map/attention_forward/pallas_call | solution.py:135
  173.4 0.6 fusion.11
  174.0 11.3 %bridge.1 = (f32[512,1536]{1,0:T(8,128)}, bf16[1024,1536]{1,0:T(8,128)(2,1)}, bf16[1536,1024]{1,0:T(8,128)(2,1)}, bf16[4,4,48,1024]{3,2,1,0:T(8,128)(2,1)}) custom-call(bf16[4,4,2,48,512]{4,3,2,1,0:T(8,128)(2,1)} %bitcast.21, bf16[1536,1536]{1,0:T(8,128)(2,1)} %bitcast.19, bf16[512,1536]{1,0:T(8,128)(2,1)} %get-tuple-element.93.x.refs_22_, ...), custom_call_target="tpu_custom_call" | custom-call | tf_op jit(solution)/shard_map/bridge/pallas_call | solution.py:1274
  185.3 15.3 %ffn_chunk.4 = (bf16[1024,512]{1,0:T(8,128)(2,1)}, bf16[1024,1024]{1,0:T(8,128)(2,1)}, bf16[4,384,1536]{2,1,0:T(8,128)(2,1)}) custom-call(bf16[1024,1536]{1,0:T(8,128)(2,1)} %get-tuple-element.95.before.second, bf16[1024,1536]{1,0:T(8,128)(2,1)} %get-tuple-element.95.before.second, bf16[1536,1024]{1,0:T(8,128)(2,1)} %get-tuple-element.96.second_t, ...), custom_call_target="tpu_custom_call" | custom-call | tf_op jit(solution)/shard_map/ffn_chunk/pallas_call | solution.py:1043
  200.7 12.0 %collective-permute-done.refs_1_.refs_11_ = bf16[3,384,1536]{2,1,0:T(8,128)(2,1)} collective-permute-done((bf16[3,384,1536]{2,1,0:T(8,128)(2,1)}, bf16[3,384,1536]{2,1,0:T(8,128)(2,1)}, u32[]{:S(2)}, u32[]{:S(2)}) %collective-permute-start) | collective-permute-done | bytes 3538976 | tf_op jit(solution)/shard_map/ppermute | solution.py:1418
  212.6 15.5 %ffn_chunk.5 = (bf16[1024,512]{1,0:T(8,128)(2,1)}, bf16[1024,1024]{1,0:T(8,128)(2,1)}, bf16[4,384,1536]{2,1,0:T(8,128)(2,1)}) custom-call(bf16[1024,512]{1,0:T(8,128)(2,1)} %get-tuple-element.100.before.refs_0_, bf16[1024,1536]{1,0:T(8,128)(2,1)} %get-tuple-element.95.before.second, bf16[1536,1024]{1,0:T(8,128)(2,1)} %get-tuple-element.96.second_t, ...), custom_call_target="tpu_custom_call" | custom-call | tf_op jit(solution)/shard_map/ffn_chunk/pallas_call | solution.py:1043
  228.1 1.3 collective-permute-start.6
  229.5 0.0 collective-permute-done.1.refs_1_.refs_13_
  229.5 15.7 %ffn_chunk.6 = (bf16[1024,512]{1,0:T(8,128)(2,1)}, bf16[1024,1024]{1,0:T(8,128)(2,1)}, bf16[4,384,1536]{2,1,0:T(8,128)(2,1)}) custom-call(bf16[1024,512]{1,0:T(8,128)(2,1)} %get-tuple-element.102.before.refs_1_, bf16[1024,1536]{1,0:T(8,128)(2,1)} %get-tuple-element.95.before.second, bf16[1536,1024]{1,0:T(8,128)(2,1)} %get-tuple-element.96.second_t, ...), custom_call_target="tpu_custom_call" | custom-call | tf_op jit(solution)/shard_map/ffn_chunk/pallas_call | solution.py:1043
  245.2 0.8 collective-permute-start.7
  246.0 0.0 collective-permute-done.4.refs_3_.refs_17_
  246.0 0.0 collective-permute-done.3.refs_2_.refs_16_
  246.0 0.0 collective-permute-done.2.refs_1_.refs_15_
  246.0 1.0 copy-done.3
  247.0 14.9 %ffn_chunk.7 = (bf16[1024,512]{1,0:T(8,128)(2,1)}, bf16[1024,1024]{1,0:T(8,128)(2,1)}, bf16[384,1536]{1,0:T(8,128)(2,1)}, bf16[384,1536]{1,0:T(8,128)(2,1)}, bf1...) custom-call(bf16[1024,512]{1,0:T(8,128)(2,1)} %get-tuple-element.104.before.refs_2_, ...), custom_call_target="tpu_custom_call" | custom-call | flops 51999997952 | tf_op jit(solution)/shard_map/ffn_chunk/pallas_call | solution.py:1043
  262.0 2.3 collective-permute-start.5
  264.2 34.9 %middle.1 = (bf16[2,256,1536]{2,1,0:T(8,128)(2,1)}, f32[512,1536]{1,0:T(8,128)}, bf16[1536,512]{1,0:T(8,128)(2,1)}, bf16[1536,512]{1,0:T(8,128)(2,1)}, f32[1,1536]{1,0:T(1,128)}) custom-call(bf16[1024,512]{1,0:T(8,128)(2,1)} %get-tuple-element.100.before.refs_0_, bf16[1024,512]{1,0:T(8,128)(2,1)} %get-tuple-element.102.before.refs_1_, ...), custom_call_target="tpu_custom_call" | custom-call | tf_op jit(solution)/shard_map/middle/pallas_call | solution.py:1385
  299.1 0.0 collective-permute-done.5
  299.1 1.9 add_convert_fusion.before
  301.0 0.0 copy-start
  301.0 0.4 collective-permute-start.8
  301.4 0.6 copy-done
  302.0 47.2 %attention_backward.1 = (bf16[1536,512]{1,0:T(8,128)(2,1)}, bf16[768,512]{1,0:T(8,128)(2,1)}, bf16[768,512]{1,0:T(8,128)(2,1)}, bf16[768,512]{1,0:T(8,128)(2,1)}...) custom-call(s32[4]{0:T(128)} %get-tuple-element.162.ids_ref, ...), custom_call_target="tpu_custom_call" | custom-call | tf_op jit(solution)/shard_map/attention_backward/pallas_call | solution.py:250
  349.2 0.0 collective-permute-done.8.refs_16_
  349.2 0.0 collective-permute-done.6.refs_14_
  349.2 0.0 collective-permute-done.7.refs_15_
  349.2 208.0 %tail.1 = (bf16[4,2,48,1536]{3,2,1,0:T(8,128)(2,1)}, bf16[4,2,48,1536]{3,2,1,0:T(8,128)(2,1)}, bf16[4,2,48,1536]{3,2,1,0:T(8,128)(2,1)}, bf16[4,2,384,1536]{3,2,...) custom-call(bf16[768,512]{1,0:T(8,128)(2,1)} %get-tuple-element.119.refs_0_, ...), custom_call_target="tpu_custom_call" | custom-call | tf_op jit(solution)/shard_map/tail/pallas_call | solution.py:911
  557.3 0.9 fusion.10
  558.1 0.6 fusion
  558.8 13.4 %assemble.1 = (f32[384,4096]{1,0:T(8,128)}, f32[384,4096]{1,0:T(8,128)}, f32[1024,1536]{1,0:T(8,128)}, f32[384,1536]{1,0:T(8,128)}, f32[384,1536]{1,0:T(8,128)}, /*index=5*/f32[384,768]{1,0:T(8,128)}, f32[384,768]{1,0:T(8,128)}) custom-call(bf16[4,2,384,1536]{3,2,1,0:T(8,128)(2,1)} %get-tuple-element.142.pack, bf16[384,1536]{1,0:T(8,128)(2,1)} %bitcast.26, ...), custom_call_target="tpu_custom_call" | custom-call | tf_op jit(solution)/shard_map/assemble/pallas_call | solution.py:1182
  572.2 1.1 copy.25
  573.3 0.8 copy-done.2
  574.1 1.1 copy.26
  (7 shorter events, 0.0 us)
Async XLA Ops:
  136.1 76.5 %collective-permute-start = (bf16[3,384,1536]{2,1,0:T(8,128)(2,1)}, bf16[3,384,1536]{2,1,0:T(8,128)(2,1)}, u32[]{:S(2)}, u32[]{:S(2)}) collective-permute-start(bf16[3,384,1536]{2,1,0:T(8,128)(2,1)} %get-tuple-element.99.refs_1_.refs_9_), channel_id=1, source_target_pairs={{0,8},{4,12},{8,0},{12,4},{16,24},{20,28},{24,16},{28,20},{1,9},{5... | collective-permute-start | bytes 10616840 | tf_op jit(solution)/shard_map/ppermute | solution.py:1418
  137.7 91.8 %collective-permute-start.1 = (bf16[3,384,1536]{2,1,0:T(8,128)(2,1)}, bf16[3,384,1536]{2,1,0:T(8,128)(2,1)}, u32[]{:S(2)}, u32[]{:S(2)}) collective-permute-start(bf16[3,384,1536]{2,1,0:T(8,128)(2,1)} %get-tuple-element.99.refs_1_.refs_9_), channel_id=1, source_target_pairs={{0,16},{4,20},{8,24},{12,28},{16,0},{20,4},{24,8},{28,12},{1,17},{... | collective-permute-start | bytes 10616840 | tf_op jit(solution)/shard_map/ppermute | solution.py:1418
  138.2 107.8 %collective-permute-start.4 = (bf16[384,1536]{1,0:T(8,128)(2,1)}, bf16[384,1536]{1,0:T(8,128)(2,1)S(1)}, u32[]{:S(2)}, u32[]{:S(2)}) collective-permute-start(bf16[384,1536]{1,0:T(8,128)(2,1)} %get-tuple-element.105.refs_0_.refs_14_), channel_id=1, source_target_pairs={{0,3},{1,0},{2,1},{3,2},{4,7},{5,4},{6,5},{7,6},{8,11},{9,8},{10,9... | collective-permute-start | bytes 3538952 | tf_op jit(solution)/shard_map/ppermute | solution.py:1436
  138.7 107.3 %collective-permute-start.3 = (bf16[384,1536]{1,0:T(8,128)(2,1)}, bf16[384,1536]{1,0:T(8,128)(2,1)}, u32[]{:S(2)}, u32[]{:S(2)}) collective-permute-start(bf16[384,1536]{1,0:T(8,128)(2,1)} %get-tuple-element.105.refs_0_.refs_14_), channel_id=1, source_target_pairs={{0,2},{1,3},{2,0},{3,1},{4,6},{5,7},{6,4},{7,5},{8,10},{9,11},{10,... | collective-permute-start | bytes 3538952 | tf_op jit(solution)/shard_map/ppermute | solution.py:1436
  141.2 104.8 %collective-permute-start.2 = (bf16[384,1536]{1,0:T(8,128)(2,1)}, bf16[384,1536]{1,0:T(8,128)(2,1)}, u32[]{:S(2)}, u32[]{:S(2)}) collective-permute-start(bf16[384,1536]{1,0:T(8,128)(2,1)} %get-tuple-element.105.refs_0_.refs_14_), channel_id=1, source_target_pairs={{0,1},{1,2},{2,3},{3,0},{4,5},{5,6},{6,7},{7,4},{8,9},{9,10},{10,1... | collective-permute-start | bytes 3538952 | tf_op jit(solution)/shard_map/ppermute | solution.py:1436
  142.4 30.9 %copy-start.4 = (f32[2,1536]{1,0:T(2,128)S(1)}, f32[2,1536]{1,0:T(2,128)}, u32[]{:S(2)}) copy-start(f32[2,1536]{1,0:T(2,128)} %get-tuple-element.94) | copy-start | bytes 36868
  228.1 121.1 %collective-permute-start.6 = (bf16[4,384,1536]{2,1,0:T(8,128)(2,1)}, bf16[4,384,1536]{2,1,0:T(8,128)(2,1)}, u32[]{:S(2)}, u32[]{:S(2)}) collective-permute-start(bf16[4,384,1536]{2,1,0:T(8,128)(2,1)} %get-tuple-element.131), channel_id=1, source_target_pairs={{0,8},{4,12},{8,0},{12,4},{16,24},{20,28},{24,16},{28,20},{1,9},{5... | collective-permute-start | bytes 14155784 | tf_op jit(solution)/shard_map/ppermute | solution.py:1418
  245.2 104.1 %collective-permute-start.7 = (bf16[4,384,1536]{2,1,0:T(8,128)(2,1)}, bf16[4,384,1536]{2,1,0:T(8,128)(2,1)}, u32[]{:S(2)}, u32[]{:S(2)}) collective-permute-start(bf16[4,384,1536]{2,1,0:T(8,128)(2,1)} %get-tuple-element.132), channel_id=1, source_target_pairs={{0,16},{4,20},{8,24},{12,28},{16,0},{20,4},{24,8},{28,12},{1,17},{... | collective-permute-start | bytes 14155784 | tf_op jit(solution)/shard_map/ppermute | solution.py:1418
  246.0 1.0 copy-start.3
  262.0 37.1 %collective-permute-start.5 = (bf16[384,1536]{1,0:T(8,128)(2,1)}, bf16[384,1536]{1,0:T(8,128)(2,1)}, u32[]{:S(2)}, u32[]{:S(2)}) collective-permute-start(bf16[384,1536]{1,0:T(8,128)(2,1)} %get-tuple-element.115), channel_id=1, source_target_pairs={{0,1},{1,2},{2,3},{3,0},{4,5},{5,6},{6,7},{7,4},{8,9},{9,10},{10,1... | collective-permute-start | bytes 3538952 | tf_op jit(solution)/shard_map/ppermute | solution.py:1436
  301.0 1.0 copy-start
  301.0 48.2 %collective-permute-start.8 = (bf16[384,1536]{1,0:T(8,128)(2,1)S(1)}, bf16[384,1536]{1,0:T(8,128)(2,1)}, u32[]{:S(2)}, u32[]{:S(2)}) collective-permute-start(bf16[384,1536]{1,0:T(8,128)(2,1)S(1)} %add_convert_fusion.before), channel_id=1, source_target_pairs={{0,1},{1,2},{2,3},{3,0},{4,5},{5,6},{6,7},{7,4},{8,9},{9,10},{10,1... | collective-permute-start | bytes 3538952 | tf_op jit(solution)/shard_map/ppermute | solution.py:1436
  558.8 13.4 %copy-start.1 = (bf16[2,256,1536]{2,1,0:T(8,128)(2,1)S(1)}, bf16[2,256,1536]{2,1,0:T(8,128)(2,1)}, u32[]{:S(2)}) copy-start(bf16[2,256,1536]{2,1,0:T(8,128)(2,1)} %get-tuple-element.182) | copy-start | bytes 4718596
  572.2 2.0 copy-start.2

commit v8 on v7

--- a/solution.py
+++ b/solution.py
@@ -97,7 +97,7 @@
             acc[h, sl][late] = o
         return 0
 
-    lax.fori_loop(0, nb + 1, step, 0)
+    lax.fori_loop(0, nb + 1, step, 0, unroll=2)
     for h, sl in chains:
         for half in range(2):
             lanes = slice(BLK * (2 * sl + half), BLK * (2 * sl + half + 1))
@@ -198,7 +198,7 @@
             dq_s[h, sl][late] += d
         return 0
 
-    lax.fori_loop(0, nb + 1, step, 0)
+    lax.fori_loop(0, nb + 1, step, 0, unroll=2)
     for h, sl in chains:
         for half in range(2):
             lanes = slice(BLK * (2 * sl + half), BLK * (2 * sl + half + 1))
@@ -1146,7 +1146,7 @@
                 at = slice((part * 8 + c * 4 + p) * fine, (part * 8 + c * 4 + p + 1) * fine)
                 gate_o[:, at] = wide[p, c, :, part * fine:(part + 1) * fine].astype(F32)
                 up_o[:, at] = wide[p, c, :, (zsize + part) * fine:(zsize + part + 1) * fine].astype(F32)
-    for p in range(2):
+    for p in range(tall.shape[0]):
         for n in range(folds):
             down_o[p * fine:(p + 1) * fine, n * fold:(n + 1) * fold] = tall[p, 0, n * fine:(n + 1) * fine].astype(F32)
     o_o[...] = o[...].astype(F32)
@@ -1158,7 +1158,7 @@
 def assemble(packs, o, q, kv, zsize, fine):
     chips, cores, rows, packed = packs.shape
     width = o.shape[1]
-    steps = 4
+    steps = chips * cores
     block = rows // steps
     two = 2 * fine * zsize
     fold = packed - two
@@ -1173,7 +1173,7 @@
             grid=(steps,),
             in_specs=[
                 pl.BlockSpec((chips, cores, block, two), lambda i: (0, 0, i, 0)),
-                pl.BlockSpec((2, 1, rows, fold), lambda i: (i % 2, i // 2, 0, two // fold)),
+                pl.BlockSpec((1, 1, rows, fold), lambda i: (i % chips, i // chips, 0, two // fold)),
                 flat(width), flat(width), flat(width),
             ],
             out_specs=[flat(ff * zsize), flat(ff * zsize), pl.BlockSpec((ff // steps, width), lambda i: (i, 0)), flat(width), flat(width), flat(width // 2), flat(width // 2)],

time: 582 us -> 581 us (level)
  no operation moved by 1% of the time
where the time goes in v8:
time: 581 us; the launch traced here: 575 us
  Pallas kernels  535 us (92%)
  waiting for transfers between devices  13.9 us (2%)
  starting transfers between devices  10.4 us (2%)
  local copies, waits for them, and re-layouts  9.59 us (2%)
    pallas_call x1, Pallas kernels, tail(): pl.pallas_call(functools.partial(tail_kernel, zsize), out_shape=[shape(ch...  208 us
    pallas_call x1, Pallas kernels, front(): pl.pallas_call(functools.partial(front_kernel, zsize), out_shape=[square,...  130 us
    pallas_call x4, Pallas kernels, ffn_chunk(): pl.pallas_call(functools.partial(ffn_kernel, len(weights), pieces), out_s...  61.5 us
    pallas_call x1, Pallas kernels, attn_bwd(): pl.pallas_call(functools.partial(bwd_kernel, nchip, per), grid_spec=grid_...  45 us
    pallas_call x1, Pallas kernels, middle_part(): pl.pallas_call(functools.partial(middle_kernel, counts), out_shape=[jax.S...  34.9 us
    pallas_call x1, Pallas kernels, attn_fwd(): pl.pallas_call(functools.partial(fwd_kernel, nchip, per), grid_spec=grid_...  29 us
    pallas_call x1, Pallas kernels, assemble(): pl.pallas_call(kernel, out_shape=[out(rows, ff * zsize), out(rows, ff * z...  14.5 us
    ppermute x4, waiting for transfers between devices, hop(): lax.ppermute(a, 'ctx', [(i, i ^ 2 * r) for i in range(lax.axis_size('ctx'...  13.9 us
  transfers between devices with their start and end apart: 9, of which 1 were waited for; matrix products, arithmetic and copies ran while one was open for 1% of the time, Pallas kernels for 32%

profile of v8, /device:TPU:0, one launch (start us, length us, event | category | flops | bytes accessed | tf_op | source)
XLA Modules:
  0.0 574.7 jit_solution(15465807143612193587)
XLA Ops:
  0.7 1.3 fusion.9
  2.0 0.6 broadcast_multiply_fusion
  2.6 0.1 convert_bitcast_fusion
  2.7 0.7 stack.9
  3.4 0.7 stack.10
  4.0 0.6 maximum_convert_fusion.refs_2_
  4.6 1.1 multiply_sine_fusion
  5.7 130.4 %front.1 = (bf16[4,4,2,48,1536]{4,3,2,1,0:T(8,128)(2,1)}, bf16[4,4,2,48,1536]{4,3,2,1,0:T(8,128)(2,1)}, bf16[4,4,2,48,1536]{4,3,2,1,0:T(8,128)(2,1)}, bf16[384,1...) custom-call(bf16[2,256,1536]{2,1,0:T(8,128)(2,1)} %refs_0_.1, ...), custom_call_target="tpu_custom_call" | custom-call | tf_op jit(solution)/shard_map/front/pallas_call | solution.py:520
  136.1 1.6 collective-permute-start
  137.7 0.5 collective-permute-start.1
  138.2 0.4 collective-permute-start.4
  138.7 2.5 collective-permute-start.3
  141.2 0.5 collective-permute-start.2
  141.7 0.1 concatenate.11
  141.8 0.6 select_reduce_fusion.inv_ref
  142.4 29.0 %attention_forward.1 = (bf16[1536,512]{1,0:T(8,128)(2,1)}, f32[8,4,1,256]{3,2,1,0:T(1,128)}) custom-call(s32[4]{0:T(128)} %get-tuple-element.162.ids_ref, s32[16]{0:T(128)} %select_reduce_fusion.inv_ref, bf16[1536,512]{1,0:T(8,128)(2,1)} %get-tuple-element.82.q_ref, bf16[768,512]{1,0:T(8,128)(2,1)} %get-tuple-element.83.rest_0_, ...), custom_call_target="tpu_custom_call" | custom-call | tf_op jit(solution)/shard_map/attention_forward/pallas_call | solution.py:135
  171.5 0.6 fusion.11
  172.1 11.3 %bridge.1 = (f32[512,1536]{1,0:T(8,128)}, bf16[1024,1536]{1,0:T(8,128)(2,1)}, bf16[1536,1024]{1,0:T(8,128)(2,1)}, bf16[4,4,48,1024]{3,2,1,0:T(8,128)(2,1)}) custom-call(bf16[4,4,2,48,512]{4,3,2,1,0:T(8,128)(2,1)} %bitcast.21, bf16[1536,1536]{1,0:T(8,128)(2,1)} %bitcast.19, bf16[512,1536]{1,0:T(8,128)(2,1)} %get-tuple-element.93.x.refs_22_, ...), custom_call_target="tpu_custom_call" | custom-call | tf_op jit(solution)/shard_map/bridge/pallas_call | solution.py:1274
  183.4 15.3 %ffn_chunk.4 = (bf16[1024,512]{1,0:T(8,128)(2,1)}, bf16[1024,1024]{1,0:T(8,128)(2,1)}, bf16[4,384,1536]{2,1,0:T(8,128)(2,1)}) custom-call(bf16[1024,1536]{1,0:T(8,128)(2,1)} %get-tuple-element.95.before.second, bf16[1024,1536]{1,0:T(8,128)(2,1)} %get-tuple-element.95.before.second, bf16[1536,1024]{1,0:T(8,128)(2,1)} %get-tuple-element.96.second_t, ...), custom_call_target="tpu_custom_call" | custom-call | tf_op jit(solution)/shard_map/ffn_chunk/pallas_call | solution.py:1043
  198.7 13.9 %collective-permute-done.refs_1_.refs_11_ = bf16[3,384,1536]{2,1,0:T(8,128)(2,1)} collective-permute-done((bf16[3,384,1536]{2,1,0:T(8,128)(2,1)}, bf16[3,384,1536]{2,1,0:T(8,128)(2,1)}, u32[]{:S(2)}, u32[]{:S(2)}) %collective-permute-start) | collective-permute-done | bytes 3538976 | tf_op jit(solution)/shard_map/ppermute | solution.py:1418
  212.6 15.5 %ffn_chunk.5 = (bf16[1024,512]{1,0:T(8,128)(2,1)}, bf16[1024,1024]{1,0:T(8,128)(2,1)}, bf16[4,384,1536]{2,1,0:T(8,128)(2,1)}) custom-call(bf16[1024,512]{1,0:T(8,128)(2,1)} %get-tuple-element.100.before.refs_0_, bf16[1024,1536]{1,0:T(8,128)(2,1)} %get-tuple-element.95.before.second, bf16[1536,1024]{1,0:T(8,128)(2,1)} %get-tuple-element.96.second_t, ...), custom_call_target="tpu_custom_call" | custom-call | tf_op jit(solution)/shard_map/ffn_chunk/pallas_call | solution.py:1043
  228.1 1.3 collective-permute-start.6
  229.5 0.0 collective-permute-done.1.refs_1_.refs_13_
  229.5 15.7 %ffn_chunk.6 = (bf16[1024,512]{1,0:T(8,128)(2,1)}, bf16[1024,1024]{1,0:T(8,128)(2,1)}, bf16[4,384,1536]{2,1,0:T(8,128)(2,1)}) custom-call(bf16[1024,512]{1,0:T(8,128)(2,1)} %get-tuple-element.102.before.refs_1_, bf16[1024,1536]{1,0:T(8,128)(2,1)} %get-tuple-element.95.before.second, bf16[1536,1024]{1,0:T(8,128)(2,1)} %get-tuple-element.96.second_t, ...), custom_call_target="tpu_custom_call" | custom-call | tf_op jit(solution)/shard_map/ffn_chunk/pallas_call | solution.py:1043
  245.2 0.8 collective-permute-start.7
  246.0 0.0 collective-permute-done.4.refs_3_.refs_17_
  246.0 0.0 collective-permute-done.3.refs_2_.refs_16_
  246.0 0.0 collective-permute-done.2.refs_1_.refs_15_
  246.0 1.0 copy-done.3
  247.0 14.9 %ffn_chunk.7 = (bf16[1024,512]{1,0:T(8,128)(2,1)}, bf16[1024,1024]{1,0:T(8,128)(2,1)}, bf16[384,1536]{1,0:T(8,128)(2,1)}, bf16[384,1536]{1,0:T(8,128)(2,1)}, bf1...) custom-call(bf16[1024,512]{1,0:T(8,128)(2,1)} %get-tuple-element.104.before.refs_2_, ...), custom_call_target="tpu_custom_call" | custom-call | flops 51999997952 | tf_op jit(solution)/shard_map/ffn_chunk/pallas_call | solution.py:1043
  262.0 2.3 collective-permute-start.5
  264.2 34.9 %middle.1 = (bf16[2,256,1536]{2,1,0:T(8,128)(2,1)}, f32[512,1536]{1,0:T(8,128)}, bf16[1536,512]{1,0:T(8,128)(2,1)}, bf16[1536,512]{1,0:T(8,128)(2,1)}, f32[1,1536]{1,0:T(1,128)}) custom-call(bf16[1024,512]{1,0:T(8,128)(2,1)} %get-tuple-element.100.before.refs_0_, bf16[1024,512]{1,0:T(8,128)(2,1)} %get-tuple-element.102.before.refs_1_, ...), custom_call_target="tpu_custom_call" | custom-call | tf_op jit(solution)/shard_map/middle/pallas_call | solution.py:1385
  299.1 0.0 collective-permute-done.5
  299.1 1.9 add_convert_fusion.before
  301.0 0.0 copy-start
  301.0 0.4 collective-permute-start.8
  301.4 0.6 copy-done
  302.0 45.0 %attention_backward.1 = (bf16[1536,512]{1,0:T(8,128)(2,1)}, bf16[768,512]{1,0:T(8,128)(2,1)}, bf16[768,512]{1,0:T(8,128)(2,1)}, bf16[768,512]{1,0:T(8,128)(2,1)}...) custom-call(s32[4]{0:T(128)} %get-tuple-element.162.ids_ref, ...), custom_call_target="tpu_custom_call" | custom-call | tf_op jit(solution)/shard_map/attention_backward/pallas_call | solution.py:250
  347.1 0.0 collective-permute-done.8.refs_16_
  347.1 0.0 collective-permute-done.6.refs_14_
  347.1 0.0 collective-permute-done.7.refs_15_
  347.1 207.9 %tail.1 = (bf16[4,2,48,1536]{3,2,1,0:T(8,128)(2,1)}, bf16[4,2,48,1536]{3,2,1,0:T(8,128)(2,1)}, bf16[4,2,48,1536]{3,2,1,0:T(8,128)(2,1)}, bf16[4,2,384,1536]{3,2,...) custom-call(bf16[768,512]{1,0:T(8,128)(2,1)} %get-tuple-element.119.refs_0_, ...), custom_call_target="tpu_custom_call" | custom-call | tf_op jit(solution)/shard_map/tail/pallas_call | solution.py:911
  555.0 0.9 fusion.10
  555.9 0.6 fusion
  556.5 14.5 %assemble.1 = (f32[384,4096]{1,0:T(8,128)}, f32[384,4096]{1,0:T(8,128)}, f32[1024,1536]{1,0:T(8,128)}, f32[384,1536]{1,0:T(8,128)}, f32[384,1536]{1,0:T(8,128)}, /*index=5*/f32[384,768]{1,0:T(8,128)}, f32[384,768]{1,0:T(8,128)}) custom-call(bf16[4,2,384,1536]{3,2,1,0:T(8,128)(2,1)} %get-tuple-element.142.pack, bf16[384,1536]{1,0:T(8,128)(2,1)} %bitcast.26, ...), custom_call_target="tpu_custom_call" | custom-call | tf_op jit(solution)/shard_map/assemble/pallas_call | solution.py:1182
  571.1 1.1 copy.25
  572.2 0.8 copy-done.2
  573.1 1.1 copy.26
  (7 shorter events, 0.0 us)
Async XLA Ops:
  136.1 76.5 %collective-permute-start = (bf16[3,384,1536]{2,1,0:T(8,128)(2,1)}, bf16[3,384,1536]{2,1,0:T(8,128)(2,1)}, u32[]{:S(2)}, u32[]{:S(2)}) collective-permute-start(bf16[3,384,1536]{2,1,0:T(8,128)(2,1)} %get-tuple-element.99.refs_1_.refs_9_), channel_id=1, source_target_pairs={{0,8},{4,12},{8,0},{12,4},{16,24},{20,28},{24,16},{28,20},{1,9},{5... | collective-permute-start | bytes 10616840 | tf_op jit(solution)/shard_map/ppermute | solution.py:1418
  137.7 91.8 %collective-permute-start.1 = (bf16[3,384,1536]{2,1,0:T(8,128)(2,1)}, bf16[3,384,1536]{2,1,0:T(8,128)(2,1)}, u32[]{:S(2)}, u32[]{:S(2)}) collective-permute-start(bf16[3,384,1536]{2,1,0:T(8,128)(2,1)} %get-tuple-element.99.refs_1_.refs_9_), channel_id=1, source_target_pairs={{0,16},{4,20},{8,24},{12,28},{16,0},{20,4},{24,8},{28,12},{1,17},{... | collective-permute-start | bytes 10616840 | tf_op jit(solution)/shard_map/ppermute | solution.py:1418
  138.2 107.8 %collective-permute-start.4 = (bf16[384,1536]{1,0:T(8,128)(2,1)}, bf16[384,1536]{1,0:T(8,128)(2,1)S(1)}, u32[]{:S(2)}, u32[]{:S(2)}) collective-permute-start(bf16[384,1536]{1,0:T(8,128)(2,1)} %get-tuple-element.105.refs_0_.refs_14_), channel_id=1, source_target_pairs={{0,3},{1,0},{2,1},{3,2},{4,7},{5,4},{6,5},{7,6},{8,11},{9,8},{10,9... | collective-permute-start | bytes 3538952 | tf_op jit(solution)/shard_map/ppermute | solution.py:1436
  138.7 107.3 %collective-permute-start.3 = (bf16[384,1536]{1,0:T(8,128)(2,1)}, bf16[384,1536]{1,0:T(8,128)(2,1)}, u32[]{:S(2)}, u32[]{:S(2)}) collective-permute-start(bf16[384,1536]{1,0:T(8,128)(2,1)} %get-tuple-element.105.refs_0_.refs_14_), channel_id=1, source_target_pairs={{0,2},{1,3},{2,0},{3,1},{4,6},{5,7},{6,4},{7,5},{8,10},{9,11},{10,... | collective-permute-start | bytes 3538952 | tf_op jit(solution)/shard_map/ppermute | solution.py:1436
  141.2 104.8 %collective-permute-start.2 = (bf16[384,1536]{1,0:T(8,128)(2,1)}, bf16[384,1536]{1,0:T(8,128)(2,1)}, u32[]{:S(2)}, u32[]{:S(2)}) collective-permute-start(bf16[384,1536]{1,0:T(8,128)(2,1)} %get-tuple-element.105.refs_0_.refs_14_), channel_id=1, source_target_pairs={{0,1},{1,2},{2,3},{3,0},{4,5},{5,6},{6,7},{7,4},{8,9},{9,10},{10,1... | collective-permute-start | bytes 3538952 | tf_op jit(solution)/shard_map/ppermute | solution.py:1436
  142.4 29.0 %copy-start.4 = (f32[2,1536]{1,0:T(2,128)S(1)}, f32[2,1536]{1,0:T(2,128)}, u32[]{:S(2)}) copy-start(f32[2,1536]{1,0:T(2,128)} %get-tuple-element.94) | copy-start | bytes 36868
  228.1 118.9 %collective-permute-start.6 = (bf16[4,384,1536]{2,1,0:T(8,128)(2,1)}, bf16[4,384,1536]{2,1,0:T(8,128)(2,1)}, u32[]{:S(2)}, u32[]{:S(2)}) collective-permute-start(bf16[4,384,1536]{2,1,0:T(8,128)(2,1)} %get-tuple-element.131), channel_id=1, source_target_pairs={{0,8},{4,12},{8,0},{12,4},{16,24},{20,28},{24,16},{28,20},{1,9},{5... | collective-permute-start | bytes 14155784 | tf_op jit(solution)/shard_map/ppermute | solution.py:1418
  245.2 101.9 %collective-permute-start.7 = (bf16[4,384,1536]{2,1,0:T(8,128)(2,1)}, bf16[4,384,1536]{2,1,0:T(8,128)(2,1)}, u32[]{:S(2)}, u32[]{:S(2)}) collective-permute-start(bf16[4,384,1536]{2,1,0:T(8,128)(2,1)} %get-tuple-element.132), channel_id=1, source_target_pairs={{0,16},{4,20},{8,24},{12,28},{16,0},{20,4},{24,8},{28,12},{1,17},{... | collective-permute-start | bytes 14155784 | tf_op jit(solution)/shard_map/ppermute | solution.py:1418
  246.0 1.0 copy-start.3
  262.0 37.1 %collective-permute-start.5 = (bf16[384,1536]{1,0:T(8,128)(2,1)}, bf16[384,1536]{1,0:T(8,128)(2,1)}, u32[]{:S(2)}, u32[]{:S(2)}) collective-permute-start(bf16[384,1536]{1,0:T(8,128)(2,1)} %get-tuple-element.115), channel_id=1, source_target_pairs={{0,1},{1,2},{2,3},{3,0},{4,5},{5,6},{6,7},{7,4},{8,9},{9,10},{10,1... | collective-permute-start | bytes 3538952 | tf_op jit(solution)/shard_map/ppermute | solution.py:1436
  301.0 1.0 copy-start
  301.0 46.0 %collective-permute-start.8 = (bf16[384,1536]{1,0:T(8,128)(2,1)S(1)}, bf16[384,1536]{1,0:T(8,128)(2,1)}, u32[]{:S(2)}, u32[]{:S(2)}) collective-permute-start(bf16[384,1536]{1,0:T(8,128)(2,1)S(1)} %add_convert_fusion.before), channel_id=1, source_target_pairs={{0,1},{1,2},{2,3},{3,0},{4,5},{5,6},{6,7},{7,4},{8,9},{9,10},{10,1... | collective-permute-start | bytes 3538952 | tf_op jit(solution)/shard_map/ppermute | solution.py:1436
  556.5 14.5 %copy-start.1 = (bf16[2,256,1536]{2,1,0:T(8,128)(2,1)S(1)}, bf16[2,256,1536]{2,1,0:T(8,128)(2,1)}, u32[]{:S(2)}) copy-start(bf16[2,256,1536]{2,1,0:T(8,128)(2,1)} %get-tuple-element.182) | copy-start | bytes 4718596
  571.1 2.0 copy-start.2
